TPU v7x, 32 devices: a whole 2x2x4 slice. The times are simulated.
32 devices in a mesh: dp: 8 (over z, x), row: 4 (over y, core).
Axes of the slice: x: 2, y: 2, z: 4, core: 2. Of those that a mesh axis runs over, the one named last changes fastest.
Arguments:
- patches: bfloat16 [2, 8, 48, 96, 384], P(None, 'dp', 'row'), may hold values from -6 to 6
- unpadded_patch_size: int32 [2, 8, 2], P(None, 'dp'), may hold values from 37 to 96, as said below
- patch_expert_index: int32 [2, 8, 48, 96, 1], P(None, 'dp', 'row'), may hold values from 0 to 15
- cotangent: bfloat16 [2, 8, 24, 48, 768], P(None, 'dp', 'row'), may hold values from -6 to 6
- query_key_value_weight: bfloat16 [384, 1152], P('dp'), may hold values from -0.3125 to 0.3125
- query_projection_bias: float32 [384], replicated, may hold values from -3 to 3
- value_projection_bias: float32 [384], replicated, may hold values from -3 to 3
- log_cosine_scale: float32 [12], replicated, may hold values from 1.6 to 3
- bias_network_first_weight: float32 [2, 512], replicated, may hold values from -4 to 4
- bias_network_first_bias: float32 [512], replicated, may hold values from -3 to 3
- bias_network_second_weight: float32 [512, 12], replicated, may hold values from -0.125 to 0.125
- output_projection_weight: bfloat16 [384, 384], P('dp'), may hold values from -0.3125 to 0.3125
- output_projection_bias: float32 [384], replicated, may hold values from -3 to 3
- attention_norm_gain: float32 [384], replicated, may hold values from 0.5 to 1.5
- attention_norm_bias: float32 [384], replicated, may hold values from -3 to 3
- routing_weight: bfloat16 [384, 16], P('dp'), may hold values from -0.15625 to 0.15625
- expert_first_weight: bfloat16 [16, 384, 1536], P('dp'), may hold values from -0.3125 to 0.3125
- expert_first_bias: float32 [16, 1536], P('dp'), may hold values from -0.625 to 0.625
- expert_second_weight: bfloat16 [16, 1536, 384], P('dp'), may hold values from -0.15625 to 0.15625
- expert_second_bias: float32 [16, 384], P('dp'), may hold values from -0.625 to 0.625
- expert_norm_gain: float32 [384], replicated, may hold values from 0.5 to 1.5
- expert_norm_bias: float32 [384], replicated, may hold values from -3 to 3
- patch_merging_weight: bfloat16 [1536, 768], P('dp'), may hold values from -0.15625 to 0.15625
- merging_norm_gain: float32 [768], replicated, may hold values from 0.5 to 1.5
- merging_norm_bias: float32 [768], replicated, may hold values from -3 to 3
Outputs:
- merged_out: bfloat16 [2, 8, 24, 48, 768], P(None, 'dp', 'row')
- patches_grad: bfloat16 [2, 8, 48, 96, 384], P(None, 'dp', 'row')
- qkv_weight_grad: float32 [384, 1152], P('dp')
- query_bias_grad: float32 [384], replicated
- value_bias_grad: float32 [384], replicated
- logit_scale_grad: float32 [12], replicated
- cpb_first_grad: float32 [2, 512], replicated
- cpb_first_bias_grad: float32 [512], replicated
- cpb_second_grad: float32 [512, 12], replicated
- proj_weight_grad: float32 [384, 384], P('dp')
- proj_bias_grad: float32 [384], replicated
- attn_gain_grad: float32 [384], replicated
- attn_shift_grad: float32 [384], replicated
- router_weight_grad: float32 [384, 16], P('dp')
- expert_in_grad: float32 [16, 384, 1536], P('dp')
- expert_in_bias_grad: float32 [16, 1536], P('dp')
- expert_out_grad: float32 [16, 1536, 384], P('dp')
- expert_out_bias_grad: float32 [16, 384], P('dp')
- moe_gain_grad: float32 [384], replicated
- moe_shift_grad: float32 [384], replicated
- merge_weight_grad: float32 [1536, 768], P('dp')
- merge_gain_grad: float32 [768], replicated
- merge_shift_grad: float32 [768], replicated
Inputs may be any that keep to these rules, and one draw needn't show every extreme that they name: `unpadded_patch_size`: valid rows lie within the last 12 rows of 48, valid columns within the last 12 columns of 96; the first image of each micro-batch is whole.
All inputs are finite; a program needn't handle non-finite values.
Results may differ from a plain program's by a relative error of at most 0.028.
Values may be sent and summed in bfloat16 or wider, within the bound.
No kernel may reach another device: no remote copies, remote signals or barrier semaphores. Data moves between devices by JAX's collectives and lax.ppermute only.
A program may use at most 320 MiB of HBM per device.

v0:
```python
import jax
import jax.numpy as jnp
from jax import lax
from jax.sharding import PartitionSpec as P

HEAD_COUNT = 12
HEAD_DIM = 32
WINDOW_SIDE = 12


PRECISION_HIGH = lax.Precision.HIGHEST
EPS_NORM = 1e-05
EPS_UNIT = 1e-06
MASK_FILL = -100.0


def passed_along(array, axis, by):
    count = lax.axis_size(axis)
    return lax.ppermute(array, axis, [(i, (i + by) % count) for i in range(count)])


def layer_norm(values, gain_vec, shift_vec):
    centred = values - jnp.mean(values, -1, keepdims=True)
    spread = jnp.mean(centred * centred, -1, keepdims=True)
    return centred * lax.rsqrt(spread + EPS_NORM) * gain_vec + shift_vec


def exact_error_gelu(values):
    return jax.nn.gelu(values, approximate=False)


def relative_position_bias(
    bias_network_first_weight, bias_network_first_bias, bias_network_second_weight
):
    span_axis = (jnp.arange(2 * WINDOW_SIDE - 1, dtype=jnp.float32) - (WINDOW_SIDE - 1)) * (
        8.0 / (WINDOW_SIDE - 1)
    )
    span_axis = jnp.sign(span_axis) * jnp.log2(jnp.abs(span_axis) + 1.0) / 3.0
    grid_rows = jnp.broadcast_to(span_axis[:, None], (2 * WINDOW_SIDE - 1, 2 * WINDOW_SIDE - 1))
    relative_coordinates = jnp.stack([grid_rows, grid_rows.T], -1)
    hidden_activation = exact_error_gelu(
        jnp.einsum(
            "plr,rt->plt", relative_coordinates, bias_network_first_weight, precision=PRECISION_HIGH
        )
        + bias_network_first_bias
    )
    bias_network_table = 16.0 * jax.nn.sigmoid(
        jnp.einsum(
            "qvw,wk->qvk", hidden_activation, bias_network_second_weight, precision=PRECISION_HIGH
        )
    )
    offsets = (
        jnp.arange(WINDOW_SIDE)[:, None] - jnp.arange(WINDOW_SIDE)[None, :] + (WINDOW_SIDE - 1)
    )
    select_rows = (offsets[:, :, None] == jnp.arange(2 * WINDOW_SIDE - 1)[None, None, :]).astype(
        jnp.float32
    )
    expert_combine = jnp.einsum(
        "fqy,uzs,ysr->rfuqz", select_rows, select_rows, bias_network_table, precision=PRECISION_HIGH
    )
    return expert_combine.reshape(
        bias_network_table.shape[-1], WINDOW_SIDE * WINDOW_SIDE, WINDOW_SIDE * WINDOW_SIDE
    )


def window_mask(row_start, total_rows, total_cols, valid_rows, valid_cols):
    half_win = WINDOW_SIDE // 2
    rows_at = row_start + jnp.arange(WINDOW_SIDE)
    cols_at = jnp.arange(total_cols)
    row_zone = (rows_at >= total_rows - WINDOW_SIDE).astype(jnp.int32) + (
        rows_at >= total_rows - half_win
    ).astype(jnp.int32)
    col_zone = (cols_at >= total_cols - WINDOW_SIDE).astype(jnp.int32) + (
        cols_at >= total_cols - half_win
    ).astype(jnp.int32)
    zone_ids = 3 * row_zone[:, None] + col_zone[None, :]
    inside = ((rows_at + half_win) % total_rows < valid_rows)[:, None] & (
        (cols_at + half_win) % total_cols < valid_cols
    )[None, :]
    win_count = total_cols // WINDOW_SIDE
    zone_ids = (
        zone_ids.reshape(WINDOW_SIDE, win_count, WINDOW_SIDE)
        .transpose(1, 0, 2)
        .reshape(win_count, WINDOW_SIDE * WINDOW_SIDE)
    )
    inside = (
        inside.reshape(WINDOW_SIDE, win_count, WINDOW_SIDE)
        .transpose(1, 0, 2)
        .reshape(win_count, WINDOW_SIDE * WINDOW_SIDE)
    )
    return jnp.where(zone_ids[:, :, None] != zone_ids[:, None, :], MASK_FILL, 0.0) + jnp.where(
        inside[:, None, :], 0.0, MASK_FILL
    )


def directions(query_raw, key_raw, log_cosine_scale):
    query_unit = query_raw * lax.rsqrt(jnp.sum(query_raw * query_raw, -1, keepdims=True) + EPS_UNIT)
    key_unit = key_raw * lax.rsqrt(jnp.sum(key_raw * key_raw, -1, keepdims=True) + EPS_UNIT)
    return (query_unit * jnp.exp(log_cosine_scale)[:, None], key_unit)


def route_tables(token_experts, experts, capacity):
    selected_expert = (token_experts[:, None] == jnp.arange(experts)[None, :]).astype(jnp.float32)
    slot_index = jnp.sum(selected_expert * (jnp.cumsum(selected_expert, 0) - 1.0), -1)
    slot_hit = (slot_index[:, None] == jnp.arange(capacity)[None, :].astype(jnp.float32)).astype(
        jnp.float32
    )
    return (
        selected_expert,
        (selected_expert[:, :, None] * slot_hit[:, None, :]).reshape(
            token_experts.shape[0], experts * capacity
        ),
    )


def fetch_weights(
    query_key_value_weight, output_projection_weight, routing_weight, patch_merging_weight
):
    return (
        lax.all_gather(query_key_value_weight, "dp", axis=0, tiled=True),
        lax.all_gather(output_projection_weight, "dp", axis=0, tiled=True),
        lax.all_gather(routing_weight, "dp", axis=0, tiled=True),
        lax.all_gather(patch_merging_weight, "dp", axis=0, tiled=True),
    )


def settle_dense(grad_qkv, grad_proj, grad_router, grad_merge):
    return (
        lax.psum_scatter(
            grad_qkv.astype(jnp.bfloat16), "dp", scatter_dimension=0, tiled=True
        ).astype(jnp.float32),
        lax.psum_scatter(
            grad_proj.astype(jnp.bfloat16), "dp", scatter_dimension=0, tiled=True
        ).astype(jnp.float32),
        lax.psum_scatter(
            grad_router.astype(jnp.bfloat16), "dp", scatter_dimension=0, tiled=True
        ).astype(jnp.float32),
        lax.psum_scatter(
            grad_merge.astype(jnp.bfloat16), "dp", scatter_dimension=0, tiled=True
        ).astype(jnp.float32),
    )


def add_tuples(first, second):
    if first is None:
        return second
    return tuple((left + right for left, right in zip(first, second)))


def on_device(
    patches,
    unpadded_patch_size,
    patch_expert_index,
    cotangent,
    query_key_value_weight,
    query_projection_bias,
    value_projection_bias,
    log_cosine_scale,
    bias_network_first_weight,
    bias_network_first_bias,
    bias_network_second_weight,
    output_projection_weight,
    output_projection_bias,
    attention_norm_gain,
    attention_norm_bias,
    routing_weight,
    expert_first_weight,
    expert_first_bias,
    expert_second_weight,
    expert_second_bias,
    expert_norm_gain,
    expert_norm_bias,
    patch_merging_weight,
    merging_norm_gain,
    merging_norm_bias,
):
    micro_count, _, band_rows, band_cols, channels = patches.shape
    half_win = WINDOW_SIDE // 2
    win_count = band_cols // WINDOW_SIDE
    win_area = WINDOW_SIDE * WINDOW_SIDE
    tokens = band_rows * band_cols
    experts = routing_weight.shape[1]
    capacity = (5 * tokens + 4 * experts - 1) // (4 * experts)
    total_rows = band_rows * lax.axis_size("row")
    row_start = band_rows * lax.axis_index("row")
    relative_bias_table, bias_table_backward = jax.vjp(
        relative_position_bias,
        bias_network_first_weight,
        bias_network_first_bias,
        bias_network_second_weight,
    )
    bf_type = jnp.bfloat16
    fl_type = jnp.float32
    dense_sums = None
    expert_sums = None
    small_sums = None
    back_table = jnp.zeros_like(relative_bias_table)
    outputs = []
    input_grads = []
    for micro_step in range(micro_count):
        fetched = fetch_weights(
            query_key_value_weight, output_projection_weight, routing_weight, patch_merging_weight
        )
        weight_qkv, weight_proj, weight_router, weight_merge = fetched
        band_in = patches[micro_step, 0]
        valid_rows = unpadded_patch_size[micro_step, 0, 0]
        valid_cols = unpadded_patch_size[micro_step, 0, 1]
        below = passed_along(band_in[:half_win], "row", -1)
        shifted = jnp.roll(jnp.concatenate([band_in[half_win:], below], 0), -half_win, 1)
        windows = (
            shifted.reshape(band_rows, win_count, WINDOW_SIDE, channels)
            .transpose(1, 0, 2, 3)
            .reshape(win_count, win_area, channels)
        )
        qkv_rows = jnp.einsum("npc,cf->npf", windows, weight_qkv, preferred_element_type=fl_type)
        query_raw = (qkv_rows[..., :channels] + query_projection_bias).reshape(
            win_count, win_area, HEAD_COUNT, HEAD_DIM
        )
        key_raw = qkv_rows[..., channels : 2 * channels].reshape(
            win_count, win_area, HEAD_COUNT, HEAD_DIM
        )
        value_raw = (qkv_rows[..., 2 * channels :] + value_projection_bias).reshape(
            win_count, win_area, HEAD_COUNT, HEAD_DIM
        )
        (query_unit, key_unit), unit_pull = jax.vjp(
            directions, query_raw, key_raw, log_cosine_scale
        )
        query_low = query_unit.astype(bf_type)
        key_low = key_unit.astype(bf_type)
        value_low = value_raw.astype(bf_type)
        window_masks = window_mask(row_start, total_rows, band_cols, valid_rows, valid_cols)[
            :, None
        ]
        scores = (
            jnp.einsum("nphd,nqhd->nhpq", query_low, key_low, preferred_element_type=fl_type)
            + relative_bias_table
            + window_masks
        )
        row_peak = jnp.max(scores, -1, keepdims=True)
        exp_scores = jnp.exp(scores - row_peak)
        sum_exp = jnp.sum(exp_scores, -1, keepdims=True)
        log_total = row_peak + jnp.log(sum_exp)
        attn_out = jnp.einsum(
            "nhpq,nqhd->nphd",
            (exp_scores / sum_exp).astype(bf_type),
            value_low,
            preferred_element_type=fl_type,
        ).astype(bf_type)
        shifted_out = (
            attn_out.reshape(win_count, WINDOW_SIDE, WINDOW_SIDE, channels)
            .transpose(1, 0, 2, 3)
            .reshape(band_rows, band_cols, channels)
        )
        shifted_out = jnp.roll(shifted_out, half_win, 1)
        arrived = passed_along(shifted_out[half_win:], "row", 1)
        attn_rows = jnp.concatenate([arrived, shifted_out[:half_win]], 0).reshape(tokens, channels)
        projected = (
            jnp.dot(attn_rows, weight_proj, preferred_element_type=fl_type) + output_projection_bias
        )
        attn_branch, attn_pull = jax.vjp(
            layer_norm, projected, attention_norm_gain, attention_norm_bias
        )
        resid_one = band_in.reshape(tokens, channels).astype(fl_type) + attn_branch
        resid_low = resid_one.astype(bf_type)
        logits = jnp.dot(resid_low, weight_router, preferred_element_type=fl_type)
        logit_exp = jnp.exp(logits - jnp.max(logits, -1, keepdims=True))
        router_probs = logit_exp / jnp.sum(logit_exp, -1, keepdims=True)
        selected_expert, expert_dispatch = route_tables(
            patch_expert_index[micro_step, 0].reshape(tokens), experts, capacity
        )
        dispatch_low = expert_dispatch.astype(bf_type)
        gate_value = jnp.sum(router_probs * selected_expert, -1)
        sent = jnp.einsum("nk,nc->kc", dispatch_low, resid_low, preferred_element_type=fl_type)
        sent = sent.astype(bf_type).reshape(experts, capacity, channels)
        received = lax.all_to_all(sent, "dp", split_axis=0, concat_axis=1, tiled=True)
        hidden_pre = (
            jnp.einsum(
                "ksc,kcf->ksf", received, expert_first_weight, preferred_element_type=fl_type
            )
            + expert_first_bias[:, None]
        )
        hidden_low = exact_error_gelu(hidden_pre).astype(bf_type)
        expert_res = (
            jnp.einsum(
                "ksf,kfc->ksc", hidden_low, expert_second_weight, preferred_element_type=fl_type
            )
            + expert_second_bias[:, None]
        )
        returned = lax.all_to_all(
            expert_res.astype(bf_type), "dp", split_axis=1, concat_axis=0, tiled=True
        )
        returned = returned.reshape(experts * capacity, channels)
        picked = jnp.einsum("nk,kc->nc", dispatch_low, returned, preferred_element_type=fl_type)
        moe_branch, moe_pull = jax.vjp(
            layer_norm, gate_value[:, None] * picked, expert_norm_gain, expert_norm_bias
        )
        resid_two = resid_one + moe_branch
        merged = resid_two.reshape(band_rows // 2, 2, band_cols // 2, 2, channels).transpose(
            0, 2, 3, 1, 4
        )
        merged = merged.reshape(tokens // 4, 4 * channels).astype(bf_type)
        reduced = jnp.dot(merged, weight_merge, preferred_element_type=fl_type)
        final_rows, merge_pull = jax.vjp(layer_norm, reduced, merging_norm_gain, merging_norm_bias)
        outputs.append(
            final_rows.astype(bf_type).reshape(band_rows // 2, band_cols // 2, 2 * channels)
        )
        back_final = cotangent[micro_step, 0].reshape(tokens // 4, 2 * channels).astype(fl_type)
        back_reduced, grad_rgain, grad_rshift = merge_pull(back_final)
        back_reduced_low = back_reduced.astype(bf_type)
        grad_merge = jnp.einsum(
            "nk,nd->kd", merged, back_reduced_low, preferred_element_type=fl_type
        )
        back_merged = jnp.einsum(
            "nd,kd->nk", back_reduced_low, weight_merge, preferred_element_type=fl_type
        )
        back_resid = back_merged.reshape(band_rows // 2, band_cols // 2, 2, 2, channels).transpose(
            0, 3, 1, 2, 4
        )
        back_resid = back_resid.reshape(tokens, channels)
        back_moe, grad_mgain, grad_mshift = moe_pull(back_resid)
        back_gate = jnp.sum(back_moe * picked, -1)
        back_picked = (back_moe * gate_value[:, None]).astype(bf_type)
        back_returned = jnp.einsum(
            "nk,nc->kc", dispatch_low, back_picked, preferred_element_type=fl_type
        )
        back_returned = back_returned.astype(bf_type).reshape(experts, capacity, channels)
        back_res = lax.all_to_all(back_returned, "dp", split_axis=0, concat_axis=1, tiled=True)
        grad_eout = jnp.einsum("ksf,ksc->kfc", hidden_low, back_res, preferred_element_type=fl_type)
        grad_eout_bias = jnp.sum(back_res.astype(fl_type), 1)
        back_hidden = jnp.einsum(
            "ksc,kfc->ksf", back_res, expert_second_weight, preferred_element_type=fl_type
        )
        _, gelu_pull = jax.vjp(exact_error_gelu, hidden_pre)
        (back_pre,) = gelu_pull(back_hidden)
        grad_ein_bias = jnp.sum(back_pre, 1)
        back_pre_low = back_pre.astype(bf_type)
        grad_ein = jnp.einsum(
            "ksc,ksf->kcf", received, back_pre_low, preferred_element_type=fl_type
        )
        back_received = jnp.einsum(
            "ksf,kcf->ksc", back_pre_low, expert_first_weight, preferred_element_type=fl_type
        ).astype(bf_type)
        back_sent = lax.all_to_all(
            back_received, "dp", split_axis=1, concat_axis=0, tiled=True
        ).reshape(experts * capacity, channels)
        back_logits = router_probs * (selected_expert - gate_value[:, None]) * back_gate[:, None]
        back_logits_low = back_logits.astype(bf_type)
        grad_router = jnp.einsum(
            "nc,ne->ce", resid_low, back_logits_low, preferred_element_type=fl_type
        )
        back_one = back_resid + jnp.einsum(
            "nk,kc->nc", dispatch_low, back_sent, preferred_element_type=fl_type
        )
        back_one = back_one + jnp.einsum(
            "ne,ce->nc", back_logits_low, weight_router, preferred_element_type=fl_type
        )
        back_projected, grad_again, grad_ashift = attn_pull(back_one)
        grad_proj_bias = jnp.sum(back_projected, 0)
        back_proj_low = back_projected.astype(bf_type)
        grad_proj = jnp.einsum(
            "nc,nd->cd", attn_rows, back_proj_low, preferred_element_type=fl_type
        )
        back_rows = jnp.einsum(
            "nd,cd->nc", back_proj_low, weight_proj, preferred_element_type=fl_type
        )
        back_rows = back_rows.astype(bf_type).reshape(band_rows, band_cols, channels)
        lifted = passed_along(back_rows[:half_win], "row", -1)
        back_shifted = jnp.roll(jnp.concatenate([back_rows[half_win:], lifted], 0), -half_win, 1)
        back_attn = back_shifted.reshape(band_rows, win_count, WINDOW_SIDE, channels).transpose(
            1, 0, 2, 3
        )
        back_attn = back_attn.reshape(win_count, win_area, HEAD_COUNT, HEAD_DIM)
        again_scores = (
            jnp.einsum("nphd,nqhd->nhpq", query_low, key_low, preferred_element_type=fl_type)
            + relative_bias_table
            + window_masks
        )
        attn_probs = jnp.exp(again_scores - log_total)
        back_probs = jnp.einsum(
            "nphd,nqhd->nhpq", back_attn, value_low, preferred_element_type=fl_type
        )
        back_value = jnp.einsum(
            "nhpq,nphd->nqhd", attn_probs.astype(bf_type), back_attn, preferred_element_type=fl_type
        )
        back_scores = attn_probs * (
            back_probs - jnp.sum(back_probs * attn_probs, -1, keepdims=True)
        )
        back_table = back_table + jnp.sum(back_scores, 0)
        back_scores_low = back_scores.astype(bf_type)
        back_qunit = jnp.einsum(
            "nhpq,nqhd->nphd", back_scores_low, key_low, preferred_element_type=fl_type
        )
        back_kunit = jnp.einsum(
            "nhpq,nphd->nqhd", back_scores_low, query_low, preferred_element_type=fl_type
        )
        back_query, back_key, grad_scale = unit_pull((back_qunit, back_kunit))
        back_query = back_query.reshape(win_count, win_area, channels)
        back_key = back_key.reshape(win_count, win_area, channels)
        back_value = back_value.reshape(win_count, win_area, channels)
        grad_qbias = jnp.sum(back_query, (0, 1))
        grad_vbias = jnp.sum(back_value, (0, 1))
        back_qkv_low = jnp.concatenate([back_query, back_key, back_value], -1).astype(bf_type)
        grad_qkv = jnp.einsum("npc,npf->cf", windows, back_qkv_low, preferred_element_type=fl_type)
        back_windows = jnp.einsum(
            "npf,cf->npc", back_qkv_low, weight_qkv, preferred_element_type=fl_type
        )
        back_band = back_windows.reshape(win_count, band_rows, WINDOW_SIDE, channels).transpose(
            1, 0, 2, 3
        )
        back_band = jnp.roll(back_band.reshape(band_rows, band_cols, channels), half_win, 1)
        passed = passed_along(back_band[half_win:].astype(jnp.bfloat16), "row", 1).astype(
            jnp.float32
        )
        back_input = jnp.concatenate([passed, back_band[:half_win]], 0).reshape(tokens, channels)
        input_grads.append(
            (back_one + back_input).astype(bf_type).reshape(band_rows, band_cols, channels)
        )
        dense_now = settle_dense(grad_qkv, grad_proj, grad_router, grad_merge)
        dense_sums = add_tuples(dense_sums, dense_now)
        expert_sums = add_tuples(expert_sums, (grad_ein, grad_ein_bias, grad_eout, grad_eout_bias))
        small_sums = add_tuples(
            small_sums,
            (
                grad_qbias,
                grad_vbias,
                grad_scale,
                grad_proj_bias,
                grad_again,
                grad_ashift,
                grad_mgain,
                grad_mshift,
                grad_rgain,
                grad_rshift,
            ),
        )
    sum_qkv, sum_proj, sum_router, sum_merge = dense_sums
    sum_ein, sum_ein_bias, sum_eout, sum_eout_bias = expert_sums
    sum_qkv, sum_proj, sum_router, sum_merge, sum_ein, sum_ein_bias, sum_eout, sum_eout_bias = (
        lax.psum(sum_qkv.astype(jnp.bfloat16), "row").astype(jnp.float32),
        lax.psum(sum_proj.astype(jnp.bfloat16), "row").astype(jnp.float32),
        lax.psum(sum_router.astype(jnp.bfloat16), "row").astype(jnp.float32),
        lax.psum(sum_merge.astype(jnp.bfloat16), "row").astype(jnp.float32),
        lax.psum(sum_ein.astype(jnp.bfloat16), "row").astype(jnp.float32),
        lax.psum(sum_ein_bias.astype(jnp.bfloat16), "row").astype(jnp.float32),
        lax.psum(sum_eout.astype(jnp.bfloat16), "row").astype(jnp.float32),
        lax.psum(sum_eout_bias.astype(jnp.bfloat16), "row").astype(jnp.float32),
    )
    grad_first, grad_first_bias, grad_second = bias_table_backward(back_table)
    (
        sum_qbias,
        sum_vbias,
        sum_scale,
        sum_proj_bias,
        sum_again,
        sum_ashift,
        sum_mgain,
        sum_mshift,
        sum_rgain,
        sum_rshift,
    ) = small_sums
    (
        sum_qbias,
        sum_vbias,
        sum_scale,
        sum_proj_bias,
        sum_again,
        sum_ashift,
        sum_mgain,
        sum_mshift,
        sum_rgain,
        sum_rshift,
        grad_first,
        grad_first_bias,
        grad_second,
    ) = lax.psum(
        (
            sum_qbias,
            sum_vbias,
            sum_scale,
            sum_proj_bias,
            sum_again,
            sum_ashift,
            sum_mgain,
            sum_mshift,
            sum_rgain,
            sum_rshift,
            grad_first,
            grad_first_bias,
            grad_second,
        ),
        ("dp", "row"),
    )
    return (
        jnp.stack(outputs)[:, None],
        jnp.stack(input_grads)[:, None],
        sum_qkv,
        sum_qbias,
        sum_vbias,
        sum_scale,
        grad_first,
        grad_first_bias,
        grad_second,
        sum_proj,
        sum_proj_bias,
        sum_again,
        sum_ashift,
        sum_router,
        sum_ein,
        sum_ein_bias,
        sum_eout,
        sum_eout_bias,
        sum_mgain,
        sum_mshift,
        sum_merge,
        sum_rgain,
        sum_rshift,
    )


def solution(mesh):
    return jax.shard_map(
        on_device,
        mesh=mesh,
        in_specs=(
            P(None, "dp", "row", None, None),
            P(None, "dp", None),
            P(None, "dp", "row", None, None),
            P(None, "dp", "row", None, None),
            P("dp", None),
            P(),
            P(),
            P(),
            P(),
            P(),
            P(),
            P("dp", None),
            P(),
            P(),
            P(),
            P("dp", None),
            P("dp", None, None),
            P("dp", None),
            P("dp", None, None),
            P("dp", None),
            P(),
            P(),
            P("dp", None),
            P(),
            P(),
        ),
        out_specs=(
            P(None, "dp", "row", None, None),
            P(None, "dp", "row", None, None),
            P("dp", None),
            P(),
            P(),
            P(),
            P(),
            P(),
            P(),
            P("dp", None),
            P(),
            P(),
            P(),
            P("dp", None),
            P("dp", None, None),
            P("dp", None),
            P("dp", None, None),
            P("dp", None),
            P(),
            P(),
            P("dp", None),
            P(),
            P(),
        ),
        check_vma=False,
    )
```

profile of v0, /device:TPU:0, one launch (start us, length us, event | category | flops | bytes accessed | tf_op | source)
XLA Modules:
  0.0 1396.8 jit_solution(11757147233866292562)
XLA Ops:
  31.6 32.6 %all_gather.16 = bf16[384,1152]{1,0:T(8,128)(2,1)S(1)} all-gather(bf16[48,1152]{1,0:T(8,128)(2,1)S(1)} %copy-done.153), channel_id=1, replica_groups=mesh['dp'=8,'row'=4] {'dp'}, dimensions={0}, use_global_device_ids=true | all-gather | bytes 995328 | tf_op jit(solution)/shard_map/all_gather | solution.py:120
  85.3 30.4 %all-gather = bf16[8,48,16]{1,2,0:T(8,128)(2,1)S(1)} all-gather(bf16[1,48,16]{1,2,0:T(8,128)(2,1)S(1)} %bitcast.437), channel_id=1, replica_groups=mesh['dp'=8,'row'=4] {'dp'}, dimensions={0}, use_global_device_ids=true | all-gather | bytes 13824 | tf_op jit(solution)/shard_map/all_gather | solution.py:122
  115.8 10.2 add.637
  129.0 31.1 %all_gather.17 = bf16[384,384]{1,0:T(8,128)(2,1)S(1)} all-gather(bf16[48,384]{1,0:T(8,128)(2,1)} %param.36), channel_id=1, replica_groups=mesh['dp'=8,'row'=4] {'dp'}, dimensions={0}, use_global_device_ids=true | all-gather | bytes 331776 | tf_op jit(solution)/shard_map/all_gather | solution.py:121
  211.2 9.8 fusion.202
  258.1 11.8 fusion.200
  359.3 10.7 all-to-all-done
  376.5 26.3 %all-to-all-done.2 = bf16[16,90,384]{2,1,0:T(8,128)(2,1)} async-done(((bf16[16,90,384]{2,1,0:T(8,128)(2,1)}), bf16[16,90,384]{2,1,0:T(8,128)(2,1)}, u32[]{:S(2)}, u32[]{:S(2)}) %all-to-all-start.2) | async-done | bytes 1105952 | tf_op jit(solution)/shard_map/all_to_all | solution.py:275
  410.9 16.6 %fusion.53 = (u8[720,1536]{1,0:T(8,128)(4,1)S(1)}, u8[720,1536]{1,0:T(8,128)(4,1)S(1)}, u8[720,1536]{1,0:T(8,128)(4,1)S(1)}, u8[720,1536]{1,0:T(8,128)(4,1)}, f32[2,720,1536]{2,1,0:T(8,128)}) fusion(f32[2,1536]{1,0:T(2,128)S(1)} %copy-done.182, f32[2,720,1536]{2,1,0:T(8,128)} %fusion.89, bf16[2,384,1536]{2,1,0:T(8,128)(2,1)S(1)} %copy-done, ...), kind=kOutput, calls=%fused_computation.149 | convolution fusion | flops 1756200960 | bytes 25595904 | tf_op jit(solution)/shard_map/ksc,kcf->ksf/dot_general | solution.py:277
  427.5 45.0 %multiply_convert_fusion.1 = (bf16[2,720,1536]{2,1,0:T(8,128)(2,1)S(1)}, f32[2,720,1536]{2,1,0:T(8,128)}, bf16[2,720,1536]{2,1,0:T(8,128)(2,1)}, f32[2,720,1536]{2,1,0:T(8,128)}) fusion(f32[2,720,1536]{2,1,0:T(8,128)} %get-tuple-element.166, f32[2,1536]{1,0:T(2,128)S(1)} %copy-done.182, u8[720,1536]{1,0:T(8,128)(4,1)S(1)} %get-tuple-element.24, ...), kind=kLoop, calls=%fused_computation.46 | loop fusion | flops 311869440 | bytes 48672768 | tf_op jit(solution)/shard_map/convert_element_type | solution.py:282
  488.5 19.3 %all-to-all-done.1 = bf16[2,720,384]{2,0,1:T(2,128)(2,1)} async-done(((bf16[2,720,384]{2,0,1:T(2,128)(2,1)}), bf16[2,720,384]{2,0,1:T(2,128)(2,1)}, u32[]{:S(2)}, u32[]{:S(2)}) %all-to-all-start.1) | async-done | bytes 1105952 | tf_op jit(solution)/shard_map/all_to_all | solution.py:289
  519.1 29.1 %all-to-all-done.3 = bf16[2,720,384]{2,0,1:T(2,128)(2,1)} async-done(((bf16[2,720,384]{2,0,1:T(2,128)(2,1)}), bf16[2,720,384]{2,0,1:T(2,128)(2,1)}, u32[]{:S(2)}, u32[]{:S(2)}) %all-to-all-start.3) | async-done | bytes 1105952 | tf_op jit(solution)/shard_map/all_to_all | solution.py:289
  665.6 20.4 %all-to-all-done.6 = bf16[16,90,384]{2,1,0:T(8,128)(2,1)} async-done(((bf16[16,90,384]{2,1,0:T(8,128)(2,1)}), bf16[16,90,384]{2,1,0:T(8,128)(2,1)}, u32[]{:S(2)}, u32[]{:S(2)}) %all-to-all-start.6) | async-done | bytes 1105952 | tf_op jit(solution)/shard_map/all_to_all | solution.py:327
  704.4 55.2 %reduce-scatter.25.cloned.1.call-done = bf16[48,16]{1,0:T(8,128)(2,1)} async-done(((bf16[384,16]{1,0:T(8,128)(2,1)}), bf16[48,16]{1,0:T(8,128)(2,1)}) %reduce-scatter.25.cloned.1.call-update) | async-done | bytes 1552
  769.5 9.8 fusion.212
  788.0 10.0 fusion.211
  802.3 14.8 %all-to-all-done.7 = bf16[2,720,384]{2,0,1:T(2,128)(2,1)S(1)} async-done(((bf16[2,720,384]{2,0,1:T(2,128)(2,1)}), bf16[2,720,384]{2,0,1:T(2,128)(2,1)S(1)}, u32[]{:S(2)}, u32[]{:S(2)}) %all-to-all-start.7) | async-done | bytes 1105952 | tf_op jit(solution)/shard_map/all_to_all | solution.py:343
  842.6 15.2 %all-to-all-done.5 = bf16[2,720,384]{2,0,1:T(2,128)(2,1)} async-done(((bf16[2,720,384]{2,0,1:T(2,128)(2,1)}), bf16[2,720,384]{2,0,1:T(2,128)(2,1)}, u32[]{:S(2)}, u32[]{:S(2)}) %all-to-all-start.5) | async-done | bytes 1105952 | tf_op jit(solution)/shard_map/all_to_all | solution.py:343
  887.4 10.8 multiply_reduce_fusion
  898.2 9.8 bitcast_convert_fusion
  930.8 10.0 multiply_reduce_fusion.1
  940.8 15.9 %fusion.26 = (f32[12,144,144]{1,2,0:T(8,128)}, bf16[8,12,144,144]{2,3,1,0:T(8,128)(2,1)}) fusion(f32[8,12,144,144]{2,3,1,0:T(8,128)} %get-tuple-element.183, f32[8,12,144]{2,1,0:T(8,128)S(1)} %get-tuple-element.182, f32[8,12,144,144]{2,3,1,0:T(8,128)} %get-tuple-element.155, f32[8,12,144]{2,1,0:T(8,128)S(1)} %copy-done.79), kind=kLoop, calls=%fused_computation.74 | loop fusion | flops 9704448 | bytes 21012480 | tf_op jit(solution)/shard_map/reduce_sum | solution.py:388
  970.1 12.8 fusion.28
  1080.5 10.0 add.710
  1090.5 20.6 %copy.293 = f32[12,12,12,12,12]{4,3,2,1,0:T(8,128)} copy(f32[12,12,12,12,12]{2,1,4,3,0:T(8,128)} %add.710) | data formatting | bytes 1990656 | tf_op jit(solution)/shard_map/add | solution.py:388
  1111.1 13.2 fusion.71
  1130.0 23.3 %reduce-scatter.13.cloned.1.call-done = bf16[48,1152]{1,0:T(8,128)(2,1)} async-done(((bf16[384,1152]{1,0:T(8,128)(2,1)}), bf16[48,1152]{1,0:T(8,128)(2,1)}) %reduce-scatter.13.cloned.1.call-update) | async-done | bytes 110608 | tf_op jit(solution)/shard_map/reduce_scatter | solution.py:129
  1160.1 41.3 %all-reduce = (f32[384]{0:T(512)}, f32[384]{0:T(512)}, f32[12]{0:T(128)}, f32[2,512]{1,0:T(2,128)}, f32[512]{0:T(512)}, /*index=5*/f32[512,12]{0,1:T(8,128)}, f3...) all-reduce(f32[384]{0:T(512)S(1)} %add.705, ...), channel_id=1, replica_groups=mesh['dp'=8,'row'=4] {'dp','row'}, use_global_device_ids=true, to_apply=%region_57.58 | all-reduce | flops 11916 | bytes 95328 | tf_op jit(solution)/shard_map/psum | solution.py:475
  1201.4 13.0 reduce-scatter.17.cloned.1.call-done
  1214.3 61.0 %reduce-scatter.19.cloned.1.call-done = bf16[48,384]{1,0:T(8,128)(2,1)} async-done(((bf16[384,384]{1,0:T(8,128)(2,1)}), bf16[48,384]{1,0:T(8,128)(2,1)}) %reduce-scatter.19.cloned.1.call-update) | async-done | bytes 36880 | tf_op jit(solution)/shard_map/reduce_scatter | solution.py:132
  1276.2 11.1 all-reduce.1
  1298.0 80.8 %all-reduce.5.cloned.1.call-done = (bf16[48,1152]{1,0:T(8,128)(2,1)}, bf16[2,384,1536]{2,1,0:T(8,128)(2,1)}, bf16[2,1536,384]{2,1,0:T(8,128)(2,1)}, bf16[192,768]{1,0:T(8,128)(2,1)}) async-done(((bf16[48,1152]{1,0:T(8,128)(2,1)}, bf16[2,384,1536]{2,1,0:T(8,128)(2,1)}, bf16[2,1536,384]{2,1,0:T(8,128)(2,1)}, bf16[192,768]{1,0:T(8,128)(2,1)}), (bf16[48,1152]{1,0:T(8,128)(2,1)}, ...) | async-done | bytes 5124112 | tf_op jit(solution)/shard_map/psum | solution.py:439
  (800 shorter events, 647.2 us)
Async XLA Ops:
  7.2 397.8 %copy-start = (bf16[2,384,1536]{2,1,0:T(8,128)(2,1)S(1)}, bf16[2,384,1536]{2,1,0:T(8,128)(2,1)}, u32[]{:S(2)}) copy-start(bf16[2,384,1536]{2,1,0:T(8,128)(2,1)} %param.41) | copy-start | bytes 7077892
  10.0 158.3 %collective-permute-start = (bf16[6,96,384]{2,1,0:T(8,128)(2,1)}, bf16[6,96,384]{2,1,0:T(8,128)(2,1)}, u32[]{:S(2)}, u32[]{:S(2)}) collective-permute-start(bf16[6,96,384]{2,1,0:T(8,128)(2,1)} %get-tuple-element.112), channel_id=1, source_target_pairs={{0,3},{1,0},{2,1},{3,2},{4,7},{5,4},{6,5},{7,6},{8,11},{9,8},{10,9... | collective-permute-start | bytes 1327112 | tf_op jit(solution)/shard_map/ppermute | solution.py:19
  12.4 147.7 %collective-permute-start.2 = (bf16[6,96,384]{2,1,0:T(8,128)(2,1)}, bf16[6,96,384]{2,1,0:T(8,128)(2,1)}, u32[]{:S(2)}, u32[]{:S(2)}) collective-permute-start(bf16[6,96,384]{2,1,0:T(8,128)(2,1)} %get-tuple-element.113), channel_id=1, source_target_pairs={{0,3},{1,0},{2,1},{3,2},{4,7},{5,4},{6,5},{7,6},{8,11},{9,8},{10,9... | collective-permute-start | bytes 1327112 | tf_op jit(solution)/shard_map/ppermute | solution.py:19
  85.3 172.8 %copy-start.172 = (f32[12]{0:T(128)}, f32[12]{0:T(128)S(1)}, u32[]{:S(2)}) copy-start(f32[12]{0:T(128)S(1)} %exp.28) | copy-start | bytes 148
  115.8 205.6 %copy-start.121 = (bf16[384,16]{0,1:T(8,128)(2,1)}, bf16[384,16]{0,1:T(8,128)(2,1)S(1)}, u32[]{:S(2)}) copy-start(bf16[384,16]{0,1:T(8,128)(2,1)S(1)} %reshape.890) | copy-start | bytes 36868
  160.2 157.5 %copy-start.45 = (bf16[384,384]{1,0:T(8,128)(2,1)}, bf16[384,384]{1,0:T(8,128)(2,1)S(1)}, u32[]{:S(2)}) copy-start(bf16[384,384]{1,0:T(8,128)(2,1)S(1)} %all_gather.17) | copy-start | bytes 884740
  256.9 53.6 %collective-permute-start.3 = (bf16[6,96,384]{2,1,0:T(8,128)(2,1)}, bf16[6,96,384]{2,1,0:T(8,128)(2,1)}, u32[]{:S(2)}, u32[]{:S(2)}) collective-permute-start(bf16[6,96,384]{2,1,0:T(8,128)(2,1)} %fusion.120), channel_id=1, source_target_pairs={{0,1},{1,2},{2,3},{3,0},{4,5},{5,6},{6,7},{7,4},{8,9},{9,10},{10,1... | collective-permute-start | bytes 1327112 | tf_op jit(solution)/shard_map/ppermute | solution.py:19
  309.7 7.8 collective-permute-start.1
  337.1 32.8 %all-to-all-start = ((bf16[16,90,384]{2,1,0:T(8,128)(2,1)}), bf16[16,90,384]{2,1,0:T(8,128)(2,1)S(1)}, u32[]{:S(2)}, u32[]{:S(2)}) async-start(bf16[16,90,384]{2,1,0:T(8,128)(2,1)} %reshape.849), calls=%async_computation | async-start | bytes 2359296 | tf_op jit(solution)/shard_map/all_to_all | solution.py:275
  369.9 32.9 %all-to-all-start.2 = ((bf16[16,90,384]{2,1,0:T(8,128)(2,1)}), bf16[16,90,384]{2,1,0:T(8,128)(2,1)}, u32[]{:S(2)}, u32[]{:S(2)}) async-start(bf16[16,90,384]{2,1,0:T(8,128)(2,1)} %reshape.859), calls=%async_computation.2 | async-start | bytes 2359296 | tf_op jit(solution)/shard_map/all_to_all | solution.py:275
  476.8 30.9 %all-to-all-start.1 = ((bf16[2,720,384]{2,0,1:T(2,128)(2,1)}), bf16[2,720,384]{2,0,1:T(2,128)(2,1)}, u32[]{:S(2)}, u32[]{:S(2)}) async-start(bf16[2,720,384]{2,0,1:T(2,128)(2,1)} %copy.243), calls=%async_computation.1 | async-start | bytes 2211840 | tf_op jit(solution)/shard_map/all_to_all | solution.py:289
  507.7 40.4 %all-to-all-start.3 = ((bf16[2,720,384]{2,0,1:T(2,128)(2,1)}), bf16[2,720,384]{2,0,1:T(2,128)(2,1)}, u32[]{:S(2)}, u32[]{:S(2)}) async-start(bf16[2,720,384]{2,0,1:T(2,128)(2,1)} %copy.256), calls=%async_computation.3 | async-start | bytes 2211840 | tf_op jit(solution)/shard_map/all_to_all | solution.py:289
  512.0 73.3 %all-gather.3.cloned.1.call-start = ((), (), s32[]{:S(2)}) async-start(), calls=%async_computation.16 | async-start | bytes 2654208 | tf_op jit(solution)/shard_map/all_gather | solution.py:123
  512.7 190.9 %reduce-scatter.27.cloned.1.call-start = ((), (), s32[]{:S(2)}) async-start(), calls=%async_computation.24 | async-start | bytes 110592
  637.5 122.1 %reduce-scatter.25.cloned.1.call-start = ((), (), s32[]{:S(2)}) async-start(), calls=%async_computation.23 | async-start | bytes 110592
  641.3 486.9 %reduce-scatter.21.cloned.1.call-start = ((), (), s32[]{:S(2)}) async-start(), calls=%async_computation.21 | async-start | bytes 2654208 | tf_op jit(solution)/shard_map/reduce_scatter | solution.py:138
  653.5 32.5 %all-to-all-start.6 = ((bf16[16,90,384]{2,1,0:T(8,128)(2,1)}), bf16[16,90,384]{2,1,0:T(8,128)(2,1)}, u32[]{:S(2)}, u32[]{:S(2)}) async-start(bf16[16,90,384]{2,1,0:T(8,128)(2,1)} %reshape.875), calls=%async_computation.6 | async-start | bytes 2359296 | tf_op jit(solution)/shard_map/all_to_all | solution.py:327
  686.0 78.6 %all-to-all-start.4 = ((bf16[16,90,384]{2,1,0:T(8,128)(2,1)}), bf16[16,90,384]{2,1,0:T(8,128)(2,1)}, u32[]{:S(2)}, u32[]{:S(2)}) async-start(bf16[16,90,384]{2,1,0:T(8,128)(2,1)} %reshape.863), calls=%async_computation.4 | async-start | bytes 2359296 | tf_op jit(solution)/shard_map/all_to_all | solution.py:327
  690.2 437.9 %reduce-scatter.23.cloned.1.call-start = ((), (), s32[]{:S(2)}) async-start(), calls=%async_computation.22 | async-start | bytes 2654208 | tf_op jit(solution)/shard_map/reduce_scatter | solution.py:138
  783.7 33.5 %all-to-all-start.7 = ((bf16[2,720,384]{2,0,1:T(2,128)(2,1)}), bf16[2,720,384]{2,0,1:T(2,128)(2,1)S(1)}, u32[]{:S(2)}, u32[]{:S(2)}) async-start(bf16[2,720,384]{2,0,1:T(2,128)(2,1)} %copy.278), calls=%async_computation.7 | async-start | bytes 2211840 | tf_op jit(solution)/shard_map/all_to_all | solution.py:343
  817.2 40.6 %all-to-all-start.5 = ((bf16[2,720,384]{2,0,1:T(2,128)(2,1)}), bf16[2,720,384]{2,0,1:T(2,128)(2,1)}, u32[]{:S(2)}, u32[]{:S(2)}) async-start(bf16[2,720,384]{2,0,1:T(2,128)(2,1)} %copy.262), calls=%async_computation.5 | async-start | bytes 2211840 | tf_op jit(solution)/shard_map/all_to_all | solution.py:343
  821.4 308.6 %reduce-scatter.15.cloned.1.call-start = ((), (), s32[]{:S(2)}) async-start(), calls=%async_computation.18 | async-start | bytes 995328 | tf_op jit(solution)/shard_map/reduce_scatter | solution.py:129
  870.0 5.8 collective-permute-start.6
  872.2 35.7 %collective-permute-start.4 = (bf16[6,96,384]{2,1,0:T(8,128)(2,1)}, bf16[6,96,384]{2,1,0:T(8,128)(2,1)}, u32[]{:S(2)}, u32[]{:S(2)}) collective-permute-start(bf16[6,96,384]{2,1,0:T(8,128)(2,1)} %bitcast.62), channel_id=1, source_target_pairs={{0,3},{1,0},{2,1},{3,2},{4,7},{5,4},{6,5},{7,6},{8,11},{9,8},{10,9... | collective-permute-start | bytes 1327112 | tf_op jit(solution)/shard_map/ppermute | solution.py:19
  1027.7 125.6 %reduce-scatter.13.cloned.1.call-start = ((), (), s32[]{:S(2)}) async-start(), calls=%async_computation.17 | async-start | bytes 995328 | tf_op jit(solution)/shard_map/reduce_scatter | solution.py:129
  1033.1 181.2 %reduce-scatter.17.cloned.1.call-start = ((), (), s32[]{:S(2)}) async-start(), calls=%async_computation.19 | async-start | bytes 331776 | tf_op jit(solution)/shard_map/reduce_scatter | solution.py:132
  1050.3 225.1 %reduce-scatter.19.cloned.1.call-start = ((), (), s32[]{:S(2)}) async-start(), calls=%async_computation.20 | async-start | bytes 331776 | tf_op jit(solution)/shard_map/reduce_scatter | solution.py:132
  1054.0 324.8 %all-reduce.5.cloned.1.call-start = ((), (), s32[]{:S(2)}) async-start(), calls=%async_computation.25 | async-start | bytes 10248192 | tf_op jit(solution)/shard_map/psum | solution.py:439
  1067.1 222.7 %collective-permute-start.7 = (bf16[6,96,384]{2,1,0:T(8,128)(2,1)}, bf16[6,96,384]{2,1,0:T(8,128)(2,1)}, u32[]{:S(2)}, u32[]{:S(2)}) collective-permute-start(bf16[6,96,384]{2,1,0:T(8,128)(2,1)} %fusion.95), channel_id=1, source_target_pairs={{0,1},{1,2},{2,3},{3,0},{4,5},{5,6},{6,7},{7,4},{8,9},{9,10},{10,1... | collective-permute-start | bytes 1327112 | tf_op jit(solution)/shard_map/ppermute | solution.py:19
  1076.5 214.3 %collective-permute-start.5 = (bf16[6,96,384]{2,1,0:T(8,128)(2,1)}, bf16[6,96,384]{2,1,0:T(8,128)(2,1)}, u32[]{:S(2)}, u32[]{:S(2)}) collective-permute-start(bf16[6,96,384]{2,1,0:T(8,128)(2,1)} %fusion.97), channel_id=1, source_target_pairs={{0,1},{1,2},{2,3},{3,0},{4,5},{5,6},{6,7},{7,4},{8,9},{9,10},{10,1... | collective-permute-start | bytes 1327112 | tf_op jit(solution)/shard_map/ppermute | solution.py:19
  1155.6 120.5 %copy-start.174 = (bf16[2,1536]{1,0:T(2,128)(2,1)S(1)}, bf16[2,1536]{1,0:T(2,128)(2,1)}, u32[]{:S(2)}) copy-start(bf16[2,1536]{1,0:T(2,128)(2,1)} %add_convert_fusion.15) | copy-start | bytes 18436
  1155.6 120.5 %copy-start.179 = (bf16[48,16]{0,1:T(8,128)(2,1)S(1)}, bf16[48,16]{0,1:T(8,128)(2,1)}, u32[]{:S(2)}) copy-start(bf16[48,16]{0,1:T(8,128)(2,1)} %add_convert_fusion.16) | copy-start | bytes 4612
  (211 other events, 1453.5 us)
Sparse Core Ops, SparseCore 0:
  515.0 60.9 all-gather.2
  637.7 58.5 reduce-scatter.26
  699.5 60.0 reduce-scatter.24
  763.0 92.9 reduce-scatter.20
  859.3 66.3 reduce-scatter.22
  1027.8 61.7 reduce-scatter.14
  1093.0 60.2 reduce-scatter.12
  1156.6 57.6 reduce-scatter.16
  1217.6 57.6 reduce-scatter.18
  1278.4 100.3 all-reduce.4
where the time goes:
time: 1410 us; the launch traced here: 1400 us
  waiting for transfers between devices  377 us (27%)
  matrix products  307 us (22%)
  local copies, waits for them, and re-layouts  266 us (19%)
  other arithmetic  238 us (17%)
  blocking collectives  147 us (10%)
  starting transfers between devices  44.5 us (3%)
  between operations  17.7 us (1%)
    psum x1, waiting for transfers between devices, on_device(): lax.psum(sum_qkv.astype(jnp.bfloat16), 'row').astype(jnp.float32)  80.8 us
    reduce_scatter x2, waiting for transfers between devices, settle_dense(): lax.psum_scatter(grad_proj.astype(jnp.bfloat16), 'dp', scatter_dimension=...  74 us
    unnamed x12, waiting for transfers between devices  56 us
    all_to_all x2, waiting for transfers between devices, on_device(): lax.all_to_all(expert_res.astype(bf_type), 'dp', split_axis=1, concat_axi...  48.3 us
    convert_element_type x1, other arithmetic, on_device(): hidden_low = exact_error_gelu(hidden_pre).astype(bf_type)  45 us
    psum x1, blocking collectives, on_device(): lax.psum((sum_qbias, sum_vbias, sum_scale, sum_proj_bias, sum_again, sum_...  41.3 us
    all_to_all x2, waiting for transfers between devices, on_device(): lax.all_to_all(sent, 'dp', split_axis=0, concat_axis=1, tiled=True)  37 us
    all_gather x1, blocking collectives, fetch_weights(): lax.all_gather(query_key_value_weight, 'dp', axis=0, tiled=True)  32.6 us
  transfers between devices with their start and end apart: 26, of which 14 were waited for; matrix products, arithmetic and copies ran while one was open for 39% of the time, Pallas kernels for 0%

commit v1 on v0

v1 whole, which is shorter than its diff:
```python
import functools

import jax
import jax.numpy as jnp
from jax import lax
from jax.experimental import pallas as pl
from jax.experimental.pallas import tpu as pltpu
from jax.sharding import PartitionSpec as P

HEAD_COUNT = 12
HEAD_DIM = 32
WINDOW_SIDE = 12
LANES = 128
TILE_HEADS = LANES // HEAD_DIM


PRECISION_HIGH = lax.Precision.HIGHEST
EPS_NORM = 1e-05
EPS_UNIT = 1e-06
MASK_FILL = -100.0
BF = jnp.bfloat16
FL = jnp.float32
VMEM_BYTES = 52 * 2**20


def passed_along(array, axis, by):
    count = lax.axis_size(axis)
    return lax.ppermute(array, axis, [(i, (i + by) % count) for i in range(count)])


def exact_error_gelu(values):
    return jax.nn.gelu(values, approximate=False)


def span_offsets():
    return jnp.arange(WINDOW_SIDE)[:, None] - jnp.arange(WINDOW_SIDE)[None, :] + (WINDOW_SIDE - 1)


def span_select():
    spans = jnp.arange(2 * WINDOW_SIDE - 1)
    return (span_offsets()[:, :, None] == spans[None, None, :]).astype(FL)


def position_table(
    bias_network_first_weight, bias_network_first_bias, bias_network_second_weight
):
    span_axis = (jnp.arange(2 * WINDOW_SIDE - 1, dtype=FL) - (WINDOW_SIDE - 1)) * (
        8.0 / (WINDOW_SIDE - 1)
    )
    span_axis = jnp.sign(span_axis) * jnp.log2(jnp.abs(span_axis) + 1.0) / 3.0
    grid_rows = jnp.broadcast_to(span_axis[:, None], (2 * WINDOW_SIDE - 1, 2 * WINDOW_SIDE - 1))
    relative_coordinates = jnp.stack([grid_rows, grid_rows.T], -1)
    hidden_activation = exact_error_gelu(
        jnp.einsum(
            "plr,rt->plt", relative_coordinates, bias_network_first_weight, precision=PRECISION_HIGH
        )
        + bias_network_first_bias
    )
    return 16.0 * jax.nn.sigmoid(
        jnp.einsum(
            "qvw,wk->qvk", hidden_activation, bias_network_second_weight, precision=PRECISION_HIGH
        )
    )


def spread_table(table):
    select = span_select()
    spread = jnp.einsum("fqy,uzs,ysr->rqzfu", select, select, table, precision=PRECISION_HIGH)
    return spread.reshape(table.shape[-1], WINDOW_SIDE * WINDOW_SIDE, WINDOW_SIDE * WINDOW_SIDE)


def gather_table(grad):
    side = WINDOW_SIDE
    spans = 2 * side - 1
    select = span_select()
    columns = jnp.einsum("jkb,ic->kijcb", select, jnp.eye(side, dtype=FL)).reshape(
        side, side * side, side * spans
    )
    part = lax.dot_general(
        grad.reshape(HEAD_COUNT * side, side * side * side),
        columns.reshape(side * side * side, side * spans),
        (((1,), (0,)), ((), ())),
        precision=PRECISION_HIGH,
    )
    part = part.reshape(HEAD_COUNT, side, side, spans)
    return jnp.einsum("hqpb,pqa->abh", part, select, precision=PRECISION_HIGH)


def window_mask(row_start, total_rows, total_cols, valid_rows, valid_cols):
    half_win = WINDOW_SIDE // 2
    rows_at = row_start + jnp.arange(WINDOW_SIDE)
    cols_at = jnp.arange(total_cols)
    row_zone = (rows_at >= total_rows - WINDOW_SIDE).astype(jnp.int32) + (
        rows_at >= total_rows - half_win
    ).astype(jnp.int32)
    col_zone = (cols_at >= total_cols - WINDOW_SIDE).astype(jnp.int32) + (
        cols_at >= total_cols - half_win
    ).astype(jnp.int32)
    zone_ids = 3 * row_zone[:, None] + col_zone[None, :]
    inside = ((rows_at + half_win) % total_rows < valid_rows)[:, None] & (
        (cols_at + half_win) % total_cols < valid_cols
    )[None, :]
    win_count = total_cols // WINDOW_SIDE
    zone_ids = (
        zone_ids.reshape(WINDOW_SIDE, win_count, WINDOW_SIDE)
        .transpose(1, 0, 2)
        .reshape(win_count, WINDOW_SIDE * WINDOW_SIDE)
    )
    inside = (
        inside.reshape(WINDOW_SIDE, win_count, WINDOW_SIDE)
        .transpose(1, 0, 2)
        .reshape(win_count, WINDOW_SIDE * WINDOW_SIDE)
    )
    mask = jnp.where(zone_ids[:, :, None] != zone_ids[:, None, :], MASK_FILL, 0.0) + jnp.where(
        inside[:, None, :], 0.0, MASK_FILL
    )
    return mask - jnp.max(mask, -1, keepdims=True)


def mm(left, right):
    return jnp.dot(left, right, preferred_element_type=FL)


def mm_nt(left, right):
    return lax.dot_general(left, right, (((1,), (1,)), ((), ())), preferred_element_type=FL)


def mm_tn(left, right):
    return lax.dot_general(left, right, (((0,), (0,)), ((), ())), preferred_element_type=FL)


def call_kernel(body, name, outs, args, scratch=(), flops=10**9):
    moved = sum(a.size * a.dtype.itemsize for a in args)
    vmem = pl.BlockSpec(memory_space=pltpu.VMEM)
    return pl.pallas_call(
        body,
        name=name,
        out_shape=[jax.ShapeDtypeStruct(s, d) for s, d in outs],
        in_specs=[vmem] * len(args),
        out_specs=[vmem] * len(outs),
        scratch_shapes=[pltpu.VMEM(s, d) for s, d in scratch],
        compiler_params=pltpu.CompilerParams(vmem_limit_bytes=VMEM_BYTES),
        cost_estimate=pl.CostEstimate(flops=flops, bytes_accessed=moved, transcendentals=0),
    )(*args)


def rows_at(start, size):
    return pl.ds(pl.multiple_of(start, 16), size)


def head_sums(values, block_ones):
    high = values.astype(BF)
    rest = (values - high.astype(FL)).astype(BF)
    return mm(jnp.concatenate([high, rest], 1), block_ones)


def tiles_of(channels):
    return [slice(LANES * t, LANES * (t + 1)) for t in range(channels // LANES)]


def to_windows(sources, grid_ref, win_ref, band_cols, channels):
    half_win = WINDOW_SIDE // 2
    pitch = band_cols + 8
    win_area = WINDOW_SIDE * WINDOW_SIDE
    for i in range(WINDOW_SIDE):
        value = sources(i).astype(FL)
        for t, lanes in enumerate(tiles_of(channels)):
            grid_ref[t, i * pitch : i * pitch + band_cols, :] = value[:, lanes]
            grid_ref[t, i * pitch + band_cols : (i + 1) * pitch, :] = value[0:8, lanes]
    for t in range(channels // LANES):
        for n in range(band_cols // WINDOW_SIDE):
            for i in range(WINDOW_SIDE):
                at = i * pitch + n * WINDOW_SIDE + half_win
                to = n * win_area + i * WINDOW_SIDE
                win_ref[t, to : to + WINDOW_SIDE, :] = grid_ref[t, at : at + WINDOW_SIDE, :]


def from_windows(put, grid_ref, win_ref, band_cols, channels):
    half_win = WINDOW_SIDE // 2
    pitch = band_cols + 8
    win_area = WINDOW_SIDE * WINDOW_SIDE
    for t in range(channels // LANES):
        for n in range(band_cols // WINDOW_SIDE):
            for i in range(WINDOW_SIDE):
                to = i * pitch + n * WINDOW_SIDE + half_win
                at = n * win_area + i * WINDOW_SIDE
                grid_ref[t, to : to + WINDOW_SIDE, :] = win_ref[t, at : at + WINDOW_SIDE, :]
        for i in range(WINDOW_SIDE):
            grid_ref[t, i * pitch : i * pitch + half_win, :] = grid_ref[
                t, i * pitch + band_cols : i * pitch + band_cols + half_win, :
            ]
    for i in range(WINDOW_SIDE):
        put(
            i,
            jnp.concatenate(
                [
                    grid_ref[t, i * pitch : i * pitch + band_cols, :]
                    for t in range(channels // LANES)
                ],
                1,
            ),
        )


def attend_forward_body(
    band_ref,
    below_ref,
    weight_ref,
    qbias_ref,
    vbias_ref,
    scale_ref,
    bias_ref,
    mask_ref,
    heads_ref,
    block_ref,
    own_ref,
    send_ref,
    win_ref,
    qkv_ref,
    inv_ref,
    grid_scr,
    win_scr,
    *,
    band_cols,
    channels,
):
    tokens = band_ref.shape[0]
    half = tokens // 2
    win_area = WINDOW_SIDE * WINDOW_SIDE
    tiles = tiles_of(channels)

    def source(i):
        if i < WINDOW_SIDE // 2:
            return band_ref[half + i * band_cols : half + (i + 1) * band_cols, :]
        at = (i - WINDOW_SIDE // 2) * band_cols
        return below_ref[at : at + band_cols, :]

    to_windows(source, grid_scr, win_scr, band_cols, channels)
    block_ones = block_ref[...]
    chunk = 2 * win_area

    def project(c, carry):
        rows = rows_at(c * chunk, chunk)
        low = jnp.concatenate([win_scr[t, rows, :] for t in range(len(tiles))], 1).astype(BF)
        win_ref[rows, :] = low
        qkv = mm(low, weight_ref[...])
        for lanes in tiles:
            key_lanes = slice(channels + lanes.start, channels + lanes.stop)
            value_lanes = slice(2 * channels + lanes.start, 2 * channels + lanes.stop)
            query = qkv[:, lanes] + qbias_ref[:, lanes]
            inverse = (
                lax.rsqrt(head_sums(query * query, block_ones) + EPS_UNIT) * scale_ref[:, lanes]
            )
            inv_ref[rows, lanes] = inverse
            qkv_ref[rows, lanes] = (query * inverse).astype(BF)
            key = qkv[:, key_lanes]
            inverse = lax.rsqrt(head_sums(key * key, block_ones) + EPS_UNIT)
            inv_ref[rows, key_lanes] = inverse
            qkv_ref[rows, key_lanes] = (key * inverse).astype(BF)
            qkv_ref[rows, value_lanes] = (qkv[:, value_lanes] + vbias_ref[:, lanes]).astype(BF)
        return carry

    lax.fori_loop(0, tokens // chunk, project, 0)
    lane = lax.broadcasted_iota(jnp.int32, (win_area, LANES), 1)
    in_head = [(lane // HEAD_DIM) == k for k in range(TILE_HEADS)]

    def attend(n, carry):
        rows = rows_at(n * win_area, win_area)
        for t, lanes in enumerate(tiles):
            query = qkv_ref[rows, lanes]
            key = qkv_ref[rows, channels + lanes.start : channels + lanes.stop]
            value = qkv_ref[rows, 2 * channels + lanes.start : 2 * channels + lanes.stop]
            total = None
            for k in range(TILE_HEADS):
                head = t * TILE_HEADS + k
                mine = heads_ref[k]
                scores = mm_nt(query * mine, key)
                powers = jnp.exp(scores + bias_ref[head] + mask_ref[n])
                mixed = mm(powers.astype(BF), value * mine + (1 - mine))
                after = in_head[(k + 1) % TILE_HEADS]
                if total is None:
                    weighted, total = mixed, mixed
                else:
                    weighted = jnp.where(in_head[k], mixed, weighted)
                    total = jnp.where(after, mixed, total)
            total = pltpu.roll(total, LANES - HEAD_DIM, 1)
            win_scr[t, rows, :] = weighted / total
        return carry

    lax.fori_loop(0, tokens // win_area, attend, 0)

    def put(i, value):
        if i < WINDOW_SIDE // 2:
            own_ref[i * band_cols : (i + 1) * band_cols, :] = value.astype(BF)
        else:
            at = (i - WINDOW_SIDE // 2) * band_cols
            send_ref[at : at + band_cols, :] = value.astype(BF)

    from_windows(put, grid_scr, win_scr, band_cols, channels)


def attend_backward_body(
    own_ref,
    lifted_ref,
    weight_ref,
    scale_ref,
    bias_ref,
    mask_ref,
    heads_ref,
    block_ref,
    win_ref,
    qkv_ref,
    inv_ref,
    dx_own_ref,
    dx_send_ref,
    dweight_ref,
    dbias_ref,
    small_ref,
    grid_scr,
    win_scr,
    dqkv_scr,
    *,
    band_cols,
    channels,
):
    half = own_ref.shape[0]
    tokens = 2 * half
    win_area = WINDOW_SIDE * WINDOW_SIDE
    tiles = tiles_of(channels)

    def source(i):
        ref = own_ref if i < WINDOW_SIDE // 2 else lifted_ref
        at = (i % (WINDOW_SIDE // 2)) * band_cols
        return ref[at : at + band_cols, :]

    to_windows(source, grid_scr, win_scr, band_cols, channels)
    block_ones = block_ref[...]
    dbias_ref[...] = jnp.zeros_like(dbias_ref)
    small_ref[...] = jnp.zeros_like(small_ref)

    def attend(n, carry):
        rows = rows_at(n * win_area, win_area)
        for t, lanes in enumerate(tiles):
            key_lanes = slice(channels + lanes.start, channels + lanes.stop)
            value_lanes = slice(2 * channels + lanes.start, 2 * channels + lanes.stop)
            query = qkv_ref[rows, lanes]
            key = qkv_ref[rows, key_lanes]
            value = qkv_ref[rows, value_lanes]
            back_low = win_scr[t, rows, :].astype(BF)
            dquery = dkey = dvalue = None
            for k in range(TILE_HEADS):
                head = t * TILE_HEADS + k
                mine = heads_ref[k]
                query_mine = query * mine
                back_mine = back_low * mine
                scores = mm_nt(key, query_mine)
                powers = jnp.exp(scores + bias_ref[head] + mask_ref[n])
                probs = powers * (1.0 / jnp.sum(powers, 0, keepdims=True))
                weighted = probs * mm_nt(value, back_mine)
                dscores = weighted - probs * jnp.sum(weighted, 0, keepdims=True)
                dbias_ref[head] += dscores
                dlow = dscores.astype(BF)
                dv = mm(probs.astype(BF), back_mine)
                dk = mm(dlow, query_mine)
                dq = mm_tn(dlow, key * mine)
                if dquery is None:
                    dquery, dkey, dvalue = dq, dk, dv
                else:
                    dquery, dkey, dvalue = dquery + dq, dkey + dk, dvalue + dv
            scale = scale_ref[:, lanes]
            unit = query.astype(FL)
            along = head_sums(unit * dquery, block_ones)
            dq_raw = inv_ref[rows, lanes] * (dquery - unit * along / (scale * scale))
            unit = key.astype(FL)
            dk_raw = inv_ref[rows, key_lanes] * (
                dkey - unit * head_sums(unit * dkey, block_ones)
            )
            dqkv_scr[rows, lanes] = dq_raw.astype(BF)
            dqkv_scr[rows, key_lanes] = dk_raw.astype(BF)
            dqkv_scr[rows, value_lanes] = dvalue.astype(BF)
            small_ref[0:1, lanes] += jnp.sum(dq_raw, 0, keepdims=True)
            small_ref[1:2, lanes] += jnp.sum(dvalue, 0, keepdims=True)
            small_ref[2:3, lanes] += jnp.sum(along, 0, keepdims=True)
        return carry

    lax.fori_loop(0, tokens // win_area, attend, 0)
    chunk = 2 * win_area

    def project(c, carry):
        rows = rows_at(c * chunk, chunk)
        back = mm_nt(dqkv_scr[rows, :], weight_ref[...])
        for t, lanes in enumerate(tiles):
            win_scr[t, rows, :] = back[:, lanes]
        return carry

    lax.fori_loop(0, tokens // chunk, project, 0)
    for part in range(3):
        lanes = slice(part * channels, (part + 1) * channels)
        dweight_ref[:, lanes] = mm_tn(win_ref[...], dqkv_scr[:, lanes])

    def put(i, value):
        if i < WINDOW_SIDE // 2:
            dx_own_ref[i * band_cols : (i + 1) * band_cols, :] = value
        else:
            at = (i - WINDOW_SIDE // 2) * band_cols
            dx_send_ref[at : at + band_cols, :] = value.astype(BF)

    from_windows(put, grid_scr, win_scr, band_cols, channels)


def lane_mean(values):
    return jnp.sum(values, -1, keepdims=True) * (1.0 / values.shape[-1])


def normalised(values):
    centred = values - lane_mean(values)
    inverse = lax.rsqrt(lane_mean(centred * centred) + EPS_NORM)
    return centred * inverse, inverse


def normalised_back(back, gain, unit, inverse):
    back = back * gain
    return inverse * (back - lane_mean(back) - unit * lane_mean(back * unit))


CHUNK = 144
PACK = 256


def pack_rows(dest_row_ref, rows_ref, out_ref):
    tokens = rows_ref.shape[0]

    def step(c, carry):
        place = lax.broadcasted_iota(jnp.int32, (PACK, tokens), 0) + c * PACK
        chosen = jnp.where(place == dest_row_ref[...], 1.0, 0.0).astype(BF)
        out_ref[rows_at(c * PACK, PACK), :] = mm(chosen, rows_ref[...]).astype(BF)
        return carry

    lax.fori_loop(0, out_ref.shape[0] // PACK, step, 0)


def unpack_rows(dest_col, buffer_ref):
    place = lax.broadcasted_iota(jnp.int32, (dest_col.shape[0], buffer_ref.shape[0]), 1)
    chosen = jnp.where(place == dest_col, 1.0, 0.0).astype(BF)
    return mm(chosen, buffer_ref[...])


def route_body(
    arrived_ref,
    own_ref,
    band_ref,
    weight_ref,
    small_ref,
    router_ref,
    expert_ref,
    dest_row_ref,
    resid_ref,
    unit_ref,
    aux_ref,
    low_ref,
    sent_ref,
    *,
    experts,
):
    half = arrived_ref.shape[0]
    lane = lax.broadcasted_iota(jnp.int32, (CHUNK, LANES), 1)
    for part, ref in enumerate((arrived_ref, own_ref)):

        def step(c, carry, part=part, ref=ref):
            rows = rows_at(part * half + c * CHUNK, CHUNK)
            projected = mm(ref[rows_at(c * CHUNK, CHUNK), :], weight_ref[...]) + small_ref[0:1, :]
            unit, inverse = normalised(projected)
            unit_ref[rows, :] = unit.astype(BF)
            resid = band_ref[rows, :].astype(FL) + unit * small_ref[1:2, :] + small_ref[2:3, :]
            resid_ref[rows, :] = resid
            low = resid.astype(BF)
            low_ref[rows, :] = low
            logits = jnp.where(lane < experts, mm(low, router_ref[...]), -1e30)
            powers = jnp.exp(logits - jnp.max(logits, -1, keepdims=True))
            probs = powers / jnp.sum(powers, -1, keepdims=True)
            gate = jnp.sum(
                jnp.where(lane == expert_ref[rows, :], probs, 0.0), -1, keepdims=True
            )
            aux_ref[rows, :] = jnp.where(
                lane == LANES - 1, gate, jnp.where(lane == LANES - 2, inverse, probs)
            )
            return carry

        lax.fori_loop(0, half // CHUNK, step, 0)
    pack_rows(dest_row_ref, low_ref, sent_ref)


def merge_body(
    returned_ref,
    dest_col_ref,
    dest_row_ref,
    expert_ref,
    aux_ref,
    resid_ref,
    small_ref,
    weight_ref,
    wide_ref,
    cotangent_ref,
    final_ref,
    merged_ref,
    dreduced_ref,
    dresid_ref,
    dlogits_ref,
    sent_ref,
    sums_ref,
    unit_scr,
    picked_scr,
    inverse_scr,
    token_scr,
    back_scr,
    *,
    experts,
    band_cols,
):
    tokens, channels = resid_ref.shape
    tiles = tiles_of(channels)
    lane = lax.broadcasted_iota(jnp.int32, (CHUNK, LANES), 1)

    def combine(c, carry):
        rows = rows_at(c * CHUNK, CHUNK)
        picked = unpack_rows(dest_col_ref[rows, :], returned_ref)
        picked_scr[rows, :] = picked
        gate = aux_ref[rows, :][:, LANES - 1 : LANES]
        unit, inverse = normalised(gate * picked)
        unit_scr[rows, :] = unit
        inverse_scr[rows, :] = jnp.broadcast_to(inverse, (CHUNK, LANES))
        resid = resid_ref[rows, :] + unit * small_ref[0:1, :] + small_ref[1:2, :]
        for t, lanes in enumerate(tiles):
            token_scr[t, rows, :] = resid[:, lanes]
        return carry

    lax.fori_loop(0, tokens // CHUNK, combine, 0)
    pairs = band_cols // 2
    for i in range(WINDOW_SIDE // 2):
        for k in range(4):
            start = (2 * i + k % 2) * band_cols + k // 2
            for t in range(len(tiles)):
                at = k * channels + t * LANES
                merged_ref[i * pairs : (i + 1) * pairs, at : at + LANES] = token_scr[
                    t, pl.ds(start, pairs, stride=2), :
                ].astype(BF)
    unit, inverse = normalised(mm(merged_ref[...], weight_ref[...]))
    final_ref[...] = (unit * wide_ref[0:1, :] + wide_ref[1:2, :]).astype(BF)
    back = cotangent_ref[...].astype(FL)
    sums_ref[...] = jnp.zeros_like(sums_ref)
    sums_ref[0:1, :] = jnp.sum(back * unit, 0, keepdims=True)
    sums_ref[1:2, :] = jnp.sum(back, 0, keepdims=True)
    dreduced = normalised_back(back, wide_ref[0:1, :], unit, inverse).astype(BF)
    dreduced_ref[...] = dreduced
    for k in range(4):
        part = mm_nt(dreduced, weight_ref[k * channels : (k + 1) * channels, :])
        for i in range(WINDOW_SIDE // 2):
            start = (2 * i + k % 2) * band_cols + k // 2
            for t, lanes in enumerate(tiles):
                token_scr[t, pl.ds(start, pairs, stride=2), :] = part[
                    i * pairs : (i + 1) * pairs, lanes
                ]

    def spread(c, carry):
        rows = rows_at(c * CHUNK, CHUNK)
        back = jnp.concatenate([token_scr[t, rows, :] for t in range(len(tiles))], 1)
        dresid_ref[rows, :] = back
        unit = unit_scr[rows, :]
        sums_ref[2:3, 0:channels] += jnp.sum(back * unit, 0, keepdims=True)
        sums_ref[3:4, 0:channels] += jnp.sum(back, 0, keepdims=True)
        back = normalised_back(back, small_ref[0:1, :], unit, inverse_scr[rows, :][:, 0:1])
        aux = aux_ref[rows, :]
        gate = aux[:, LANES - 1 : LANES]
        dgate = jnp.sum(back * picked_scr[rows, :], -1, keepdims=True)
        back_scr[rows, :] = (back * gate).astype(BF)
        probs = jnp.where(lane < experts, aux, 0.0)
        chosen = jnp.where(lane == expert_ref[rows, :], 1.0, 0.0)
        dlogits_ref[rows, :] = (probs * (chosen - gate) * dgate).astype(BF)
        return carry

    lax.fori_loop(0, tokens // CHUNK, spread, 0)
    pack_rows(dest_row_ref, back_scr, sent_ref)


def settle_body(
    sent_ref,
    dest_col_ref,
    dresid_ref,
    dlogits_ref,
    router_ref,
    unit_ref,
    aux_ref,
    small_ref,
    weight_ref,
    done_ref,
    low_ref,
    rows_ref,
    sums_ref,
):
    tokens, channels = dresid_ref.shape
    sums_ref[...] = jnp.zeros_like(sums_ref)

    def step(c, carry):
        rows = rows_at(c * CHUNK, CHUNK)
        back = dresid_ref[rows, :] + unpack_rows(dest_col_ref[rows, :], sent_ref)
        back = back + mm_nt(dlogits_ref[rows, :], router_ref[...])
        done_ref[rows, :] = back
        unit = unit_ref[rows, :].astype(FL)
        sums_ref[1:2, :] += jnp.sum(back * unit, 0, keepdims=True)
        sums_ref[2:3, :] += jnp.sum(back, 0, keepdims=True)
        inverse = aux_ref[rows, :][:, LANES - 2 : LANES - 1]
        back = normalised_back(back, small_ref[1:2, :], unit, inverse)
        sums_ref[0:1, :] += jnp.sum(back, 0, keepdims=True)
        low = back.astype(BF)
        low_ref[rows, :] = low
        rows_ref[rows, :] = mm_nt(low, weight_ref[...]).astype(BF)
        return carry

    lax.fori_loop(0, tokens // CHUNK, step, 0)


def dense_body(*refs):
    (*ins, proj_ref, router_ref) = refs
    arrived, own, low, resid, dlogits = (ins[i::5] for i in range(5))
    half = arrived[0].shape[0]
    proj = router = None
    for a, o, b, r, d in zip(arrived, own, low, resid, dlogits):
        now = mm_tn(a[...], b[0:half, :]) + mm_tn(o[...], b[half:, :])
        then = mm_tn(r[...], d[...])
        proj = now if proj is None else proj + now
        router = then if router is None else router + then
    proj_ref[...] = proj.astype(BF)
    router_ref[...] = router.astype(BF)


def merge_weight_body(*refs):
    (*ins, out_ref) = refs
    total = None
    for left, right in zip(ins[0::2], ins[1::2]):
        now = mm_tn(left[...], right[...])
        total = now if total is None else total + now
    out_ref[...] = total.astype(BF)


def merge_weight_grad(merged, dreduced, channels):
    args, specs = [], []
    for left, right in zip(merged, dreduced):
        args += [left, right]
        specs += [
            pl.BlockSpec((left.shape[0], channels), lambda k: (0, k)),
            pl.BlockSpec(right.shape, lambda k: (0, 0)),
        ]
    return pl.pallas_call(
        merge_weight_body,
        name="merge_weight_grad",
        grid=(4,),
        out_shape=jax.ShapeDtypeStruct((merged[0].shape[1], dreduced[0].shape[1]), BF),
        in_specs=specs,
        out_specs=pl.BlockSpec((channels, dreduced[0].shape[1]), lambda k: (k, 0)),
        compiler_params=pltpu.CompilerParams(vmem_limit_bytes=VMEM_BYTES),
    )(*args)


FF_CHUNK = 512


def expert_forward_body(
    rows_ref, win_ref, bin_ref, wout_ref, bout_ref, result_ref, hidden_ref, slope_ref, pre_scr, sum_scr
):
    step = pl.program_id(1)
    sources, slots, channels = rows_ref.shape
    rows = rows_ref[...].reshape(sources * slots, channels)
    pre_scr[...] = mm(rows, win_ref[0]) + bin_ref[0]
    block = 64

    def activate(c, carry):
        at = rows_at(c * block, block)
        pre = pre_scr[at, :]
        cdf = 0.5 * (1.0 + lax.erf(pre * 0.7071067811865476))
        hidden_ref[0, at, :] = (pre * cdf).astype(BF)
        slope_ref[0, at, :] = (
            cdf + pre * (0.3989422804014327 * jnp.exp(-0.5 * pre * pre))
        ).astype(BF)
        return carry

    lax.fori_loop(0, sources * slots // block, activate, 0)

    now = mm(hidden_ref[0], wout_ref[0])

    @pl.when(step == 0)
    def _():
        sum_scr[...] = now + bout_ref[0]

    @pl.when(step > 0)
    def _():
        sum_scr[...] += now

    @pl.when(step == pl.num_programs(1) - 1)
    def _():
        result_ref[...] = sum_scr[...].astype(BF).reshape(sources, slots, channels)


def expert_forward(rows, first_weight, first_bias, second_weight, second_bias, local):
    sources, both, channels = rows.shape
    slots = both // local
    hidden = first_weight.shape[-1]
    count = sources * slots
    wide = jax.ShapeDtypeStruct((local, count, hidden), BF)
    return pl.pallas_call(
        expert_forward_body,
        name="expert_forward",
        grid=(local, hidden // FF_CHUNK),
        out_shape=[jax.ShapeDtypeStruct(rows.shape, BF), wide, wide],
        in_specs=[
            pl.BlockSpec((sources, slots, channels), lambda e, f: (0, e, 0)),
            pl.BlockSpec((1, channels, FF_CHUNK), lambda e, f: (e, 0, f)),
            pl.BlockSpec((1, 1, FF_CHUNK), lambda e, f: (e, 0, f)),
            pl.BlockSpec((1, FF_CHUNK, channels), lambda e, f: (e, f, 0)),
            pl.BlockSpec((1, 1, channels), lambda e, f: (e, 0, 0)),
        ],
        out_specs=[
            pl.BlockSpec((sources, slots, channels), lambda e, f: (0, e, 0)),
            pl.BlockSpec((1, count, FF_CHUNK), lambda e, f: (e, 0, f)),
            pl.BlockSpec((1, count, FF_CHUNK), lambda e, f: (e, 0, f)),
        ],
        scratch_shapes=[pltpu.VMEM((count, FF_CHUNK), FL), pltpu.VMEM((count, channels), FL)],
        compiler_params=pltpu.CompilerParams(vmem_limit_bytes=VMEM_BYTES),
        cost_estimate=pl.CostEstimate(
            flops=4 * local * count * hidden * channels,
            bytes_accessed=8 * local * count * hidden,
            transcendentals=local * count * hidden,
        ),
    )(rows, first_weight, first_bias, second_weight, second_bias)


def expert_backward_body(
    rows_ref, win_ref, wout_ref, slope_ref, result_ref, dpre_ref, dbias_ref, sum_scr
):
    step = pl.program_id(1)
    sources, slots, channels = rows_ref.shape
    rows = rows_ref[...].reshape(sources * slots, channels)
    dpre = mm_nt(rows, wout_ref[0]) * slope_ref[0].astype(FL)
    dbias_ref[0] = jnp.sum(dpre, 0, keepdims=True)
    dpre_ref[0] = dpre.astype(BF)
    now = mm_nt(dpre_ref[0], win_ref[0])

    @pl.when(step == 0)
    def _():
        sum_scr[...] = now

    @pl.when(step > 0)
    def _():
        sum_scr[...] += now

    @pl.when(step == pl.num_programs(1) - 1)
    def _():
        result_ref[...] = sum_scr[...].astype(BF).reshape(sources, slots, channels)


def expert_backward(rows, first_weight, second_weight, slope, local):
    sources, both, channels = rows.shape
    slots = both // local
    hidden = first_weight.shape[-1]
    count = sources * slots
    return pl.pallas_call(
        expert_backward_body,
        name="expert_backward",
        grid=(local, hidden // FF_CHUNK),
        out_shape=[
            jax.ShapeDtypeStruct(rows.shape, BF),
            jax.ShapeDtypeStruct((local, count, hidden), BF),
            jax.ShapeDtypeStruct((local, 1, hidden), FL),
        ],
        in_specs=[
            pl.BlockSpec((sources, slots, channels), lambda e, f: (0, e, 0)),
            pl.BlockSpec((1, channels, FF_CHUNK), lambda e, f: (e, 0, f)),
            pl.BlockSpec((1, FF_CHUNK, channels), lambda e, f: (e, f, 0)),
            pl.BlockSpec((1, count, FF_CHUNK), lambda e, f: (e, 0, f)),
        ],
        out_specs=[
            pl.BlockSpec((sources, slots, channels), lambda e, f: (0, e, 0)),
            pl.BlockSpec((1, count, FF_CHUNK), lambda e, f: (e, 0, f)),
            pl.BlockSpec((1, 1, FF_CHUNK), lambda e, f: (e, 0, f)),
        ],
        scratch_shapes=[pltpu.VMEM((count, channels), FL)],
        compiler_params=pltpu.CompilerParams(vmem_limit_bytes=VMEM_BYTES),
        cost_estimate=pl.CostEstimate(
            flops=4 * local * count * hidden * channels,
            bytes_accessed=6 * local * count * hidden,
            transcendentals=0,
        ),
    )(rows, first_weight, second_weight, slope)


def expert_weight_body(*refs):
    (*ins, din_ref, dout_ref, dbias_ref) = refs
    din = dout = dbias = None
    for rows_ref, dpre_ref, hidden_ref, back_ref in zip(*(ins[i::4] for i in range(4))):
        sources, slots, channels = rows_ref.shape
        rows = rows_ref[...].reshape(sources * slots, channels)
        back = back_ref[...].reshape(sources * slots, channels)
        now = mm_tn(rows, dpre_ref[0])
        then = mm_tn(hidden_ref[0], back)
        sums = jnp.sum(back.astype(FL), 0, keepdims=True)
        if din is None:
            din, dout, dbias = now, then, sums
        else:
            din, dout, dbias = din + now, dout + then, dbias + sums
    din_ref[0] = din.astype(BF)
    dout_ref[0] = dout.astype(BF)
    dbias_ref[0] = dbias


def expert_weight_grads(rows, dpre, hidden, back, local):
    sources, both, channels = rows[0].shape
    slots = both // local
    count = sources * slots
    width = hidden[0].shape[-1]
    args, specs = [], []
    token_spec = pl.BlockSpec((sources, slots, channels), lambda e, f: (0, e, 0))
    wide_spec = pl.BlockSpec((1, count, FF_CHUNK), lambda e, f: (e, 0, f))
    for four in zip(rows, dpre, hidden, back):
        args += four
        specs += [token_spec, wide_spec, wide_spec, token_spec]
    return pl.pallas_call(
        expert_weight_body,
        name="expert_weight_grads",
        grid=(local, width // FF_CHUNK),
        out_shape=[
            jax.ShapeDtypeStruct((local, channels, width), BF),
            jax.ShapeDtypeStruct((local, width, channels), BF),
            jax.ShapeDtypeStruct((local, 1, channels), FL),
        ],
        in_specs=specs,
        out_specs=[
            pl.BlockSpec((1, channels, FF_CHUNK), lambda e, f: (e, 0, f)),
            pl.BlockSpec((1, FF_CHUNK, channels), lambda e, f: (e, f, 0)),
            pl.BlockSpec((1, 1, channels), lambda e, f: (e, 0, 0)),
        ],
        compiler_params=pltpu.CompilerParams(vmem_limit_bytes=VMEM_BYTES),
        cost_estimate=pl.CostEstimate(
            flops=8 * local * count * width * channels,
            bytes_accessed=8 * local * count * width,
            transcendentals=0,
        ),
    )(*args)


def swapped(rows):
    return lax.all_to_all(rows, "dp", split_axis=0, concat_axis=0, tiled=True)


def gathered(shard):
    count = lax.axis_size("dp")
    copies = jnp.broadcast_to(shard[None], (count,) + shard.shape)
    return swapped(copies).reshape(count * shard.shape[0], shard.shape[1])


def crossed(array, axis, bit):
    count = lax.axis_size(axis)
    return lax.ppermute(array, axis, [(i, i ^ bit) for i in range(count)])


def summed(array, axes):
    for axis in axes:
        bit = 1
        while bit < lax.axis_size(axis):
            array = array + crossed(array, axis, bit)
            bit *= 2
    return array


def dense_sum(grad):
    count = lax.axis_size("dp")
    grad = grad.reshape(count, grad.shape[0] // count, grad.shape[1])
    part = jnp.sum(swapped(grad).astype(FL), 0).astype(BF)
    bit = 1
    held = part[None]
    while bit < lax.axis_size("row"):
        held = jnp.concatenate([held, crossed(held, "row", bit)], 0)
        bit *= 2
    return jnp.sum(held.astype(FL), 0)


def on_device(
    patches,
    unpadded_patch_size,
    patch_expert_index,
    cotangent,
    query_key_value_weight,
    query_projection_bias,
    value_projection_bias,
    log_cosine_scale,
    bias_network_first_weight,
    bias_network_first_bias,
    bias_network_second_weight,
    output_projection_weight,
    output_projection_bias,
    attention_norm_gain,
    attention_norm_bias,
    routing_weight,
    expert_first_weight,
    expert_first_bias,
    expert_second_weight,
    expert_second_bias,
    expert_norm_gain,
    expert_norm_bias,
    patch_merging_weight,
    merging_norm_gain,
    merging_norm_bias,
):
    micro_count, _, band_rows, band_cols, channels = patches.shape
    micros = range(micro_count)
    half_rows = band_rows // 2
    win_count = band_cols // WINDOW_SIDE
    win_area = WINDOW_SIDE * WINDOW_SIDE
    tokens = band_rows * band_cols
    half = tokens // 2
    experts = routing_weight.shape[1]
    dp_size = lax.axis_size("dp")
    local = experts // dp_size
    capacity = (5 * tokens + 4 * experts - 1) // (4 * experts)
    slots = -(-capacity // 16) * 16
    buffer_rows = experts * slots
    total_rows = band_rows * lax.axis_size("row")
    row_start = band_rows * lax.axis_index("row")

    weight_qkv = gathered(query_key_value_weight)
    weight_late = gathered(
        jnp.concatenate(
            [output_projection_weight, jnp.pad(routing_weight, ((0, 0), (0, LANES - experts)))], 1
        )
    )
    weight_proj, weight_router = weight_late[:, :channels], weight_late[:, channels:]
    weight_merge = lax.all_gather(patch_merging_weight, "dp", axis=0, tiled=True)

    bands = patches.reshape(micro_count, tokens, channels)
    below = passed_along(bands[:, :half], "row", -1)

    table, table_back = jax.vjp(
        position_table,
        bias_network_first_weight,
        bias_network_first_bias,
        bias_network_second_weight,
    )
    bias_keys = spread_table(table)
    bias_rows = jnp.swapaxes(bias_keys, 1, 2)
    masks = [
        window_mask(
            row_start,
            total_rows,
            band_cols,
            unpadded_patch_size[m, 0, 0],
            unpadded_patch_size[m, 0, 1],
        )
        for m in micros
    ]
    masks_keys = [jnp.swapaxes(mask, 1, 2) for mask in masks]

    chosen = patch_expert_index.reshape(micro_count, tokens)
    one_hot = (chosen[:, :, None] == jnp.arange(experts)[None, None, :]).astype(FL)
    before = jnp.cumsum(one_hot, 1) - 1.0
    slot = jnp.sum(one_hot * before, -1).astype(jnp.int32)
    dest = jnp.where(slot < capacity, chosen * slots + slot, -1)

    lane = jnp.arange(LANES)
    head_marks = jnp.broadcast_to(
        ((lane // HEAD_DIM)[None, None, :] == jnp.arange(TILE_HEADS)[:, None, None]),
        (TILE_HEADS, win_area, LANES),
    ).astype(BF)
    block_ones = (
        ((jnp.arange(2 * LANES) % LANES) // HEAD_DIM)[:, None] == (lane // HEAD_DIM)[None, :]
    ).astype(BF)
    scale_lanes = jnp.repeat(jnp.exp(log_cosine_scale), HEAD_DIM)[None, :]
    qbias = query_projection_bias[None, :]
    vbias = value_projection_bias[None, :]
    attn_small = jnp.stack([output_projection_bias, attention_norm_gain, attention_norm_bias])
    moe_small = jnp.stack([expert_norm_gain, expert_norm_bias])
    merge_small = jnp.stack([merging_norm_gain, merging_norm_bias])
    first_bias = expert_first_bias[:, None, :]
    second_bias = expert_second_bias[:, None, :]

    grid_scratch = ((channels // LANES, band_rows * (band_cols + 8), LANES), FL)
    win_scratch = ((channels // LANES, tokens, LANES), FL)

    attended = [None] * micro_count
    arrived = [None] * micro_count
    routed = [None] * micro_count
    received = [None] * micro_count
    expert_out = [None] * micro_count
    returned = [None] * micro_count
    merged = [None] * micro_count
    back_res = [None] * micro_count
    expert_back = [None] * micro_count
    back_sent = [None] * micro_count
    settled = [None] * micro_count
    finished = [None] * micro_count
    outputs = [None] * micro_count
    input_grads = [None] * micro_count

    for m in micros:
        attended[m] = call_kernel(
            functools.partial(attend_forward_body, band_cols=band_cols, channels=channels),
            "attend_forward",
            [
                ((half, channels), BF),
                ((half, channels), BF),
                ((tokens, channels), BF),
                ((tokens, 3 * channels), BF),
                ((tokens, 2 * channels), FL),
            ],
            [
                bands[m],
                below[m],
                weight_qkv,
                qbias,
                vbias,
                scale_lanes,
                bias_rows,
                masks[m],
                head_marks,
                block_ones,
            ],
            [grid_scratch, win_scratch],
            flops=8 * 10**9,
        )
        arrived[m] = passed_along(attended[m][1], "row", 1)
        routed[m] = call_kernel(
            functools.partial(route_body, experts=experts),
            "route",
            [
                ((tokens, channels), FL),
                ((tokens, channels), BF),
                ((tokens, LANES), FL),
                ((tokens, channels), BF),
                ((buffer_rows, channels), BF),
            ],
            [
                arrived[m],
                attended[m][0],
                bands[m],
                weight_proj,
                attn_small,
                weight_router,
                chosen[m][:, None],
                dest[m][None, :],
            ],
            flops=4 * 10**9,
        )
        received[m] = swapped(routed[m][4].reshape(dp_size, local * slots, channels))
    for m in micros:
        expert_out[m] = expert_forward(
            received[m], expert_first_weight, first_bias, expert_second_weight, second_bias, local
        )
        returned[m] = swapped(expert_out[m][0])
    for m in micros:
        merged[m] = call_kernel(
            functools.partial(merge_body, experts=experts, band_cols=band_cols),
            "merge",
            [
                ((tokens // 4, 2 * channels), BF),
                ((tokens // 4, 4 * channels), BF),
                ((tokens // 4, 2 * channels), BF),
                ((tokens, channels), FL),
                ((tokens, LANES), BF),
                ((buffer_rows, channels), BF),
                ((8, 2 * channels), FL),
            ],
            [
                returned[m].reshape(buffer_rows, channels),
                dest[m][:, None],
                dest[m][None, :],
                chosen[m][:, None],
                routed[m][2],
                routed[m][0],
                moe_small,
                weight_merge,
                merge_small,
                cotangent[m, 0].reshape(tokens // 4, 2 * channels),
            ],
            [
                ((tokens, channels), FL),
                ((tokens, channels), FL),
                ((tokens, LANES), FL),
                ((channels // LANES, tokens, LANES), FL),
                ((tokens, channels), BF),
            ],
            flops=6 * 10**9,
        )
        outputs[m] = merged[m][0].reshape(band_rows // 2, band_cols // 2, 2 * channels)
        back_res[m] = swapped(merged[m][5].reshape(dp_size, local * slots, channels))
    for m in micros:
        expert_back[m] = expert_backward(
            back_res[m], expert_first_weight, expert_second_weight, expert_out[m][2], local
        )
        back_sent[m] = swapped(expert_back[m][0])

    grad_ein, grad_eout, grad_eout_bias = expert_weight_grads(
        received, [b[1] for b in expert_back], [b[1] for b in expert_out], back_res, local
    )
    grad_ein_bias = sum(b[2] for b in expert_back)
    grad_merge = merge_weight_grad([b[1] for b in merged], [b[2] for b in merged], channels)
    sum_ein, sum_eout = lax.psum((grad_ein, grad_eout), "row")
    sum_merge = dense_sum(grad_merge)
    expert_bias = summed(
        jnp.concatenate([grad_ein_bias[:, 0], grad_eout_bias[:, 0]], 1), ("row",)
    )

    for m in micros:
        settled[m] = call_kernel(
            settle_body,
            "settle",
            [
                ((tokens, channels), FL),
                ((tokens, channels), BF),
                ((tokens, channels), BF),
                ((8, channels), FL),
            ],
            [
                back_sent[m].reshape(buffer_rows, channels),
                dest[m][:, None],
                merged[m][3],
                merged[m][4],
                weight_router,
                routed[m][1],
                routed[m][2],
                attn_small,
                weight_proj,
            ],
            flops=3 * 10**9,
        )
        lifted = passed_along(settled[m][2][:half], "row", -1)
        finished[m] = call_kernel(
            functools.partial(attend_backward_body, band_cols=band_cols, channels=channels),
            "attend_backward",
            [
                ((half, channels), FL),
                ((half, channels), BF),
                ((channels, 3 * channels), FL),
                ((HEAD_COUNT, win_area, win_area), FL),
                ((8, channels), FL),
            ],
            [
                settled[m][2][half:],
                lifted,
                weight_qkv,
                scale_lanes,
                bias_keys,
                masks_keys[m],
                head_marks,
                block_ones,
                *attended[m][2:],
            ],
            [grid_scratch, win_scratch, ((tokens, 3 * channels), BF)],
            flops=16 * 10**9,
        )
        passed = passed_along(finished[m][1], "row", 1).astype(FL)
        input_grads[m] = (
            (settled[m][0] + jnp.concatenate([passed, finished[m][0]], 0))
            .astype(BF)
            .reshape(band_rows, band_cols, channels)
        )

    dense_args = []
    for m in micros:
        dense_args += [arrived[m], attended[m][0], settled[m][1], routed[m][3], merged[m][4]]
    grad_proj, grad_router = call_kernel(
        dense_body,
        "dense_weight_grads",
        [((channels, channels), BF), ((channels, LANES), BF)],
        dense_args,
    )
    sum_late = dense_sum(jnp.concatenate([grad_proj, grad_router], 1))
    sum_proj = sum_late[:, :channels]
    sum_router = sum_late[:, channels : channels + experts]
    sum_qkv = dense_sum(sum(f[2] for f in finished).astype(BF))

    both = ("row", "dp")
    settle_sums = sum(s[3] for s in settled)
    merge_sums = sum(b[6] for b in merged)
    early = summed(jnp.concatenate([settle_sums, merge_sums], 1), both)
    settle_sums, merge_sums = early[:, :channels], early[:, channels:]
    attn_sums = sum(f[4] for f in finished)
    dtable = gather_table(sum(f[3] for f in finished))
    late = jnp.concatenate([dtable.reshape(-1), attn_sums[:3].reshape(-1)])
    late = jnp.pad(late, (0, -late.size % 1024)).reshape(-1, 1024)
    late = summed(late, both).reshape(-1)
    dtable = late[: dtable.size].reshape(dtable.shape)
    attn_sums = late[dtable.size : dtable.size + 3 * channels].reshape(3, channels)
    grad_first, grad_first_bias, grad_second = table_back(dtable)
    sum_qbias, sum_vbias, sum_scale = attn_sums[0], attn_sums[1], attn_sums[2, ::HEAD_DIM]
    sum_proj_bias, sum_again, sum_ashift = settle_sums[0], settle_sums[1], settle_sums[2]
    sum_mgain, sum_mshift = merge_sums[2, :channels], merge_sums[3, :channels]
    sum_rgain, sum_rshift = merge_sums[0], merge_sums[1]
    hidden = expert_first_weight.shape[-1]
    sum_ein_bias, sum_eout_bias = expert_bias[:, :hidden], expert_bias[:, hidden:]
    return (
        jnp.stack(outputs)[:, None],
        jnp.stack(input_grads)[:, None],
        sum_qkv,
        sum_qbias,
        sum_vbias,
        sum_scale,
        grad_first,
        grad_first_bias,
        grad_second,
        sum_proj,
        sum_proj_bias,
        sum_again,
        sum_ashift,
        sum_router,
        sum_ein.astype(FL),
        sum_ein_bias,
        sum_eout.astype(FL),
        sum_eout_bias,
        sum_mgain,
        sum_mshift,
        sum_merge,
        sum_rgain,
        sum_rshift,
    )


def solution(mesh):
    return jax.shard_map(
        on_device,
        mesh=mesh,
        in_specs=(
            P(None, "dp", "row", None, None),
            P(None, "dp", None),
            P(None, "dp", "row", None, None),
            P(None, "dp", "row", None, None),
            P("dp", None),
            P(),
            P(),
            P(),
            P(),
            P(),
            P(),
            P("dp", None),
            P(),
            P(),
            P(),
            P("dp", None),
            P("dp", None, None),
            P("dp", None),
            P("dp", None, None),
            P("dp", None),
            P(),
            P(),
            P("dp", None),
            P(),
            P(),
        ),
        out_specs=(
            P(None, "dp", "row", None, None),
            P(None, "dp", "row", None, None),
            P("dp", None),
            P(),
            P(),
            P(),
            P(),
            P(),
            P(),
            P("dp", None),
            P(),
            P(),
            P(),
            P("dp", None),
            P("dp", None, None),
            P("dp", None),
            P("dp", None, None),
            P("dp", None),
            P(),
            P(),
            P("dp", None),
            P(),
            P(),
        ),
        check_vma=False,
    )
```

time: 1410 us -> 688 us (0.49)
  matrix products: 307 us -> 33.1 us
  Pallas kernels: 0 us -> 267 us
  waiting for transfers between devices: 377 us -> 154 us
  local copies, waits for them, and re-layouts: 266 us -> 65.1 us
  other arithmetic: 238 us -> 54 us
  blocking collectives: 147 us -> 0 us
  starting transfers between devices: 44.5 us -> 87.1 us
    dot_general x65 -> x9, matrix products: 307 us -> 33.1 us  [the longest x3 10.1 us: position_table(): jnp.einsum('qvw,wk->qvk', hidden_activation, bias_network_second_weight,...]
    pallas_call x0 -> x17, Pallas kernels: none -> 267 us  [the longest x11 194 us: call_kernel(): pl.pallas_call(body, name=name, out_shape=[jax.ShapeDtypeStruct(s, d) for...]
    reduce_scatter x6 -> x0, waiting for transfers between devices: 97.3 us -> none  [the longest x2 74 us: settle_dense(): lax.psum_scatter(grad_proj.astype(jnp.bfloat16), 'dp', scatter_dimension=...]
    all_gather x3 -> x0, blocking collectives: 94.1 us -> none  [the longest x1 32.6 us: fetch_weights(): lax.all_gather(query_key_value_weight, 'dp', axis=0, tiled=True)]
    reduce_sum x36 -> x7, other arithmetic: 95 us -> 7.29 us  [the longest x3 4.21 us: dense_sum(): part = jnp.sum(swapped(grad).astype(FL), 0).astype(BF)]
    psum x1, waiting for transfers between devices: 80.8 us -> 0.01 us  [on_device(): sum_ein, sum_eout = lax.psum((grad_ein, grad_eout), 'row')]
    reshape x34 -> x6, local copies, waits for them, and re-layouts: 92.4 us -> 13.5 us  [the longest x2 13.3 us: spread_table(): spread.reshape(table.shape[-1], WINDOW_SIDE * WINDOW_SIDE, WINDOW_SIDE *...]
    convert_element_type x28 -> x10, other arithmetic: 77.3 us -> 13.3 us  [the longest x1 4.65 us: on_device(): sum_ein.astype(FL)]
  transfers between devices with their start and end apart: 26 -> 40, of which waited for: 14 -> 17; matrix products, arithmetic and copies ran while one was open for 39% -> 21% of each run, Pallas kernels for 0% -> 38%
where the time goes in v1:
time: 688 us; the launch traced here: 676 us
  Pallas kernels  267 us (39%)
  waiting for transfers between devices  154 us (22%)
  starting transfers between devices  87.1 us (13%)
  local copies, waits for them, and re-layouts  65.1 us (9%)
  other arithmetic  54 us (8%)
  matrix products  33.1 us (5%)
  between operations  16 us (2%)
    pallas_call x11, Pallas kernels, call_kernel(): pl.pallas_call(body, name=name, out_shape=[jax.ShapeDtypeStruct(s, d) for...  194 us
    all_to_all x13, waiting for transfers between devices, swapped(): return lax.all_to_all(rows, 'dp', split_axis=0, concat_axis=0, tiled=True)  125 us
    all_to_all x13, starting transfers between devices, swapped(): return lax.all_to_all(rows, 'dp', split_axis=0, concat_axis=0, tiled=True)  64.2 us
    pallas_call x2, Pallas kernels, expert_forward(): pl.pallas_call(expert_forward_body, name='expert_forward', grid=(local, h...  31.1 us
    pallas_call x2, Pallas kernels, expert_backward(): pl.pallas_call(expert_backward_body, name='expert_backward', grid=(local,...  22 us
    ppermute x18, starting transfers between devices, crossed(): return lax.ppermute(array, axis, [(i, i ^ bit) for i in range(count)])  20.3 us
    pallas_call x1, Pallas kernels, expert_weight_grads(): pl.pallas_call(expert_weight_body, name='expert_weight_grads', grid=(loca...  14.6 us
    ppermute x18, waiting for transfers between devices, crossed(): return lax.ppermute(array, axis, [(i, i ^ bit) for i in range(count)])  14.1 us
  transfers between devices with their start and end apart: 40, of which 17 were waited for; matrix products, arithmetic and copies ran while one was open for 21% of the time, Pallas kernels for 38%

profile of v1, /device:TPU:0, one launch (start us, length us, event | category | flops | bytes accessed | tf_op | source)
XLA Modules:
  0.0 676.4 jit_solution(12989548142661565284)
XLA Ops:
  9.1 7.4 %all-to-all-start = ((bf16[8,48,1152]{2,1,0:T(8,128)(2,1)}), bf16[8,48,1152]{2,1,0:T(8,128)(2,1)}, u32[]{:S(2)}, u32[]{:S(2)}) async-start(bf16[8,48,1152]{2,1,0:T(8,128)(2,1)} %broadcast_in_dim.58), calls=%async_computation | async-start | bytes 1769472 | tf_op jit(solution)/shard_map/all_to_all | solution.py:850
  24.3 9.1 %reduce-window.6 = f32[2,16,9,128]{3,2,1,0:T(8,128)S(1)} reduce-window(f32[2,16,9,128]{3,2,1,0:T(8,128)S(1)} %fusion.19, f32[]{:T(128)} %constant.153.clone.1), window={size=1x1x1x128 pad=0_0x0_0x0_0x127_0}, to_apply=%region_1.2 | reduce-window | flops 4681728 | bytes 294916 | tf_op jit(solution)/shard_map/reduce-window
  43.0 9.0 %convolution_bitcast_fusion = f32[12,12,12,12,12]{2,1,4,3,0:T(8,128)} fusion(f32[23,12,12,12,1]{0,3,4,2,1:T(8,128)S(1)} %convolution_bitcast_fusion.1, s32[12,12]{1,0:T(8,128)S(1)} %subtract_add_fusion), kind=kOutput, calls=%fused_computation.1 | convolution fusion | flops 68680944 | bytes 1154880 | tf_op jit(solution)/shard_map/fqy,uzs,ysr->rqzfu/dot_general | solution.py:68
  52.1 10.2 %reshape.394 = f32[12,144,144]{1,2,0:T(8,128)} reshape(f32[12,12,12,12,12]{2,1,4,3,0:T(8,128)} %convolution_bitcast_fusion) | data formatting | bytes 1990656 | tf_op jit(solution)/shard_map/reshape | solution.py:69
  76.9 16.3 %attend_forward.3 = (bf16[576,384]{1,0:T(8,128)(2,1)S(1)}, bf16[576,384]{1,0:T(8,128)(2,1)S(1)}, bf16[1152,384]{1,0:T(8,128)(2,1)}, bf16[1152,1152]{1,0:T(8,128)(2,1)}, f32[1152,768]{1,0:T(8,128)}) custom-call(bf16[1152,384]{1,0:T(8,128)(2,1)} %bitcast.137, bf16[576,384]{1,0:T(8,128)(2,1)S(1)} %get-tuple-element.254.below_ref, ...), custom_call_target="tpu_custom_call" | custom-call | flops 8000000000 | bytes 4088320 | tf_op jit(solution)/shard_map/attend_forward/pallas_call | solution.py:135
  93.9 7.0 %collective-permute-done.2.arrived_ref.refs_5_ = bf16[576,384]{1,0:T(8,128)(2,1)S(1)} collective-permute-done((bf16[576,384]{1,0:T(8,128)(2,1)S(1)}, bf16[576,384]{1,0:T(8,128)(2,1)S(1)}, u32[]{:S(2)}, u32[]{:S(2)}) %collective-permute-start.2) | collective-permute-done | bytes 442400 | tf_op jit(solution)/shard_map/ppermute | solution.py:28
  100.9 12.5 %route.3 = (f32[1152,384]{1,0:T(8,128)}, bf16[1152,384]{1,0:T(8,128)(2,1)}, f32[1152,128]{1,0:T(8,128)S(1)}, bf16[1152,384]{1,0:T(8,128)(2,1)}, bf16[1536,384]{1,0:T(8,128)(2,1)}) custom-call(bf16[576,384]{1,0:T(8,128)(2,1)S(1)} %collective-permute-done.2.arrived_ref.refs_5_, bf16[576,384]{1,0:T(8,128)(2,1)S(1)} %get-tuple-element.100.own_ref.refs_6_, ...), custom_call_target="tpu_custom_call" | custom-call | flops 4000000000 | bytes 2176512 | tf_op jit(solution)/shard_map/route/pallas_call | solution.py:135
  114.2 6.0 all-to-all-start.4
  120.3 16.5 %attend_forward.2 = (bf16[576,384]{1,0:T(8,128)(2,1)S(1)}, bf16[576,384]{1,0:T(8,128)(2,1)S(1)}, bf16[1152,384]{1,0:T(8,128)(2,1)}, bf16[1152,1152]{1,0:T(8,128)(2,1)}, f32[1152,768]{1,0:T(8,128)}) custom-call(bf16[1152,384]{1,0:T(8,128)(2,1)} %bitcast.135, bf16[576,384]{1,0:T(8,128)(2,1)S(1)} %get-tuple-element.253.below_ref, ...), custom_call_target="tpu_custom_call" | custom-call | flops 8000000000 | bytes 4088320 | tf_op jit(solution)/shard_map/attend_forward/pallas_call | solution.py:135
  138.1 6.4 collective-permute-done.1.arrived_ref.refs_0_
  144.5 12.5 %route.2 = (f32[1152,384]{1,0:T(8,128)}, bf16[1152,384]{1,0:T(8,128)(2,1)}, f32[1152,128]{1,0:T(8,128)S(1)}, bf16[1152,384]{1,0:T(8,128)(2,1)}, bf16[1536,384]{1,0:T(8,128)(2,1)}) custom-call(bf16[576,384]{1,0:T(8,128)(2,1)S(1)} %collective-permute-done.1.arrived_ref.refs_0_, bf16[576,384]{1,0:T(8,128)(2,1)S(1)} %get-tuple-element.93.own_ref.refs_1_, ...), custom_call_target="tpu_custom_call" | custom-call | flops 4000000000 | bytes 2176512 | tf_op jit(solution)/shard_map/route/pallas_call | solution.py:135
  164.5 15.5 %expert_forward.3 = (bf16[8,192,384]{2,1,0:T(8,128)(2,1)}, bf16[2,768,1536]{2,1,0:T(8,128)(2,1)}, bf16[2,768,1536]{2,1,0:T(8,128)(2,1)}) custom-call(bf16[8,192,384]{2,1,0:T(8,128)(2,1)} %all-to-all-done.4.rows_ref.refs_4_, bf16[2,384,1536]{2,1,0:T(8,128)(2,1)} %win_ref.7, f32[2,1,1536]{2,1,0:T(1,128)S(1)} %broadcast_in_dim.122.bin_ref, ...), custom_call_target="tpu_custom_call" | custom-call | flops 3623878656 | bytes 18874368 | tf_op jit(solution)/shard_map/expert_forward/pallas_call | solution.py:709
  180.0 21.0 %all-to-all-done.2.rows_ref.refs_0_ = bf16[8,192,384]{2,1,0:T(8,128)(2,1)S(1)} async-done(((bf16[8,192,384]{2,1,0:T(8,128)(2,1)}), bf16[8,192,384]{2,1,0:T(8,128)(2,1)S(1)}, u32[]{:S(2)}, u32[]{:S(2)}) %all-to-all-start.2) | async-done | bytes 1179680 | tf_op jit(solution)/shard_map/all_to_all | solution.py:850
  205.6 15.6 %expert_forward.2 = (bf16[8,192,384]{2,1,0:T(8,128)(2,1)}, bf16[2,768,1536]{2,1,0:T(8,128)(2,1)}, bf16[2,768,1536]{2,1,0:T(8,128)(2,1)}) custom-call(bf16[8,192,384]{2,1,0:T(8,128)(2,1)} %copy-done.1, bf16[2,384,1536]{2,1,0:T(8,128)(2,1)} %win_ref.7, f32[2,1,1536]{2,1,0:T(1,128)S(1)} %broadcast_in_dim.122.bin_ref, bf16[2,1536,384]{2,1,0:T(8,128)(2,1)} %wout_ref.7, ...), custom_call_target="tpu_custom_call" | custom-call | flops 3623878656 | bytes 18874368 | tf_op jit(solution)/shard_map/expert_forward/pallas_call | solution.py:709
  221.2 29.6 %all-to-all-done.5 = bf16[8,192,384]{2,1,0:T(8,128)(2,1)S(1)} async-done(((bf16[8,192,384]{2,1,0:T(8,128)(2,1)}), bf16[8,192,384]{2,1,0:T(8,128)(2,1)S(1)}, u32[]{:S(2)}, u32[]{:S(2)}) %all-to-all-start.5) | async-done | bytes 1179680 | tf_op jit(solution)/shard_map/all_to_all | solution.py:850
  259.0 18.0 %merge.3 = (bf16[288,768]{1,0:T(8,128)(2,1)S(1)}, bf16[288,1536]{1,0:T(8,128)(2,1)}, bf16[288,768]{1,0:T(8,128)(2,1)S(1)}, f32[1152,384]{1,0:T(8,128)}, bf16[115...) custom-call(bf16[1536,384]{1,0:T(8,128)(2,1)} %bitcast.127, s32[1152,1]{1,0:T(8,128)} %copy.83.dest_col_ref, ...), custom_call_target="tpu_custom_call" | custom-call | flops 6000000000 | bytes 6363648 | tf_op jit(solution)/shard_map/merge/pallas_call | solution.py:135
  277.0 8.4 %all-to-all-done.3 = bf16[8,192,384]{2,1,0:T(8,128)(2,1)} async-done(((bf16[8,192,384]{2,1,0:T(8,128)(2,1)}), bf16[8,192,384]{2,1,0:T(8,128)(2,1)}, u32[]{:S(2)}, u32[]{:S(2)}) %all-to-all-start.3) | async-done | bytes 1179680 | tf_op jit(solution)/shard_map/all_to_all | solution.py:850
  290.9 18.0 %merge.2 = (bf16[288,768]{1,0:T(8,128)(2,1)S(1)}, bf16[288,1536]{1,0:T(8,128)(2,1)}, bf16[288,768]{1,0:T(8,128)(2,1)S(1)}, f32[1152,384]{1,0:T(8,128)}, bf16[115...) custom-call(bf16[1536,384]{1,0:T(8,128)(2,1)} %bitcast.21.returned_ref, ...), custom_call_target="tpu_custom_call" | custom-call | flops 6000000000 | bytes 6363648 | tf_op jit(solution)/shard_map/merge/pallas_call | solution.py:135
  311.1 7.1 %all-to-all-done.8.rows_ref.refs_7_ = bf16[8,192,384]{2,1,0:T(8,128)(2,1)} async-done(((bf16[8,192,384]{2,1,0:T(8,128)(2,1)}), bf16[8,192,384]{2,1,0:T(8,128)(2,1)}, u32[]{:S(2)}, u32[]{:S(2)}) %all-to-all-start.8) | async-done | bytes 1179680 | tf_op jit(solution)/shard_map/all_to_all | solution.py:850
  322.4 11.1 %expert_backward.3 = (bf16[8,192,384]{2,1,0:T(8,128)(2,1)}, bf16[2,768,1536]{2,1,0:T(8,128)(2,1)}, f32[2,1,1536]{2,1,0:T(1,128)S(1)}) custom-call(bf16[8,192,384]{2,1,0:T(8,128)(2,1)} %all-to-all-done.8.rows_ref.refs_7_, bf16[2,384,1536]{2,1,0:T(8,128)(2,1)} %win_ref.7, bf16[2,1536,384]{2,1,0:T(8,128)(2,1)} %wout_ref.7, ...), custom_call_target="tpu_custom_call" | custom-call | flops 3623878656 | bytes 14155776 | tf_op jit(solution)/shard_map/expert_backward/pallas_call | solution.py:765
  333.5 17.2 %all-to-all-done.6.rows_ref.refs_3_ = bf16[8,192,384]{2,1,0:T(8,128)(2,1)} async-done(((bf16[8,192,384]{2,1,0:T(8,128)(2,1)}), bf16[8,192,384]{2,1,0:T(8,128)(2,1)}, u32[]{:S(2)}, u32[]{:S(2)}) %all-to-all-start.6) | async-done | bytes 1179680 | tf_op jit(solution)/shard_map/all_to_all | solution.py:850
  355.0 11.0 %expert_backward.2 = (bf16[8,192,384]{2,1,0:T(8,128)(2,1)}, bf16[2,768,1536]{2,1,0:T(8,128)(2,1)}, f32[2,1,1536]{2,1,0:T(1,128)S(1)}) custom-call(bf16[8,192,384]{2,1,0:T(8,128)(2,1)} %all-to-all-done.6.rows_ref.refs_3_, bf16[2,384,1536]{2,1,0:T(8,128)(2,1)} %win_ref.7, bf16[2,1536,384]{2,1,0:T(8,128)(2,1)} %wout_ref.7, ...), custom_call_target="tpu_custom_call" | custom-call | flops 3623878656 | bytes 14155776 | tf_op jit(solution)/shard_map/expert_backward/pallas_call | solution.py:765
  365.9 17.3 %all-to-all-done.9 = bf16[8,192,384]{2,1,0:T(8,128)(2,1)} async-done(((bf16[8,192,384]{2,1,0:T(8,128)(2,1)}), bf16[8,192,384]{2,1,0:T(8,128)(2,1)}, u32[]{:S(2)}, u32[]{:S(2)}) %all-to-all-start.9) | async-done | bytes 1179680 | tf_op jit(solution)/shard_map/all_to_all | solution.py:850
  394.5 21.3 %all-to-all-done.7 = bf16[8,192,384]{2,1,0:T(8,128)(2,1)} async-done(((bf16[8,192,384]{2,1,0:T(8,128)(2,1)}), bf16[8,192,384]{2,1,0:T(8,128)(2,1)}, u32[]{:S(2)}, u32[]{:S(2)}) %all-to-all-start.7) | async-done | bytes 1179680 | tf_op jit(solution)/shard_map/all_to_all | solution.py:850
  420.4 14.6 %expert_weight_grads.1 = (bf16[2,384,1536]{2,1,0:T(8,128)(2,1)}, bf16[2,1536,384]{2,1,0:T(8,128)(2,1)}, f32[2,1,384]{2,1,0:T(1,128)S(1)}) custom-call(bf16[8,192,384]{2,1,0:T(8,128)(2,1)S(1)} %copy-done.2, bf16[2,768,1536]{2,1,0:T(8,128)(2,1)} %get-tuple-element.148.refs_1_, bf16[2,768,1536]{2,1,0:T(8,128)(2,1)} %get-tuple-element.149.refs_2_, ...), custom_call_target="tpu_custom_call" | custom-call | flops 7247757312 | bytes 18874368 | tf_op jit(solution)/shard_map/expert_weight_grads/pallas_call | solution.py:825
  435.1 6.9 %multiply_bitcast_fusion = f32[12,12,12,12,23]{4,3,2,1,0:T(8,128)} fusion(f32[12,12,23]{2,0,1:T(8,128)S(1)} %copy-done.47, f32[12,12]{1,0:T(8,128)S(1)} %copy-done.60), kind=kLoop, calls=%fused_computation | loop fusion | flops 476928 | bytes 1921536 | tf_op jit(solution)/shard_map/jkb,ic->kijcb/transpose | solution.py:76
  445.0 10.6 %reshape_reshape.3 = f32[1728,276]{1,0:T(8,128)} reshape(f32[12,12,12,12,23]{4,3,2,1,0:T(8,128)} %multiply_bitcast_fusion) | data formatting | bytes 3815424 | tf_op jit(solution)/shard_map/reshape;reshape | solution.py:81
  463.2 10.0 %settle.3 = (f32[1152,384]{1,0:T(8,128)}, bf16[1152,384]{1,0:T(8,128)(2,1)}, bf16[1152,384]{1,0:T(8,128)(2,1)}, f32[8,384]{1,0:T(8,128)S(1)}) custom-call(bf16[1536,384]{1,0:T(8,128)(2,1)} %bitcast.40.sent_ref, s32[1152,1]{1,0:T(8,128)S(1)} %copy-done.4, f32[1152,384]{1,0:T(8,128)} %get-tuple-element.122.dresid_ref, bf16[1152,128]{1,0:T(8,128)(2,1)S(1)} %copy-done.11, ...), custom_call_target="tpu_custom_call" | custom-call | flops 3000000000 | bytes 5121024 | tf_op jit(solution)/shard_map/settle/pallas_call | solution.py:135
  473.2 10.0 %settle.2 = (f32[1152,384]{1,0:T(8,128)}, bf16[1152,384]{1,0:T(8,128)(2,1)}, bf16[1152,384]{1,0:T(8,128)(2,1)}, f32[8,384]{1,0:T(8,128)S(1)}) custom-call(bf16[1536,384]{1,0:T(8,128)(2,1)} %bitcast.37.sent_ref, s32[1152,1]{1,0:T(8,128)S(1)} %copy-done.5, f32[1152,384]{1,0:T(8,128)} %get-tuple-element.109.dresid_ref, bf16[1152,128]{1,0:T(8,128)(2,1)S(1)} %copy-done.13, ...), custom_call_target="tpu_custom_call" | custom-call | flops 3000000000 | bytes 5121024 | tf_op jit(solution)/shard_map/settle/pallas_call | solution.py:135
  508.5 37.9 %attend_backward.3 = (f32[576,384]{1,0:T(8,128)}, bf16[576,384]{1,0:T(8,128)(2,1)S(1)}, f32[384,1152]{1,0:T(8,128)}, f32[12,144,144]{2,1,0:T(8,128)}, f32[8,384]{1,0:T(8,128)S(1)}) custom-call(bf16[576,384]{1,0:T(8,128)(2,1)S(1)} %get-tuple-element.250.own_ref, bf16[576,384]{1,0:T(8,128)(2,1)} %collective-permute-done.5.lifted_ref, ...), custom_call_target="tpu_custom_call" | custom-call | flops 16000000000 | bytes 10720768 | tf_op jit(solution)/shard_map/attend_backward/pallas_call | solution.py:135
  546.4 38.5 %attend_backward.2 = (f32[576,384]{1,0:T(8,128)}, bf16[576,384]{1,0:T(8,128)(2,1)S(1)}, f32[384,1152]{1,0:T(8,128)}, f32[12,144,144]{2,1,0:T(8,128)}, f32[8,384]{1,0:T(8,128)S(1)}) custom-call(bf16[576,384]{1,0:T(8,128)(2,1)S(1)} %get-tuple-element.248.own_ref, bf16[576,384]{1,0:T(8,128)(2,1)S(1)} %collective-permute-done.3.lifted_ref, ...), custom_call_target="tpu_custom_call" | custom-call | flops 16000000000 | bytes 10720768 | tf_op jit(solution)/shard_map/attend_backward/pallas_call | solution.py:135
  588.8 8.6 %fusion.6 = f32[12,12,12,23]{3,1,2,0:T(8,128)S(1)} fusion(f32[12,23,1728,1]{2,1,0,3:T(8,128)} %reshape.390, f32[12,12,1728,1]{2,1,0,3:T(8,128)} %reshape.389), kind=kOutput, calls=%fused_computation.20 | convolution fusion | flops 824131584 | bytes 3062016 | tf_op jit(solution)/shard_map/dot_general | solution.py:79
  (387 shorter events, 199.4 us)
Async XLA Ops:
  9.1 61.0 %all-to-all-start = ((bf16[8,48,1152]{2,1,0:T(8,128)(2,1)}), bf16[8,48,1152]{2,1,0:T(8,128)(2,1)}, u32[]{:S(2)}, u32[]{:S(2)}) async-start(bf16[8,48,1152]{2,1,0:T(8,128)(2,1)} %broadcast_in_dim.58), calls=%async_computation | async-start | bytes 1769472 | tf_op jit(solution)/shard_map/all_to_all | solution.py:850
  17.6 51.2 %collective-permute-start = (bf16[2,576,384]{2,1,0:T(8,128)(2,1)}, bf16[2,576,384]{2,1,0:T(8,128)(2,1)}, u32[]{:S(2)}, u32[]{:S(2)}) collective-permute-start(bf16[2,576,384]{2,1,0:T(8,128)(2,1)} %slice.187), channel_id=1, source_target_pairs={{0,3},{1,0},{2,1},{3,2},{4,7},{5,4},{6,5},{7,6},{8,11},{9,8},{10,9... | collective-permute-start | bytes 2654216 | tf_op jit(solution)/shard_map/ppermute | solution.py:28
  70.9 22.9 %all-to-all-start.1 = ((bf16[8,48,512]{2,1,0:T(8,128)(2,1)}), bf16[8,48,512]{2,1,0:T(8,128)(2,1)S(1)}, u32[]{:S(2)}, u32[]{:S(2)}) async-start(bf16[8,48,512]{2,1,0:T(8,128)(2,1)} %broadcast_in_dim.120), calls=%async_computation.1 | async-start | bytes 786432 | tf_op jit(solution)/shard_map/all_to_all | solution.py:850
  93.2 7.7 %collective-permute-start.2 = (bf16[576,384]{1,0:T(8,128)(2,1)S(1)}, bf16[576,384]{1,0:T(8,128)(2,1)S(1)}, u32[]{:S(2)}, u32[]{:S(2)}) collective-permute-start(bf16[576,384]{1,0:T(8,128)(2,1)S(1)} %get-tuple-element.99), channel_id=1, source_target_pairs={{0,1},{1,2},{2,3},{3,0},{4,5},{5,6},{6,7},{7,4},{8,9},{9,10},{10,1... | collective-permute-start | bytes 1327112 | tf_op jit(solution)/shard_map/ppermute | solution.py:28
  114.2 42.7 %all-to-all-start.4 = ((bf16[8,192,384]{2,1,0:T(8,128)(2,1)}), bf16[8,192,384]{2,1,0:T(8,128)(2,1)}, u32[]{:S(2)}, u32[]{:S(2)}) async-start(bf16[8,192,384]{2,1,0:T(8,128)(2,1)} %bitcast.129), calls=%async_computation.4 | async-start | bytes 2359296 | tf_op jit(solution)/shard_map/all_to_all | solution.py:850
  136.8 7.7 %collective-permute-start.1 = (bf16[576,384]{1,0:T(8,128)(2,1)S(1)}, bf16[576,384]{1,0:T(8,128)(2,1)S(1)}, u32[]{:S(2)}, u32[]{:S(2)}) collective-permute-start(bf16[576,384]{1,0:T(8,128)(2,1)S(1)} %get-tuple-element.92), channel_id=1, source_target_pairs={{0,1},{1,2},{2,3},{3,0},{4,5},{5,6},{6,7},{7,4},{8,9},{9,10},{10,1... | collective-permute-start | bytes 1327112 | tf_op jit(solution)/shard_map/ppermute | solution.py:28
  157.8 43.3 %all-to-all-start.2 = ((bf16[8,192,384]{2,1,0:T(8,128)(2,1)}), bf16[8,192,384]{2,1,0:T(8,128)(2,1)S(1)}, u32[]{:S(2)}, u32[]{:S(2)}) async-start(bf16[8,192,384]{2,1,0:T(8,128)(2,1)} %bitcast.130), calls=%async_computation.2 | async-start | bytes 2359296 | tf_op jit(solution)/shard_map/all_to_all | solution.py:850
  163.8 95.2 %all-gather.2.cloned.1.call-start = ((), (), s32[]{:S(2)}) async-start(), calls=%async_computation.13 | async-start | bytes 2654208 | tf_op jit(solution)/shard_map/all_gather | solution.py:935
  202.1 48.8 %all-to-all-start.5 = ((bf16[8,192,384]{2,1,0:T(8,128)(2,1)}), bf16[8,192,384]{2,1,0:T(8,128)(2,1)S(1)}, u32[]{:S(2)}, u32[]{:S(2)}) async-start(bf16[8,192,384]{2,1,0:T(8,128)(2,1)} %get-tuple-element.102), calls=%async_computation.5 | async-start | bytes 2359296 | tf_op jit(solution)/shard_map/all_to_all | solution.py:850
  251.9 33.6 %all-to-all-start.3 = ((bf16[8,192,384]{2,1,0:T(8,128)(2,1)}), bf16[8,192,384]{2,1,0:T(8,128)(2,1)}, u32[]{:S(2)}, u32[]{:S(2)}) async-start(bf16[8,192,384]{2,1,0:T(8,128)(2,1)} %get-tuple-element.95), calls=%async_computation.3 | async-start | bytes 2359296 | tf_op jit(solution)/shard_map/all_to_all | solution.py:850
  285.4 32.7 %all-to-all-start.8 = ((bf16[8,192,384]{2,1,0:T(8,128)(2,1)}), bf16[8,192,384]{2,1,0:T(8,128)(2,1)}, u32[]{:S(2)}, u32[]{:S(2)}) async-start(bf16[8,192,384]{2,1,0:T(8,128)(2,1)} %bitcast.128), calls=%async_computation.8 | async-start | bytes 2359296 | tf_op jit(solution)/shard_map/all_to_all | solution.py:850
  318.2 32.5 %all-to-all-start.6 = ((bf16[8,192,384]{2,1,0:T(8,128)(2,1)}), bf16[8,192,384]{2,1,0:T(8,128)(2,1)}, u32[]{:S(2)}, u32[]{:S(2)}) async-start(bf16[8,192,384]{2,1,0:T(8,128)(2,1)} %bitcast.131), calls=%async_computation.6 | async-start | bytes 2359296 | tf_op jit(solution)/shard_map/all_to_all | solution.py:850
  350.7 32.5 %all-to-all-start.9 = ((bf16[8,192,384]{2,1,0:T(8,128)(2,1)}), bf16[8,192,384]{2,1,0:T(8,128)(2,1)}, u32[]{:S(2)}, u32[]{:S(2)}) async-start(bf16[8,192,384]{2,1,0:T(8,128)(2,1)} %get-tuple-element.121), calls=%async_computation.9 | async-start | bytes 2359296 | tf_op jit(solution)/shard_map/all_to_all | solution.py:850
  383.2 32.6 %all-to-all-start.7 = ((bf16[8,192,384]{2,1,0:T(8,128)(2,1)}), bf16[8,192,384]{2,1,0:T(8,128)(2,1)}, u32[]{:S(2)}, u32[]{:S(2)}) async-start(bf16[8,192,384]{2,1,0:T(8,128)(2,1)} %get-tuple-element.108), calls=%async_computation.7 | async-start | bytes 2359296 | tf_op jit(solution)/shard_map/all_to_all | solution.py:850
  415.8 87.4 %all-to-all-start.12 = ((bf16[8,192,768]{2,1,0:T(8,128)(2,1)}), bf16[8,192,768]{2,1,0:T(8,128)(2,1)}, u32[]{:S(2)}, u32[]{:S(2)}) async-start(bf16[8,192,768]{2,1,0:T(8,128)(2,1)} %bitcast.118), calls=%async_computation.12 | async-start | bytes 4718592 | tf_op jit(solution)/shard_map/all_to_all | solution.py:850
  420.3 196.3 %all-reduce.5.cloned.1.call-start = ((), (), s32[]{:S(2)}) async-start(), calls=%async_computation.14 | async-start | bytes 9437184 | tf_op jit(solution)/shard_map/psum | solution.py:1103
  435.0 26.7 %collective-permute-start.21 = (f32[2,1920]{1,0:T(2,128)S(1)}, f32[2,1920]{1,0:T(2,128)S(1)}, u32[]{:S(2)}, u32[]{:S(2)}) collective-permute-start(f32[2,1920]{1,0:T(2,128)S(1)} %pad_maximum_fusion.8), channel_id=1, source_target_pairs={{0,1},{1,0},{2,3},{3,2},{4,5},{5,4},{6,7},{7,6},{8,9},{9,8},{10,11... | collective-permute-start | bytes 46088 | tf_op jit(solution)/shard_map/ppermute | solution.py:861
  461.8 25.7 %collective-permute-start.22 = (f32[2,1920]{1,0:T(2,128)S(1)}, f32[2,1920]{1,0:T(2,128)}, u32[]{:S(2)}, u32[]{:S(2)}) collective-permute-start(f32[2,1920]{1,0:T(2,128)S(1)} %fusion.59), channel_id=1, source_target_pairs={{0,2},{1,3},{2,0},{3,1},{4,6},{5,7},{6,4},{7,5},{8,10},{9,11},{10,... | collective-permute-start | bytes 46088 | tf_op jit(solution)/shard_map/ppermute | solution.py:861
  484.4 24.2 %collective-permute-start.5 = (bf16[576,384]{1,0:T(8,128)(2,1)}, bf16[576,384]{1,0:T(8,128)(2,1)}, u32[]{:S(2)}, u32[]{:S(2)}) collective-permute-start(bf16[576,384]{1,0:T(8,128)(2,1)} %get-tuple-element.249), channel_id=1, source_target_pairs={{0,3},{1,0},{2,1},{3,2},{4,7},{5,4},{6,5},{7,6},{8,11},{9,8},{10,9... | collective-permute-start | bytes 1327112 | tf_op jit(solution)/shard_map/ppermute | solution.py:28
  485.0 8.2 %collective-permute-start.17 = (f32[8,1152]{1,0:T(8,128)S(1)}, f32[8,1152]{1,0:T(8,128)S(1)}, u32[]{:S(2)}, u32[]{:S(2)}) collective-permute-start(f32[8,1152]{1,0:T(8,128)S(1)} %fusion.58), channel_id=1, source_target_pairs={{0,2},{1,3},{2,0},{3,1},{4,6},{5,7},{6,4},{7,5},{8,10},{9,11},{10,... | collective-permute-start | bytes 110600 | tf_op jit(solution)/shard_map/ppermute | solution.py:861
  497.0 49.4 %collective-permute-start.3 = (bf16[576,384]{1,0:T(8,128)(2,1)}, bf16[576,384]{1,0:T(8,128)(2,1)S(1)}, u32[]{:S(2)}, u32[]{:S(2)}) collective-permute-start(bf16[576,384]{1,0:T(8,128)(2,1)} %get-tuple-element.247), channel_id=1, source_target_pairs={{0,3},{1,0},{2,1},{3,2},{4,7},{5,4},{6,5},{7,6},{8,11},{9,8},{10,9... | collective-permute-start | bytes 1327112 | tf_op jit(solution)/shard_map/ppermute | solution.py:28
  497.2 8.9 %collective-permute-start.19 = (f32[8,1152]{1,0:T(8,128)S(1)}, f32[8,1152]{1,0:T(8,128)S(1)}, u32[]{:S(2)}, u32[]{:S(2)}) collective-permute-start(f32[8,1152]{1,0:T(8,128)S(1)} %add.335), channel_id=1, source_target_pairs={{0,8},{4,12},{8,0},{12,4},{16,24},{20,28},{24,16},{28,20},{1,9},{5... | collective-permute-start | bytes 110600 | tf_op jit(solution)/shard_map/ppermute | solution.py:861
  506.1 107.7 %collective-permute-start.23 = (bf16[1,192,768]{2,1,0:T(8,128)(2,1)}, bf16[1,192,768]{2,1,0:T(8,128)(2,1)}, u32[]{:S(2)}, u32[]{:S(2)}) collective-permute-start(bf16[1,192,768]{2,1,0:T(8,128)(2,1)} %bitcast.57), channel_id=1, source_target_pairs={{0,1},{1,0},{2,3},{3,2},{4,5},{5,4},{6,7},{7,6},{8,9},{9,8},{10,11... | collective-permute-start | bytes 884744 | tf_op jit(solution)/shard_map/ppermute | solution.py:861
  506.1 97.2 %collective-permute-start.20 = (f32[8,1152]{1,0:T(8,128)S(1)}, f32[8,1152]{1,0:T(8,128)S(1)}, u32[]{:S(2)}, u32[]{:S(2)}) collective-permute-start(f32[8,1152]{1,0:T(8,128)S(1)} %add.336), channel_id=1, source_target_pairs={{0,16},{4,20},{8,24},{12,28},{16,0},{20,4},{24,8},{28,12},{1,17},{... | collective-permute-start | bytes 110600 | tf_op jit(solution)/shard_map/ppermute | solution.py:861
  599.5 31.0 %all-to-all-start.11 = ((bf16[8,48,512]{2,1,0:T(8,128)(2,1)}), bf16[8,48,512]{2,1,0:T(8,128)(2,1)S(1)}, u32[]{:S(2)}, u32[]{:S(2)}) async-start(bf16[8,48,512]{2,1,0:T(8,128)(2,1)} %bitcast.54), calls=%async_computation.11 | async-start | bytes 786432 | tf_op jit(solution)/shard_map/all_to_all | solution.py:850
  611.3 13.9 %collective-permute-start.12 = (f32[8,1024]{1,0:T(8,128)S(1)}, f32[8,1024]{1,0:T(8,128)S(1)}, u32[]{:S(2)}, u32[]{:S(2)}) collective-permute-start(f32[8,1024]{1,0:T(8,128)S(1)} %add.328), channel_id=1, source_target_pairs={{0,8},{4,12},{8,0},{12,4},{16,24},{20,28},{24,16},{28,20},{1,9},{5... | collective-permute-start | bytes 98312 | tf_op jit(solution)/shard_map/ppermute | solution.py:861
  615.7 47.2 %collective-permute-start.24 = (bf16[2,192,768]{2,1,0:T(8,128)(2,1)}, bf16[2,192,768]{2,1,0:T(8,128)(2,1)}, u32[]{:S(2)}, u32[]{:S(2)}) collective-permute-start(bf16[2,192,768]{2,1,0:T(8,128)(2,1)} %pad_maximum_fusion), channel_id=1, source_target_pairs={{0,2},{1,3},{2,0},{3,1},{4,6},{5,7},{6,4},{7,5},{8,10},{9,11},{10,... | collective-permute-start | bytes 1769480 | tf_op jit(solution)/shard_map/ppermute | solution.py:861
  624.0 27.2 %collective-permute-start.6 = (bf16[576,384]{1,0:T(8,128)(2,1)S(1)}, bf16[576,384]{1,0:T(8,128)(2,1)}, u32[]{:S(2)}, u32[]{:S(2)}) collective-permute-start(bf16[576,384]{1,0:T(8,128)(2,1)S(1)} %get-tuple-element.130), channel_id=1, source_target_pairs={{0,1},{1,2},{2,3},{3,0},{4,5},{5,6},{6,7},{7,4},{8,9},{9,10},{10,1... | collective-permute-start | bytes 1327112 | tf_op jit(solution)/shard_map/ppermute | solution.py:28
  624.0 28.4 %collective-permute-start.4 = (bf16[576,384]{1,0:T(8,128)(2,1)S(1)}, bf16[576,384]{1,0:T(8,128)(2,1)}, u32[]{:S(2)}, u32[]{:S(2)}) collective-permute-start(bf16[576,384]{1,0:T(8,128)(2,1)S(1)} %get-tuple-element.117), channel_id=1, source_target_pairs={{0,1},{1,2},{2,3},{3,0},{4,5},{5,6},{6,7},{7,4},{8,9},{9,10},{10,1... | collective-permute-start | bytes 1327112 | tf_op jit(solution)/shard_map/ppermute | solution.py:28
  630.6 26.8 %all-to-all-start.10 = ((bf16[8,48,1152]{2,1,0:T(8,128)(2,1)}), bf16[8,48,1152]{2,1,0:T(8,128)(2,1)}, u32[]{:S(2)}, u32[]{:S(2)}) async-start(bf16[8,48,1152]{2,1,0:T(8,128)(2,1)} %bitcast.124), calls=%async_computation.10 | async-start | bytes 1769472 | tf_op jit(solution)/shard_map/all_to_all | solution.py:850
  644.5 5.3 collective-permute-start.15
  660.4 7.9 %collective-permute-start.8 = (bf16[2,48,1152]{2,1,0:T(8,128)(2,1)S(1)}, bf16[2,48,1152]{2,1,0:T(8,128)(2,1)S(1)}, u32[]{:S(2)}, u32[]{:S(2)}) collective-permute-start(bf16[2,48,1152]{2,1,0:T(8,128)(2,1)S(1)} %pad_maximum_fusion.2), channel_id=1, source_target_pairs={{0,2},{1,3},{2,0},{3,1},{4,6},{5,7},{6,4},{7,5},{8,10},{9,11},{10,... | collective-permute-start | bytes 663560 | tf_op jit(solution)/shard_map/ppermute | solution.py:861
  (87 other events, 909.2 us)
Sparse Core Ops, SparseCore 0:
  166.8 81.1 all-gather.1
  487.5 99.3 all-reduce.4

commit v2 on v1

v2 whole, which is shorter than its diff:
```python
import functools

import jax
import jax.numpy as jnp
from jax import lax
from jax.experimental import pallas as pl
from jax.experimental.pallas import tpu as pltpu
from jax.sharding import PartitionSpec as P

HEAD_COUNT = 12
HEAD_DIM = 32
WINDOW_SIDE = 12
LANES = 128
SHEAR = 384
ZONES = 16
UNROLL = 2
COST_SCALE = 0.4
TILE_HEADS = LANES // HEAD_DIM


PRECISION_HIGH = lax.Precision.HIGHEST
EPS_NORM = 1e-05
EPS_UNIT = 1e-06
MASK_FILL = -100.0
BF = jnp.bfloat16
FL = jnp.float32
VMEM_BYTES = 52 * 2**20


def cost(micros):
    return pl.CostEstimate(
        flops=int(micros * COST_SCALE * 1.1e9), bytes_accessed=10**5, transcendentals=0
    )


def passed_along(array, axis, by):
    count = lax.axis_size(axis)
    return lax.ppermute(array, axis, [(i, (i + by) % count) for i in range(count)])


def exact_error_gelu(values):
    return jax.nn.gelu(values, approximate=False)


def position_table(
    bias_network_first_weight, bias_network_first_bias, bias_network_second_weight
):
    span_axis = (jnp.arange(2 * WINDOW_SIDE - 1, dtype=FL) - (WINDOW_SIDE - 1)) * (
        8.0 / (WINDOW_SIDE - 1)
    )
    span_axis = jnp.sign(span_axis) * jnp.log2(jnp.abs(span_axis) + 1.0) / 3.0
    grid_rows = jnp.broadcast_to(span_axis[:, None], (2 * WINDOW_SIDE - 1, 2 * WINDOW_SIDE - 1))
    relative_coordinates = jnp.stack([grid_rows, grid_rows.T], -1)
    hidden_activation = exact_error_gelu(
        jnp.einsum(
            "plr,rt->plt", relative_coordinates, bias_network_first_weight, precision=PRECISION_HIGH
        )
        + bias_network_first_bias
    )
    return 16.0 * jax.nn.sigmoid(
        jnp.einsum(
            "qvw,wk->qvk", hidden_activation, bias_network_second_weight, precision=PRECISION_HIGH
        )
    )


def toeplitz_lines(table):
    side = WINDOW_SIDE
    heads = table.shape[-1]
    by_head = table.transpose(2, 0, 1)
    above = by_head[:, :, side - 1 :].reshape(heads, -1)
    below = jnp.pad(by_head[:, :, : side - 1], ((0, 0), (0, 0), (1, 0))).reshape(heads, -1)
    lines = jnp.pad(
        jnp.stack([above, below], 1), ((0, 0), (0, 0), (0, SHEAR - above.shape[1]))
    )
    lines = jnp.stack(
        [
            jnp.roll(lines[:, 0], -side * (side - 1), -1),
            jnp.roll(lines[:, 1], -side * side, -1),
        ],
        1,
    )
    back = jnp.roll(jnp.flip(lines, -1), 1, -1)
    return jnp.concatenate([lines, back], 1)


def table_of_lines(lines):
    side = WINDOW_SIDE
    spans = 2 * side - 1
    above = lines[:, 0, side - 1 : side - 1 + spans * side].reshape(-1, spans, side)
    below = jnp.pad(lines[:, 1], ((0, 0), (1, 0)))[:, : spans * side].reshape(-1, spans, side)
    return jnp.concatenate([below[:, :, 1:], above], 2).transpose(1, 2, 0)


def mask_operands(row_start, total_rows, total_cols, valid_rows, valid_cols):
    half_win = WINDOW_SIDE // 2
    rows_at = row_start + jnp.arange(WINDOW_SIDE)
    cols_at = jnp.arange(total_cols)
    row_zone = (rows_at >= total_rows - WINDOW_SIDE).astype(jnp.int32) + (
        rows_at >= total_rows - half_win
    ).astype(jnp.int32)
    col_zone = (cols_at >= total_cols - WINDOW_SIDE).astype(jnp.int32) + (
        cols_at >= total_cols - half_win
    ).astype(jnp.int32)
    zone_ids = 3 * row_zone[:, None] + col_zone[None, :]
    outside = ((rows_at + half_win) % total_rows >= valid_rows)[:, None] | (
        (cols_at + half_win) % total_cols >= valid_cols
    )[None, :]
    codes = zone_ids + jnp.where(outside, ZONES, 0)
    win_count = total_cols // WINDOW_SIDE
    codes = (
        codes.reshape(WINDOW_SIDE, win_count, WINDOW_SIDE)
        .transpose(1, 0, 2)
        .reshape(win_count, WINDOW_SIDE * WINDOW_SIDE)
    )
    zones, out = codes % ZONES, codes // ZONES
    mask = jnp.where(zones[:, :, None] != zones[:, None, :], MASK_FILL, 0.0) + jnp.where(
        out[:, None, :] > 0, MASK_FILL, 0.0
    )
    peak = jnp.max(mask, -1)[:, :, None]
    lane = jnp.arange(LANES)
    same = zones[:, :, None] == lane
    query = jnp.where(
        lane < ZONES,
        jnp.where(same, -MASK_FILL, 0.0),
        jnp.where(lane == ZONES, MASK_FILL, jnp.where(lane == ZONES + 1, MASK_FILL - peak, 0.0)),
    )
    key = jnp.where(
        lane < ZONES,
        jnp.where(same, 1.0, 0.0),
        jnp.where(lane == ZONES, out[:, :, None], jnp.where(lane == ZONES + 1, 1.0, 0.0)),
    )
    return (
        query.astype(BF).reshape(-1, LANES),
        key.astype(BF).reshape(-1, LANES),
    )


def plus(left, right):
    return left.astype(FL) + right.astype(FL)


def mm(left, right):
    return jnp.dot(left, right, preferred_element_type=FL)


def mm_nt(left, right):
    return lax.dot_general(left, right, (((1,), (1,)), ((), ())), preferred_element_type=FL)


def mm_tn(left, right):
    return lax.dot_general(left, right, (((0,), (0,)), ((), ())), preferred_element_type=FL)


def skipping(body, count, extra):
    def run(*refs):
        return body(*refs[:count], *refs[count + extra :])

    return run


def call_kernel(body, name, outs, args, scratch=(), micros=5, after=()):
    specs, arrays = [], []
    for arg in args:
        array, spec = arg if isinstance(arg, tuple) else (arg, None)
        if spec is None:
            spec = pl.BlockSpec(array.shape, lambda i, rank=array.ndim: (0,) * rank)
        specs.append(spec)
        arrays.append(array)
    return pl.pallas_call(
        skipping(body, len(args), len(after)),
        name=name,
        grid=(1,),
        out_shape=[jax.ShapeDtypeStruct(s, d) for s, d in outs],
        in_specs=specs + [pl.BlockSpec(memory_space=pl.ANY)] * len(after),
        out_specs=[pl.BlockSpec(s, lambda i, rank=len(s): (0,) * rank) for s, _ in outs],
        scratch_shapes=[pltpu.VMEM(s, d) for s, d in scratch],
        compiler_params=pltpu.CompilerParams(vmem_limit_bytes=VMEM_BYTES),
        cost_estimate=cost(micros),
    )(*arrays, *after)


def rows_at(start, size):
    return pl.ds(pl.multiple_of(start, 16), size)


def head_sums(values, block_ones):
    high = values.astype(BF)
    rest = (values - high.astype(FL)).astype(BF)
    return mm(jnp.concatenate([high, rest], 1), block_ones)


def tiles_of(channels):
    return [slice(LANES * t, LANES * (t + 1)) for t in range(channels // LANES)]


def to_windows(sources, grid_ref, win_ref, band_cols, channels):
    half_win = WINDOW_SIDE // 2
    pitch = band_cols + 8
    win_area = WINDOW_SIDE * WINDOW_SIDE
    for i in range(WINDOW_SIDE):
        value = sources(i).astype(FL)
        for t, lanes in enumerate(tiles_of(channels)):
            grid_ref[t, i * pitch : i * pitch + band_cols, :] = value[:, lanes]
            grid_ref[t, i * pitch + band_cols : (i + 1) * pitch, :] = value[0:8, lanes]
    for t in range(channels // LANES):
        for n in range(band_cols // WINDOW_SIDE):
            for i in range(WINDOW_SIDE):
                at = i * pitch + n * WINDOW_SIDE + half_win
                to = n * win_area + i * WINDOW_SIDE
                win_ref[t, to : to + WINDOW_SIDE, :] = grid_ref[t, at : at + WINDOW_SIDE, :]


def from_windows(put, grid_ref, win_ref, band_cols, channels):
    half_win = WINDOW_SIDE // 2
    pitch = band_cols + 8
    win_area = WINDOW_SIDE * WINDOW_SIDE
    for t in range(channels // LANES):
        for n in range(band_cols // WINDOW_SIDE):
            for i in range(WINDOW_SIDE):
                to = i * pitch + n * WINDOW_SIDE + half_win
                at = n * win_area + i * WINDOW_SIDE
                grid_ref[t, to : to + WINDOW_SIDE, :] = win_ref[t, at : at + WINDOW_SIDE, :]
        for i in range(WINDOW_SIDE):
            grid_ref[t, i * pitch : i * pitch + half_win, :] = grid_ref[
                t, i * pitch + band_cols : i * pitch + band_cols + half_win, :
            ]
    for i in range(WINDOW_SIDE):
        put(
            i,
            jnp.concatenate(
                [
                    grid_ref[t, i * pitch : i * pitch + band_cols, :]
                    for t in range(channels // LANES)
                ],
                1,
            ),
        )


def stacked(tile, heads_ref):
    return jnp.concatenate([tile] * TILE_HEADS, 0) * heads_ref[...]


def spread_body(lines_ref, rows_ref, keys_ref):
    area = WINDOW_SIDE * WINDOW_SIDE
    row = lax.broadcasted_iota(jnp.int32, (area, area), 0) % WINDOW_SIDE
    lane = lax.broadcasted_iota(jnp.int32, (area, area), 1) % WINDOW_SIDE

    def shear(line):
        wide = jnp.broadcast_to(line, (area, SHEAR))
        return pltpu.roll(wide, 0, 1, stride=1, stride_axis=0)[:, 0:area]

    def step(t, carry):
        rows, keys = [], []
        for k in range(TILE_HEADS):
            lines = lines_ref[t * TILE_HEADS + k]
            keys.append(jnp.where(lane >= row, shear(lines[0:1]), shear(lines[1:2])))
            rows.append(jnp.where(row >= lane, shear(lines[2:3]), shear(lines[3:4])))
        rows_ref[t] = jnp.concatenate(rows, 1)
        keys_ref[t] = jnp.concatenate(keys, 1)
        return carry

    lax.fori_loop(0, rows_ref.shape[0], step, 0)


def fold_body(*refs):
    (*ins, out_ref) = refs
    area = WINDOW_SIDE * WINDOW_SIDE
    row = lax.broadcasted_iota(jnp.int32, (area, area), 0)
    lane = lax.broadcasted_iota(jnp.int32, (area, area), 1)
    turn = jnp.where(row + lane == area - 1, 1.0, 0.0).astype(BF)
    later = lane % WINDOW_SIDE >= (area - 1 - row) % WINDOW_SIDE
    blank = jnp.zeros((area, SHEAR - area), FL)

    def fold(values):
        wide = jnp.concatenate([values, blank], 1)
        return jnp.sum(pltpu.roll(wide, 0, 1, stride=1, stride_axis=0), 0, keepdims=True)

    def step(value, head):
        total = None
        for _ in range(3):
            part = value.astype(BF)
            value = value - part.astype(FL)
            now = mm(turn, part)
            total = now if total is None else total + now
        out_ref[head, 0:1, :] = fold(jnp.where(later, total, 0.0))
        out_ref[head, 1:2, :] = fold(jnp.where(later, 0.0, total))

    for t, ref in enumerate(ins):
        value = ref[...]
        for k in range(TILE_HEADS):
            step(value[:, k * area : (k + 1) * area], t * TILE_HEADS + k)


def slot_body(
    place_ref,
    experts_ref,
    column_ref,
    dest_column_ref,
    dest_row_ref,
    *,
    experts,
    local,
    slots,
    capacity,
):
    tokens = experts_ref.shape[1]

    def place(expert):
        upper = jnp.where(expert >= experts // 2, 1, 0)
        inner = expert - upper * (experts // 2)
        apart = upper ^ place_ref[0]
        member = (inner // local) ^ place_ref[1]
        return ((2 * member + apart) * local + inner % local) * slots

    block = LANES
    lower = (
        lax.broadcasted_iota(jnp.int32, (block, block), 0)
        > lax.broadcasted_iota(jnp.int32, (block, block), 1)
    ).astype(FL).astype(BF)
    upper = (
        lax.broadcasted_iota(jnp.int32, (block, block), 0)
        < lax.broadcasted_iota(jnp.int32, (block, block), 1)
    ).astype(FL).astype(BF)
    lane = lax.broadcasted_iota(jnp.int32, (block, LANES), 1)
    sublane = lax.broadcasted_iota(jnp.int32, (LANES, block), 0)
    seen_row = jnp.zeros((1, LANES), FL)
    seen_column = jnp.zeros((LANES, 1), FL)
    for c in range(tokens // block):
        line = experts_ref[:, c * block : (c + 1) * block]
        across = jnp.where(sublane == line, 1.0, 0.0)
        column = jnp.broadcast_to(line.astype(FL), (block, block)).T[:, 0:1].astype(jnp.int32)
        down = jnp.where(lane == column, 1.0, 0.0)
        before = mm(lower, down.astype(BF)) + seen_row
        slot = jnp.sum(down * before, 1, keepdims=True).astype(jnp.int32)
        column_ref[c * block : (c + 1) * block, :] = column
        dest_column_ref[c * block : (c + 1) * block, :] = jnp.where(
            slot < capacity, place(column) + slot, -1
        )
        before = mm(across.astype(BF), upper) + seen_column
        slot = jnp.sum(across * before, 0, keepdims=True).astype(jnp.int32)
        dest_row_ref[:, c * block : (c + 1) * block] = jnp.where(
            slot < capacity, place(line) + slot, -1
        )
        seen_row = seen_row + jnp.sum(down, 0, keepdims=True)
        seen_column = seen_column + jnp.sum(across, 1, keepdims=True)


def slot_tables(chosen, my_place, experts, local, slots, capacity):
    tokens = chosen.shape[1]
    vmem = pl.BlockSpec(memory_space=pltpu.VMEM)
    column = jax.ShapeDtypeStruct((tokens, 1), jnp.int32)
    return pl.pallas_call(
        functools.partial(
            slot_body, experts=experts, local=local, slots=slots, capacity=capacity
        ),
        name="slot_tables",
        in_specs=[pl.BlockSpec(memory_space=pltpu.SMEM), vmem],
        out_specs=[vmem] * 3,
        out_shape=[column, column, jax.ShapeDtypeStruct((1, tokens), jnp.int32)],
    )(my_place, chosen)


def attend_forward_body(
    band_ref,
    below_ref,
    weight_ref,
    qbias_ref,
    vbias_ref,
    scale_ref,
    bias_ref,
    query_zone_ref,
    key_zone_ref,
    heads_ref,
    block_ref,
    own_ref,
    send_ref,
    win_ref,
    qkv_ref,
    inv_ref,
    grid_scr,
    win_scr,
    *,
    band_cols,
    channels,
):
    tokens = band_ref.shape[0]
    half = tokens // 2
    win_area = WINDOW_SIDE * WINDOW_SIDE
    tiles = tiles_of(channels)

    def source(i):
        if i < WINDOW_SIDE // 2:
            return band_ref[half + i * band_cols : half + (i + 1) * band_cols, :]
        at = (i - WINDOW_SIDE // 2) * band_cols
        return below_ref[at : at + band_cols, :]

    to_windows(source, grid_scr, win_scr, band_cols, channels)
    block_ones = block_ref[...]
    chunk = 2 * win_area

    def project(c, carry):
        rows = rows_at(c * chunk, chunk)
        low = jnp.concatenate([win_scr[t, rows, :] for t in range(len(tiles))], 1).astype(BF)
        win_ref[rows, :] = low
        qkv = mm(low, weight_ref[...])
        for lanes in tiles:
            key_lanes = slice(channels + lanes.start, channels + lanes.stop)
            value_lanes = slice(2 * channels + lanes.start, 2 * channels + lanes.stop)
            query = qkv[:, lanes] + qbias_ref[:, lanes]
            inverse = (
                lax.rsqrt(head_sums(query * query, block_ones) + EPS_UNIT) * scale_ref[:, lanes]
            )
            inv_ref[rows, lanes] = inverse
            qkv_ref[rows, lanes] = (query * inverse).astype(BF)
            key = qkv[:, key_lanes]
            inverse = lax.rsqrt(head_sums(key * key, block_ones) + EPS_UNIT)
            inv_ref[rows, key_lanes] = inverse
            qkv_ref[rows, key_lanes] = (key * inverse).astype(BF)
            qkv_ref[rows, value_lanes] = (qkv[:, value_lanes] + vbias_ref[:, lanes]).astype(BF)
        return carry

    lax.fori_loop(0, tokens // chunk, project, 0)

    def attend(n, carry):
        rows = rows_at(n * win_area, win_area)
        query_zone = query_zone_ref[rows, :]
        key_zone = jnp.concatenate([key_zone_ref[rows, :]] * TILE_HEADS, 0)
        for t, lanes in enumerate(tiles):
            query = qkv_ref[rows, lanes]
            key = qkv_ref[rows, channels + lanes.start : channels + lanes.stop]
            value = qkv_ref[rows, 2 * channels + lanes.start : 2 * channels + lanes.stop]
            scores = mm_nt(
                jnp.concatenate([query, query_zone], 1),
                jnp.concatenate([stacked(key, heads_ref), key_zone], 1),
            )
            powers = jnp.exp(scores + bias_ref[t]).astype(BF)
            mixed = mm(powers, jnp.concatenate([stacked(value, heads_ref), heads_ref[...]], 1))
            win_scr[t, rows, :] = mixed[:, :LANES] / mixed[:, LANES:]
        return carry

    lax.fori_loop(0, tokens // win_area, attend, 0, unroll=UNROLL)

    def put(i, value):
        if i < WINDOW_SIDE // 2:
            own_ref[i * band_cols : (i + 1) * band_cols, :] = value.astype(BF)
        else:
            at = (i - WINDOW_SIDE // 2) * band_cols
            send_ref[at : at + band_cols, :] = value.astype(BF)

    from_windows(put, grid_scr, win_scr, band_cols, channels)


def window_body(own_ref, lifted_ref, out_ref, grid_scr, win_scr, *, band_cols, channels):
    def source(i):
        ref = own_ref if i < WINDOW_SIDE // 2 else lifted_ref
        at = (i % (WINDOW_SIDE // 2)) * band_cols
        return ref[at : at + band_cols, :]

    to_windows(source, grid_scr, win_scr, band_cols, channels)
    for t, lanes in enumerate(tiles_of(channels)):
        out_ref[:, lanes] = win_scr[t].astype(BF)


def attend_backward_body(*refs, summed_before):
    (
        back_ref,
        query_ref,
        key_ref,
        value_ref,
        query_inv_ref,
        key_inv_ref,
        scale_ref,
        win_ref,
        bias_ref,
        query_zone_ref,
        key_zone_ref,
        heads_ref,
        block_ref,
        *rest,
    ) = refs
    if summed_before:
        dweight_before_ref, dbias_before_ref, *rest = rest
    dqkv_ref, dweight_ref, dbias_ref, small_ref = rest
    tokens = back_ref.shape[0]
    win_area = WINDOW_SIDE * WINDOW_SIDE
    block_ones = block_ref[...]
    if summed_before:
        dbias_ref[...] = dbias_before_ref[...]
    else:
        dbias_ref[...] = jnp.zeros_like(dbias_ref)
    small_ref[...] = jnp.zeros_like(small_ref)

    def attend(n, carry):
        rows = rows_at(n * win_area, win_area)
        query = query_ref[rows, :]
        key = key_ref[rows, :]
        queries = stacked(query, heads_ref)
        backs = stacked(back_ref[rows, :], heads_ref)
        query_zone = jnp.concatenate([query_zone_ref[rows, :]] * TILE_HEADS, 0)
        scores = mm_nt(
            jnp.concatenate([key, key_zone_ref[rows, :]], 1),
            jnp.concatenate([queries, query_zone], 1),
        )
        powers = jnp.exp(scores + bias_ref[0])
        probs = powers * (1.0 / jnp.sum(powers, 0, keepdims=True))
        weighted = probs * mm_nt(value_ref[rows, :], backs)
        dscores = weighted - probs * jnp.sum(weighted, 0, keepdims=True)
        dbias_ref[...] += dscores
        dlow = dscores.astype(BF)
        dvalue = mm(probs.astype(BF), backs)
        dkey = mm(dlow, queries)
        dquery = mm_tn(dlow, key) * heads_ref[...].astype(FL)
        dquery = sum(dquery[k * win_area : (k + 1) * win_area] for k in range(TILE_HEADS))
        scale = scale_ref[...]
        unit = query.astype(FL)
        along = head_sums(unit * dquery, block_ones)
        dquery = query_inv_ref[rows, :] * (dquery - unit * along / (scale * scale))
        unit = key.astype(FL)
        dkey = key_inv_ref[rows, :] * (dkey - unit * head_sums(unit * dkey, block_ones))
        for part, grad in enumerate((dquery, dkey, dvalue)):
            dqkv_ref[rows, part * LANES : (part + 1) * LANES] = grad.astype(BF)
        small_ref[0:1, :] += jnp.sum(dquery, 0, keepdims=True)
        small_ref[1:2, :] += jnp.sum(dvalue, 0, keepdims=True)
        small_ref[2:3, :] += jnp.sum(along, 0, keepdims=True)
        return carry

    lax.fori_loop(0, tokens // win_area, attend, 0, unroll=UNROLL)
    dweight = mm_tn(win_ref[...], dqkv_ref[...])
    if summed_before:
        dweight = dweight + dweight_before_ref[...]
    dweight_ref[...] = dweight.astype(dweight_ref.dtype)


def input_grad_body(
    first_ref,
    second_ref,
    third_ref,
    weight_ref,
    own_ref,
    send_ref,
    grid_scr,
    win_scr,
    *,
    band_cols,
    channels,
):
    tokens = first_ref.shape[0]
    tiles = tiles_of(channels)
    chunk = 2 * WINDOW_SIDE * WINDOW_SIDE

    def project(c, carry):
        rows = rows_at(c * chunk, chunk)
        parts = [ref[rows, :] for ref in (first_ref, second_ref, third_ref)]
        wide = jnp.concatenate([p[:, lanes] for lanes in tiles for p in parts], 1)
        back = mm_nt(wide, weight_ref[...])
        for t, lanes in enumerate(tiles):
            win_scr[t, rows, :] = back[:, lanes]
        return carry

    lax.fori_loop(0, tokens // chunk, project, 0)

    def put(i, value):
        if i < WINDOW_SIDE // 2:
            own_ref[i * band_cols : (i + 1) * band_cols, :] = value
        else:
            at = (i - WINDOW_SIDE // 2) * band_cols
            send_ref[at : at + band_cols, :] = value.astype(BF)

    from_windows(put, grid_scr, win_scr, band_cols, channels)


def lane_mean(values):
    return jnp.sum(values, -1, keepdims=True) * (1.0 / values.shape[-1])


def normalised(values):
    centred = values - lane_mean(values)
    inverse = lax.rsqrt(lane_mean(centred * centred) + EPS_NORM)
    return centred * inverse, inverse


def normalised_back(back, gain, unit, inverse):
    back = back * gain
    return inverse * (back - lane_mean(back) - unit * lane_mean(back * unit))


CHUNK = 576


def pack_rows(dest_row_ref, rows_ref, out_refs):
    tokens = rows_ref.shape[0]
    start = 0
    for ref in out_refs:
        place = lax.broadcasted_iota(jnp.int32, (ref.shape[0], tokens), 0) + start
        chosen = jnp.where(place == dest_row_ref[...], 1.0, 0.0).astype(BF)
        ref[...] = mm(chosen, rows_ref[...]).astype(BF)
        start += ref.shape[0]


def unpack_rows(dest_col, buffer):
    place = lax.broadcasted_iota(jnp.int32, (dest_col.shape[0], buffer.shape[0]), 1)
    chosen = jnp.where(place == dest_col, 1.0, 0.0).astype(BF)
    return mm(chosen, buffer)


def route_body(
    arrived_ref,
    own_ref,
    band_ref,
    weight_ref,
    small_ref,
    router_ref,
    expert_ref,
    dest_row_ref,
    resid_ref,
    unit_ref,
    aux_ref,
    low_ref,
    *sent_refs,
    experts,
):
    half = arrived_ref.shape[0]
    lane = lax.broadcasted_iota(jnp.int32, (CHUNK, LANES), 1)
    for part, ref in enumerate((arrived_ref, own_ref)):

        def step(c, carry, part=part, ref=ref):
            rows = rows_at(part * half + c * CHUNK, CHUNK)
            projected = mm(ref[rows_at(c * CHUNK, CHUNK), :], weight_ref[...]) + small_ref[0:1, :]
            unit, inverse = normalised(projected)
            unit_ref[rows, :] = unit.astype(BF)
            resid = band_ref[rows, :].astype(FL) + unit * small_ref[1:2, :] + small_ref[2:3, :]
            resid_ref[rows, :] = resid
            low = resid.astype(BF)
            low_ref[rows, :] = low
            logits = jnp.where(lane < experts, mm(low, router_ref[...]), -1e30)
            powers = jnp.exp(logits - jnp.max(logits, -1, keepdims=True))
            probs = powers / jnp.sum(powers, -1, keepdims=True)
            gate = jnp.sum(
                jnp.where(lane == expert_ref[rows, :], probs, 0.0), -1, keepdims=True
            )
            aux_ref[rows, :] = jnp.where(
                lane == LANES - 1, gate, jnp.where(lane == LANES - 2, inverse, probs)
            )
            return carry

        lax.fori_loop(0, half // CHUNK, step, 0)
    pack_rows(dest_row_ref, low_ref, sent_refs)


def merge_body(*refs, experts, band_cols, members):
    returned_refs, refs = refs[:members], refs[members:]
    (
        dest_col_ref,
        dest_row_ref,
        expert_ref,
        aux_ref,
        resid_ref,
        small_ref,
        weight_ref,
        wide_ref,
        cotangent_ref,
        final_ref,
        merged_ref,
        dreduced_ref,
        dresid_ref,
        dlogits_ref,
        sums_ref,
    ) = refs[:15]
    sent_refs = refs[15 : 15 + members]
    unit_scr, picked_scr, inverse_scr, token_scr, back_scr = refs[15 + members :]
    returned = jnp.concatenate([ref[...] for ref in returned_refs], 0)
    tokens, channels = resid_ref.shape
    tiles = tiles_of(channels)
    lane = lax.broadcasted_iota(jnp.int32, (CHUNK, LANES), 1)

    def combine(c, carry):
        rows = rows_at(c * CHUNK, CHUNK)
        picked = unpack_rows(dest_col_ref[rows, :], returned)
        picked_scr[rows, :] = picked
        gate = aux_ref[rows, :][:, LANES - 1 : LANES]
        unit, inverse = normalised(gate * picked)
        unit_scr[rows, :] = unit
        inverse_scr[rows, :] = jnp.broadcast_to(inverse, (CHUNK, LANES))
        resid = resid_ref[rows, :] + unit * small_ref[0:1, :] + small_ref[1:2, :]
        for t, lanes in enumerate(tiles):
            token_scr[t, rows, :] = resid[:, lanes]
        return carry

    lax.fori_loop(0, tokens // CHUNK, combine, 0)
    pairs = band_cols // 2
    for i in range(WINDOW_SIDE // 2):
        for k in range(4):
            start = (2 * i + k % 2) * band_cols + k // 2
            for t in range(len(tiles)):
                at = k * channels + t * LANES
                merged_ref[i * pairs : (i + 1) * pairs, at : at + LANES] = token_scr[
                    t, pl.ds(start, pairs, stride=2), :
                ].astype(BF)
    unit, inverse = normalised(mm(merged_ref[...], weight_ref[...]))
    final_ref[...] = (unit * wide_ref[0:1, :] + wide_ref[1:2, :]).astype(BF)
    back = cotangent_ref[...].astype(FL)
    sums_ref[...] = jnp.zeros_like(sums_ref)
    sums_ref[0:1, :] = jnp.sum(back * unit, 0, keepdims=True)
    sums_ref[1:2, :] = jnp.sum(back, 0, keepdims=True)
    dreduced = normalised_back(back, wide_ref[0:1, :], unit, inverse).astype(BF)
    dreduced_ref[...] = dreduced
    for k in range(4):
        part = mm_nt(dreduced, weight_ref[k * channels : (k + 1) * channels, :])
        for i in range(WINDOW_SIDE // 2):
            start = (2 * i + k % 2) * band_cols + k // 2
            for t, lanes in enumerate(tiles):
                token_scr[t, pl.ds(start, pairs, stride=2), :] = part[
                    i * pairs : (i + 1) * pairs, lanes
                ]

    def spread(c, carry):
        rows = rows_at(c * CHUNK, CHUNK)
        back = jnp.concatenate([token_scr[t, rows, :] for t in range(len(tiles))], 1)
        dresid_ref[rows, :] = back
        unit = unit_scr[rows, :]
        sums_ref[2:3, 0:channels] += jnp.sum(back * unit, 0, keepdims=True)
        sums_ref[3:4, 0:channels] += jnp.sum(back, 0, keepdims=True)
        back = normalised_back(back, small_ref[0:1, :], unit, inverse_scr[rows, :][:, 0:1])
        aux = aux_ref[rows, :]
        gate = aux[:, LANES - 1 : LANES]
        dgate = jnp.sum(back * picked_scr[rows, :], -1, keepdims=True)
        back_scr[rows, :] = (back * gate).astype(BF)
        probs = jnp.where(lane < experts, aux, 0.0)
        chosen = jnp.where(lane == expert_ref[rows, :], 1.0, 0.0)
        dlogits_ref[rows, :] = (probs * (chosen - gate) * dgate).astype(BF)
        return carry

    lax.fori_loop(0, tokens // CHUNK, spread, 0)
    pack_rows(dest_row_ref, back_scr, sent_refs)


def settle_body(*refs, members):
    sent_refs, refs = refs[:members], refs[members:]
    (
        dest_col_ref,
        dresid_ref,
        dlogits_ref,
        router_ref,
        unit_ref,
        aux_ref,
        small_ref,
        weight_ref,
        done_ref,
        low_ref,
        rows_ref,
        sums_ref,
    ) = refs
    sent = jnp.concatenate([ref[...] for ref in sent_refs], 0)
    tokens, channels = dresid_ref.shape
    sums_ref[...] = jnp.zeros_like(sums_ref)

    def step(c, carry):
        rows = rows_at(c * CHUNK, CHUNK)
        back = dresid_ref[rows, :] + unpack_rows(dest_col_ref[rows, :], sent)
        back = back + mm_nt(dlogits_ref[rows, :], router_ref[...])
        done_ref[rows, :] = back
        unit = unit_ref[rows, :].astype(FL)
        sums_ref[1:2, :] += jnp.sum(back * unit, 0, keepdims=True)
        sums_ref[2:3, :] += jnp.sum(back, 0, keepdims=True)
        inverse = aux_ref[rows, :][:, LANES - 2 : LANES - 1]
        back = normalised_back(back, small_ref[1:2, :], unit, inverse)
        sums_ref[0:1, :] += jnp.sum(back, 0, keepdims=True)
        low = back.astype(BF)
        low_ref[rows, :] = low
        rows_ref[rows, :] = mm_nt(low, weight_ref[...]).astype(BF)
        return carry

    lax.fori_loop(0, tokens // CHUNK, step, 0)


def dense_body(*refs):
    (*ins, proj_ref, router_ref) = refs
    arrived, own, low, resid, dlogits = (ins[i::5] for i in range(5))
    half = arrived[0].shape[0]
    proj = router = None
    for a, o, b, r, d in zip(arrived, own, low, resid, dlogits):
        now = mm_tn(a[...], b[0:half, :]) + mm_tn(o[...], b[half:, :])
        then = mm_tn(r[...], d[...])
        proj = now if proj is None else proj + now
        router = then if router is None else router + then
    proj_ref[...] = proj.astype(BF)
    router_ref[...] = router.astype(BF)


def merge_weight_body(*refs):
    (*ins, out_ref) = refs
    total = None
    for left, right in zip(ins[0::2], ins[1::2]):
        now = mm_tn(left[...], right[...])
        total = now if total is None else total + now
    out_ref[...] = total.astype(BF)


def merge_weight_grad(merged, dreduced, channels, after):
    args, specs = [], []
    for left, right in zip(merged, dreduced):
        args += [left, right]
        specs += [
            pl.BlockSpec((left.shape[0], channels), lambda k: (0, k)),
            pl.BlockSpec(right.shape, lambda k: (0, 0)),
        ]
    return pl.pallas_call(
        skipping(merge_weight_body, len(args), len(after)),
        name="merge_weight_grad",
        grid=(4,),
        out_shape=jax.ShapeDtypeStruct((merged[0].shape[1], dreduced[0].shape[1]), BF),
        in_specs=specs + [pl.BlockSpec(memory_space=pl.ANY)] * len(after),
        out_specs=pl.BlockSpec((channels, dreduced[0].shape[1]), lambda k: (k, 0)),
        compiler_params=pltpu.CompilerParams(vmem_limit_bytes=VMEM_BYTES),
        cost_estimate=cost(5),
    )(*args, *after)


PIECE = 384


def spot_of(member, me, bits):
    apart = member ^ me
    spot = 0
    for k in range(bits):
        spot = spot | (((apart >> k) & 1) << (bits - 1 - k))
    return spot


def piece_home(expert, chunk, row_size, chunks):
    piece = expert * chunks + chunk
    return piece % row_size, piece // row_size


def expert_weight(own, other_refs, expert, chunk, local, chunks, me):
    row_size = len(other_refs)
    member, _ = piece_home(jnp.maximum(expert - local, 0), chunk, row_size, chunks)
    spot = spot_of(member, me, row_size.bit_length() - 1)
    weight = own
    for k, ref in enumerate(other_refs):
        weight = jnp.where((expert >= local) & (spot == k), ref[0], weight)
    return weight


def taken(refs, *counts):
    lists = []
    for count in counts:
        lists.append(refs[:count])
        refs = refs[count:]
    return lists + [refs]


def joined(refs):
    return jnp.concatenate([ref[...] for ref in refs], 0)


def put_parts(refs, value):
    start = 0
    for ref in refs:
        ref[...] = value[start : start + ref.shape[0]].astype(BF)
        start += ref.shape[0]


def expert_forward_body(me_ref, *refs, local, members, row_size):
    row_refs, (in_ref, in_bias_ref, out_ref, out_bias_ref), in_others, out_others, refs = taken(
        refs, members, 4, row_size, row_size
    )
    result_refs, (hidden_ref, slope_ref, pre_scr) = taken(refs, members)
    expert = pl.program_id(0)
    rows = joined(row_refs)
    count = rows.shape[0]
    chunks = in_ref.shape[2] // PIECE
    block = 64
    total = None
    for chunk in range(chunks):
        lanes = slice(chunk * PIECE, (chunk + 1) * PIECE)
        weight = expert_weight(
            in_ref[0, :, lanes], in_others, expert, chunk, local, chunks, me_ref[0]
        )
        pre_scr[...] = mm(rows, weight) + in_bias_ref[0, :, lanes]

        def activate(c, carry, lanes=lanes):
            at = rows_at(c * block, block)
            pre = pre_scr[at, :]
            cdf = 0.5 * (1.0 + lax.erf(pre * 0.7071067811865476))
            hidden_ref[0, at, lanes] = (pre * cdf).astype(BF)
            slope_ref[0, at, lanes] = (
                cdf + pre * (0.3989422804014327 * jnp.exp(-0.5 * pre * pre))
            ).astype(BF)
            return carry

        lax.fori_loop(0, count // block, activate, 0)
        weight = expert_weight(
            out_ref[0, lanes, :], out_others, expert, chunk, local, chunks, me_ref[0]
        )
        now = mm(hidden_ref[0, :, lanes], weight)
        total = now if total is None else total + now
    put_parts(result_refs, total + out_bias_ref[0])


def expert_specs(members, slots, channels, hidden, local, row_size):
    chunks = hidden // PIECE

    def other_at(k, me):
        return (jnp.maximum(k - local, 0) * chunks // row_size, 0, 0)

    def own_at(k, me):
        return (jnp.minimum(k, local - 1), 0, 0)

    return dict(
        tokens=pl.BlockSpec((slots, channels), lambda k, me: (k, 0)),
        wide=pl.BlockSpec((1, members * slots, hidden), lambda k, me: (k, 0, 0)),
        first=pl.BlockSpec((1, channels, hidden), own_at),
        second=pl.BlockSpec((1, hidden, channels), own_at),
        other=pl.BlockSpec((1, PIECE, PIECE), other_at),
        bias=pl.BlockSpec((1, 1, hidden), lambda k, me: (k, 0, 0)),
        low_bias=pl.BlockSpec((1, 1, channels), lambda k, me: (k, 0, 0)),
    )


def call_expert(
    body, name, me, steps, in_specs, out_specs, outs, scratch, args, micros, after=()
):
    return pl.pallas_call(
        skipping(body, 1 + len(args), len(after)),
        name=name,
        grid_spec=pltpu.PrefetchScalarGridSpec(
            num_scalar_prefetch=1,
            grid=(steps,),
            in_specs=in_specs + [pl.BlockSpec(memory_space=pl.ANY)] * len(after),
            out_specs=out_specs,
            scratch_shapes=scratch,
        ),
        out_shape=outs,
        compiler_params=pltpu.CompilerParams(vmem_limit_bytes=VMEM_BYTES),
        cost_estimate=cost(micros),
    )(me, *args, *after)


def expert_forward(
    me, rows, first, second, first_other, second_other, first_bias, second_bias, after
):
    members, row_size = len(rows), len(first_other)
    local, channels, hidden = first.shape
    slots = rows[0].shape[0] // (2 * local)
    count = members * slots
    spec = expert_specs(members, slots, channels, hidden, local, row_size)
    wide = jax.ShapeDtypeStruct((2 * local, count, hidden), BF)
    outs = call_expert(
        functools.partial(
            expert_forward_body, local=local, members=members, row_size=row_size
        ),
        "expert_forward",
        me,
        2 * local,
        [spec["tokens"]] * members
        + [spec["first"], spec["bias"], spec["second"], spec["low_bias"]]
        + [spec["other"]] * (2 * row_size),
        [spec["tokens"]] * members + [spec["wide"], spec["wide"]],
        [jax.ShapeDtypeStruct(rows[0].shape, BF)] * members + [wide, wide],
        [pltpu.VMEM((count, PIECE), FL)],
        [*rows, first, first_bias, second, second_bias, *first_other, *second_other],
        19,
        after,
    )
    return outs[:members], outs[members], outs[members + 1]


def expert_backward_body(me_ref, *refs, local, members, row_size):
    row_refs, (in_ref, out_ref, slope_ref), in_others, out_others, refs = taken(
        refs, members, 3, row_size, row_size
    )
    result_refs, (dpre_ref, dbias_ref) = taken(refs, members)
    expert = pl.program_id(0)
    rows = joined(row_refs)
    chunks = in_ref.shape[2] // PIECE
    total = None
    for chunk in range(chunks):
        lanes = slice(chunk * PIECE, (chunk + 1) * PIECE)
        weight = expert_weight(
            out_ref[0, lanes, :], out_others, expert, chunk, local, chunks, me_ref[0]
        )
        dpre = mm_nt(rows, weight) * slope_ref[0, :, lanes].astype(FL)
        dbias_ref[0, :, lanes] = jnp.sum(dpre, 0, keepdims=True)
        low = dpre.astype(BF)
        dpre_ref[0, :, lanes] = low
        weight = expert_weight(
            in_ref[0, :, lanes], in_others, expert, chunk, local, chunks, me_ref[0]
        )
        now = mm_nt(low, weight)
        total = now if total is None else total + now
    put_parts(result_refs, total)


def expert_backward(me, rows, first, second, first_other, second_other, slope, after):
    members, row_size = len(rows), len(first_other)
    local, channels, hidden = first.shape
    slots = rows[0].shape[0] // (2 * local)
    count = members * slots
    spec = expert_specs(members, slots, channels, hidden, local, row_size)
    outs = call_expert(
        functools.partial(
            expert_backward_body, local=local, members=members, row_size=row_size
        ),
        "expert_backward",
        me,
        2 * local,
        [spec["tokens"]] * members
        + [spec["first"], spec["second"], spec["wide"]]
        + [spec["other"]] * (2 * row_size),
        [spec["tokens"]] * members + [spec["wide"], spec["bias"]],
        [jax.ShapeDtypeStruct(rows[0].shape, BF)] * members
        + [
            jax.ShapeDtypeStruct((2 * local, count, hidden), BF),
            jax.ShapeDtypeStruct((2 * local, 1, hidden), FL),
        ],
        [],
        [*rows, first, second, slope, *first_other, *second_other],
        12,
        after,
    )
    return outs[:members], outs[members], outs[members + 1]


def expert_weight_body(me_ref, *refs, local, members, micros, tokens_left):
    token_refs, wide_refs, (keep_ref, send_ref, dbias_ref) = taken(
        refs, members * micros, micros
    )
    expert = pl.program_id(0)
    half = keep_ref.shape[1]
    row_size = 2 * half
    chunks = wide_refs[0].shape[2] // PIECE
    rows = [joined(token_refs[m * members : (m + 1) * members]) for m in range(micros)]
    dbias_ref[0] = sum(jnp.sum(part.astype(FL), 0, keepdims=True) for part in rows)
    for chunk in range(chunks):
        lanes = slice(chunk * PIECE, (chunk + 1) * PIECE)
        total = None
        for part, ref in zip(rows, wide_refs):
            wide = ref[0, :, lanes]
            now = mm_tn(part, wide) if tokens_left else mm_tn(wide, part)
            total = now if total is None else total + now
        low = total.astype(BF)
        member, _ = piece_home(expert % local, chunk, row_size, chunks)
        spot = spot_of(member, me_ref[0], row_size.bit_length() - 1)

        @pl.when(spot < half)
        def _():
            keep_ref[0, spot, 0] = low

        @pl.when(spot >= half)
        def _():
            send_ref[0, spot - half, 0] = low


def expert_weight_grads(me, tokens, wide, local, row_size, tokens_left, after):
    members, micros = len(tokens[0]), len(tokens)
    together, channels = tokens[0][0].shape
    slots = together // (2 * local)
    width = wide[0].shape[-1]
    chunks = width // PIECE
    subs = local * chunks // row_size
    spec = expert_specs(members, slots, channels, width, local, row_size)
    half_shape = (2, row_size // 2, subs, PIECE, PIECE)
    half_spec = pl.BlockSpec(
        (1, row_size // 2, 1, PIECE, PIECE),
        lambda k, me: (k // local, 0, (k % local) * chunks // row_size, 0, 0),
    )
    half_out = jax.ShapeDtypeStruct(half_shape, BF)
    return call_expert(
        functools.partial(
            expert_weight_body,
            local=local,
            members=members,
            micros=micros,
            tokens_left=tokens_left,
        ),
        "expert_weight_grads",
        me,
        2 * local,
        [spec["tokens"]] * (members * micros) + [spec["wide"]] * micros,
        [half_spec] * 2 + [spec["low_bias"]],
        [half_out] * 2 + [jax.ShapeDtypeStruct((2 * local, 1, channels), FL)],
        [],
        [part for parts in tokens for part in parts] + list(wide),
        13,
        after,
    )


def add_pieces_body(keep_ref, got_ref, *out_refs):
    half = keep_ref.shape[1] // 2
    for group in range(2):
        if half:
            for k in range(half):
                out_refs[0][group, k] = plus(keep_ref[group, k], got_ref[group, k]).astype(BF)
                at = half + k
                out_refs[1][group, k] = plus(keep_ref[group, at], got_ref[group, at]).astype(BF)
        else:
            total = plus(keep_ref[group, 0], got_ref[group, 0])
            out_refs[group][...] = total.astype(out_refs[group].dtype)


def add_pieces(keep, got, after):
    groups, count = keep.shape[:2]
    if count > 1:
        shape = (groups, count // 2) + keep.shape[2:]
        outs = [(shape, BF), (shape, BF)]
    else:
        outs = [(keep.shape[2:], FL), (keep.shape[2:], BF)]
    return call_kernel(add_pieces_body, "add_pieces", outs, [keep, got], micros=3, after=after)


def add_halves_body(own_ref, got_ref, out_ref):
    out_ref[...] = plus(own_ref[...], got_ref[...]).astype(BF)


def add_halves(own, got, after):
    (total,) = call_kernel(
        add_halves_body, "add_halves", [(own.shape, BF)], [own, got], micros=2, after=after
    )
    return total


def place_body(me_ref, *refs, chunks, first):
    (*piece_refs, full_ref) = refs
    row_size = len(piece_refs)
    for c in range(chunks):
        member, _ = piece_home(pl.program_id(0), c, row_size, chunks)
        spot = spot_of(member, me_ref[0], row_size.bit_length() - 1)
        span = slice(c * PIECE, (c + 1) * PIECE)
        value = piece_refs[0][0]
        for k in range(1, row_size):
            value = jnp.where(spot == k, piece_refs[k][0], value)
        if first:
            full_ref[0, :, span] = value.astype(FL)
        else:
            full_ref[0, span, :] = value.astype(FL)


def place_pieces(me, pieces, local, hidden, first, after):
    row_size = len(pieces)
    chunks = hidden // PIECE
    shape = (local, PIECE, hidden) if first else (local, hidden, PIECE)
    return call_expert(
        functools.partial(place_body, chunks=chunks, first=first),
        "place_pieces",
        me,
        local,
        [pl.BlockSpec((1, PIECE, PIECE), lambda e, me: (e * chunks // row_size, 0, 0))]
        * row_size,
        [pl.BlockSpec((1,) + shape[1:], lambda e, me: (e, 0, 0))],
        [jax.ShapeDtypeStruct(shape, FL)],
        [],
        list(pieces),
        4,
        after,
    )[0]


def swapped(rows):
    return lax.all_to_all(rows, "dp", split_axis=0, concat_axis=0, tiled=True)


def exchanged(blocks):
    return [blocks[0]] + [crossed(block, "dp", k) for k, block in enumerate(blocks) if k]


def bits_of(axis):
    return [1 << k for k in reversed(range(lax.axis_size(axis).bit_length() - 1))]


def spread_over_row(piece):
    held = [piece]
    for bit in bits_of("row"):
        held = held + [crossed(part, "row", bit) for part in held]
    return held


def gathered(shard):
    count = lax.axis_size("dp")
    copies = jnp.broadcast_to(shard[None], (count,) + shard.shape)
    return swapped(copies).reshape(count * shard.shape[0], shard.shape[1])


def copy_body(in_ref, out_ref):
    out_ref[...] = in_ref[...]


def held_back(array, after):
    (copy,) = call_kernel(
        copy_body, "hold", [(array.shape, array.dtype)], [array], micros=1, after=after
    )
    return copy


def crossed(array, axis, bit):
    count = lax.axis_size(axis)
    return lax.ppermute(array, axis, [(i, i ^ bit) for i in range(count)])


def summed(array, axes):
    for axis in axes:
        bit = 1
        while bit < lax.axis_size(axis):
            array = array + crossed(array, axis, bit)
            bit *= 2
    return array


def dense_sum(grad):
    count = lax.axis_size("dp")
    half = count // 2
    place = lax.axis_index("dp")
    rows = grad.shape[0] // count
    grad = grad.reshape(2, half, rows, grad.shape[1])
    blocks = [
        lax.dynamic_index_in_dim(grad, (place % half) ^ k, 1, keepdims=False) for k in range(half)
    ]
    part = sum(block.astype(FL) for block in exchanged(blocks))
    mine = lax.dynamic_index_in_dim(part, place // half, 0, keepdims=False)
    other = lax.dynamic_index_in_dim(part, 1 - place // half, 0, keepdims=False).astype(BF)
    part = plus(mine, crossed(other, "dp", half)).astype(BF)
    held = spread_over_row(part)
    sums = held
    while len(sums) > 1:
        sums = [plus(left, right) for left, right in zip(sums[::2], sums[1::2])]
    return sums[0].astype(FL), [other, part, held[-1]]


def on_device(
    patches,
    unpadded_patch_size,
    patch_expert_index,
    cotangent,
    query_key_value_weight,
    query_projection_bias,
    value_projection_bias,
    log_cosine_scale,
    bias_network_first_weight,
    bias_network_first_bias,
    bias_network_second_weight,
    output_projection_weight,
    output_projection_bias,
    attention_norm_gain,
    attention_norm_bias,
    routing_weight,
    expert_first_weight,
    expert_first_bias,
    expert_second_weight,
    expert_second_bias,
    expert_norm_gain,
    expert_norm_bias,
    patch_merging_weight,
    merging_norm_gain,
    merging_norm_bias,
):
    micro_count, _, band_rows, band_cols, channels = patches.shape
    micros = range(micro_count)
    half_rows = band_rows // 2
    win_count = band_cols // WINDOW_SIDE
    win_area = WINDOW_SIDE * WINDOW_SIDE
    tokens = band_rows * band_cols
    half = tokens // 2
    experts = routing_weight.shape[1]
    dp_size = lax.axis_size("dp")
    local = experts // dp_size
    capacity = (5 * tokens + 4 * experts - 1) // (4 * experts)
    slots = -(-capacity // 16) * 16
    block_rows = 2 * local * slots
    members = dp_size // 2
    row_size = lax.axis_size("row")
    me = lax.axis_index("row").astype(jnp.int32)[None]
    my_place = lax.axis_index("dp").astype(jnp.int32)
    my_place = jnp.stack([my_place // members, my_place % members])
    total_rows = band_rows * lax.axis_size("row")
    row_start = band_rows * lax.axis_index("row")

    dense = gathered(
        jnp.concatenate(
            [
                query_key_value_weight,
                output_projection_weight,
                jnp.pad(routing_weight, ((0, 0), (0, LANES - experts))),
            ],
            1,
        )
    )
    weight_qkv = dense[:, : 3 * channels]
    weight_proj = dense[:, 3 * channels : 4 * channels]
    weight_router = dense[:, 4 * channels :]

    bands = patches.reshape(micro_count, tokens, channels)
    below = passed_along(bands[:, :half], "row", -1)

    table, table_back = jax.vjp(
        position_table,
        bias_network_first_weight,
        bias_network_first_bias,
        bias_network_second_weight,
    )
    tile_count = channels // LANES
    bias_shape = ((tile_count, win_area, TILE_HEADS * win_area), FL)
    bias_rows, bias_keys = call_kernel(
        spread_body, "spread_bias", [bias_shape, bias_shape], [toeplitz_lines(table)]
    )
    zones = [
        mask_operands(
            row_start,
            total_rows,
            band_cols,
            unpadded_patch_size[m, 0, 0],
            unpadded_patch_size[m, 0, 1],
        )
        for m in micros
    ]

    dest_cols, dest_rows, chosen_cols = [], [], []
    for m in micros:
        chosen = patch_expert_index[m].reshape(1, tokens)
        column, dest_col, dest_row = slot_tables(
            chosen, my_place, experts, local, slots, capacity
        )
        chosen_cols.append(column)
        dest_cols.append(dest_col)
        dest_rows.append(dest_row)

    hidden = expert_first_weight.shape[-1]
    chunks = hidden // PIECE
    subs = local * chunks // row_size
    first_piece, second_piece = [], []
    for sub in range(subs):
        piece = sub * row_size + me[0]
        at, start = piece // chunks, (piece % chunks) * PIECE
        first_piece.append(
            lax.dynamic_slice(expert_first_weight, (at, 0, start), (1, channels, PIECE))
        )
        second_piece.append(
            lax.dynamic_slice(expert_second_weight, (at, start, 0), (1, PIECE, channels))
        )
    first_got = crossed(jnp.concatenate(first_piece), "dp", members)
    second_got = crossed(held_back(jnp.concatenate(second_piece), [first_got]), "dp", members)
    first_other = spread_over_row(first_got)
    second_other = spread_over_row(second_got)
    expert_bias = jnp.concatenate([expert_first_bias, expert_second_bias], 1)
    expert_bias = jnp.concatenate([expert_bias, crossed(expert_bias, "dp", members)], 0)

    lane = jnp.arange(LANES)
    head_marks = jnp.repeat(
        (lane // HEAD_DIM)[None, :] == jnp.arange(TILE_HEADS)[:, None], win_area, 0
    ).astype(BF)
    block_ones = (
        ((jnp.arange(2 * LANES) % LANES) // HEAD_DIM)[:, None] == (lane // HEAD_DIM)[None, :]
    ).astype(BF)
    scale_lanes = jnp.repeat(jnp.exp(log_cosine_scale), HEAD_DIM)[None, :]
    qbias = query_projection_bias[None, :]
    vbias = value_projection_bias[None, :]
    attn_small = jnp.stack([output_projection_bias, attention_norm_gain, attention_norm_bias])
    moe_small = jnp.stack([expert_norm_gain, expert_norm_bias])
    merge_small = jnp.stack([merging_norm_gain, merging_norm_bias])
    first_bias = expert_bias[:, None, :hidden]
    second_bias = expert_bias[:, None, hidden:]

    grid_scratch = ((channels // LANES, band_rows * (band_cols + 8), LANES), FL)
    win_scratch = ((channels // LANES, tokens, LANES), FL)

    none = [None] * micro_count
    attended, arrived, routed, received = list(none), list(none), list(none), list(none)
    expert_out, returned, merged, back_res = list(none), list(none), list(none), list(none)
    expert_back, back_sent, settled, finished = list(none), list(none), list(none), list(none)
    outputs, input_grads, input_parts = list(none), list(none), list(none)

    forward_after = [[first_got], []]
    route_after = [[second_got, first_other[1]], []]
    for m in micros:
        attended[m] = call_kernel(
            functools.partial(attend_forward_body, band_cols=band_cols, channels=channels),
            "attend_forward",
            [
                ((half, channels), BF),
                ((half, channels), BF),
                ((tokens, channels), BF),
                ((tokens, 3 * channels), BF),
                ((tokens, 2 * channels), FL),
            ],
            [
                bands[m],
                below[m],
                weight_qkv,
                qbias,
                vbias,
                scale_lanes,
                bias_rows,
                *zones[m],
                head_marks,
                block_ones,
            ],
            [grid_scratch, win_scratch],
            micros=16,
            after=(forward_after[m] if m < 2 else []) + [a[0] for a in attended[:m][-1:]],
        )
        arrived[m] = passed_along(attended[m][1], "row", 1)
    for m in micros:
        routed[m] = call_kernel(
            functools.partial(route_body, experts=experts),
            "route",
            [
                ((tokens, channels), FL),
                ((tokens, channels), BF),
                ((tokens, LANES), FL),
                ((tokens, channels), BF),
            ]
            + [((block_rows, channels), BF)] * members,
            [
                arrived[m],
                attended[m][0],
                bands[m],
                weight_proj,
                attn_small,
                weight_router,
                chosen_cols[m],
                dest_rows[m],
            ],
            micros=12,
            after=[attended[-1][0] if m == 0 else routed[m - 1][2]]
            + (route_after[m] if m < 2 else []),
        )
        if m == 0:
            shard = held_back(patch_merging_weight, [routed[m][2]])
            weight_merge = lax.all_gather(shard, "dp", axis=0, tiled=True)
        received[m] = exchanged(routed[m][4:])
    for m in micros:
        expert_out[m] = expert_forward(
            me,
            received[m],
            expert_first_weight,
            expert_second_weight,
            first_other,
            second_other,
            first_bias,
            second_bias,
            [routed[-1][2] if m == 0 else expert_out[m - 1][0][0]],
        )
        returned[m] = exchanged(expert_out[m][0])
    for m in micros:
        merged[m] = call_kernel(
            functools.partial(
                merge_body, experts=experts, band_cols=band_cols, members=members
            ),
            "merge",
            [
                ((tokens // 4, 2 * channels), BF),
                ((tokens // 4, 4 * channels), BF),
                ((tokens // 4, 2 * channels), BF),
                ((tokens, channels), FL),
                ((tokens, LANES), BF),
                ((8, 2 * channels), FL),
            ]
            + [((block_rows, channels), BF)] * members,
            [
                *returned[m],
                dest_cols[m],
                dest_rows[m],
                chosen_cols[m],
                routed[m][2],
                routed[m][0],
                moe_small,
                weight_merge,
                merge_small,
                cotangent[m, 0].reshape(tokens // 4, 2 * channels),
            ],
            [
                ((tokens, channels), FL),
                ((tokens, channels), FL),
                ((tokens, LANES), FL),
                ((channels // LANES, tokens, LANES), FL),
                ((tokens, channels), BF),
            ],
            micros=14,
            after=[expert_out[-1][0][0] if m == 0 else merged[m - 1][0]],
        )
        outputs[m] = merged[m][0].reshape(band_rows // 2, band_cols // 2, 2 * channels)
        back_res[m] = exchanged(merged[m][6:])
    for m in micros:
        expert_back[m] = expert_backward(
            me,
            back_res[m],
            expert_first_weight,
            expert_second_weight,
            first_other,
            second_other,
            expert_out[m][2],
            [merged[-1][0] if m == 0 else expert_back[m - 1][2]],
        )
        back_sent[m] = exchanged(expert_back[m][0])

    def settle(m, after):
        return call_kernel(
            functools.partial(settle_body, members=members),
            "settle",
            [
                ((tokens, channels), FL),
                ((tokens, channels), BF),
                ((tokens, channels), BF),
                ((8, channels), FL),
            ],
            [
                *back_sent[m],
                dest_cols[m],
                merged[m][3],
                merged[m][4],
                weight_router,
                routed[m][1],
                routed[m][2],
                attn_small,
                weight_proj,
            ],
            micros=7,
            after=after,
        )

    grad_merge = merge_weight_grad(
        [b[1] for b in merged], [b[2] for b in merged], channels, [expert_back[-1][2]]
    )
    sum_merge, merge_steps = dense_sum(grad_merge)
    settled[0] = settle(0, [grad_merge])
    in_keep, in_send, _ = expert_weight_grads(
        me, received, [b[1] for b in expert_back], local, row_size, True, [settled[0][3]]
    )
    for m in micros[1:]:
        settled[m] = settle(m, [in_keep])
    out_keep, out_send, grad_eout_bias = expert_weight_grads(
        me, back_res, [b[1] for b in expert_out], local, row_size, False, [settled[-1][3]]
    )

    state = dict(
        first=dict(keep=in_keep, send=in_send), second=dict(keep=out_keep, send=out_send)
    )
    row_bits = list(reversed(bits_of("row")))
    latest = out_keep

    def transfer(kind):
        at = state[kind]
        step = at.setdefault("step", 0)
        if step < len(row_bits):
            at["got"] = crossed(at["send"], "row", row_bits[step])
        else:
            at["got"] = crossed(at["send"], "dp", members)

    def advance(kind):
        nonlocal latest
        at = state[kind]
        if at["step"] < len(row_bits):
            at["keep"], at["send"] = add_pieces(at["keep"], at["got"], [latest])
            latest = at["send"]
        else:
            at["held"] = spread_over_row(add_halves(at["keep"], at["got"], [latest]))
            latest = at["held"][0]
            return
        at["step"] += 1
        transfer(kind)

    transfer("first")
    transfer("second")
    plan = {
        "start": ["first"],
        (0, 1): ["first", "second"],
        (1, 0): ["first", "second"],
        "end": ["second"],
    }
    for _ in range(len(row_bits) - 2):
        plan[(0, 1)] = plan[(0, 1)] + ["first", "second"]

    def advance_at(place):
        for kind in plan.get(place, ()):
            advance(kind)

    advance_at("start")
    dense_args = []
    for m in micros:
        dense_args += [arrived[m], attended[m][0], settled[m][1], routed[m][3], merged[m][4]]
    grad_proj, grad_router = call_kernel(
        dense_body,
        "dense_weight_grads",
        [((channels, channels), BF), ((channels, LANES), BF)],
        dense_args,
        micros=4,
        after=[latest, merge_steps[0]],
    )
    latest = grad_router

    tile_after = {(0, 1): merge_steps[1:2], (1, 0): merge_steps[2:]}
    tile_sums = [None] * tile_count
    tile_smalls = [None] * tile_count
    weight_grads = [grad_proj, grad_router]
    for m in micros:
        lifted = passed_along(settled[m][2][:half], "row", -1)
        (back_windows,) = call_kernel(
            functools.partial(window_body, band_cols=band_cols, channels=channels),
            "window_grads",
            [((tokens, channels), BF)],
            [settled[m][2][half:], lifted],
            [grid_scratch, win_scratch],
            micros=3,
            after=[latest],
        )
        latest = back_windows
        win, qkv, inverse = attended[m][2:]
        last = m == micro_count - 1
        grads = []
        for t in range(tile_count):

            def part(array, rows, at):
                return (array, pl.BlockSpec((rows, LANES), lambda i, at=at: (0, at)))

            args = [
                part(back_windows, tokens, t),
                part(qkv, tokens, t),
                part(qkv, tokens, tile_count + t),
                part(qkv, tokens, 2 * tile_count + t),
                part(inverse, tokens, t),
                part(inverse, tokens, tile_count + t),
                part(scale_lanes, 1, t),
                win,
                (
                    bias_keys,
                    pl.BlockSpec((1,) + bias_shape[0][1:], lambda i, t=t: (t, 0, 0)),
                ),
                *zones[m],
                head_marks,
                block_ones,
            ]
            if m:
                args += tile_sums[t]
            dqkv, dweight, dbias, small = call_kernel(
                functools.partial(attend_backward_body, summed_before=m > 0),
                "attend_backward",
                [
                    ((tokens, 3 * LANES), BF),
                    ((channels, 3 * LANES), BF if last else FL),
                    (bias_shape[0][1:], FL),
                    ((8, LANES), FL),
                ],
                args,
                micros=10,
                after=[latest] + tile_after.get((m, t), []),
            )
            latest = small
            tile_sums[t] = [dweight, dbias]
            tile_smalls[t] = small if m == 0 else tile_smalls[t] + small
            grads.append(dqkv)
            if last:
                weight_grads.append(dweight)
                if t == tile_count - 2:
                    sum_first, _ = dense_sum(jnp.concatenate(weight_grads, 1))
                if t == tile_count - 1:
                    sum_last, last_steps = dense_sum(dweight)
            advance_at((m, t))
        if last:
            (lines,) = call_kernel(
                fold_body,
                "fold_bias",
                [((HEAD_COUNT, 8, SHEAR), FL)],
                [sums[1] for sums in tile_sums],
                micros=3,
                after=[latest],
            )
            latest = lines
        input_parts[m] = call_kernel(
            functools.partial(input_grad_body, band_cols=band_cols, channels=channels),
            "input_grad",
            [((half, channels), FL), ((half, channels), BF)],
            grads + [weight_qkv],
            [grid_scratch, win_scratch],
            micros=5,
            after=[latest],
        )
        latest = input_parts[m][1]
        passed = passed_along(input_parts[m][1], "row", 1).astype(FL)
        input_grads[m] = (
            (settled[m][0] + jnp.concatenate([passed, input_parts[m][0]], 0))
            .astype(BF)
            .reshape(band_rows, band_cols, channels)
        )
    advance_at("end")
    sum_ein = place_pieces(me, state["first"]["held"], local, hidden, True, [latest])
    sum_eout = place_pieces(me, state["second"]["held"], local, hidden, False, [])
    sum_proj = sum_first[:, :channels]
    sum_router = sum_first[:, channels : channels + experts]
    sum_qkv = jnp.concatenate([sum_first[:, channels + LANES :], sum_last], 1)
    sum_qkv = sum_qkv.reshape(-1, tile_count, 3, LANES).swapaxes(1, 2).reshape(-1, 3 * channels)

    settle_sums = sum(s[3] for s in settled)
    merge_sums = sum(b[5] for b in merged)
    dtable = table_of_lines(lines)
    attn_sums = jnp.concatenate(tile_smalls, 1)[:3]
    parts = [
        dtable,
        attn_sums,
        settle_sums[:3],
        merge_sums[:2],
        merge_sums[2:4, :channels],
    ]
    bias_parts = [sum(b[2] for b in expert_back), grad_eout_bias]
    flat = jnp.concatenate([part.reshape(-1) for part in parts])
    flat = jnp.pad(flat, (0, -flat.size % 1024)).reshape(-1, 1024)
    biases = jnp.concatenate([part.reshape(-1) for part in bias_parts])
    biases = jnp.pad(biases, (0, -biases.size % 1024)).reshape(-1, 1024)
    both = summed(jnp.concatenate([flat, biases], 0), ("row",))
    flat, biases = summed(both[: flat.shape[0]], ("dp",)).reshape(-1), both[flat.shape[0] :]
    found, at = [], 0
    for part in parts:
        found.append(flat[at : at + part.size].reshape(part.shape))
        at += part.size
    dtable, attn_sums, settle_sums, merge_sums, moe_sums = found
    biases = biases.reshape(-1)
    in_bias = biases[: 2 * local * hidden].reshape(2 * local, hidden)
    out_bias = biases[2 * local * hidden : 2 * local * (hidden + channels)]
    out_bias = out_bias.reshape(2 * local, channels)
    other_bias = crossed(
        jnp.concatenate([in_bias[local:], out_bias[local:]], 1), "dp", members
    )
    sum_ein_bias = in_bias[:local] + other_bias[:, :hidden]
    sum_eout_bias = out_bias[:local] + other_bias[:, hidden:]
    grad_first, grad_first_bias, grad_second = table_back(dtable)
    sum_qbias, sum_vbias, sum_scale = attn_sums[0], attn_sums[1], attn_sums[2, ::HEAD_DIM]
    sum_proj_bias, sum_again, sum_ashift = settle_sums[0], settle_sums[1], settle_sums[2]
    sum_rgain, sum_rshift = merge_sums[0], merge_sums[1]
    sum_mgain, sum_mshift = moe_sums[0], moe_sums[1]
    return (
        jnp.stack(outputs)[:, None],
        jnp.stack(input_grads)[:, None],
        sum_qkv,
        sum_qbias,
        sum_vbias,
        sum_scale,
        grad_first,
        grad_first_bias,
        grad_second,
        sum_proj,
        sum_proj_bias,
        sum_again,
        sum_ashift,
        sum_router,
        sum_ein,
        sum_ein_bias,
        sum_eout,
        sum_eout_bias,
        sum_mgain,
        sum_mshift,
        sum_merge,
        sum_rgain,
        sum_rshift,
    )


def solution(mesh):
    return jax.shard_map(
        on_device,
        mesh=mesh,
        in_specs=(
            P(None, "dp", "row", None, None),
            P(None, "dp", None),
            P(None, "dp", "row", None, None),
            P(None, "dp", "row", None, None),
            P("dp", None),
            P(),
            P(),
            P(),
            P(),
            P(),
            P(),
            P("dp", None),
            P(),
            P(),
            P(),
            P("dp", None),
            P("dp", None, None),
            P("dp", None),
            P("dp", None, None),
            P("dp", None),
            P(),
            P(),
            P("dp", None),
            P(),
            P(),
        ),
        out_specs=(
            P(None, "dp", "row", None, None),
            P(None, "dp", "row", None, None),
            P("dp", None),
            P(),
            P(),
            P(),
            P(),
            P(),
            P(),
            P("dp", None),
            P(),
            P(),
            P(),
            P("dp", None),
            P("dp", None, None),
            P("dp", None),
            P("dp", None, None),
            P("dp", None),
            P(),
            P(),
            P("dp", None),
            P(),
            P(),
        ),
        check_vma=False,
    )
```

time: 688 us -> 588 us (0.85); the launches traced: 676 us -> 584 us
  waiting for transfers between devices: 154 us -> 103 us
  other arithmetic: 54 us -> 23.7 us
  matrix products: 33.1 us -> 13.4 us
  Pallas kernels: 267 us -> 281 us
    all_to_all x13 -> x1, waiting for transfers between devices: 125 us -> 0.01 us  [swapped(): return lax.all_to_all(rows, 'dp', split_axis=0, concat_axis=0, tiled=True)]
    ppermute x18 -> x72, waiting for transfers between devices: 14.1 us -> 95 us  [crossed(): return lax.ppermute(array, axis, [(i, i ^ bit) for i in range(count)])]
    all_to_all x13 -> x1, starting transfers between devices: 64.2 us -> 5.81 us  [swapped(): return lax.all_to_all(rows, 'dp', split_axis=0, concat_axis=0, tiled=True)]
    ppermute x18 -> x72, starting transfers between devices: 20.3 us -> 70.9 us  [crossed(): return lax.ppermute(array, axis, [(i, i ^ bit) for i in range(count)])]
    unnamed x163 -> x243, local copies, waits for them, and re-layouts: 6.9 us -> 29.4 us
    dot_general x4 -> x0, matrix products: 18.9 us -> none  [the longest x2 9.72 us: spread_table(): jnp.einsum('fqy,uzs,ysr->rqzfu', select, select, table, precision=PRECISI...]
    another operation x9 -> x7, local copies, waits for them, and re-layouts: 16.8 us -> 1.72 us  [the longest x2 1.35 us: on_device(): chosen = patch_expert_index[m].reshape(1, tokens)]
    pallas_call x17 -> x40, Pallas kernels: 267 us -> 281 us  [the longest x29 173 us: call_kernel(): pl.pallas_call(skipping(body, len(args), len(after)), name=name, grid=(1,...]
  transfers between devices with their start and end apart: 40 -> 81, of which waited for: 17 -> 16; matrix products, arithmetic and copies ran while one was open for 21% -> 12% of each run, Pallas kernels for 38% -> 46%
where the time goes in v2:
time: 588 us; the launch traced here: 584 us
  Pallas kernels  281 us (48%)
  waiting for transfers between devices  103 us (18%)
  starting transfers between devices  81.7 us (14%)
  local copies, waits for them, and re-layouts  65.3 us (11%)
  other arithmetic  23.7 us (4%)
  between operations  16.3 us (3%)
  matrix products  13.4 us (2%)
    pallas_call x29, Pallas kernels, call_kernel(): pl.pallas_call(skipping(body, len(args), len(after)), name=name, grid=(1,...  173 us
    pallas_call x8, Pallas kernels, call_expert(): pl.pallas_call(skipping(body, 1 + len(args), len(after)), name=name, grid...  96.1 us
    ppermute x72, waiting for transfers between devices, crossed(): return lax.ppermute(array, axis, [(i, i ^ bit) for i in range(count)])  95 us
    ppermute x72, starting transfers between devices, crossed(): return lax.ppermute(array, axis, [(i, i ^ bit) for i in range(count)])  70.9 us
    unnamed x243, local copies, waits for them, and re-layouts  29.4 us
  transfers between devices with their start and end apart: 81, of which 16 were waited for; matrix products, arithmetic and copies ran while one was open for 12% of the time, Pallas kernels for 46%

profile of v2, /device:TPU:0, one launch (start us, length us, event | category | flops | bytes accessed | tf_op | source)
XLA Modules:
  0.0 583.8 jit_solution(13277049786046455419)
XLA Ops:
  13.1 5.8 all-to-all-start
  54.0 20.6 %collective-permute-done.1.refs_11_.refs_1_.refs_9_.refs_8_ = bf16[2,384,384]{2,1,0:T(8,128)(2,1)S(1)} collective-permute-done((bf16[2,384,384]{2,1,0:T(8,128)(2,1)S(1)}, bf16[2,384,384]{2,1,0:T(8,128)(2,1)S(1)}, u32[]{:S(2)}, u32[]{:S(2)}) %collective-permute-start.1) | collective-permute-done | bytes 589856 | tf_op jit(solution)/shard_map/ppermute | solution.py:1200
  82.7 13.1 %attend_forward.2 = (bf16[576,384]{1,0:T(8,128)(2,1)S(1)}, bf16[576,384]{1,0:T(8,128)(2,1)S(1)}, bf16[1152,384]{1,0:T(8,128)(2,1)}, bf16[1152,1152]{1,0:T(8,128)(2,1)}, f32[1152,768]{1,0:T(8,128)}) custom-call(bf16[1152,384]{1,0:T(8,128)(2,1)} %bitcast.147, bf16[576,384]{1,0:T(8,128)(2,1)} %get-tuple-element.420.refs_1_, ...), custom_call_target="tpu_custom_call" | custom-call | flops 7040000000 | bytes 100000 | tf_op jit(solution)/shard_map/attend_forward/pallas_call | solution.py:170
  96.6 13.3 %attend_forward.3 = (bf16[576,384]{1,0:T(8,128)(2,1)S(1)}, bf16[576,384]{1,0:T(8,128)(2,1)S(1)}, bf16[1152,384]{1,0:T(8,128)(2,1)}, bf16[1152,1152]{1,0:T(8,128)(2,1)}, f32[1152,768]{1,0:T(8,128)}) custom-call(bf16[1152,384]{1,0:T(8,128)(2,1)} %bitcast.145, bf16[576,384]{1,0:T(8,128)(2,1)} %get-tuple-element.421.refs_1_, ...), custom_call_target="tpu_custom_call" | custom-call | flops 7040000000 | bytes 100000 | tf_op jit(solution)/shard_map/attend_forward/pallas_call | solution.py:170
  111.5 5.2 route.2
  134.1 8.0 %collective-permute-done.11.refs_14_.refs_13_ = bf16[2,384,384]{2,1,0:T(8,128)(2,1)} collective-permute-done((bf16[2,384,384]{2,1,0:T(8,128)(2,1)}, bf16[2,384,384]{2,1,0:T(8,128)(2,1)}, u32[]{:S(2)}, u32[]{:S(2)}) %collective-permute-start.11) | collective-permute-done | bytes 589856 | tf_op jit(solution)/shard_map/ppermute | solution.py:1200
  147.2 5.1 route.3
  158.0 11.6 %collective-permute-done.7.refs_4_ = bf16[384,384]{1,0:T(8,128)(2,1)S(1)} collective-permute-done((bf16[384,384]{1,0:T(8,128)(2,1)}, bf16[384,384]{1,0:T(8,128)(2,1)S(1)}, u32[]{:S(2)}, u32[]{:S(2)}) %collective-permute-start.7) | collective-permute-done | bytes 294944 | tf_op jit(solution)/shard_map/ppermute | solution.py:1200
  170.3 19.7 %expert_forward.2 = (bf16[384,384]{1,0:T(8,128)(2,1)S(1)}, bf16[384,384]{1,0:T(8,128)(2,1)S(1)}, bf16[384,384]{1,0:T(8,128)(2,1)S(1)}, bf16[384,384]{1,0:T(8,128...) custom-call(s32[1]{0:T(128)} %bitcast.refs_0_, bf16[384,384]{1,0:T(8,128)(2,1)S(1)} %copy-done.58, ...), custom_call_target="tpu_custom_call" | custom-call | flops 8360000000 | bytes 100000 | tf_op jit(solution)/shard_map/expert_forward/pallas_call | solution.py:926
  195.0 19.9 %expert_forward.3 = (bf16[384,384]{1,0:T(8,128)(2,1)S(1)}, bf16[384,384]{1,0:T(8,128)(2,1)}, bf16[384,384]{1,0:T(8,128)(2,1)}, bf16[384,384]{1,0:T(8,128)(2,1)},...) custom-call(s32[1]{0:T(128)} %bitcast.refs_0_, bf16[384,384]{1,0:T(8,128)(2,1)S(1)} %get-tuple-element.173.refs_1_.refs_5_, ...), custom_call_target="tpu_custom_call" | custom-call | flops 8360000000 | bytes 100000 | tf_op jit(solution)/shard_map/expert_forward/pallas_call | solution.py:926
  220.6 12.5 %merge.2 = (bf16[288,768]{1,0:T(8,128)(2,1)}, bf16[288,1536]{1,0:T(8,128)(2,1)}, bf16[288,768]{1,0:T(8,128)(2,1)}, f32[1152,384]{1,0:T(8,128)}, bf16[1152,128]{1...) custom-call(bf16[384,384]{1,0:T(8,128)(2,1)S(1)} %copy-done.65, ...), custom_call_target="tpu_custom_call" | custom-call | flops 6160000000 | bytes 100000 | tf_op jit(solution)/shard_map/merge/pallas_call | solution.py:170
  236.7 12.9 %merge.3 = (bf16[288,768]{1,0:T(8,128)(2,1)}, bf16[288,1536]{1,0:T(8,128)(2,1)}, bf16[288,768]{1,0:T(8,128)(2,1)}, f32[1152,384]{1,0:T(8,128)}, bf16[1152,128]{1...) custom-call(bf16[384,384]{1,0:T(8,128)(2,1)S(1)} %copy-done.63, ...), custom_call_target="tpu_custom_call" | custom-call | flops 6160000000 | bytes 100000 | tf_op jit(solution)/shard_map/merge/pallas_call | solution.py:170
  254.0 11.5 %expert_backward.2 = (bf16[384,384]{1,0:T(8,128)(2,1)S(1)}, bf16[384,384]{1,0:T(8,128)(2,1)S(1)}, bf16[384,384]{1,0:T(8,128)(2,1)S(1)}, bf16[384,384]{1,0:T(8,12...) custom-call(s32[1]{0:T(128)} %bitcast.refs_0_, bf16[384,384]{1,0:T(8,128)(2,1)S(1)} %get-tuple-element.185.refs_1_, ...), custom_call_target="tpu_custom_call" | custom-call | flops 5280000000 | bytes 100000 | tf_op jit(solution)/shard_map/expert_backward/pallas_call | solution.py:926
  269.9 11.7 %expert_backward.3 = (bf16[384,384]{1,0:T(8,128)(2,1)S(1)}, bf16[384,384]{1,0:T(8,128)(2,1)S(1)}, bf16[384,384]{1,0:T(8,128)(2,1)S(1)}, bf16[384,384]{1,0:T(8,12...) custom-call(s32[1]{0:T(128)} %bitcast.refs_0_, ...), custom_call_target="tpu_custom_call" | custom-call | flops 5280000000 | bytes 100000 | tf_op jit(solution)/shard_map/expert_backward/pallas_call | solution.py:926
  283.8 5.5 merge_weight_grad.1.refs_12_
  295.5 7.6 %settle.2 = (f32[1152,384]{1,0:T(8,128)}, bf16[1152,384]{1,0:T(8,128)(2,1)}, bf16[1152,384]{1,0:T(8,128)(2,1)}, f32[8,384]{1,0:T(8,128)S(1)}) custom-call(bf16[384,384]{1,0:T(8,128)(2,1)S(1)} %get-tuple-element.190.refs_0_, bf16[384,384]{1,0:T(8,128)(2,1)S(1)} %collective-permute-done.27.refs_1_, bf16[384,384]{1,0:T(8,128)(2,1)S(1)} %collective-permute-done.28.refs_2_, ...), custom_call_target="tpu_custom_call" | custom-call | flops 3080000000 | bytes 100000 | tf_op jit(solution)/shard_map/settle/pallas_call | solution.py:170
  305.1 13.0 %expert_weight_grads.2 = (bf16[2,2,2,384,384]{4,3,2,1,0:T(8,128)(2,1)}, bf16[2,2,2,384,384]{4,3,2,1,0:T(8,128)(2,1)}, f32[4,1,384]{2,1,0:T(1,128)}) custom-call(s32[1]{0:T(128)} %bitcast.refs_0_, bf16[384,384]{1,0:T(8,128)(2,1)S(1)} %copy-done.59, bf16[384,384]{1,0:T(8,128)(2,1)S(1)} %copy-done.26, bf16[384,384]{1,0:T(8,128)(2,1)S(1)} %copy-done.28, ...), custom_call_target="tpu_custom_call" | custom-call | flops 5720000000 | bytes 100000 | tf_op jit(solution)/shard_map/expert_weight_grads/pallas_call | solution.py:926
  321.2 7.5 %settle.3 = (f32[1152,384]{1,0:T(8,128)}, bf16[1152,384]{1,0:T(8,128)(2,1)}, bf16[1152,384]{1,0:T(8,128)(2,1)}, f32[8,384]{1,0:T(8,128)S(1)}) custom-call(bf16[384,384]{1,0:T(8,128)(2,1)S(1)} %copy-done.51, bf16[384,384]{1,0:T(8,128)(2,1)S(1)} %collective-permute-done.34.refs_1_, bf16[384,384]{1,0:T(8,128)(2,1)S(1)} %copy-done.41, ...), custom_call_target="tpu_custom_call" | custom-call | flops 3080000000 | bytes 100000 | tf_op jit(solution)/shard_map/settle/pallas_call | solution.py:170
  331.7 13.2 %expert_weight_grads.3 = (bf16[2,2,2,384,384]{4,3,2,1,0:T(8,128)(2,1)}, bf16[2,2,2,384,384]{4,3,2,1,0:T(8,128)(2,1)}, f32[4,1,384]{2,1,0:T(1,128)S(1)}) custom-call(s32[1]{0:T(128)} %bitcast.refs_0_, bf16[384,384]{1,0:T(8,128)(2,1)S(1)} %copy-done.53, bf16[384,384]{1,0:T(8,128)(2,1)S(1)} %collective-permute-done.24.refs_2_, bf16[384,384]{1,0:T(8,128)(2,1)S(1)} %copy-done.32, ...), custom_call_target="tpu_custom_call" | custom-call | flops 5720000000 | bytes 100000 | tf_op jit(solution)/shard_map/expert_weight_grads/pallas_call | solution.py:926
  351.6 5.8 collective-permute-done.46
  372.3 9.2 %attend_backward.6 = (bf16[1152,384]{1,0:T(8,128)(2,1)}, f32[384,384]{1,0:T(8,128)S(1)}, f32[144,576]{1,0:T(8,128)S(1)}, f32[8,128]{1,0:T(8,128)S(1)}) custom-call(bf16[1152,384]{1,0:T(8,128)(2,1)} %copy-done.1, bf16[1152,1152]{1,0:T(8,128)(2,1)} %get-tuple-element.232.refs_1_.refs_2_.refs_3_, bf16[1152,1152]{1,0:T(8,128)(2,1)} %get-tuple-element.232.refs_1_.refs_2_.refs_3_, ...), custom_call_target="tpu_custom_call" | custom-call | flops 4400000000 | bytes 100000 | tf_op jit(solution)/shard_map/attend_backward/pallas_call | solution.py:170
  382.2 10.0 %attend_backward.7 = (bf16[1152,384]{1,0:T(8,128)(2,1)}, f32[384,384]{1,0:T(8,128)}, f32[144,576]{1,0:T(8,128)S(1)}, f32[8,128]{1,0:T(8,128)S(1)}) custom-call(bf16[1152,384]{1,0:T(8,128)(2,1)} %copy-done.1, bf16[1152,1152]{1,0:T(8,128)(2,1)} %get-tuple-element.232.refs_1_.refs_2_.refs_3_, bf16[1152,1152]{1,0:T(8,128)(2,1)} %get-tuple-element.232.refs_1_.refs_2_.refs_3_, ...), custom_call_target="tpu_custom_call" | custom-call | flops 4400000000 | bytes 100000 | tf_op jit(solution)/shard_map/attend_backward/pallas_call | solution.py:170
  401.9 9.1 %attend_backward.8 = (bf16[1152,384]{1,0:T(8,128)(2,1)}, f32[384,384]{1,0:T(8,128)S(1)}, f32[144,576]{1,0:T(8,128)S(1)}, f32[8,128]{1,0:T(8,128)S(1)}) custom-call(bf16[1152,384]{1,0:T(8,128)(2,1)} %copy-done.1, bf16[1152,1152]{1,0:T(8,128)(2,1)} %get-tuple-element.232.refs_1_.refs_2_.refs_3_, bf16[1152,1152]{1,0:T(8,128)(2,1)} %get-tuple-element.232.refs_1_.refs_2_.refs_3_, ...), custom_call_target="tpu_custom_call" | custom-call | flops 4400000000 | bytes 100000 | tf_op jit(solution)/shard_map/attend_backward/pallas_call | solution.py:170
  411.0 4.6 input_grad.2
  417.0 10.0 %attend_backward.9 = (bf16[1152,384]{1,0:T(8,128)(2,1)}, bf16[384,384]{1,0:T(8,128)(2,1)S(1)}, f32[144,576]{1,0:T(8,128)S(1)}, f32[8,128]{1,0:T(8,128)S(1)}) custom-call(bf16[1152,384]{1,0:T(8,128)(2,1)} %window_grads.3.refs_0_.refs_15_, bf16[1152,1152]{1,0:T(8,128)(2,1)} %get-tuple-element.250.refs_1_.refs_2_.refs_3_, ...), custom_call_target="tpu_custom_call" | custom-call | flops 4400000000 | bytes 100000 | tf_op jit(solution)/shard_map/attend_backward/pallas_call | solution.py:170
  427.0 5.1 collective-permute-done.44
  440.9 9.3 %attend_backward.10 = (bf16[1152,384]{1,0:T(8,128)(2,1)}, bf16[384,384]{1,0:T(8,128)(2,1)S(1)}, f32[144,576]{1,0:T(8,128)S(1)}, f32[8,128]{1,0:T(8,128)S(1)}) custom-call(bf16[1152,384]{1,0:T(8,128)(2,1)} %window_grads.3.refs_0_.refs_15_, bf16[1152,1152]{1,0:T(8,128)(2,1)} %get-tuple-element.250.refs_1_.refs_2_.refs_3_, ...), custom_call_target="tpu_custom_call" | custom-call | flops 4400000000 | bytes 100000 | tf_op jit(solution)/shard_map/attend_backward/pallas_call | solution.py:170
  450.3 9.4 %attend_backward.11 = (bf16[1152,384]{1,0:T(8,128)(2,1)}, bf16[384,384]{1,0:T(8,128)(2,1)S(1)}, f32[144,576]{1,0:T(8,128)S(1)}, f32[8,128]{1,0:T(8,128)S(1)}) custom-call(bf16[1152,384]{1,0:T(8,128)(2,1)} %window_grads.3.refs_0_.refs_15_, bf16[1152,1152]{1,0:T(8,128)(2,1)} %get-tuple-element.250.refs_1_.refs_2_.refs_3_, ...), custom_call_target="tpu_custom_call" | custom-call | flops 4400000000 | bytes 100000 | tf_op jit(solution)/shard_map/attend_backward/pallas_call | solution.py:170
  469.1 4.4 input_grad.3
  495.2 5.6 collective-permute-done.68
  508.3 24.6 %collective-permute-done.69 = f32[11,1024]{1,0:T(8,128)S(1)} collective-permute-done((f32[11,1024]{1,0:T(8,128)S(1)}, f32[11,1024]{1,0:T(8,128)S(1)}, u32[]{:S(2)}, u32[]{:S(2)}) %collective-permute-start.69) | collective-permute-done | bytes 45088 | tf_op jit(solution)/shard_map/ppermute | solution.py:1200
  561.7 8.1 %collective-permute-done.75.refs_2_ = bf16[2,384,384]{2,1,0:T(8,128)(2,1)S(1)} collective-permute-done((bf16[2,384,384]{2,1,0:T(8,128)(2,1)}, bf16[2,384,384]{2,1,0:T(8,128)(2,1)S(1)}, u32[]{:S(2)}, u32[]{:S(2)}) %collective-permute-start.75) | collective-permute-done | bytes 589856 | tf_op jit(solution)/shard_map/ppermute | solution.py:1200
  (607 shorter events, 235.0 us)
Async XLA Ops:
  9.5 66.9 %collective-permute-start = (bf16[2,576,384]{2,1,0:T(8,128)(2,1)}, bf16[2,576,384]{2,1,0:T(8,128)(2,1)}, u32[]{:S(2)}, u32[]{:S(2)}) collective-permute-start(bf16[2,576,384]{2,1,0:T(8,128)(2,1)} %slice.316), channel_id=1, source_target_pairs={{0,3},{1,0},{2,1},{3,2},{4,7},{5,4},{6,5},{7,6},{8,11},{9,8},{10,9... | collective-permute-start | bytes 2654216 | tf_op jit(solution)/shard_map/ppermute | solution.py:38
  13.1 65.4 %all-to-all-start = ((bf16[8,48,1664]{2,1,0:T(8,128)(2,1)}), bf16[8,48,1664]{2,1,0:T(8,128)(2,1)}, u32[]{:S(2)}, u32[]{:S(2)}) async-start(bf16[8,48,1664]{2,1,0:T(8,128)(2,1)} %broadcast_in_dim.218), calls=%async_computation | async-start | bytes 2555904 | tf_op jit(solution)/shard_map/all_to_all | solution.py:1163
  18.9 201.6 %all-gather.2.cloned.1.call-start = ((), (), s32[]{:S(2)}) async-start(), calls=%async_computation.1 | async-start | bytes 2654208 | tf_op jit(solution)/shard_map/all_gather | solution.py:1431
  20.5 54.1 %collective-permute-start.1 = (bf16[2,384,384]{2,1,0:T(8,128)(2,1)S(1)}, bf16[2,384,384]{2,1,0:T(8,128)(2,1)S(1)}, u32[]{:S(2)}, u32[]{:S(2)}) collective-permute-start(bf16[2,384,384]{2,1,0:T(8,128)(2,1)S(1)} %pad_maximum_fusion.1), channel_id=1, source_target_pairs={{0,16},{4,20},{8,24},{12,28},{16,0},{20,4},{24,8},{28,12},{1,17},{... | collective-permute-start | bytes 1769480 | tf_op jit(solution)/shard_map/ppermute | solution.py:1200
  74.7 36.7 %collective-permute-start.3 = (bf16[2,384,384]{2,1,0:T(8,128)(2,1)S(1)}, bf16[2,384,384]{2,1,0:T(8,128)(2,1)}, u32[]{:S(2)}, u32[]{:S(2)}) collective-permute-start(bf16[2,384,384]{2,1,0:T(8,128)(2,1)S(1)} %hold.2), channel_id=1, source_target_pairs={{0,16},{4,20},{8,24},{12,28},{16,0},{20,4},{24,8},{28,12},{1,17},{... | collective-permute-start | bytes 1769480 | tf_op jit(solution)/shard_map/ppermute | solution.py:1200
  74.8 36.6 %collective-permute-start.4 = (bf16[2,384,384]{2,1,0:T(8,128)(2,1)S(1)}, bf16[2,384,384]{2,1,0:T(8,128)(2,1)}, u32[]{:S(2)}, u32[]{:S(2)}) collective-permute-start(bf16[2,384,384]{2,1,0:T(8,128)(2,1)S(1)} %collective-permute-done.1.refs_11_.refs_1_.refs_9_.refs_8_), channel_id=1, source_target_pairs={{0,2},{1,3},{2,0},{3,1},{4,6},{5,7},{6,4},{7,5},{8,10},{9,11},{10,... | collective-permute-start | bytes 1769480 | tf_op jit(solution)/shard_map/ppermute | solution.py:1200
  152.4 39.7 %collective-permute-start.18 = (bf16[384,384]{1,0:T(8,128)(2,1)S(1)}, bf16[384,384]{1,0:T(8,128)(2,1)S(1)}, u32[]{:S(2)}, u32[]{:S(2)}) collective-permute-start(bf16[384,384]{1,0:T(8,128)(2,1)S(1)} %get-tuple-element.174), channel_id=1, source_target_pairs={{0,4},{4,0},{8,12},{12,8},{16,20},{20,16},{24,28},{28,24},{1,5},{5... | collective-permute-start | bytes 884744 | tf_op jit(solution)/shard_map/ppermute | solution.py:1200
  153.7 40.5 %collective-permute-start.19 = (bf16[384,384]{1,0:T(8,128)(2,1)S(1)}, bf16[384,384]{1,0:T(8,128)(2,1)S(1)}, u32[]{:S(2)}, u32[]{:S(2)}) collective-permute-start(bf16[384,384]{1,0:T(8,128)(2,1)S(1)} %get-tuple-element.175), channel_id=1, source_target_pairs={{0,8},{4,12},{8,0},{12,4},{16,24},{20,28},{24,16},{28,20},{1,9},{5... | collective-permute-start | bytes 884744 | tf_op jit(solution)/shard_map/ppermute | solution.py:1200
  155.6 38.5 %collective-permute-start.20 = (bf16[384,384]{1,0:T(8,128)(2,1)S(1)}, bf16[384,384]{1,0:T(8,128)(2,1)S(1)}, u32[]{:S(2)}, u32[]{:S(2)}) collective-permute-start(bf16[384,384]{1,0:T(8,128)(2,1)S(1)} %get-tuple-element.176), channel_id=1, source_target_pairs={{0,12},{4,8},{8,4},{12,0},{16,28},{20,24},{24,20},{28,16},{1,13},{... | collective-permute-start | bytes 884744 | tf_op jit(solution)/shard_map/ppermute | solution.py:1200
  190.7 27.1 %collective-permute-start.15 = (bf16[384,384]{1,0:T(8,128)(2,1)S(1)}, bf16[384,384]{1,0:T(8,128)(2,1)S(1)}, u32[]{:S(2)}, u32[]{:S(2)}) collective-permute-start(bf16[384,384]{1,0:T(8,128)(2,1)S(1)} %get-tuple-element.168), channel_id=1, source_target_pairs={{0,4},{4,0},{8,12},{12,8},{16,20},{20,16},{24,28},{28,24},{1,5},{5... | collective-permute-start | bytes 884744 | tf_op jit(solution)/shard_map/ppermute | solution.py:1200
  192.1 27.7 %collective-permute-start.16 = (bf16[384,384]{1,0:T(8,128)(2,1)S(1)}, bf16[384,384]{1,0:T(8,128)(2,1)S(1)}, u32[]{:S(2)}, u32[]{:S(2)}) collective-permute-start(bf16[384,384]{1,0:T(8,128)(2,1)S(1)} %get-tuple-element.169), channel_id=1, source_target_pairs={{0,8},{4,12},{8,0},{12,4},{16,24},{20,28},{24,16},{28,20},{1,9},{5... | collective-permute-start | bytes 884744 | tf_op jit(solution)/shard_map/ppermute | solution.py:1200
  192.1 28.4 %collective-permute-start.17 = (bf16[384,384]{1,0:T(8,128)(2,1)S(1)}, bf16[384,384]{1,0:T(8,128)(2,1)}, u32[]{:S(2)}, u32[]{:S(2)}) collective-permute-start(bf16[384,384]{1,0:T(8,128)(2,1)S(1)} %get-tuple-element.170), channel_id=1, source_target_pairs={{0,12},{4,8},{8,4},{12,0},{16,28},{20,24},{24,20},{28,16},{1,13},{... | collective-permute-start | bytes 884744 | tf_op jit(solution)/shard_map/ppermute | solution.py:1200
  265.5 26.5 %collective-permute-start.27 = (bf16[384,384]{1,0:T(8,128)(2,1)S(1)}, bf16[384,384]{1,0:T(8,128)(2,1)S(1)}, u32[]{:S(2)}, u32[]{:S(2)}) collective-permute-start(bf16[384,384]{1,0:T(8,128)(2,1)S(1)} %get-tuple-element.191), channel_id=1, source_target_pairs={{0,4},{4,0},{8,12},{12,8},{16,20},{20,16},{24,28},{28,24},{1,5},{5... | collective-permute-start | bytes 884744 | tf_op jit(solution)/shard_map/ppermute | solution.py:1200
  267.0 26.9 %collective-permute-start.28 = (bf16[384,384]{1,0:T(8,128)(2,1)S(1)}, bf16[384,384]{1,0:T(8,128)(2,1)S(1)}, u32[]{:S(2)}, u32[]{:S(2)}) collective-permute-start(bf16[384,384]{1,0:T(8,128)(2,1)S(1)} %get-tuple-element.192), channel_id=1, source_target_pairs={{0,8},{4,12},{8,0},{12,4},{16,24},{20,28},{24,16},{28,20},{1,9},{5... | collective-permute-start | bytes 884744 | tf_op jit(solution)/shard_map/ppermute | solution.py:1200
  267.1 28.3 %collective-permute-start.29 = (bf16[384,384]{1,0:T(8,128)(2,1)S(1)}, bf16[384,384]{1,0:T(8,128)(2,1)S(1)}, u32[]{:S(2)}, u32[]{:S(2)}) collective-permute-start(bf16[384,384]{1,0:T(8,128)(2,1)S(1)} %get-tuple-element.193), channel_id=1, source_target_pairs={{0,12},{4,8},{8,4},{12,0},{16,28},{20,24},{24,20},{28,16},{1,13},{... | collective-permute-start | bytes 884744 | tf_op jit(solution)/shard_map/ppermute | solution.py:1200
  283.7 34.3 %collective-permute-start.35 = (bf16[384,384]{1,0:T(8,128)(2,1)S(1)}, bf16[384,384]{1,0:T(8,128)(2,1)S(1)}, u32[]{:S(2)}, u32[]{:S(2)}) collective-permute-start(bf16[384,384]{1,0:T(8,128)(2,1)S(1)} %get-tuple-element.214), channel_id=1, source_target_pairs={{0,8},{4,12},{8,0},{12,4},{16,24},{20,28},{24,16},{28,20},{1,9},{5... | collective-permute-start | bytes 884744 | tf_op jit(solution)/shard_map/ppermute | solution.py:1200
  291.9 27.3 %collective-permute-start.36 = (bf16[384,384]{1,0:T(8,128)(2,1)}, bf16[384,384]{1,0:T(8,128)(2,1)}, u32[]{:S(2)}, u32[]{:S(2)}) collective-permute-start(bf16[384,384]{1,0:T(8,128)(2,1)} %get-tuple-element.215), channel_id=1, source_target_pairs={{0,12},{4,8},{8,4},{12,0},{16,28},{20,24},{24,20},{28,16},{1,13},{... | collective-permute-start | bytes 884744 | tf_op jit(solution)/shard_map/ppermute | solution.py:1200
  293.9 34.8 %collective-permute-start.38 = (bf16[2,192,768]{2,1,0:T(8,128)(2,1)}, bf16[2,192,768]{2,1,0:T(8,128)(2,1)}, u32[]{:S(2)}, u32[]{:S(2)}) collective-permute-start(bf16[2,192,768]{2,1,0:T(8,128)(2,1)} %get-tuple-element.402), channel_id=1, source_target_pairs={{0,4},{4,0},{8,12},{12,8},{16,20},{20,16},{24,28},{28,24},{1,5},{5... | collective-permute-start | bytes 1769480 | tf_op jit(solution)/shard_map/ppermute | solution.py:1200
  295.4 33.3 %collective-permute-start.40 = (bf16[2,192,768]{2,1,0:T(8,128)(2,1)}, bf16[2,192,768]{2,1,0:T(8,128)(2,1)}, u32[]{:S(2)}, u32[]{:S(2)}) collective-permute-start(bf16[2,192,768]{2,1,0:T(8,128)(2,1)} %get-tuple-element.403), channel_id=1, source_target_pairs={{0,12},{4,8},{8,4},{12,0},{16,28},{20,24},{24,20},{28,16},{1,13},{... | collective-permute-start | bytes 1769480 | tf_op jit(solution)/shard_map/ppermute | solution.py:1200
  318.1 40.6 %collective-permute-start.37 = (bf16[2,2,2,384,384]{4,3,2,1,0:T(8,128)(2,1)}, bf16[2,2,2,384,384]{4,3,2,1,0:T(8,128)(2,1)}, u32[]{:S(2)}, u32[]{:S(2)}) collective-permute-start(bf16[2,2,2,384,384]{4,3,2,1,0:T(8,128)(2,1)} %get-tuple-element.225), channel_id=1, source_target_pairs={{0,1},{1,0},{2,3},{3,2},{4,5},{5,4},{6,7},{7,6},{8,9},{9,8},{10,11... | collective-permute-start | bytes 7077896 | tf_op jit(solution)/shard_map/ppermute | solution.py:1200
  345.0 51.9 %collective-permute-start.42 = (bf16[2,2,2,384,384]{4,3,2,1,0:T(8,128)(2,1)}, bf16[2,2,2,384,384]{4,3,2,1,0:T(8,128)(2,1)}, u32[]{:S(2)}, u32[]{:S(2)}) collective-permute-start(bf16[2,2,2,384,384]{4,3,2,1,0:T(8,128)(2,1)} %get-tuple-element.239), channel_id=1, source_target_pairs={{0,1},{1,0},{2,3},{3,2},{4,5},{5,4},{6,7},{7,6},{8,9},{9,8},{10,11... | collective-permute-start | bytes 7077896 | tf_op jit(solution)/shard_map/ppermute | solution.py:1200
  351.0 64.6 %collective-permute-start.45 = (bf16[576,384]{1,0:T(8,128)(2,1)S(1)}, bf16[576,384]{1,0:T(8,128)(2,1)S(1)}, u32[]{:S(2)}, u32[]{:S(2)}) collective-permute-start(bf16[576,384]{1,0:T(8,128)(2,1)S(1)} %get-tuple-element.416), channel_id=1, source_target_pairs={{0,3},{1,0},{2,1},{3,2},{4,7},{5,4},{6,5},{7,6},{8,11},{9,8},{10,9... | collective-permute-start | bytes 1327112 | tf_op jit(solution)/shard_map/ppermute | solution.py:38
  365.1 27.6 %collective-permute-start.43 = (bf16[2,1,2,384,384]{4,3,2,1,0:T(8,128)(2,1)}, bf16[2,1,2,384,384]{4,3,2,1,0:T(8,128)(2,1)S(1)}, u32[]{:S(2)}, u32[]{:S(2)}) collective-permute-start(bf16[2,1,2,384,384]{4,3,2,1,0:T(8,128)(2,1)} %get-tuple-element.230.refs_10_), channel_id=1, source_target_pairs={{0,2},{1,3},{2,0},{3,1},{4,6},{5,7},{6,4},{7,5},{8,10},{9,11},{10,... | collective-permute-start | bytes 3538952 | tf_op jit(solution)/shard_map/ppermute | solution.py:1200
  396.6 36.7 %collective-permute-start.49 = (bf16[2,384,384]{2,1,0:T(8,128)(2,1)S(1)}, bf16[2,384,384]{2,1,0:T(8,128)(2,1)S(1)}, u32[]{:S(2)}, u32[]{:S(2)}) collective-permute-start(bf16[2,384,384]{2,1,0:T(8,128)(2,1)S(1)} %get-tuple-element.242.refs_2_), channel_id=1, source_target_pairs={{0,16},{4,20},{8,24},{12,28},{16,0},{20,4},{24,8},{28,12},{1,17},{... | collective-permute-start | bytes 1769480 | tf_op jit(solution)/shard_map/ppermute | solution.py:1200
  400.6 35.8 %collective-permute-start.48 = (bf16[2,1,2,384,384]{4,3,2,1,0:T(8,128)(2,1)}, bf16[2,1,2,384,384]{4,3,2,1,0:T(8,128)(2,1)S(1)}, u32[]{:S(2)}, u32[]{:S(2)}) collective-permute-start(bf16[2,1,2,384,384]{4,3,2,1,0:T(8,128)(2,1)} %get-tuple-element.243.refs_13_), channel_id=1, source_target_pairs={{0,2},{1,3},{2,0},{3,1},{4,6},{5,7},{6,4},{7,5},{8,10},{9,11},{10,... | collective-permute-start | bytes 3538952 | tf_op jit(solution)/shard_map/ppermute | solution.py:1200
  434.7 66.1 %collective-permute-start.70 = (bf16[2,384,384]{2,1,0:T(8,128)(2,1)S(1)}, bf16[2,384,384]{2,1,0:T(8,128)(2,1)S(1)}, u32[]{:S(2)}, u32[]{:S(2)}) collective-permute-start(bf16[2,384,384]{2,1,0:T(8,128)(2,1)S(1)} %add_halves.2.refs_2_.refs_1_), channel_id=1, source_target_pairs={{0,2},{1,3},{2,0},{3,1},{4,6},{5,7},{6,4},{7,5},{8,10},{9,11},{10,... | collective-permute-start | bytes 1769480 | tf_op jit(solution)/shard_map/ppermute | solution.py:1200
  474.3 28.3 %collective-permute-start.51 = (bf16[2,48,1280]{2,1,0:T(8,128)(2,1)}, bf16[2,48,1280]{2,1,0:T(8,128)(2,1)}, u32[]{:S(2)}, u32[]{:S(2)}) collective-permute-start(bf16[2,48,1280]{2,1,0:T(8,128)(2,1)} %get-tuple-element.411), channel_id=1, source_target_pairs={{0,4},{4,0},{8,12},{12,8},{16,20},{20,16},{24,28},{28,24},{1,5},{5... | collective-permute-start | bytes 737288 | tf_op jit(solution)/shard_map/ppermute | solution.py:1200
  500.8 57.0 %collective-permute-start.71 = (bf16[2,384,384]{2,1,0:T(8,128)(2,1)S(1)}, bf16[2,384,384]{2,1,0:T(8,128)(2,1)S(1)}, u32[]{:S(2)}, u32[]{:S(2)}) collective-permute-start(bf16[2,384,384]{2,1,0:T(8,128)(2,1)S(1)} %add_halves.2.refs_2_.refs_1_), channel_id=1, source_target_pairs={{0,1},{1,0},{2,3},{3,2},{4,5},{5,4},{6,7},{7,6},{8,9},{9,8},{10,11... | collective-permute-start | bytes 1769480 | tf_op jit(solution)/shard_map/ppermute | solution.py:1200
  500.8 50.9 %collective-permute-start.73 = (bf16[2,384,384]{2,1,0:T(8,128)(2,1)S(1)}, bf16[2,384,384]{2,1,0:T(8,128)(2,1)}, u32[]{:S(2)}, u32[]{:S(2)}) collective-permute-start(bf16[2,384,384]{2,1,0:T(8,128)(2,1)S(1)} %copy-done.3), channel_id=1, source_target_pairs={{0,16},{4,20},{8,24},{12,28},{16,0},{20,4},{24,8},{28,12},{1,17},{... | collective-permute-start | bytes 1769480 | tf_op jit(solution)/shard_map/ppermute | solution.py:1200
  502.6 46.9 %collective-permute-start.50 = (bf16[576,384]{1,0:T(8,128)(2,1)}, bf16[576,384]{1,0:T(8,128)(2,1)}, u32[]{:S(2)}, u32[]{:S(2)}) collective-permute-start(bf16[576,384]{1,0:T(8,128)(2,1)} %copy-done.20), channel_id=1, source_target_pairs={{0,1},{1,2},{2,3},{3,0},{4,5},{5,6},{6,7},{7,4},{8,9},{9,10},{10,1... | collective-permute-start | bytes 1327112 | tf_op jit(solution)/shard_map/ppermute | solution.py:38
  503.0 55.3 %collective-permute-start.72 = (bf16[2,384,384]{2,1,0:T(8,128)(2,1)S(1)}, bf16[2,384,384]{2,1,0:T(8,128)(2,1)}, u32[]{:S(2)}, u32[]{:S(2)}) collective-permute-start(bf16[2,384,384]{2,1,0:T(8,128)(2,1)S(1)} %collective-permute-done.70.refs_2_), channel_id=1, source_target_pairs={{0,1},{1,0},{2,3},{3,2},{4,5},{5,4},{6,7},{7,6},{8,9},{9,8},{10,11... | collective-permute-start | bytes 1769480 | tf_op jit(solution)/shard_map/ppermute | solution.py:1200
  503.3 29.7 %collective-permute-start.69 = (f32[11,1024]{1,0:T(8,128)S(1)}, f32[11,1024]{1,0:T(8,128)S(1)}, u32[]{:S(2)}, u32[]{:S(2)}) collective-permute-start(f32[11,1024]{1,0:T(8,128)S(1)} %add.736), channel_id=1, source_target_pairs={{0,16},{4,20},{8,24},{12,28},{16,0},{20,4},{24,8},{28,12},{1,17},{... | collective-permute-start | bytes 135176 | tf_op jit(solution)/shard_map/ppermute | solution.py:1200
  (166 other events, 1411.8 us)
Sparse Core Ops, SparseCore 0:
  122.3 69.1 all-gather.1

commit v3 on v2

--- a/solution.py
+++ b/solution.py
@@ -42,54 +42,41 @@
     return jax.nn.gelu(values, approximate=False)
 
 
-def position_table(
-    bias_network_first_weight, bias_network_first_bias, bias_network_second_weight
-):
-    span_axis = (jnp.arange(2 * WINDOW_SIDE - 1, dtype=FL) - (WINDOW_SIDE - 1)) * (
-        8.0 / (WINDOW_SIDE - 1)
-    )
-    span_axis = jnp.sign(span_axis) * jnp.log2(jnp.abs(span_axis) + 1.0) / 3.0
-    grid_rows = jnp.broadcast_to(span_axis[:, None], (2 * WINDOW_SIDE - 1, 2 * WINDOW_SIDE - 1))
-    relative_coordinates = jnp.stack([grid_rows, grid_rows.T], -1)
-    hidden_activation = exact_error_gelu(
-        jnp.einsum(
-            "plr,rt->plt", relative_coordinates, bias_network_first_weight, precision=PRECISION_HIGH
-        )
-        + bias_network_first_bias
-    )
-    return 16.0 * jax.nn.sigmoid(
-        jnp.einsum(
-            "qvw,wk->qvk", hidden_activation, bias_network_second_weight, precision=PRECISION_HIGH
-        )
-    )
-
-
-def toeplitz_lines(table):
-    side = WINDOW_SIDE
-    heads = table.shape[-1]
-    by_head = table.transpose(2, 0, 1)
-    above = by_head[:, :, side - 1 :].reshape(heads, -1)
-    below = jnp.pad(by_head[:, :, : side - 1], ((0, 0), (0, 0), (1, 0))).reshape(heads, -1)
-    lines = jnp.pad(
-        jnp.stack([above, below], 1), ((0, 0), (0, 0), (0, SHEAR - above.shape[1]))
-    )
-    lines = jnp.stack(
-        [
-            jnp.roll(lines[:, 0], -side * (side - 1), -1),
-            jnp.roll(lines[:, 1], -side * side, -1),
-        ],
-        1,
-    )
-    back = jnp.roll(jnp.flip(lines, -1), 1, -1)
-    return jnp.concatenate([lines, back], 1)
-
-
-def table_of_lines(lines):
-    side = WINDOW_SIDE
-    spans = 2 * side - 1
-    above = lines[:, 0, side - 1 : side - 1 + spans * side].reshape(-1, spans, side)
-    below = jnp.pad(lines[:, 1], ((0, 0), (1, 0)))[:, : spans * side].reshape(-1, spans, side)
-    return jnp.concatenate([below[:, :, 1:], above], 2).transpose(1, 2, 0)
+SPANS = 2 * WINDOW_SIDE - 1
+AREA = WINDOW_SIDE * WINDOW_SIDE
+
+
+def span_coordinate(steps):
+    size = jnp.abs(steps) * (8.0 / (WINDOW_SIDE - 1))
+    value = jnp.log2(size + 1.0) / 3.0
+    return jnp.where(steps < 0, -value, value)
+
+
+def bias_network(first_ref, second_ref):
+    shape = (2 * SHEAR, 1)
+    row = lax.broadcasted_iota(jnp.int32, shape, 0)
+    below = row >= SHEAR
+    place = jnp.where(below, row - SHEAR + 1, row - (WINDOW_SIDE - 1))
+    held = jnp.clip(place, 0, SPANS * WINDOW_SIDE - 1)
+    column = held % WINDOW_SIDE
+    valid = (held == place) & (jnp.logical_not(below) | (column > 0))
+    rows_apart = (held // WINDOW_SIDE - (WINDOW_SIDE - 1)).astype(FL)
+    columns_apart = jnp.where(below, column - WINDOW_SIDE, column).astype(FL)
+    down, across = span_coordinate(rows_apart), span_coordinate(columns_apart)
+    pre = down * first_ref[0:1, :] + across * first_ref[1:2, :] + first_ref[2:3, :]
+    cdf = 0.5 * (1.0 + lax.erf(pre * 0.7071067811865476))
+    hidden = pre * cdf
+    slope = cdf + pre * (0.3989422804014327 * jnp.exp(-0.5 * pre * pre))
+    level = jax.nn.sigmoid(
+        lax.dot_general(
+            hidden,
+            second_ref[...],
+            (((1,), (0,)), ((), ())),
+            precision=PRECISION_HIGH,
+            preferred_element_type=FL,
+        )
+    )
+    return down, across, valid, hidden, slope, level
 
 
 def mask_operands(row_start, total_rows, total_cols, valid_rows, valid_cols):
@@ -242,55 +229,111 @@
     return jnp.concatenate([tile] * TILE_HEADS, 0) * heads_ref[...]
 
 
-def spread_body(lines_ref, rows_ref, keys_ref):
-    area = WINDOW_SIDE * WINDOW_SIDE
-    row = lax.broadcasted_iota(jnp.int32, (area, area), 0) % WINDOW_SIDE
-    lane = lax.broadcasted_iota(jnp.int32, (area, area), 1) % WINDOW_SIDE
+def spread_body(first_ref, second_ref, rows_ref, keys_ref):
+    row = lax.broadcasted_iota(jnp.int32, (AREA, AREA), 0) % WINDOW_SIDE
+    lane = lax.broadcasted_iota(jnp.int32, (AREA, AREA), 1) % WINDOW_SIDE
+    *_, level = bias_network(first_ref, second_ref)
+    wide = jnp.concatenate([16.0 * level, jnp.zeros((2 * SHEAR, LANES - HEAD_COUNT), FL)], 1)
+    lines = wide.T
 
     def shear(line):
-        wide = jnp.broadcast_to(line, (area, SHEAR))
-        return pltpu.roll(wide, 0, 1, stride=1, stride_axis=0)[:, 0:area]
-
-    def step(t, carry):
+        wide = pltpu.roll(jnp.broadcast_to(line, (AREA, SHEAR)), SHEAR - (AREA - 1), 1)
+        return pltpu.roll(wide, 0, 1, stride=1, stride_axis=0)[:, 0:AREA]
+
+    for t in range(rows_ref.shape[0]):
         rows, keys = [], []
         for k in range(TILE_HEADS):
-            lines = lines_ref[t * TILE_HEADS + k]
-            keys.append(jnp.where(lane >= row, shear(lines[0:1]), shear(lines[1:2])))
-            rows.append(jnp.where(row >= lane, shear(lines[2:3]), shear(lines[3:4])))
+            line = lines[t * TILE_HEADS + k : t * TILE_HEADS + k + 1]
+            key = jnp.where(lane >= row, shear(line[:, :SHEAR]), shear(line[:, SHEAR:]))
+            keys.append(key)
+            rows.append(key.T)
         rows_ref[t] = jnp.concatenate(rows, 1)
         keys_ref[t] = jnp.concatenate(keys, 1)
-        return carry
-
-    lax.fori_loop(0, rows_ref.shape[0], step, 0)
-
-
-def fold_body(*refs):
-    (*ins, out_ref) = refs
-    area = WINDOW_SIDE * WINDOW_SIDE
-    row = lax.broadcasted_iota(jnp.int32, (area, area), 0)
-    lane = lax.broadcasted_iota(jnp.int32, (area, area), 1)
-    turn = jnp.where(row + lane == area - 1, 1.0, 0.0).astype(BF)
-    later = lane % WINDOW_SIDE >= (area - 1 - row) % WINDOW_SIDE
-    blank = jnp.zeros((area, SHEAR - area), FL)
+
+
+LINE_ROWS = 2 * HEAD_COUNT
+ATTN_AT = LINE_ROWS
+SETTLE_AT = ATTN_AT + 3
+MERGE_AT = SETTLE_AT + 3
+SUM_ROWS = 40
+
+
+def fold_body(*refs, tile_count, micro_count):
+    dbias_refs, attn_refs, settle_refs, merge_refs, dpre_refs, (dout_ref, out_ref) = taken(
+        refs, tile_count, tile_count * micro_count, micro_count, micro_count, micro_count
+    )
+    row = lax.broadcasted_iota(jnp.int32, (AREA, AREA), 0)
+    lane = lax.broadcasted_iota(jnp.int32, (AREA, AREA), 1)
+    turn = jnp.where(row + lane == AREA - 1, 1.0, 0.0).astype(BF)
+    later = lane % WINDOW_SIDE >= (AREA - 1 - row) % WINDOW_SIDE
+    blank = jnp.zeros((AREA, SHEAR - AREA), FL)
 
     def fold(values):
         wide = jnp.concatenate([values, blank], 1)
         return jnp.sum(pltpu.roll(wide, 0, 1, stride=1, stride_axis=0), 0, keepdims=True)
 
-    def step(value, head):
-        total = None
-        for _ in range(3):
-            part = value.astype(BF)
-            value = value - part.astype(FL)
-            now = mm(turn, part)
-            total = now if total is None else total + now
-        out_ref[head, 0:1, :] = fold(jnp.where(later, total, 0.0))
-        out_ref[head, 1:2, :] = fold(jnp.where(later, 0.0, total))
-
-    for t, ref in enumerate(ins):
-        value = ref[...]
+    channels = out_ref.shape[1]
+    out_ref[...] = jnp.zeros_like(out_ref)
+    for t, ref in enumerate(dbias_refs):
+        values = ref[...]
         for k in range(TILE_HEADS):
-            step(value[:, k * area : (k + 1) * area], t * TILE_HEADS + k)
+            value = values[:, k * AREA : (k + 1) * AREA]
+            total = None
+            for _ in range(3):
+                part = value.astype(BF)
+                value = value - part.astype(FL)
+                now = mm(turn, part)
+                total = now if total is None else total + now
+            head = t * TILE_HEADS + k
+            out_ref[head : head + 1, :] = fold(jnp.where(later, total, 0.0))
+            at = HEAD_COUNT + head
+            out_ref[at : at + 1, :] = fold(jnp.where(later, 0.0, total))
+        lanes = slice(t * LANES, (t + 1) * LANES)
+        out_ref[ATTN_AT : ATTN_AT + 3, lanes] = sum(
+            attn_refs[m * tile_count + t][0:3, :] for m in range(micro_count)
+        )
+    out_ref[SETTLE_AT : SETTLE_AT + 3, :] = sum(ref[0:3, :] for ref in settle_refs)
+    merge = sum(ref[0:4, :] for ref in merge_refs)
+    for k, (at, half) in enumerate(((0, 0), (0, 1), (1, 0), (1, 1), (2, 0), (3, 0))):
+        out_ref[MERGE_AT + k : MERGE_AT + k + 1, :] = merge[
+            at : at + 1, half * channels : (half + 1) * channels
+        ]
+    experts, _, hidden = dpre_refs[0].shape
+    chunks = hidden // channels
+    for e in range(experts):
+        total = sum(ref[e] for ref in dpre_refs)
+        for c in range(chunks):
+            at = SUM_ROWS + e * chunks + c
+            out_ref[at : at + 1, :] = total[:, c * channels : (c + 1) * channels]
+        at = SUM_ROWS + experts * chunks + e
+        out_ref[at : at + 1, :] = dout_ref[e]
+
+
+def bias_network_back_body(sums_ref, first_ref, second_ref, dfirst_ref, dsecond_ref):
+    down, across, valid, hidden, slope, level = bias_network(first_ref, second_ref)
+    lines = jnp.concatenate(
+        [sums_ref[0:HEAD_COUNT, :], sums_ref[HEAD_COUNT : 2 * HEAD_COUNT, :]], 1
+    )
+    lines = jnp.concatenate([lines, jnp.zeros((LANES - HEAD_COUNT, 2 * SHEAR), FL)], 0)
+    grad = lines.T[:, 0:HEAD_COUNT]
+    grad = jnp.where(valid, grad * 16.0 * level * (1.0 - level), 0.0)
+    dsecond_ref[...] = lax.dot_general(
+        hidden,
+        grad,
+        (((0,), (0,)), ((), ())),
+        precision=PRECISION_HIGH,
+        preferred_element_type=FL,
+    )
+    dpre = slope * lax.dot_general(
+        grad,
+        second_ref[...],
+        (((1,), (1,)), ((), ())),
+        precision=PRECISION_HIGH,
+        preferred_element_type=FL,
+    )
+    dfirst_ref[0:1, :] = jnp.sum(down * dpre, 0, keepdims=True)
+    dfirst_ref[1:2, :] = jnp.sum(across * dpre, 0, keepdims=True)
+    dfirst_ref[2:3, :] = jnp.sum(dpre, 0, keepdims=True)
 
 
 def slot_body(
@@ -347,19 +390,28 @@
         seen_column = seen_column + jnp.sum(across, 1, keepdims=True)
 
 
-def slot_tables(chosen, my_place, experts, local, slots, capacity):
+def slot_tables(chosen, my_place, experts, local, slots, capacity, after):
     tokens = chosen.shape[1]
     vmem = pl.BlockSpec(memory_space=pltpu.VMEM)
     column = jax.ShapeDtypeStruct((tokens, 1), jnp.int32)
     return pl.pallas_call(
-        functools.partial(
-            slot_body, experts=experts, local=local, slots=slots, capacity=capacity
+        skipping(
+            functools.partial(
+                slot_body, experts=experts, local=local, slots=slots, capacity=capacity
+            ),
+            2,
+            1,
         ),
         name="slot_tables",
-        in_specs=[pl.BlockSpec(memory_space=pltpu.SMEM), vmem],
+        in_specs=[
+            pl.BlockSpec(memory_space=pltpu.SMEM),
+            vmem,
+            pl.BlockSpec(memory_space=pl.ANY),
+        ],
         out_specs=[vmem] * 3,
         out_shape=[column, column, jax.ShapeDtypeStruct((1, tokens), jnp.int32)],
-    )(my_place, chosen)
+        cost_estimate=cost(3),
+    )(my_place, chosen, after)
 
 
 def attend_forward_body(
@@ -1113,14 +1165,32 @@
 
 
 def add_halves_body(own_ref, got_ref, out_ref):
-    out_ref[...] = plus(own_ref[...], got_ref[...]).astype(BF)
-
-
-def add_halves(own, got, after):
+    out_ref[...] = plus(own_ref[...], got_ref[...]).astype(out_ref.dtype)
+
+
+def add_halves(own, got, after, dtype=BF, micros=2):
     (total,) = call_kernel(
-        add_halves_body, "add_halves", [(own.shape, BF)], [own, got], micros=2, after=after
+        add_halves_body, "add_halves", [(own.shape, dtype)], [own, got], micros=micros, after=after
     )
     return total
+
+
+def add_blocks_body(*refs):
+    (*block_refs, mine_ref, other_ref) = refs
+    for half, ref in enumerate((mine_ref, other_ref)):
+        ref[...] = sum(block[half].astype(FL) for block in block_refs).astype(ref.dtype)
+
+
+def add_blocks(blocks, after):
+    shape = blocks[0].shape[1:]
+    return call_kernel(
+        add_blocks_body,
+        "add_blocks",
+        [(shape, FL), (shape, BF)],
+        blocks,
+        micros=0.2,
+        after=after,
+    )
 
 
 def place_body(me_ref, *refs, chunks, first):
@@ -1178,10 +1248,47 @@
     return held
 
 
+def join_body(me_ref, *refs, count):
+    part_refs, out_refs = taken(refs, count)
+    width = part_refs[0].shape[1]
+    for c in range(count):
+        spot = spot_of(c, me_ref[0], count.bit_length() - 1)
+        value = part_refs[0][...]
+        for k in range(1, count):
+            value = jnp.where(spot == k, part_refs[k][...], value)
+        start = 0
+        for ref in out_refs:
+            low, high = max(start, c * width), min(start + ref.shape[1], (c + 1) * width)
+            if low < high:
+                ref[:, low - start : high - start] = value[:, low - c * width : high - c * width]
+            start += ref.shape[1]
+
+
+def join_columns(me, parts, widths):
+    rows = parts[0].shape[0]
+    vmem = pl.BlockSpec(memory_space=pltpu.VMEM)
+    return pl.pallas_call(
+        functools.partial(join_body, count=len(parts)),
+        name="join_columns",
+        in_specs=[pl.BlockSpec(memory_space=pltpu.SMEM)] + [vmem] * len(parts),
+        out_specs=[vmem] * len(widths),
+        out_shape=[jax.ShapeDtypeStruct((rows, width), BF) for width in widths],
+        cost_estimate=cost(2),
+    )(me, *parts)
+
+
 def gathered(shard):
     count = lax.axis_size("dp")
     copies = jnp.broadcast_to(shard[None], (count,) + shard.shape)
     return swapped(copies).reshape(count * shard.shape[0], shard.shape[1])
+
+
+def side_by_side_body(*refs):
+    (*ins, out_ref) = refs
+    start = 0
+    for ref in ins:
+        out_ref[:, start : start + ref.shape[1]] = ref[...]
+        start += ref.shape[1]
 
 
 def copy_body(in_ref, out_ref):
@@ -1209,24 +1316,33 @@
     return array
 
 
-def dense_sum(grad):
+def dense_blocks(grad):
     count = lax.axis_size("dp")
     half = count // 2
     place = lax.axis_index("dp")
     rows = grad.shape[0] // count
     grad = grad.reshape(2, half, rows, grad.shape[1])
+    mine, other = place // half, 1 - place // half
     blocks = [
-        lax.dynamic_index_in_dim(grad, (place % half) ^ k, 1, keepdims=False) for k in range(half)
+        jnp.concatenate(
+            [
+                lax.dynamic_slice(
+                    grad, (h, (place % half) ^ k, 0, 0), (1, 1, rows, grad.shape[3])
+                )[0]
+                for h in (mine, other)
+            ]
+        )
+        for k in range(half)
     ]
-    part = sum(block.astype(FL) for block in exchanged(blocks))
-    mine = lax.dynamic_index_in_dim(part, place // half, 0, keepdims=False)
-    other = lax.dynamic_index_in_dim(part, 1 - place // half, 0, keepdims=False).astype(BF)
-    part = plus(mine, crossed(other, "dp", half)).astype(BF)
+    return exchanged(blocks)
+
+
+def dense_spread(part):
     held = spread_over_row(part)
     sums = held
     while len(sums) > 1:
         sums = [plus(left, right) for left, right in zip(sums[::2], sums[1::2])]
-    return sums[0].astype(FL), [other, part, held[-1]]
+    return sums[0].astype(FL), held
 
 
 def on_device(
@@ -1277,34 +1393,23 @@
     total_rows = band_rows * lax.axis_size("row")
     row_start = band_rows * lax.axis_index("row")
 
-    dense = gathered(
-        jnp.concatenate(
-            [
-                query_key_value_weight,
-                output_projection_weight,
-                jnp.pad(routing_weight, ((0, 0), (0, LANES - experts))),
-            ],
-            1,
-        )
-    )
-    weight_qkv = dense[:, : 3 * channels]
-    weight_proj = dense[:, 3 * channels : 4 * channels]
-    weight_router = dense[:, 4 * channels :]
+    wide = 4 * channels + LANES
+    shard = jnp.concatenate(
+        [query_key_value_weight, output_projection_weight, routing_weight], 1
+    )
+    parts = -(-wide // (8 * LANES)) * 8 * LANES
+    shard = jnp.pad(shard, ((0, 0), (0, parts - shard.shape[1])))
+    parts //= row_size
+    shard = lax.dynamic_slice(shard, (0, me[0] * parts), (shard.shape[0], parts))
+    columns = gathered(shard)
+    held = spread_over_row(columns)
+    weight_qkv, weight_proj, weight_router = join_columns(
+        me, held, [3 * channels, channels, LANES]
+    )
 
     bands = patches.reshape(micro_count, tokens, channels)
     below = passed_along(bands[:, :half], "row", -1)
 
-    table, table_back = jax.vjp(
-        position_table,
-        bias_network_first_weight,
-        bias_network_first_bias,
-        bias_network_second_weight,
-    )
-    tile_count = channels // LANES
-    bias_shape = ((tile_count, win_area, TILE_HEADS * win_area), FL)
-    bias_rows, bias_keys = call_kernel(
-        spread_body, "spread_bias", [bias_shape, bias_shape], [toeplitz_lines(table)]
-    )
     zones = [
         mask_operands(
             row_start,
@@ -1320,12 +1425,20 @@
     for m in micros:
         chosen = patch_expert_index[m].reshape(1, tokens)
         column, dest_col, dest_row = slot_tables(
-            chosen, my_place, experts, local, slots, capacity
+            chosen, my_place, experts, local, slots, capacity, columns
         )
         chosen_cols.append(column)
         dest_cols.append(dest_col)
         dest_rows.append(dest_row)
 
+    network_first = jnp.concatenate(
+        [bias_network_first_weight, bias_network_first_bias[None]], 0
+    )
+    tile_count = channels // LANES
+    bias_shape = ((tile_count, win_area, TILE_HEADS * win_area), FL)
+    bias_rows, bias_keys = call_kernel(
+        spread_body, "spread_bias", [bias_shape, bias_shape], [network_first, bias_network_second_weight], after=[held[1], dest_rows[-1]]
+    )
     hidden = expert_first_weight.shape[-1]
     chunks = hidden // PIECE
     subs = local * chunks // row_size
@@ -1371,7 +1484,7 @@
     expert_back, back_sent, settled, finished = list(none), list(none), list(none), list(none)
     outputs, input_grads, input_parts = list(none), list(none), list(none)
 
-    forward_after = [[first_got], []]
+    forward_after = [[first_got, *dest_rows], []]
     route_after = [[second_got, first_other[1]], []]
     for m in micros:
         attended[m] = call_kernel(
@@ -1424,7 +1537,8 @@
             ],
             micros=12,
             after=[attended[-1][0] if m == 0 else routed[m - 1][2]]
-            + (route_after[m] if m < 2 else []),
+            + (route_after[m] if m < 2 else [])
+            + (received[m - 1][1:] if m else []),
         )
         if m == 0:
             shard = held_back(patch_merging_weight, [routed[m][2]])
@@ -1520,19 +1634,20 @@
             after=after,
         )
 
-    grad_merge = merge_weight_grad(
-        [b[1] for b in merged], [b[2] for b in merged], channels, [expert_back[-1][2]]
-    )
-    sum_merge, merge_steps = dense_sum(grad_merge)
-    settled[0] = settle(0, [grad_merge])
+    settled[0] = settle(0, [expert_back[-1][2]])
     in_keep, in_send, _ = expert_weight_grads(
         me, received, [b[1] for b in expert_back], local, row_size, True, [settled[0][3]]
     )
     for m in micros[1:]:
         settled[m] = settle(m, [in_keep])
+    grad_merge = merge_weight_grad(
+        [b[1] for b in merged], [b[2] for b in merged], channels, [settled[-1][3]]
+    )
     out_keep, out_send, grad_eout_bias = expert_weight_grads(
-        me, back_res, [b[1] for b in expert_out], local, row_size, False, [settled[-1][3]]
-    )
+        me, back_res, [b[1] for b in expert_out], local, row_size, False, [grad_merge]
+    )
+
+    merge_blocks = dense_blocks(grad_merge)
 
     state = dict(
         first=dict(keep=in_keep, send=in_send), second=dict(keep=out_keep, send=out_send)
@@ -1567,14 +1682,23 @@
         "start": ["first"],
         (0, 1): ["first", "second"],
         (1, 0): ["first", "second"],
-        "end": ["second"],
     }
     for _ in range(len(row_bits) - 2):
         plan[(0, 1)] = plan[(0, 1)] + ["first", "second"]
 
     def advance_at(place):
+        nonlocal latest, merge_sums, sum_merge
+        if place == (0, 0):
+            merge_sums = add_blocks(merge_blocks, [latest])
+            latest = merge_sums[0]
+        elif place == (0, tile_count - 1):
+            mine, other = merge_sums
+            latest = add_halves(mine, crossed(other, "dp", members), [latest])
+            sum_merge, _ = dense_spread(latest)
         for kind in plan.get(place, ()):
             advance(kind)
+
+    merge_sums = sum_merge = None
 
     advance_at("start")
     dense_args = []
@@ -1586,13 +1710,12 @@
         [((channels, channels), BF), ((channels, LANES), BF)],
         dense_args,
         micros=4,
-        after=[latest, merge_steps[0]],
+        after=[latest],
     )
     latest = grad_router
 
-    tile_after = {(0, 1): merge_steps[1:2], (1, 0): merge_steps[2:]}
     tile_sums = [None] * tile_count
-    tile_smalls = [None] * tile_count
+    tile_smalls = []
     weight_grads = [grad_proj, grad_router]
     for m in micros:
         lifted = passed_along(settled[m][2][:half], "row", -1)
@@ -1643,30 +1766,45 @@
                     ((8, LANES), FL),
                 ],
                 args,
-                micros=10,
-                after=[latest] + tile_after.get((m, t), []),
+                micros=0.5 if last and t else 10,
+                after=[latest],
             )
             latest = small
             tile_sums[t] = [dweight, dbias]
-            tile_smalls[t] = small if m == 0 else tile_smalls[t] + small
+            tile_smalls.append(small)
             grads.append(dqkv)
             if last:
                 weight_grads.append(dweight)
-                if t == tile_count - 2:
-                    sum_first, _ = dense_sum(jnp.concatenate(weight_grads, 1))
-                if t == tile_count - 1:
-                    sum_last, last_steps = dense_sum(dweight)
             advance_at((m, t))
         if last:
-            (lines,) = call_kernel(
-                fold_body,
+            tall = SUM_ROWS + 2 * local * (hidden // channels + 1)
+            (sums,) = call_kernel(
+                functools.partial(
+                    fold_body, tile_count=tile_count, micro_count=micro_count
+                ),
                 "fold_bias",
-                [((HEAD_COUNT, 8, SHEAR), FL)],
-                [sums[1] for sums in tile_sums],
+                [((-(-tall // 8) * 8, channels), FL)],
+                [sums[1] for sums in tile_sums]
+                + tile_smalls
+                + [part[3] for part in settled]
+                + [part[5] for part in merged]
+                + [part[2] for part in expert_back]
+                + [grad_eout_bias],
                 micros=3,
+                after=[latest, state["second"]["got"]],
+            )
+            latest = sums
+            advance("second")
+            (joined_grads,) = call_kernel(
+                side_by_side_body,
+                "join_grads",
+                [((channels, sum(w.shape[1] for w in weight_grads)), BF)],
+                weight_grads,
+                micros=2,
                 after=[latest],
             )
-            latest = lines
+            latest = joined_grads
+            dense = dense_blocks(joined_grads)
         input_parts[m] = call_kernel(
             functools.partial(input_grad_body, band_cols=band_cols, channels=channels),
             "input_grad",
@@ -1683,51 +1821,53 @@
             .astype(BF)
             .reshape(band_rows, band_cols, channels)
         )
-    advance_at("end")
-    sum_ein = place_pieces(me, state["first"]["held"], local, hidden, True, [latest])
-    sum_eout = place_pieces(me, state["second"]["held"], local, hidden, False, [])
-    sum_proj = sum_first[:, :channels]
-    sum_router = sum_first[:, channels : channels + experts]
-    sum_qkv = jnp.concatenate([sum_first[:, channels + LANES :], sum_last], 1)
-    sum_qkv = sum_qkv.reshape(-1, tile_count, 3, LANES).swapaxes(1, 2).reshape(-1, 3 * channels)
-
-    settle_sums = sum(s[3] for s in settled)
-    merge_sums = sum(b[5] for b in merged)
-    dtable = table_of_lines(lines)
-    attn_sums = jnp.concatenate(tile_smalls, 1)[:3]
-    parts = [
-        dtable,
-        attn_sums,
-        settle_sums[:3],
-        merge_sums[:2],
-        merge_sums[2:4, :channels],
-    ]
-    bias_parts = [sum(b[2] for b in expert_back), grad_eout_bias]
-    flat = jnp.concatenate([part.reshape(-1) for part in parts])
-    flat = jnp.pad(flat, (0, -flat.size % 1024)).reshape(-1, 1024)
-    biases = jnp.concatenate([part.reshape(-1) for part in bias_parts])
-    biases = jnp.pad(biases, (0, -biases.size % 1024)).reshape(-1, 1024)
-    both = summed(jnp.concatenate([flat, biases], 0), ("row",))
-    flat, biases = summed(both[: flat.shape[0]], ("dp",)).reshape(-1), both[flat.shape[0] :]
-    found, at = [], 0
-    for part in parts:
-        found.append(flat[at : at + part.size].reshape(part.shape))
-        at += part.size
-    dtable, attn_sums, settle_sums, merge_sums, moe_sums = found
-    biases = biases.reshape(-1)
-    in_bias = biases[: 2 * local * hidden].reshape(2 * local, hidden)
-    out_bias = biases[2 * local * hidden : 2 * local * (hidden + channels)]
-    out_bias = out_bias.reshape(2 * local, channels)
+    steps = [("row", 1 << k) for k in range(row_size.bit_length() - 1)]
+    steps += [("dp", 1 << k) for k in range(dp_size.bit_length() - 1)]
+    tail = ["blocks", "first", "part"]
+    for k, (axis, bit) in enumerate(steps):
+        if axis == "dp" and steps[k - 1][0] == "row":
+            sums, biases = sums[:SUM_ROWS], sums[SUM_ROWS:tall]
+        sums = latest = add_halves(sums, crossed(sums, axis, bit), [latest], FL, 0.2)
+        job = tail.pop(0) if tail else None
+        if job == "blocks":
+            mine, other = add_blocks(dense, [latest])
+            latest = mine
+        elif job == "first":
+            latest = sum_ein = place_pieces(
+                me, state["first"]["held"], local, hidden, True, [latest]
+            )
+        elif job == "part":
+            latest = part = add_halves(mine, crossed(other, "dp", members), [latest], BF, 0.2)
+    sum_dense, held = dense_spread(part)
+    sum_eout = place_pieces(me, state["second"]["held"], local, hidden, False, [latest])
+    sum_proj = sum_dense[:, :channels]
+    sum_router = sum_dense[:, channels : channels + experts]
+    sum_qkv = sum_dense[:, channels + LANES :].reshape(-1, tile_count, 3, LANES)
+    sum_qkv = sum_qkv.swapaxes(1, 2).reshape(-1, 3 * channels)
+    in_bias = biases[: 2 * local * chunks].reshape(2 * local, hidden)
+    out_bias = biases[2 * local * chunks :]
     other_bias = crossed(
         jnp.concatenate([in_bias[local:], out_bias[local:]], 1), "dp", members
     )
     sum_ein_bias = in_bias[:local] + other_bias[:, :hidden]
     sum_eout_bias = out_bias[:local] + other_bias[:, hidden:]
-    grad_first, grad_first_bias, grad_second = table_back(dtable)
-    sum_qbias, sum_vbias, sum_scale = attn_sums[0], attn_sums[1], attn_sums[2, ::HEAD_DIM]
-    sum_proj_bias, sum_again, sum_ashift = settle_sums[0], settle_sums[1], settle_sums[2]
-    sum_rgain, sum_rshift = merge_sums[0], merge_sums[1]
-    sum_mgain, sum_mshift = moe_sums[0], moe_sums[1]
+    grad_first, grad_second = call_kernel(
+        bias_network_back_body,
+        "bias_network_back",
+        [(network_first.shape, FL), (bias_network_second_weight.shape, FL)],
+        [sums, network_first, bias_network_second_weight],
+        micros=0.2,
+    )
+    grad_first, grad_first_bias = grad_first[:2], grad_first[2]
+    sum_qbias, sum_vbias, sum_scale = (
+        sums[ATTN_AT],
+        sums[ATTN_AT + 1],
+        sums[ATTN_AT + 2, ::HEAD_DIM],
+    )
+    sum_proj_bias, sum_again, sum_ashift = (sums[SETTLE_AT + k] for k in range(3))
+    sum_rgain = sums[MERGE_AT : MERGE_AT + 2].reshape(2 * channels)
+    sum_rshift = sums[MERGE_AT + 2 : MERGE_AT + 4].reshape(2 * channels)
+    sum_mgain, sum_mshift = sums[MERGE_AT + 4], sums[MERGE_AT + 5]
     return (
         jnp.stack(outputs)[:, None],
         jnp.stack(input_grads)[:, None],

time: 588 us -> 532 us (0.905)
  waiting for transfers between devices: 103 us -> 76.6 us
  local copies, waits for them, and re-layouts: 65.3 us -> 44.2 us
  Pallas kernels: 281 us -> 295 us
  matrix products: 13.4 us -> 0 us
  other arithmetic: 23.7 us -> 16.3 us
    ppermute x72 -> x68, waiting for transfers between devices: 95 us -> 42.9 us  [crossed(): return lax.ppermute(array, axis, [(i, i ^ bit) for i in range(count)])]
    all_to_all x1, waiting for transfers between devices: 0.01 us -> 16.1 us  [swapped(): return lax.all_to_all(rows, 'dp', split_axis=0, concat_axis=0, tiled=True)]
    dot_general x5 -> x0, matrix products: 13.4 us -> none  [the longest x3 9.35 us: position_table(): jnp.einsum('qvw,wk->qvk', hidden_activation, bias_network_second_weight,...]
    pallas_call x29 -> x40, Pallas kernels: 173 us -> 185 us  [call_kernel(): pl.pallas_call(skipping(body, len(args), len(after)), name=name, grid=(1,...]
    ppermute x7, waiting for transfers between devices: 7.55 us -> 17.6 us  [passed_along(): lax.ppermute(array, axis, [(i, (i + by) % count) for i in range(count)])]
    unnamed x243 -> x247, local copies, waits for them, and re-layouts: 29.4 us -> 23.7 us
    ppermute x72 -> x68, starting transfers between devices: 70.9 us -> 69.3 us  [crossed(): return lax.ppermute(array, axis, [(i, i ^ bit) for i in range(count)])]
  transfers between devices with their start and end apart: 81 -> 77, of which waited for: 16 -> 17; matrix products, arithmetic and copies ran while one was open for 12% -> 7% of each run, Pallas kernels for 46% -> 54%
where the time goes in v3:
time: 532 us; the launch traced here: 527 us
  Pallas kernels  295 us (55%)
  starting transfers between devices  78.8 us (15%)
  waiting for transfers between devices  76.6 us (14%)
  local copies, waits for them, and re-layouts  44.2 us (8%)
  other arithmetic  16.3 us (3%)
  between operations  16.1 us (3%)
    pallas_call x40, Pallas kernels, call_kernel(): pl.pallas_call(skipping(body, len(args), len(after)), name=name, grid=(1,...  185 us
    pallas_call x8, Pallas kernels, call_expert(): pl.pallas_call(skipping(body, 1 + len(args), len(after)), name=name, grid...  95.9 us
    ppermute x68, starting transfers between devices, crossed(): return lax.ppermute(array, axis, [(i, i ^ bit) for i in range(count)])  69.3 us
    ppermute x68, waiting for transfers between devices, crossed(): return lax.ppermute(array, axis, [(i, i ^ bit) for i in range(count)])  42.9 us
    unnamed x247, local copies, waits for them, and re-layouts  23.7 us
    ppermute x7, waiting for transfers between devices, passed_along(): lax.ppermute(array, axis, [(i, (i + by) % count) for i in range(count)])  17.6 us
    all_to_all x1, waiting for transfers between devices, swapped(): return lax.all_to_all(rows, 'dp', split_axis=0, concat_axis=0, tiled=True)  16.1 us
  transfers between devices with their start and end apart: 77, of which 17 were waited for; matrix products, arithmetic and copies ran while one was open for 7% of the time, Pallas kernels for 54%

profile of v3, /device:TPU:0, one launch (start us, length us, event | category | flops | bytes accessed | tf_op | source)
XLA Modules:
  0.0 527.5 jit_solution(5358032367905402415)
XLA Ops:
  32.2 16.1 %all-to-all-done = bf16[8,48,512]{2,1,0:T(8,128)(2,1)} async-done(((bf16[8,48,512]{2,1,0:T(8,128)(2,1)}), bf16[8,48,512]{2,1,0:T(8,128)(2,1)}, u32[]{:S(2)}, u32[]{:S(2)}) %all-to-all-start) | async-done | bytes 393248 | tf_op jit(solution)/shard_map/all_to_all | solution.py:1233
  62.9 6.7 %spread_bias.1 = (f32[3,144,576]{2,1,0:T(8,128)S(1)}, f32[3,144,576]{2,1,0:T(8,128)}) custom-call(f32[3,512]{1,0:T(4,128)S(1)} %pad_maximum_fusion.11.refs_0_.refs_1_, f32[512,12]{1,0:T(8,128)S(1)} %copy.65.refs_1_.refs_2_, bf16[384,512]{1,0:T(8,128)(2,1)} %collective-permute-done.1.refs_1_.refs_2_, s32[1,1152]{1,0:T(1,128)S(1)} %copy-done.75), custom_call_target="tpu_custom_call" | custom-call | flops 2200000000 | bytes 100000 | tf_op jit(solution)/shard_map/spread_bias/pallas_call | solution.py:157
  73.9 13.0 %attend_forward.2 = (bf16[576,384]{1,0:T(8,128)(2,1)S(1)}, bf16[576,384]{1,0:T(8,128)(2,1)S(1)}, bf16[1152,384]{1,0:T(8,128)(2,1)}, bf16[1152,1152]{1,0:T(8,128)(2,1)}, f32[1152,768]{1,0:T(8,128)}) custom-call(bf16[1152,384]{1,0:T(8,128)(2,1)} %bitcast.86, bf16[576,384]{1,0:T(8,128)(2,1)} %get-tuple-element.407.refs_1_, ...), custom_call_target="tpu_custom_call" | custom-call | flops 7040000000 | bytes 100000 | tf_op jit(solution)/shard_map/attend_forward/pallas_call | solution.py:157
  88.2 13.3 %attend_forward.3 = (bf16[576,384]{1,0:T(8,128)(2,1)S(1)}, bf16[576,384]{1,0:T(8,128)(2,1)S(1)}, bf16[1152,384]{1,0:T(8,128)(2,1)}, bf16[1152,1152]{1,0:T(8,128)(2,1)}, f32[1152,768]{1,0:T(8,128)}) custom-call(bf16[1152,384]{1,0:T(8,128)(2,1)} %bitcast.84, bf16[576,384]{1,0:T(8,128)(2,1)} %get-tuple-element.408.refs_1_, ...), custom_call_target="tpu_custom_call" | custom-call | flops 7040000000 | bytes 100000 | tf_op jit(solution)/shard_map/attend_forward/pallas_call | solution.py:157
  103.1 5.3 route.2
  122.8 9.0 %collective-permute-done.14.refs_14_.refs_13_ = bf16[2,384,384]{2,1,0:T(8,128)(2,1)S(1)} collective-permute-done((bf16[2,384,384]{2,1,0:T(8,128)(2,1)}, bf16[2,384,384]{2,1,0:T(8,128)(2,1)S(1)}, u32[]{:S(2)}, u32[]{:S(2)}) %collective-permute-start.14) | collective-permute-done | bytes 589856 | tf_op jit(solution)/shard_map/ppermute | solution.py:1307
  131.8 4.6 collective-permute-done.17.refs_0_.refs_5_
  139.5 4.9 collective-permute-done.9.refs_10_.refs_3_
  146.1 5.3 route.3
  156.2 19.7 %expert_forward.2 = (bf16[384,384]{1,0:T(8,128)(2,1)S(1)}, bf16[384,384]{1,0:T(8,128)(2,1)S(1)}, bf16[384,384]{1,0:T(8,128)(2,1)S(1)}, bf16[384,384]{1,0:T(8,128...) custom-call(s32[1]{0:T(128)} %bitcast.me_ref.refs_0_, bf16[384,384]{1,0:T(8,128)(2,1)S(1)} %copy-done.59, ...), custom_call_target="tpu_custom_call" | custom-call | flops 8360000000 | bytes 100000 | tf_op jit(solution)/shard_map/expert_forward/pallas_call | solution.py:978
  181.5 19.8 %expert_forward.3 = (bf16[384,384]{1,0:T(8,128)(2,1)S(1)}, bf16[384,384]{1,0:T(8,128)(2,1)}, bf16[384,384]{1,0:T(8,128)(2,1)}, bf16[384,384]{1,0:T(8,128)(2,1)S(...) custom-call(s32[1]{0:T(128)} %bitcast.me_ref.refs_0_, ...), custom_call_target="tpu_custom_call" | custom-call | flops 8360000000 | bytes 100000 | tf_op jit(solution)/shard_map/expert_forward/pallas_call | solution.py:978
  207.2 12.5 %merge.2 = (bf16[288,768]{1,0:T(8,128)(2,1)}, bf16[288,1536]{1,0:T(8,128)(2,1)}, bf16[288,768]{1,0:T(8,128)(2,1)}, f32[1152,384]{1,0:T(8,128)}, bf16[1152,128]{1...) custom-call(bf16[384,384]{1,0:T(8,128)(2,1)S(1)} %copy-done.74, ...), custom_call_target="tpu_custom_call" | custom-call | flops 6160000000 | bytes 100000 | tf_op jit(solution)/shard_map/merge/pallas_call | solution.py:157
  223.3 12.9 %merge.3 = (bf16[288,768]{1,0:T(8,128)(2,1)}, bf16[288,1536]{1,0:T(8,128)(2,1)}, bf16[288,768]{1,0:T(8,128)(2,1)}, f32[1152,384]{1,0:T(8,128)}, bf16[1152,128]{1...) custom-call(bf16[384,384]{1,0:T(8,128)(2,1)S(1)} %copy-done.72, ...), custom_call_target="tpu_custom_call" | custom-call | flops 6160000000 | bytes 100000 | tf_op jit(solution)/shard_map/merge/pallas_call | solution.py:157
  241.2 11.5 %expert_backward.2 = (bf16[384,384]{1,0:T(8,128)(2,1)S(1)}, bf16[384,384]{1,0:T(8,128)(2,1)S(1)}, bf16[384,384]{1,0:T(8,128)(2,1)S(1)}, bf16[384,384]{1,0:T(8,12...) custom-call(s32[1]{0:T(128)} %bitcast.me_ref.refs_0_, ...), custom_call_target="tpu_custom_call" | custom-call | flops 5280000000 | bytes 100000 | tf_op jit(solution)/shard_map/expert_backward/pallas_call | solution.py:978
  257.1 11.7 %expert_backward.3 = (bf16[384,384]{1,0:T(8,128)(2,1)S(1)}, bf16[384,384]{1,0:T(8,128)(2,1)}, bf16[384,384]{1,0:T(8,128)(2,1)}, bf16[384,384]{1,0:T(8,128)(2,1)}...) custom-call(s32[1]{0:T(128)} %bitcast.me_ref.refs_0_, ...), custom_call_target="tpu_custom_call" | custom-call | flops 5280000000 | bytes 100000 | tf_op jit(solution)/shard_map/expert_backward/pallas_call | solution.py:978
  273.1 7.7 %settle.2 = (f32[1152,384]{1,0:T(8,128)}, bf16[1152,384]{1,0:T(8,128)(2,1)}, bf16[1152,384]{1,0:T(8,128)(2,1)}, f32[8,384]{1,0:T(8,128)S(1)}) custom-call(bf16[384,384]{1,0:T(8,128)(2,1)S(1)} %get-tuple-element.202.refs_0_, bf16[384,384]{1,0:T(8,128)(2,1)S(1)} %collective-permute-done.30.refs_1_, bf16[384,384]{1,0:T(8,128)(2,1)S(1)} %collective-permute-done.31.refs_2_, ...), custom_call_target="tpu_custom_call" | custom-call | flops 3080000000 | bytes 100000 | tf_op jit(solution)/shard_map/settle/pallas_call | solution.py:157
  280.8 12.9 %expert_weight_grads.2 = (bf16[2,2,2,384,384]{4,3,2,1,0:T(8,128)(2,1)}, bf16[2,2,2,384,384]{4,3,2,1,0:T(8,128)(2,1)}, f32[4,1,384]{2,1,0:T(1,128)}) custom-call(s32[1]{0:T(128)} %bitcast.me_ref.refs_0_, bf16[384,384]{1,0:T(8,128)(2,1)S(1)} %copy-done.60, bf16[384,384]{1,0:T(8,128)(2,1)S(1)} %copy-done.24, bf16[384,384]{1,0:T(8,128)(2,1)S(1)} %copy-done.26, ...), custom_call_target="tpu_custom_call" | custom-call | flops 5720000000 | bytes 100000 | tf_op jit(solution)/shard_map/expert_weight_grads/pallas_call | solution.py:978
  296.1 7.8 %settle.3 = (f32[1152,384]{1,0:T(8,128)}, bf16[1152,384]{1,0:T(8,128)(2,1)}, bf16[1152,384]{1,0:T(8,128)(2,1)}, f32[8,384]{1,0:T(8,128)S(1)}) custom-call(bf16[384,384]{1,0:T(8,128)(2,1)S(1)} %copy-done.52, bf16[384,384]{1,0:T(8,128)(2,1)} %collective-permute-done.37.refs_1_, bf16[384,384]{1,0:T(8,128)(2,1)} %collective-permute-done.38.refs_2_, ...), custom_call_target="tpu_custom_call" | custom-call | flops 3080000000 | bytes 100000 | tf_op jit(solution)/shard_map/settle/pallas_call | solution.py:157
  303.9 5.6 %merge_weight_grad.1.refs_11_ = bf16[1536,768]{1,0:T(8,128)(2,1)} custom-call(bf16[288,1536]{1,0:T(8,128)(2,1)S(1)} %copy-done.47, bf16[288,768]{1,0:T(8,128)(2,1)S(1)} %copy-done.48, bf16[288,1536]{1,0:T(8,128)(2,1)} %get-tuple-element.238.refs_2_, bf16[288,768]{1,0:T(8,128)(2,1)S(1)} %copy-done.49, f32[8,384]{1,0:T(8,128)S(1)} %get-tuple-element.240.refs_4_.refs_10_), custom_call_target="tpu_custom_call" | custom-call | flops 2200000000 | bytes 100000 | tf_op jit(solution)/shard_map/merge_weight_grad/pallas_call | solution.py:861
  309.5 13.3 %expert_weight_grads.3 = (bf16[2,2,2,384,384]{4,3,2,1,0:T(8,128)(2,1)}, bf16[2,2,2,384,384]{4,3,2,1,0:T(8,128)(2,1)}, f32[4,1,384]{2,1,0:T(1,128)S(1)}) custom-call(s32[1]{0:T(128)} %bitcast.me_ref.refs_0_, bf16[384,384]{1,0:T(8,128)(2,1)S(1)} %copy-done.54, bf16[384,384]{1,0:T(8,128)(2,1)S(1)} %copy-done.28, bf16[384,384]{1,0:T(8,128)(2,1)S(1)} %copy-done.30, ...), custom_call_target="tpu_custom_call" | custom-call | flops 5720000000 | bytes 100000 | tf_op jit(solution)/shard_map/expert_weight_grads/pallas_call | solution.py:978
  340.8 9.1 %attend_backward.6 = (bf16[1152,384]{1,0:T(8,128)(2,1)}, f32[384,384]{1,0:T(8,128)S(1)}, f32[144,576]{1,0:T(8,128)S(1)}, f32[8,128]{1,0:T(8,128)S(1)}) custom-call(bf16[1152,384]{1,0:T(8,128)(2,1)} %copy-done, bf16[1152,1152]{1,0:T(8,128)(2,1)} %get-tuple-element.244.refs_1_.refs_2_.refs_3_, bf16[1152,1152]{1,0:T(8,128)(2,1)} %get-tuple-element.244.refs_1_.refs_2_.refs_3_, ...), custom_call_target="tpu_custom_call" | custom-call | flops 4400000000 | bytes 100000 | tf_op jit(solution)/shard_map/attend_backward/pallas_call | solution.py:157
  359.0 9.2 %attend_backward.7 = (bf16[1152,384]{1,0:T(8,128)(2,1)}, f32[384,384]{1,0:T(8,128)S(1)}, f32[144,576]{1,0:T(8,128)S(1)}, f32[8,128]{1,0:T(8,128)S(1)}) custom-call(bf16[1152,384]{1,0:T(8,128)(2,1)} %copy-done, bf16[1152,1152]{1,0:T(8,128)(2,1)} %get-tuple-element.244.refs_1_.refs_2_.refs_3_, bf16[1152,1152]{1,0:T(8,128)(2,1)} %get-tuple-element.244.refs_1_.refs_2_.refs_3_, ...), custom_call_target="tpu_custom_call" | custom-call | flops 4400000000 | bytes 100000 | tf_op jit(solution)/shard_map/attend_backward/pallas_call | solution.py:157
  376.5 9.1 %attend_backward.8 = (bf16[1152,384]{1,0:T(8,128)(2,1)}, f32[384,384]{1,0:T(8,128)S(1)}, f32[144,576]{1,0:T(8,128)S(1)}, f32[8,128]{1,0:T(8,128)S(1)}) custom-call(bf16[1152,384]{1,0:T(8,128)(2,1)} %copy-done, bf16[1152,1152]{1,0:T(8,128)(2,1)} %get-tuple-element.244.refs_1_.refs_2_.refs_3_, bf16[1152,1152]{1,0:T(8,128)(2,1)} %get-tuple-element.244.refs_1_.refs_2_.refs_3_, ...), custom_call_target="tpu_custom_call" | custom-call | flops 4400000000 | bytes 100000 | tf_op jit(solution)/shard_map/attend_backward/pallas_call | solution.py:157
  393.0 9.4 %attend_backward.9 = (bf16[1152,384]{1,0:T(8,128)(2,1)}, bf16[384,384]{1,0:T(8,128)(2,1)S(1)}, f32[144,576]{1,0:T(8,128)S(1)}, f32[8,128]{1,0:T(8,128)S(1)}) custom-call(bf16[1152,384]{1,0:T(8,128)(2,1)} %window_grads.3.refs_0_.refs_15_, bf16[1152,1152]{1,0:T(8,128)(2,1)} %get-tuple-element.264.refs_1_.refs_2_.refs_3_, ...), custom_call_target="tpu_custom_call" | custom-call | flops 4400000000 | bytes 100000 | tf_op jit(solution)/shard_map/attend_backward/pallas_call | solution.py:157
  402.4 8.1 %collective-permute-done.72 = bf16[192,768]{1,0:T(8,128)(2,1)S(1)} collective-permute-done((bf16[192,768]{1,0:T(8,128)(2,1)S(1)}, bf16[192,768]{1,0:T(8,128)(2,1)S(1)}, u32[]{:S(2)}, u32[]{:S(2)}) %collective-permute-start.72) | collective-permute-done | bytes 294944 | tf_op jit(solution)/shard_map/ppermute | solution.py:1307
  424.4 9.3 %attend_backward.10 = (bf16[1152,384]{1,0:T(8,128)(2,1)}, bf16[384,384]{1,0:T(8,128)(2,1)S(1)}, f32[144,576]{1,0:T(8,128)S(1)}, f32[8,128]{1,0:T(8,128)S(1)}) custom-call(bf16[1152,384]{1,0:T(8,128)(2,1)} %window_grads.3.refs_0_.refs_15_, bf16[1152,1152]{1,0:T(8,128)(2,1)} %get-tuple-element.264.refs_1_.refs_2_.refs_3_, ...), custom_call_target="tpu_custom_call" | custom-call | flops 220000000 | bytes 100000 | tf_op jit(solution)/shard_map/attend_backward/pallas_call | solution.py:157
  433.7 9.3 %attend_backward.11 = (bf16[1152,384]{1,0:T(8,128)(2,1)}, bf16[384,384]{1,0:T(8,128)(2,1)S(1)}, f32[144,576]{1,0:T(8,128)S(1)}, f32[8,128]{1,0:T(8,128)S(1)}) custom-call(bf16[1152,384]{1,0:T(8,128)(2,1)} %window_grads.3.refs_0_.refs_15_, bf16[1152,1152]{1,0:T(8,128)(2,1)} %get-tuple-element.264.refs_1_.refs_2_.refs_3_, ...), custom_call_target="tpu_custom_call" | custom-call | flops 220000000 | bytes 100000 | tf_op jit(solution)/shard_map/attend_backward/pallas_call | solution.py:157
  443.0 5.2 collective-permute-done.51.refs_17_.refs_1_
  459.9 5.2 input_grad.3
  469.0 4.4 collective-permute-done.54.refs_2_
  484.8 8.5 %collective-permute-done.52 = bf16[576,384]{1,0:T(8,128)(2,1)} collective-permute-done((bf16[576,384]{1,0:T(8,128)(2,1)}, bf16[576,384]{1,0:T(8,128)(2,1)}, u32[]{:S(2)}, u32[]{:S(2)}) %collective-permute-start.52) | collective-permute-done | bytes 442400 | tf_op jit(solution)/shard_map/ppermute | solution.py:38
  501.9 6.8 %bias_network_back.1 = (f32[3,512]{1,0:T(4,128)S(1)}, f32[512,12]{1,0:T(8,128)S(1)}) custom-call(f32[40,384]{1,0:T(8,128)S(1)} %add_halves.17.refs_0_.refs_5_, f32[3,512]{1,0:T(4,128)S(1)} %copy-done.15, f32[512,12]{1,0:T(8,128)S(1)} %copy.65.refs_1_.refs_2_), custom_call_target="tpu_custom_call" | custom-call | flops 88000000 | bytes 100000 | tf_op jit(solution)/shard_map/bias_network_back/pallas_call | solution.py:157
  (542 shorter events, 204.2 us)
Async XLA Ops:
  9.6 40.9 %collective-permute-start.4 = (bf16[2,384,384]{2,1,0:T(8,128)(2,1)}, bf16[2,384,384]{2,1,0:T(8,128)(2,1)S(1)}, u32[]{:S(2)}, u32[]{:S(2)}) collective-permute-start(bf16[2,384,384]{2,1,0:T(8,128)(2,1)} %pad_maximum_fusion), channel_id=1, source_target_pairs={{0,16},{4,20},{8,24},{12,28},{16,0},{20,4},{24,8},{28,12},{1,17},{... | collective-permute-start | bytes 1769480 | tf_op jit(solution)/shard_map/ppermute | solution.py:1307
  14.5 33.8 %all-to-all-start = ((bf16[8,48,512]{2,1,0:T(8,128)(2,1)}), bf16[8,48,512]{2,1,0:T(8,128)(2,1)}, u32[]{:S(2)}, u32[]{:S(2)}) async-start(bf16[8,48,512]{2,1,0:T(8,128)(2,1)} %broadcast_in_dim.211), calls=%async_computation | async-start | bytes 786432 | tf_op jit(solution)/shard_map/all_to_all | solution.py:1233
  18.7 187.6 %all-gather.2.cloned.1.call-start = ((), (), s32[]{:S(2)}) async-start(), calls=%async_computation.1 | async-start | bytes 2654208 | tf_op jit(solution)/shard_map/all_gather | solution.py:1545
  19.7 41.0 %collective-permute-start = (bf16[2,576,384]{2,1,0:T(8,128)(2,1)}, bf16[2,576,384]{2,1,0:T(8,128)(2,1)}, u32[]{:S(2)}, u32[]{:S(2)}) collective-permute-start(bf16[2,576,384]{2,1,0:T(8,128)(2,1)} %slice.185), channel_id=1, source_target_pairs={{0,3},{1,0},{2,1},{3,2},{4,7},{5,4},{6,5},{7,6},{8,11},{9,8},{10,9... | collective-permute-start | bytes 2654216 | tf_op jit(solution)/shard_map/ppermute | solution.py:38
  50.5 52.5 %collective-permute-start.6 = (bf16[2,384,384]{2,1,0:T(8,128)(2,1)S(1)}, bf16[2,384,384]{2,1,0:T(8,128)(2,1)}, u32[]{:S(2)}, u32[]{:S(2)}) collective-permute-start(bf16[2,384,384]{2,1,0:T(8,128)(2,1)S(1)} %hold.2), channel_id=1, source_target_pairs={{0,16},{4,20},{8,24},{12,28},{16,0},{20,4},{24,8},{28,12},{1,17},{... | collective-permute-start | bytes 1769480 | tf_op jit(solution)/shard_map/ppermute | solution.py:1307
  53.1 49.9 %collective-permute-start.7 = (bf16[2,384,384]{2,1,0:T(8,128)(2,1)S(1)}, bf16[2,384,384]{2,1,0:T(8,128)(2,1)}, u32[]{:S(2)}, u32[]{:S(2)}) collective-permute-start(bf16[2,384,384]{2,1,0:T(8,128)(2,1)S(1)} %collective-permute-done.4.refs_11_.refs_1_.refs_9_.refs_8_), channel_id=1, source_target_pairs={{0,2},{1,3},{2,0},{3,1},{4,6},{5,7},{6,4},{7,5},{8,10},{9,11},{10,... | collective-permute-start | bytes 1769480 | tf_op jit(solution)/shard_map/ppermute | solution.py:1307
  122.1 22.3 %collective-permute-start.9 = (bf16[384,384]{1,0:T(8,128)(2,1)S(1)}, bf16[384,384]{1,0:T(8,128)(2,1)S(1)}, u32[]{:S(2)}, u32[]{:S(2)}) collective-permute-start(bf16[384,384]{1,0:T(8,128)(2,1)S(1)} %copy-done.36), channel_id=1, source_target_pairs={{0,8},{4,12},{8,0},{12,4},{16,24},{20,28},{24,16},{28,20},{1,9},{5... | collective-permute-start | bytes 884744 | tf_op jit(solution)/shard_map/ppermute | solution.py:1307
  151.4 28.2 %collective-permute-start.21 = (bf16[384,384]{1,0:T(8,128)(2,1)S(1)}, bf16[384,384]{1,0:T(8,128)(2,1)S(1)}, u32[]{:S(2)}, u32[]{:S(2)}) collective-permute-start(bf16[384,384]{1,0:T(8,128)(2,1)S(1)} %get-tuple-element.186), channel_id=1, source_target_pairs={{0,4},{4,0},{8,12},{12,8},{16,20},{20,16},{24,28},{28,24},{1,5},{5... | collective-permute-start | bytes 884744 | tf_op jit(solution)/shard_map/ppermute | solution.py:1307
  153.2 26.9 %collective-permute-start.22 = (bf16[384,384]{1,0:T(8,128)(2,1)S(1)}, bf16[384,384]{1,0:T(8,128)(2,1)S(1)}, u32[]{:S(2)}, u32[]{:S(2)}) collective-permute-start(bf16[384,384]{1,0:T(8,128)(2,1)S(1)} %get-tuple-element.187), channel_id=1, source_target_pairs={{0,8},{4,12},{8,0},{12,4},{16,24},{20,28},{24,16},{28,20},{1,9},{5... | collective-permute-start | bytes 884744 | tf_op jit(solution)/shard_map/ppermute | solution.py:1307
  154.6 26.2 %collective-permute-start.23 = (bf16[384,384]{1,0:T(8,128)(2,1)S(1)}, bf16[384,384]{1,0:T(8,128)(2,1)S(1)}, u32[]{:S(2)}, u32[]{:S(2)}) collective-permute-start(bf16[384,384]{1,0:T(8,128)(2,1)S(1)} %get-tuple-element.188), channel_id=1, source_target_pairs={{0,12},{4,8},{8,4},{12,0},{16,28},{20,24},{24,20},{28,16},{1,13},{... | collective-permute-start | bytes 884744 | tf_op jit(solution)/shard_map/ppermute | solution.py:1307
  176.6 27.8 %collective-permute-start.18 = (bf16[384,384]{1,0:T(8,128)(2,1)S(1)}, bf16[384,384]{1,0:T(8,128)(2,1)S(1)}, u32[]{:S(2)}, u32[]{:S(2)}) collective-permute-start(bf16[384,384]{1,0:T(8,128)(2,1)S(1)} %get-tuple-element.180), channel_id=1, source_target_pairs={{0,4},{4,0},{8,12},{12,8},{16,20},{20,16},{24,28},{28,24},{1,5},{5... | collective-permute-start | bytes 884744 | tf_op jit(solution)/shard_map/ppermute | solution.py:1307
  178.1 27.4 %collective-permute-start.19 = (bf16[384,384]{1,0:T(8,128)(2,1)S(1)}, bf16[384,384]{1,0:T(8,128)(2,1)S(1)}, u32[]{:S(2)}, u32[]{:S(2)}) collective-permute-start(bf16[384,384]{1,0:T(8,128)(2,1)S(1)} %get-tuple-element.181), channel_id=1, source_target_pairs={{0,8},{4,12},{8,0},{12,4},{16,24},{20,28},{24,16},{28,20},{1,9},{5... | collective-permute-start | bytes 884744 | tf_op jit(solution)/shard_map/ppermute | solution.py:1307
  179.6 26.7 %collective-permute-start.20 = (bf16[384,384]{1,0:T(8,128)(2,1)S(1)}, bf16[384,384]{1,0:T(8,128)(2,1)}, u32[]{:S(2)}, u32[]{:S(2)}) collective-permute-start(bf16[384,384]{1,0:T(8,128)(2,1)S(1)} %get-tuple-element.182), channel_id=1, source_target_pairs={{0,12},{4,8},{8,4},{12,0},{16,28},{20,24},{24,20},{28,16},{1,13},{... | collective-permute-start | bytes 884744 | tf_op jit(solution)/shard_map/ppermute | solution.py:1307
  269.5 26.5 %collective-permute-start.37 = (bf16[384,384]{1,0:T(8,128)(2,1)}, bf16[384,384]{1,0:T(8,128)(2,1)}, u32[]{:S(2)}, u32[]{:S(2)}) collective-permute-start(bf16[384,384]{1,0:T(8,128)(2,1)} %get-tuple-element.221), channel_id=1, source_target_pairs={{0,4},{4,0},{8,12},{12,8},{16,20},{20,16},{24,28},{28,24},{1,5},{5... | collective-permute-start | bytes 884744 | tf_op jit(solution)/shard_map/ppermute | solution.py:1307
  270.5 25.5 %collective-permute-start.38 = (bf16[384,384]{1,0:T(8,128)(2,1)}, bf16[384,384]{1,0:T(8,128)(2,1)}, u32[]{:S(2)}, u32[]{:S(2)}) collective-permute-start(bf16[384,384]{1,0:T(8,128)(2,1)} %get-tuple-element.222), channel_id=1, source_target_pairs={{0,8},{4,12},{8,0},{12,4},{16,24},{20,28},{24,16},{28,20},{1,9},{5... | collective-permute-start | bytes 884744 | tf_op jit(solution)/shard_map/ppermute | solution.py:1307
  271.9 24.1 %collective-permute-start.39 = (bf16[384,384]{1,0:T(8,128)(2,1)}, bf16[384,384]{1,0:T(8,128)(2,1)}, u32[]{:S(2)}, u32[]{:S(2)}) collective-permute-start(bf16[384,384]{1,0:T(8,128)(2,1)} %get-tuple-element.223), channel_id=1, source_target_pairs={{0,12},{4,8},{8,4},{12,0},{16,28},{20,24},{24,20},{28,16},{1,13},{... | collective-permute-start | bytes 884744 | tf_op jit(solution)/shard_map/ppermute | solution.py:1307
  293.7 34.0 %collective-permute-start.40 = (bf16[2,2,2,384,384]{4,3,2,1,0:T(8,128)(2,1)}, bf16[2,2,2,384,384]{4,3,2,1,0:T(8,128)(2,1)}, u32[]{:S(2)}, u32[]{:S(2)}) collective-permute-start(bf16[2,2,2,384,384]{4,3,2,1,0:T(8,128)(2,1)} %get-tuple-element.233), channel_id=1, source_target_pairs={{0,1},{1,0},{2,3},{3,2},{4,5},{5,4},{6,7},{7,6},{8,9},{9,8},{10,11... | collective-permute-start | bytes 7077896 | tf_op jit(solution)/shard_map/ppermute | solution.py:1307
  322.8 48.6 %collective-permute-start.44 = (bf16[2,2,2,384,384]{4,3,2,1,0:T(8,128)(2,1)}, bf16[2,2,2,384,384]{4,3,2,1,0:T(8,128)(2,1)}, u32[]{:S(2)}, u32[]{:S(2)}) collective-permute-start(bf16[2,2,2,384,384]{4,3,2,1,0:T(8,128)(2,1)} %get-tuple-element.252), channel_id=1, source_target_pairs={{0,1},{1,0},{2,3},{3,2},{4,5},{5,4},{6,7},{7,6},{8,9},{9,8},{10,11... | collective-permute-start | bytes 7077896 | tf_op jit(solution)/shard_map/ppermute | solution.py:1307
  323.5 26.5 %collective-permute-start.43 = (bf16[2,192,768]{2,1,0:T(8,128)(2,1)S(1)}, bf16[2,192,768]{2,1,0:T(8,128)(2,1)S(1)}, u32[]{:S(2)}, u32[]{:S(2)}) collective-permute-start(bf16[2,192,768]{2,1,0:T(8,128)(2,1)S(1)} %pad_maximum_fusion.5), channel_id=1, source_target_pairs={{0,12},{4,8},{8,4},{12,0},{16,28},{20,24},{24,20},{28,16},{1,13},{... | collective-permute-start | bytes 1769480 | tf_op jit(solution)/shard_map/ppermute | solution.py:1307
  325.4 26.4 %collective-permute-start.42 = (bf16[2,192,768]{2,1,0:T(8,128)(2,1)S(1)}, bf16[2,192,768]{2,1,0:T(8,128)(2,1)S(1)}, u32[]{:S(2)}, u32[]{:S(2)}) collective-permute-start(bf16[2,192,768]{2,1,0:T(8,128)(2,1)S(1)} %pad_maximum_fusion.4), channel_id=1, source_target_pairs={{0,8},{4,12},{8,0},{12,4},{16,24},{20,28},{24,16},{28,20},{1,9},{5... | collective-permute-start | bytes 1769480 | tf_op jit(solution)/shard_map/ppermute | solution.py:1307
  331.5 36.8 %collective-permute-start.45 = (bf16[2,1,2,384,384]{4,3,2,1,0:T(8,128)(2,1)}, bf16[2,1,2,384,384]{4,3,2,1,0:T(8,128)(2,1)}, u32[]{:S(2)}, u32[]{:S(2)}) collective-permute-start(bf16[2,1,2,384,384]{4,3,2,1,0:T(8,128)(2,1)} %get-tuple-element.242.refs_10_), channel_id=1, source_target_pairs={{0,2},{1,3},{2,0},{3,1},{4,6},{5,7},{6,4},{7,5},{8,10},{9,11},{10,... | collective-permute-start | bytes 3538952 | tf_op jit(solution)/shard_map/ppermute | solution.py:1307
  350.0 40.7 %collective-permute-start.48 = (bf16[576,384]{1,0:T(8,128)(2,1)S(1)}, bf16[576,384]{1,0:T(8,128)(2,1)S(1)}, u32[]{:S(2)}, u32[]{:S(2)}) collective-permute-start(bf16[576,384]{1,0:T(8,128)(2,1)S(1)} %get-tuple-element.403), channel_id=1, source_target_pairs={{0,3},{1,0},{2,1},{3,2},{4,7},{5,4},{6,5},{7,6},{8,11},{9,8},{10,9... | collective-permute-start | bytes 1327112 | tf_op jit(solution)/shard_map/ppermute | solution.py:38
  355.2 30.3 %collective-permute-start.46 = (bf16[192,768]{1,0:T(8,128)(2,1)S(1)}, bf16[192,768]{1,0:T(8,128)(2,1)S(1)}, u32[]{:S(2)}, u32[]{:S(2)}) collective-permute-start(bf16[192,768]{1,0:T(8,128)(2,1)S(1)} %get-tuple-element.258), channel_id=1, source_target_pairs={{0,16},{4,20},{8,24},{12,28},{16,0},{20,4},{24,8},{28,12},{1,17},{... | collective-permute-start | bytes 884744 | tf_op jit(solution)/shard_map/ppermute | solution.py:1307
  375.0 41.9 %collective-permute-start.49 = (bf16[2,1,2,384,384]{4,3,2,1,0:T(8,128)(2,1)}, bf16[2,1,2,384,384]{4,3,2,1,0:T(8,128)(2,1)S(1)}, u32[]{:S(2)}, u32[]{:S(2)}) collective-permute-start(bf16[2,1,2,384,384]{4,3,2,1,0:T(8,128)(2,1)} %get-tuple-element.256.refs_13_), channel_id=1, source_target_pairs={{0,2},{1,3},{2,0},{3,1},{4,6},{5,7},{6,4},{7,5},{8,10},{9,11},{10,... | collective-permute-start | bytes 3538952 | tf_op jit(solution)/shard_map/ppermute | solution.py:1307
  385.6 24.9 %collective-permute-start.72 = (bf16[192,768]{1,0:T(8,128)(2,1)S(1)}, bf16[192,768]{1,0:T(8,128)(2,1)S(1)}, u32[]{:S(2)}, u32[]{:S(2)}) collective-permute-start(bf16[192,768]{1,0:T(8,128)(2,1)S(1)} %add_halves.9.refs_4_), channel_id=1, source_target_pairs={{0,2},{1,3},{2,0},{3,1},{4,6},{5,7},{6,4},{7,5},{8,10},{9,11},{10,... | collective-permute-start | bytes 884744 | tf_op jit(solution)/shard_map/ppermute | solution.py:1307
  386.3 35.7 %collective-permute-start.73 = (bf16[192,768]{1,0:T(8,128)(2,1)S(1)}, bf16[192,768]{1,0:T(8,128)(2,1)S(1)}, u32[]{:S(2)}, u32[]{:S(2)}) collective-permute-start(bf16[192,768]{1,0:T(8,128)(2,1)S(1)} %add_halves.9.refs_4_), channel_id=1, source_target_pairs={{0,1},{1,0},{2,3},{3,2},{4,5},{5,4},{6,7},{7,6},{8,9},{9,8},{10,11... | collective-permute-start | bytes 884744 | tf_op jit(solution)/shard_map/ppermute | solution.py:1307
  386.3 29.3 %collective-permute-start.50 = (bf16[2,384,384]{2,1,0:T(8,128)(2,1)S(1)}, bf16[2,384,384]{2,1,0:T(8,128)(2,1)S(1)}, u32[]{:S(2)}, u32[]{:S(2)}) collective-permute-start(bf16[2,384,384]{2,1,0:T(8,128)(2,1)S(1)} %get-tuple-element.255.refs_2_), channel_id=1, source_target_pairs={{0,16},{4,20},{8,24},{12,28},{16,0},{20,4},{24,8},{28,12},{1,17},{... | collective-permute-start | bytes 1769480 | tf_op jit(solution)/shard_map/ppermute | solution.py:1307
  390.7 22.7 %collective-permute-start.47 = (bf16[576,384]{1,0:T(8,128)(2,1)S(1)}, bf16[576,384]{1,0:T(8,128)(2,1)S(1)}, u32[]{:S(2)}, u32[]{:S(2)}) collective-permute-start(bf16[576,384]{1,0:T(8,128)(2,1)S(1)} %get-tuple-element.260.refs_2_), channel_id=1, source_target_pairs={{0,1},{1,2},{2,3},{3,0},{4,5},{5,6},{6,7},{7,4},{8,9},{9,10},{10,1... | collective-permute-start | bytes 1327112 | tf_op jit(solution)/shard_map/ppermute | solution.py:38
  420.9 27.4 %collective-permute-start.51 = (bf16[2,384,384]{2,1,0:T(8,128)(2,1)S(1)}, bf16[2,384,384]{2,1,0:T(8,128)(2,1)S(1)}, u32[]{:S(2)}, u32[]{:S(2)}) collective-permute-start(bf16[2,384,384]{2,1,0:T(8,128)(2,1)S(1)} %get-tuple-element.275.refs_15_), channel_id=1, source_target_pairs={{0,16},{4,20},{8,24},{12,28},{16,0},{20,4},{24,8},{28,12},{1,17},{... | collective-permute-start | bytes 1769480 | tf_op jit(solution)/shard_map/ppermute | solution.py:1307
  423.0 42.1 %collective-permute-start.60 = (bf16[2,384,384]{2,1,0:T(8,128)(2,1)S(1)}, bf16[2,384,384]{2,1,0:T(8,128)(2,1)S(1)}, u32[]{:S(2)}, u32[]{:S(2)}) collective-permute-start(bf16[2,384,384]{2,1,0:T(8,128)(2,1)S(1)} %add_halves.10.refs_2_.refs_1_), channel_id=1, source_target_pairs={{0,2},{1,3},{2,0},{3,1},{4,6},{5,7},{6,4},{7,5},{8,10},{9,11},{10,... | collective-permute-start | bytes 1769480 | tf_op jit(solution)/shard_map/ppermute | solution.py:1307
  473.3 39.0 %collective-permute-start.69 = (bf16[2,384,384]{2,1,0:T(8,128)(2,1)}, bf16[2,384,384]{2,1,0:T(8,128)(2,1)}, u32[]{:S(2)}, u32[]{:S(2)}) collective-permute-start(bf16[2,384,384]{2,1,0:T(8,128)(2,1)} %add_halves.11.refs_5_.refs_1_), channel_id=1, source_target_pairs={{0,2},{1,3},{2,0},{3,1},{4,6},{5,7},{6,4},{7,5},{8,10},{9,11},{10,... | collective-permute-start | bytes 1769480 | tf_op jit(solution)/shard_map/ppermute | solution.py:1307
  474.8 41.1 %collective-permute-start.70 = (bf16[2,384,384]{2,1,0:T(8,128)(2,1)}, bf16[2,384,384]{2,1,0:T(8,128)(2,1)}, u32[]{:S(2)}, u32[]{:S(2)}) collective-permute-start(bf16[2,384,384]{2,1,0:T(8,128)(2,1)} %add_halves.11.refs_5_.refs_1_), channel_id=1, source_target_pairs={{0,1},{1,0},{2,3},{3,2},{4,5},{5,4},{6,7},{7,6},{8,9},{9,8},{10,11... | collective-permute-start | bytes 1769480 | tf_op jit(solution)/shard_map/ppermute | solution.py:1307
  (166 other events, 1439.7 us)
Sparse Core Ops, SparseCore 0:
  112.7 73.4 all-gather.1

commit v4 on v3

--- a/solution.py
+++ b/solution.py
@@ -13,7 +13,7 @@
 LANES = 128
 SHEAR = 384
 ZONES = 16
-UNROLL = 2
+UNROLL = 4
 COST_SCALE = 0.4
 TILE_HEADS = LANES // HEAD_DIM
 
@@ -886,14 +886,26 @@
     return piece % row_size, piece // row_size
 
 
-def expert_weight(own, other_refs, expert, chunk, local, chunks, me):
+def take_weights(own_ref, other_refs, out_scr, expert, local, me, first):
     row_size = len(other_refs)
-    member, _ = piece_home(jnp.maximum(expert - local, 0), chunk, row_size, chunks)
-    spot = spot_of(member, me, row_size.bit_length() - 1)
-    weight = own
-    for k, ref in enumerate(other_refs):
-        weight = jnp.where((expert >= local) & (spot == k), ref[0], weight)
-    return weight
+    chunks = out_scr.shape[1 if first else 0] // PIECE
+
+    @pl.when(expert < local)
+    def _():
+        out_scr[...] = own_ref[0]
+
+    for chunk in range(chunks):
+        member, _ = piece_home(jnp.maximum(expert - local, 0), chunk, row_size, chunks)
+        spot = spot_of(member, me, row_size.bit_length() - 1)
+        span = slice(chunk * PIECE, (chunk + 1) * PIECE)
+        for k, ref in enumerate(other_refs):
+
+            @pl.when((expert >= local) & (spot == k))
+            def _(ref=ref, span=span):
+                if first:
+                    out_scr[:, span] = ref[0]
+                else:
+                    out_scr[span, :] = ref[0]
 
 
 def taken(refs, *counts):
@@ -919,37 +931,20 @@
     row_refs, (in_ref, in_bias_ref, out_ref, out_bias_ref), in_others, out_others, refs = taken(
         refs, members, 4, row_size, row_size
     )
-    result_refs, (hidden_ref, slope_ref, pre_scr) = taken(refs, members)
+    result_refs, (hidden_ref, slope_ref, pre_scr, in_scr, out_scr) = taken(refs, members)
     expert = pl.program_id(0)
-    rows = joined(row_refs)
-    count = rows.shape[0]
-    chunks = in_ref.shape[2] // PIECE
-    block = 64
-    total = None
-    for chunk in range(chunks):
+    take_weights(in_ref, in_others, in_scr, expert, local, me_ref[0], True)
+    take_weights(out_ref, out_others, out_scr, expert, local, me_ref[0], False)
+    pre_scr[...] = mm(joined(row_refs), in_scr[...]) + in_bias_ref[0]
+    for chunk in range(in_scr.shape[1] // PIECE):
         lanes = slice(chunk * PIECE, (chunk + 1) * PIECE)
-        weight = expert_weight(
-            in_ref[0, :, lanes], in_others, expert, chunk, local, chunks, me_ref[0]
-        )
-        pre_scr[...] = mm(rows, weight) + in_bias_ref[0, :, lanes]
-
-        def activate(c, carry, lanes=lanes):
-            at = rows_at(c * block, block)
-            pre = pre_scr[at, :]
-            cdf = 0.5 * (1.0 + lax.erf(pre * 0.7071067811865476))
-            hidden_ref[0, at, lanes] = (pre * cdf).astype(BF)
-            slope_ref[0, at, lanes] = (
-                cdf + pre * (0.3989422804014327 * jnp.exp(-0.5 * pre * pre))
-            ).astype(BF)
-            return carry
-
-        lax.fori_loop(0, count // block, activate, 0)
-        weight = expert_weight(
-            out_ref[0, lanes, :], out_others, expert, chunk, local, chunks, me_ref[0]
-        )
-        now = mm(hidden_ref[0, :, lanes], weight)
-        total = now if total is None else total + now
-    put_parts(result_refs, total + out_bias_ref[0])
+        pre = pre_scr[:, lanes]
+        cdf = 0.5 * (1.0 + lax.erf(pre * 0.7071067811865476))
+        hidden_ref[0, :, lanes] = (pre * cdf).astype(BF)
+        slope_ref[0, :, lanes] = (
+            cdf + pre * (0.3989422804014327 * jnp.exp(-0.5 * pre * pre))
+        ).astype(BF)
+    put_parts(result_refs, mm(hidden_ref[0], out_scr[...]) + out_bias_ref[0])
 
 
 def expert_specs(members, slots, channels, hidden, local, row_size):
@@ -1012,7 +1007,11 @@
         + [spec["other"]] * (2 * row_size),
         [spec["tokens"]] * members + [spec["wide"], spec["wide"]],
         [jax.ShapeDtypeStruct(rows[0].shape, BF)] * members + [wide, wide],
-        [pltpu.VMEM((count, PIECE), FL)],
+        [
+            pltpu.VMEM((count, hidden), FL),
+            pltpu.VMEM((channels, hidden), BF),
+            pltpu.VMEM((hidden, channels), BF),
+        ],
         [*rows, first, first_bias, second, second_bias, *first_other, *second_other],
         19,
         after,
@@ -1024,26 +1023,17 @@
     row_refs, (in_ref, out_ref, slope_ref), in_others, out_others, refs = taken(
         refs, members, 3, row_size, row_size
     )
-    result_refs, (dpre_ref, dbias_ref) = taken(refs, members)
+    result_refs, (dpre_ref, dbias_ref, dhidden_scr, in_scr, out_scr) = taken(refs, members)
     expert = pl.program_id(0)
-    rows = joined(row_refs)
-    chunks = in_ref.shape[2] // PIECE
-    total = None
-    for chunk in range(chunks):
+    take_weights(in_ref, in_others, in_scr, expert, local, me_ref[0], True)
+    take_weights(out_ref, out_others, out_scr, expert, local, me_ref[0], False)
+    dhidden_scr[...] = mm_nt(joined(row_refs), out_scr[...])
+    for chunk in range(in_scr.shape[1] // PIECE):
         lanes = slice(chunk * PIECE, (chunk + 1) * PIECE)
-        weight = expert_weight(
-            out_ref[0, lanes, :], out_others, expert, chunk, local, chunks, me_ref[0]
-        )
-        dpre = mm_nt(rows, weight) * slope_ref[0, :, lanes].astype(FL)
+        dpre = dhidden_scr[:, lanes] * slope_ref[0, :, lanes].astype(FL)
         dbias_ref[0, :, lanes] = jnp.sum(dpre, 0, keepdims=True)
-        low = dpre.astype(BF)
-        dpre_ref[0, :, lanes] = low
-        weight = expert_weight(
-            in_ref[0, :, lanes], in_others, expert, chunk, local, chunks, me_ref[0]
-        )
-        now = mm_nt(low, weight)
-        total = now if total is None else total + now
-    put_parts(result_refs, total)
+        dpre_ref[0, :, lanes] = dpre.astype(BF)
+    put_parts(result_refs, mm_nt(dpre_ref[0], in_scr[...]))
 
 
 def expert_backward(me, rows, first, second, first_other, second_other, slope, after):
@@ -1068,7 +1058,11 @@
             jax.ShapeDtypeStruct((2 * local, count, hidden), BF),
             jax.ShapeDtypeStruct((2 * local, 1, hidden), FL),
         ],
-        [],
+        [
+            pltpu.VMEM((count, hidden), FL),
+            pltpu.VMEM((channels, hidden), BF),
+            pltpu.VMEM((hidden, channels), BF),
+        ],
         [*rows, first, second, slope, *first_other, *second_other],
         12,
         after,
@@ -1086,24 +1080,24 @@
     chunks = wide_refs[0].shape[2] // PIECE
     rows = [joined(token_refs[m * members : (m + 1) * members]) for m in range(micros)]
     dbias_ref[0] = sum(jnp.sum(part.astype(FL), 0, keepdims=True) for part in rows)
+    total = None
+    for part, ref in zip(rows, wide_refs):
+        now = mm_tn(part, ref[0]) if tokens_left else mm_tn(ref[0], part)
+        total = now if total is None else total + now
+    low = total.astype(BF)
     for chunk in range(chunks):
-        lanes = slice(chunk * PIECE, (chunk + 1) * PIECE)
-        total = None
-        for part, ref in zip(rows, wide_refs):
-            wide = ref[0, :, lanes]
-            now = mm_tn(part, wide) if tokens_left else mm_tn(wide, part)
-            total = now if total is None else total + now
-        low = total.astype(BF)
+        span = slice(chunk * PIECE, (chunk + 1) * PIECE)
+        piece = low[:, span] if tokens_left else low[span, :]
         member, _ = piece_home(expert % local, chunk, row_size, chunks)
         spot = spot_of(member, me_ref[0], row_size.bit_length() - 1)
 
         @pl.when(spot < half)
-        def _():
-            keep_ref[0, spot, 0] = low
+        def _(piece=piece, spot=spot):
+            keep_ref[0, spot, 0] = piece
 
         @pl.when(spot >= half)
-        def _():
-            send_ref[0, spot - half, 0] = low
+        def _(piece=piece, spot=spot):
+            send_ref[0, spot - half, 0] = piece
 
 
 def expert_weight_grads(me, tokens, wide, local, row_size, tokens_left, after):
@@ -1452,7 +1446,7 @@
         second_piece.append(
             lax.dynamic_slice(expert_second_weight, (at, start, 0), (1, PIECE, channels))
         )
-    first_got = crossed(jnp.concatenate(first_piece), "dp", members)
+    first_got = crossed(held_back(jnp.concatenate(first_piece), [columns]), "dp", members)
     second_got = crossed(held_back(jnp.concatenate(second_piece), [first_got]), "dp", members)
     first_other = spread_over_row(first_got)
     second_other = spread_over_row(second_got)

time: 532 us -> 512 us (0.962)
  Pallas kernels: 295 us -> 276 us
    pallas_call x8, Pallas kernels: 95.9 us -> 79 us  [call_expert(): pl.pallas_call(skipping(body, 1 + len(args), len(after)), name=name, grid...]
    all_to_all x1, waiting for transfers between devices: 16.1 us -> 0.01 us  [swapped(): return lax.all_to_all(rows, 'dp', split_axis=0, concat_axis=0, tiled=True)]
    ppermute x7, waiting for transfers between devices: 17.6 us -> 27.3 us  [passed_along(): lax.ppermute(array, axis, [(i, (i + by) % count) for i in range(count)])]
    ppermute x68, waiting for transfers between devices: 42.9 us -> 51.8 us  [crossed(): return lax.ppermute(array, axis, [(i, i ^ bit) for i in range(count)])]
    pallas_call x40 -> x41, Pallas kernels: 185 us -> 182 us  [call_kernel(): pl.pallas_call(skipping(body, len(args), len(after)), name=name, grid=(1,...]
    unnamed x247 -> x241, local copies, waits for them, and re-layouts: 23.7 us -> 22.9 us
  transfers between devices with their start and end apart: 77 -> 77, of which waited for: 17 -> 16; matrix products, arithmetic and copies ran while one was open for 7% -> 7% of each run, Pallas kernels for 54% -> 52%
where the time goes in v4:
time: 512 us; the launch traced here: 507 us
  Pallas kernels  276 us (54%)
  waiting for transfers between devices  79.1 us (15%)
  starting transfers between devices  75.5 us (15%)
  local copies, waits for them, and re-layouts  44.6 us (9%)
  between operations  16.2 us (3%)
  other arithmetic  15.9 us (3%)
    pallas_call x41, Pallas kernels, call_kernel(): pl.pallas_call(skipping(body, len(args), len(after)), name=name, grid=(1,...  182 us
    pallas_call x8, Pallas kernels, call_expert(): pl.pallas_call(skipping(body, 1 + len(args), len(after)), name=name, grid...  79 us
    ppermute x68, starting transfers between devices, crossed(): return lax.ppermute(array, axis, [(i, i ^ bit) for i in range(count)])  64 us
    ppermute x68, waiting for transfers between devices, crossed(): return lax.ppermute(array, axis, [(i, i ^ bit) for i in range(count)])  51.8 us
    ppermute x7, waiting for transfers between devices, passed_along(): lax.ppermute(array, axis, [(i, (i + by) % count) for i in range(count)])  27.3 us
    unnamed x241, local copies, waits for them, and re-layouts  22.9 us
  transfers between devices with their start and end apart: 77, of which 16 were waited for; matrix products, arithmetic and copies ran while one was open for 7% of the time, Pallas kernels for 52%

profile of v4, /device:TPU:0, one launch (start us, length us, event | category | flops | bytes accessed | tf_op | source)
XLA Modules:
  0.0 507.1 jit_solution(657553962799794421)
XLA Ops:
  9.6 7.3 %all-to-all-start = ((bf16[8,48,512]{2,1,0:T(8,128)(2,1)}), bf16[8,48,512]{2,1,0:T(8,128)(2,1)}, u32[]{:S(2)}, u32[]{:S(2)}) async-start(bf16[8,48,512]{2,1,0:T(8,128)(2,1)} %broadcast_in_dim.211), calls=%async_computation | async-start | bytes 786432 | tf_op jit(solution)/shard_map/all_to_all | solution.py:1227
  46.1 6.7 %spread_bias.1 = (f32[3,144,576]{2,1,0:T(8,128)S(1)}, f32[3,144,576]{2,1,0:T(8,128)}) custom-call(f32[3,512]{1,0:T(4,128)S(1)} %pad_maximum_fusion.11.refs_0_.refs_1_, f32[512,12]{1,0:T(8,128)S(1)} %copy.65.refs_1_.refs_2_, bf16[384,512]{1,0:T(8,128)(2,1)} %collective-permute-done.1.refs_1_.refs_2_, s32[1,1152]{1,0:T(1,128)S(1)} %copy-done.75), custom_call_target="tpu_custom_call" | custom-call | flops 2200000000 | bytes 100000 | tf_op jit(solution)/shard_map/spread_bias/pallas_call | solution.py:157
  52.8 11.0 %collective-permute-done.4.refs_11_.refs_1_.refs_9_.refs_8_ = bf16[2,384,384]{2,1,0:T(8,128)(2,1)S(1)} collective-permute-done((bf16[2,384,384]{2,1,0:T(8,128)(2,1)S(1)}, bf16[2,384,384]{2,1,0:T(8,128)(2,1)S(1)}, u32[]{:S(2)}, u32[]{:S(2)}) %collective-permute-start.4) | collective-permute-done | bytes 589856 | tf_op jit(solution)/shard_map/ppermute | solution.py:1301
  67.1 12.8 %attend_forward.2 = (bf16[576,384]{1,0:T(8,128)(2,1)S(1)}, bf16[576,384]{1,0:T(8,128)(2,1)S(1)}, bf16[1152,384]{1,0:T(8,128)(2,1)}, bf16[1152,1152]{1,0:T(8,128)(2,1)}, f32[1152,768]{1,0:T(8,128)}) custom-call(bf16[1152,384]{1,0:T(8,128)(2,1)} %bitcast.86, bf16[576,384]{1,0:T(8,128)(2,1)} %get-tuple-element.407.refs_1_, ...), custom_call_target="tpu_custom_call" | custom-call | flops 7040000000 | bytes 100000 | tf_op jit(solution)/shard_map/attend_forward/pallas_call | solution.py:157
  80.7 12.7 %attend_forward.3 = (bf16[576,384]{1,0:T(8,128)(2,1)S(1)}, bf16[576,384]{1,0:T(8,128)(2,1)S(1)}, bf16[1152,384]{1,0:T(8,128)(2,1)}, bf16[1152,1152]{1,0:T(8,128)(2,1)}, f32[1152,768]{1,0:T(8,128)}) custom-call(bf16[1152,384]{1,0:T(8,128)(2,1)} %bitcast.84, bf16[576,384]{1,0:T(8,128)(2,1)} %get-tuple-element.408.refs_1_, ...), custom_call_target="tpu_custom_call" | custom-call | flops 7040000000 | bytes 100000 | tf_op jit(solution)/shard_map/attend_forward/pallas_call | solution.py:157
  95.0 5.3 %route.2 = (f32[1152,384]{1,0:T(8,128)}, bf16[1152,384]{1,0:T(8,128)(2,1)}, f32[1152,128]{1,0:T(8,128)}, bf16[1152,384]{1,0:T(8,128)(2,1)}, bf16[384,384]{1,0:T(...) custom-call(bf16[576,384]{1,0:T(8,128)(2,1)S(1)} %collective-permute-done., ...), custom_call_target="tpu_custom_call" | custom-call | flops 5280000000 | bytes 100000 | tf_op jit(solution)/shard_map/route/pallas_call | solution.py:157
  114.9 13.7 %collective-permute-done.17.refs_0_.refs_5_ = bf16[576,384]{1,0:T(8,128)(2,1)S(1)} collective-permute-done((bf16[576,384]{1,0:T(8,128)(2,1)S(1)}, bf16[576,384]{1,0:T(8,128)(2,1)S(1)}, u32[]{:S(2)}, u32[]{:S(2)}) %collective-permute-start.17) | collective-permute-done | bytes 442400 | tf_op jit(solution)/shard_map/ppermute | solution.py:38
  131.9 5.9 %collective-permute-done.9.refs_10_.refs_3_ = bf16[384,384]{1,0:T(8,128)(2,1)S(1)} collective-permute-done((bf16[384,384]{1,0:T(8,128)(2,1)S(1)}, bf16[384,384]{1,0:T(8,128)(2,1)S(1)}, u32[]{:S(2)}, u32[]{:S(2)}) %collective-permute-start.9) | collective-permute-done | bytes 294944 | tf_op jit(solution)/shard_map/ppermute | solution.py:1301
  139.5 5.3 %route.3 = (f32[1152,384]{1,0:T(8,128)}, bf16[1152,384]{1,0:T(8,128)(2,1)}, f32[1152,128]{1,0:T(8,128)}, bf16[1152,384]{1,0:T(8,128)(2,1)}, bf16[384,384]{1,0:T(...) custom-call(bf16[576,384]{1,0:T(8,128)(2,1)} %copy-done.88, ...), custom_call_target="tpu_custom_call" | custom-call | flops 5280000000 | bytes 100000 | tf_op jit(solution)/shard_map/route/pallas_call | solution.py:157
  149.4 14.0 %expert_forward.2 = (bf16[384,384]{1,0:T(8,128)(2,1)S(1)}, bf16[384,384]{1,0:T(8,128)(2,1)S(1)}, bf16[384,384]{1,0:T(8,128)(2,1)S(1)}, bf16[384,384]{1,0:T(8,128...) custom-call(s32[1]{0:T(128)} %bitcast.me_ref.refs_0_, bf16[384,384]{1,0:T(8,128)(2,1)S(1)} %copy-done.59, ...), custom_call_target="tpu_custom_call" | custom-call | flops 8360000000 | bytes 100000 | tf_op jit(solution)/shard_map/expert_forward/pallas_call | solution.py:973
  167.6 7.4 %collective-permute-done.23.refs_4_.refs_8_ = bf16[384,384]{1,0:T(8,128)(2,1)S(1)} collective-permute-done((bf16[384,384]{1,0:T(8,128)(2,1)S(1)}, bf16[384,384]{1,0:T(8,128)(2,1)S(1)}, u32[]{:S(2)}, u32[]{:S(2)}) %collective-permute-start.23) | collective-permute-done | bytes 294944 | tf_op jit(solution)/shard_map/ppermute | solution.py:1301
  175.8 13.8 %expert_forward.3 = (bf16[384,384]{1,0:T(8,128)(2,1)S(1)}, bf16[384,384]{1,0:T(8,128)(2,1)}, bf16[384,384]{1,0:T(8,128)(2,1)}, bf16[384,384]{1,0:T(8,128)(2,1)S(...) custom-call(s32[1]{0:T(128)} %bitcast.me_ref.refs_0_, ...), custom_call_target="tpu_custom_call" | custom-call | flops 8360000000 | bytes 100000 | tf_op jit(solution)/shard_map/expert_forward/pallas_call | solution.py:973
  195.5 12.7 %merge.2 = (bf16[288,768]{1,0:T(8,128)(2,1)}, bf16[288,1536]{1,0:T(8,128)(2,1)}, bf16[288,768]{1,0:T(8,128)(2,1)}, f32[1152,384]{1,0:T(8,128)}, bf16[1152,128]{1...) custom-call(bf16[384,384]{1,0:T(8,128)(2,1)S(1)} %copy-done.74, ...), custom_call_target="tpu_custom_call" | custom-call | flops 6160000000 | bytes 100000 | tf_op jit(solution)/shard_map/merge/pallas_call | solution.py:157
  211.7 12.5 %merge.3 = (bf16[288,768]{1,0:T(8,128)(2,1)}, bf16[288,1536]{1,0:T(8,128)(2,1)}, bf16[288,768]{1,0:T(8,128)(2,1)}, f32[1152,384]{1,0:T(8,128)}, bf16[1152,128]{1...) custom-call(bf16[384,384]{1,0:T(8,128)(2,1)S(1)} %copy-done.72, ...), custom_call_target="tpu_custom_call" | custom-call | flops 6160000000 | bytes 100000 | tf_op jit(solution)/shard_map/merge/pallas_call | solution.py:157
  229.2 11.6 %expert_backward.2 = (bf16[384,384]{1,0:T(8,128)(2,1)S(1)}, bf16[384,384]{1,0:T(8,128)(2,1)S(1)}, bf16[384,384]{1,0:T(8,128)(2,1)S(1)}, bf16[384,384]{1,0:T(8,12...) custom-call(s32[1]{0:T(128)} %bitcast.me_ref.refs_0_, ...), custom_call_target="tpu_custom_call" | custom-call | flops 5280000000 | bytes 100000 | tf_op jit(solution)/shard_map/expert_backward/pallas_call | solution.py:973
  245.1 11.9 %expert_backward.3 = (bf16[384,384]{1,0:T(8,128)(2,1)S(1)}, bf16[384,384]{1,0:T(8,128)(2,1)}, bf16[384,384]{1,0:T(8,128)(2,1)}, bf16[384,384]{1,0:T(8,128)(2,1)}...) custom-call(s32[1]{0:T(128)} %bitcast.me_ref.refs_0_, ...), custom_call_target="tpu_custom_call" | custom-call | flops 5280000000 | bytes 100000 | tf_op jit(solution)/shard_map/expert_backward/pallas_call | solution.py:973
  261.4 7.5 %settle.2 = (f32[1152,384]{1,0:T(8,128)}, bf16[1152,384]{1,0:T(8,128)(2,1)}, bf16[1152,384]{1,0:T(8,128)(2,1)}, f32[8,384]{1,0:T(8,128)S(1)}) custom-call(bf16[384,384]{1,0:T(8,128)(2,1)S(1)} %get-tuple-element.202.refs_0_, bf16[384,384]{1,0:T(8,128)(2,1)S(1)} %collective-permute-done.30.refs_1_, bf16[384,384]{1,0:T(8,128)(2,1)S(1)} %collective-permute-done.31.refs_2_, ...), custom_call_target="tpu_custom_call" | custom-call | flops 3080000000 | bytes 100000 | tf_op jit(solution)/shard_map/settle/pallas_call | solution.py:157
  268.9 9.9 %expert_weight_grads.2 = (bf16[2,2,2,384,384]{4,3,2,1,0:T(8,128)(2,1)}, bf16[2,2,2,384,384]{4,3,2,1,0:T(8,128)(2,1)}, f32[4,1,384]{2,1,0:T(1,128)}) custom-call(s32[1]{0:T(128)} %bitcast.me_ref.refs_0_, bf16[384,384]{1,0:T(8,128)(2,1)S(1)} %copy-done.60, bf16[384,384]{1,0:T(8,128)(2,1)S(1)} %copy-done.24, bf16[384,384]{1,0:T(8,128)(2,1)S(1)} %copy-done.26, ...), custom_call_target="tpu_custom_call" | custom-call | flops 5720000000 | bytes 100000 | tf_op jit(solution)/shard_map/expert_weight_grads/pallas_call | solution.py:973
  281.2 7.8 %settle.3 = (f32[1152,384]{1,0:T(8,128)}, bf16[1152,384]{1,0:T(8,128)(2,1)}, bf16[1152,384]{1,0:T(8,128)(2,1)}, f32[8,384]{1,0:T(8,128)S(1)}) custom-call(bf16[384,384]{1,0:T(8,128)(2,1)S(1)} %copy-done.52, bf16[384,384]{1,0:T(8,128)(2,1)} %collective-permute-done.37.refs_1_, bf16[384,384]{1,0:T(8,128)(2,1)} %collective-permute-done.38.refs_2_, ...), custom_call_target="tpu_custom_call" | custom-call | flops 3080000000 | bytes 100000 | tf_op jit(solution)/shard_map/settle/pallas_call | solution.py:157
  289.0 5.6 %merge_weight_grad.1.refs_11_ = bf16[1536,768]{1,0:T(8,128)(2,1)} custom-call(bf16[288,1536]{1,0:T(8,128)(2,1)S(1)} %copy-done.47, bf16[288,768]{1,0:T(8,128)(2,1)S(1)} %copy-done.48, bf16[288,1536]{1,0:T(8,128)(2,1)} %get-tuple-element.238.refs_2_, bf16[288,768]{1,0:T(8,128)(2,1)S(1)} %copy-done.49, f32[8,384]{1,0:T(8,128)S(1)} %get-tuple-element.240.refs_4_.refs_10_), custom_call_target="tpu_custom_call" | custom-call | flops 2200000000 | bytes 100000 | tf_op jit(solution)/shard_map/merge_weight_grad/pallas_call | solution.py:861
  294.7 10.6 %expert_weight_grads.3 = (bf16[2,2,2,384,384]{4,3,2,1,0:T(8,128)(2,1)}, bf16[2,2,2,384,384]{4,3,2,1,0:T(8,128)(2,1)}, f32[4,1,384]{2,1,0:T(1,128)S(1)}) custom-call(s32[1]{0:T(128)} %bitcast.me_ref.refs_0_, bf16[384,384]{1,0:T(8,128)(2,1)S(1)} %copy-done.54, bf16[384,384]{1,0:T(8,128)(2,1)S(1)} %copy-done.28, bf16[384,384]{1,0:T(8,128)(2,1)S(1)} %copy-done.30, ...), custom_call_target="tpu_custom_call" | custom-call | flops 5720000000 | bytes 100000 | tf_op jit(solution)/shard_map/expert_weight_grads/pallas_call | solution.py:973
  323.5 8.9 %attend_backward.6 = (bf16[1152,384]{1,0:T(8,128)(2,1)}, f32[384,384]{1,0:T(8,128)S(1)}, f32[144,576]{1,0:T(8,128)S(1)}, f32[8,128]{1,0:T(8,128)S(1)}) custom-call(bf16[1152,384]{1,0:T(8,128)(2,1)} %copy-done, bf16[1152,1152]{1,0:T(8,128)(2,1)} %get-tuple-element.244.refs_1_.refs_2_.refs_3_, bf16[1152,1152]{1,0:T(8,128)(2,1)} %get-tuple-element.244.refs_1_.refs_2_.refs_3_, ...), custom_call_target="tpu_custom_call" | custom-call | flops 4400000000 | bytes 100000 | tf_op jit(solution)/shard_map/attend_backward/pallas_call | solution.py:157
  339.0 9.0 %attend_backward.7 = (bf16[1152,384]{1,0:T(8,128)(2,1)}, f32[384,384]{1,0:T(8,128)S(1)}, f32[144,576]{1,0:T(8,128)S(1)}, f32[8,128]{1,0:T(8,128)S(1)}) custom-call(bf16[1152,384]{1,0:T(8,128)(2,1)} %copy-done, bf16[1152,1152]{1,0:T(8,128)(2,1)} %get-tuple-element.244.refs_1_.refs_2_.refs_3_, bf16[1152,1152]{1,0:T(8,128)(2,1)} %get-tuple-element.244.refs_1_.refs_2_.refs_3_, ...), custom_call_target="tpu_custom_call" | custom-call | flops 4400000000 | bytes 100000 | tf_op jit(solution)/shard_map/attend_backward/pallas_call | solution.py:157
  355.4 8.8 %attend_backward.8 = (bf16[1152,384]{1,0:T(8,128)(2,1)}, f32[384,384]{1,0:T(8,128)S(1)}, f32[144,576]{1,0:T(8,128)S(1)}, f32[8,128]{1,0:T(8,128)S(1)}) custom-call(bf16[1152,384]{1,0:T(8,128)(2,1)} %copy-done, bf16[1152,1152]{1,0:T(8,128)(2,1)} %get-tuple-element.244.refs_1_.refs_2_.refs_3_, bf16[1152,1152]{1,0:T(8,128)(2,1)} %get-tuple-element.244.refs_1_.refs_2_.refs_3_, ...), custom_call_target="tpu_custom_call" | custom-call | flops 4400000000 | bytes 100000 | tf_op jit(solution)/shard_map/attend_backward/pallas_call | solution.py:157
  373.7 9.1 %attend_backward.9 = (bf16[1152,384]{1,0:T(8,128)(2,1)}, bf16[384,384]{1,0:T(8,128)(2,1)S(1)}, f32[144,576]{1,0:T(8,128)S(1)}, f32[8,128]{1,0:T(8,128)S(1)}) custom-call(bf16[1152,384]{1,0:T(8,128)(2,1)} %window_grads.3.refs_0_.refs_15_, bf16[1152,1152]{1,0:T(8,128)(2,1)} %get-tuple-element.264.refs_1_.refs_2_.refs_3_, ...), custom_call_target="tpu_custom_call" | custom-call | flops 4400000000 | bytes 100000 | tf_op jit(solution)/shard_map/attend_backward/pallas_call | solution.py:157
  382.9 7.4 %collective-permute-done.72 = bf16[192,768]{1,0:T(8,128)(2,1)S(1)} collective-permute-done((bf16[192,768]{1,0:T(8,128)(2,1)S(1)}, bf16[192,768]{1,0:T(8,128)(2,1)S(1)}, u32[]{:S(2)}, u32[]{:S(2)}) %collective-permute-start.72) | collective-permute-done | bytes 294944 | tf_op jit(solution)/shard_map/ppermute | solution.py:1301
  404.2 9.1 %attend_backward.10 = (bf16[1152,384]{1,0:T(8,128)(2,1)}, bf16[384,384]{1,0:T(8,128)(2,1)S(1)}, f32[144,576]{1,0:T(8,128)S(1)}, f32[8,128]{1,0:T(8,128)S(1)}) custom-call(bf16[1152,384]{1,0:T(8,128)(2,1)} %window_grads.3.refs_0_.refs_15_, bf16[1152,1152]{1,0:T(8,128)(2,1)} %get-tuple-element.264.refs_1_.refs_2_.refs_3_, ...), custom_call_target="tpu_custom_call" | custom-call | flops 220000000 | bytes 100000 | tf_op jit(solution)/shard_map/attend_backward/pallas_call | solution.py:157
  413.3 9.3 %attend_backward.11 = (bf16[1152,384]{1,0:T(8,128)(2,1)}, bf16[384,384]{1,0:T(8,128)(2,1)S(1)}, f32[144,576]{1,0:T(8,128)S(1)}, f32[8,128]{1,0:T(8,128)S(1)}) custom-call(bf16[1152,384]{1,0:T(8,128)(2,1)} %window_grads.3.refs_0_.refs_15_, bf16[1152,1152]{1,0:T(8,128)(2,1)} %get-tuple-element.264.refs_1_.refs_2_.refs_3_, ...), custom_call_target="tpu_custom_call" | custom-call | flops 220000000 | bytes 100000 | tf_op jit(solution)/shard_map/attend_backward/pallas_call | solution.py:157
  422.6 5.3 %collective-permute-done.51.refs_17_.refs_1_ = bf16[2,384,384]{2,1,0:T(8,128)(2,1)S(1)} collective-permute-done((bf16[2,384,384]{2,1,0:T(8,128)(2,1)S(1)}, bf16[2,384,384]{2,1,0:T(8,128)(2,1)S(1)}, u32[]{:S(2)}, u32[]{:S(2)}) %collective-permute-start.51) | collective-permute-done | bytes 589856 | tf_op jit(solution)/shard_map/ppermute | solution.py:1301
  439.5 5.2 %input_grad.3 = (f32[576,384]{1,0:T(8,128)S(1)}, bf16[576,384]{1,0:T(8,128)(2,1)}) custom-call(bf16[1152,384]{1,0:T(8,128)(2,1)} %get-tuple-element.269.refs_0_, bf16[1152,384]{1,0:T(8,128)(2,1)} %get-tuple-element.276.refs_1_, bf16[1152,384]{1,0:T(8,128)(2,1)} %get-tuple-element.280.refs_2_, bf16[384,1152]{1,0:T(8,128)(2,1)} %get-tuple-element.161.refs_2_.refs_3_, ...), custom_call_target="tpu_custom_call" | custom-call | flops 2200000000 | bytes 100000 | tf_op jit(solution)/shard_map/input_grad/pallas_call | solution.py:157
  464.1 9.1 %collective-permute-done.52 = bf16[576,384]{1,0:T(8,128)(2,1)} collective-permute-done((bf16[576,384]{1,0:T(8,128)(2,1)}, bf16[576,384]{1,0:T(8,128)(2,1)}, u32[]{:S(2)}, u32[]{:S(2)}) %collective-permute-start.52) | collective-permute-done | bytes 442400 | tf_op jit(solution)/shard_map/ppermute | solution.py:38
  481.4 6.8 %bias_network_back.1 = (f32[3,512]{1,0:T(4,128)S(1)}, f32[512,12]{1,0:T(8,128)S(1)}) custom-call(f32[40,384]{1,0:T(8,128)S(1)} %add_halves.17.refs_0_.refs_5_, f32[3,512]{1,0:T(4,128)S(1)} %copy-done.15, f32[512,12]{1,0:T(8,128)S(1)} %copy.65.refs_1_.refs_2_), custom_call_target="tpu_custom_call" | custom-call | flops 88000000 | bytes 100000 | tf_op jit(solution)/shard_map/bias_network_back/pallas_call | solution.py:157
  (537 shorter events, 197.2 us)
Async XLA Ops:
  9.6 22.4 %all-to-all-start = ((bf16[8,48,512]{2,1,0:T(8,128)(2,1)}), bf16[8,48,512]{2,1,0:T(8,128)(2,1)}, u32[]{:S(2)}, u32[]{:S(2)}) async-start(bf16[8,48,512]{2,1,0:T(8,128)(2,1)} %broadcast_in_dim.211), calls=%async_computation | async-start | bytes 786432 | tf_op jit(solution)/shard_map/all_to_all | solution.py:1227
  16.9 177.6 %all-gather.2.cloned.1.call-start = ((), (), s32[]{:S(2)}) async-start(), calls=%async_computation.1 | async-start | bytes 2654208 | tf_op jit(solution)/shard_map/all_gather | solution.py:1539
  19.1 24.8 %collective-permute-start = (bf16[2,576,384]{2,1,0:T(8,128)(2,1)}, bf16[2,576,384]{2,1,0:T(8,128)(2,1)}, u32[]{:S(2)}, u32[]{:S(2)}) collective-permute-start(bf16[2,576,384]{2,1,0:T(8,128)(2,1)} %slice.185), channel_id=1, source_target_pairs={{0,3},{1,0},{2,1},{3,2},{4,7},{5,4},{6,5},{7,6},{8,11},{9,8},{10,9... | collective-permute-start | bytes 2654216 | tf_op jit(solution)/shard_map/ppermute | solution.py:38
  34.2 30.4 %collective-permute-start.2 = (bf16[384,512]{1,0:T(8,128)(2,1)}, bf16[384,512]{1,0:T(8,128)(2,1)}, u32[]{:S(2)}, u32[]{:S(2)}) collective-permute-start(bf16[384,512]{1,0:T(8,128)(2,1)} %bitcast.4.refs_0_.refs_2_.refs_1_), channel_id=1, source_target_pairs={{0,1},{1,0},{2,3},{3,2},{4,5},{5,4},{6,7},{7,6},{8,9},{9,8},{10,11... | collective-permute-start | bytes 1179656 | tf_op jit(solution)/shard_map/ppermute | solution.py:1301
  34.4 29.4 %collective-permute-start.4 = (bf16[2,384,384]{2,1,0:T(8,128)(2,1)S(1)}, bf16[2,384,384]{2,1,0:T(8,128)(2,1)S(1)}, u32[]{:S(2)}, u32[]{:S(2)}) collective-permute-start(bf16[2,384,384]{2,1,0:T(8,128)(2,1)S(1)} %hold.3), channel_id=1, source_target_pairs={{0,16},{4,20},{8,24},{12,28},{16,0},{20,4},{24,8},{28,12},{1,17},{... | collective-permute-start | bytes 1769480 | tf_op jit(solution)/shard_map/ppermute | solution.py:1301
  63.9 31.0 %collective-permute-start.6 = (bf16[2,384,384]{2,1,0:T(8,128)(2,1)S(1)}, bf16[2,384,384]{2,1,0:T(8,128)(2,1)}, u32[]{:S(2)}, u32[]{:S(2)}) collective-permute-start(bf16[2,384,384]{2,1,0:T(8,128)(2,1)S(1)} %hold.4), channel_id=1, source_target_pairs={{0,16},{4,20},{8,24},{12,28},{16,0},{20,4},{24,8},{28,12},{1,17},{... | collective-permute-start | bytes 1769480 | tf_op jit(solution)/shard_map/ppermute | solution.py:1301
  64.0 30.9 %collective-permute-start.7 = (bf16[2,384,384]{2,1,0:T(8,128)(2,1)S(1)}, bf16[2,384,384]{2,1,0:T(8,128)(2,1)}, u32[]{:S(2)}, u32[]{:S(2)}) collective-permute-start(bf16[2,384,384]{2,1,0:T(8,128)(2,1)S(1)} %collective-permute-done.4.refs_11_.refs_1_.refs_9_.refs_8_), channel_id=1, source_target_pairs={{0,2},{1,3},{2,0},{3,1},{4,6},{5,7},{6,4},{7,5},{8,10},{9,11},{10,... | collective-permute-start | bytes 1769480 | tf_op jit(solution)/shard_map/ppermute | solution.py:1301
  107.4 24.0 %collective-permute-start.14 = (bf16[2,384,384]{2,1,0:T(8,128)(2,1)}, bf16[2,384,384]{2,1,0:T(8,128)(2,1)S(1)}, u32[]{:S(2)}, u32[]{:S(2)}) collective-permute-start(bf16[2,384,384]{2,1,0:T(8,128)(2,1)} %collective-permute-done.6.refs_9_.refs_13_.refs_12_), channel_id=1, source_target_pairs={{0,2},{1,3},{2,0},{3,1},{4,6},{5,7},{6,4},{7,5},{8,10},{9,11},{10,... | collective-permute-start | bytes 1769480 | tf_op jit(solution)/shard_map/ppermute | solution.py:1301
  114.3 23.5 %collective-permute-start.9 = (bf16[384,384]{1,0:T(8,128)(2,1)S(1)}, bf16[384,384]{1,0:T(8,128)(2,1)S(1)}, u32[]{:S(2)}, u32[]{:S(2)}) collective-permute-start(bf16[384,384]{1,0:T(8,128)(2,1)S(1)} %copy-done.36), channel_id=1, source_target_pairs={{0,8},{4,12},{8,0},{12,4},{16,24},{20,28},{24,16},{28,20},{1,9},{5... | collective-permute-start | bytes 884744 | tf_op jit(solution)/shard_map/ppermute | solution.py:1301
  144.9 22.7 %collective-permute-start.22 = (bf16[384,384]{1,0:T(8,128)(2,1)S(1)}, bf16[384,384]{1,0:T(8,128)(2,1)S(1)}, u32[]{:S(2)}, u32[]{:S(2)}) collective-permute-start(bf16[384,384]{1,0:T(8,128)(2,1)S(1)} %get-tuple-element.187), channel_id=1, source_target_pairs={{0,8},{4,12},{8,0},{12,4},{16,24},{20,28},{24,16},{28,20},{1,9},{5... | collective-permute-start | bytes 884744 | tf_op jit(solution)/shard_map/ppermute | solution.py:1301
  145.8 29.2 %collective-permute-start.23 = (bf16[384,384]{1,0:T(8,128)(2,1)S(1)}, bf16[384,384]{1,0:T(8,128)(2,1)S(1)}, u32[]{:S(2)}, u32[]{:S(2)}) collective-permute-start(bf16[384,384]{1,0:T(8,128)(2,1)S(1)} %get-tuple-element.188), channel_id=1, source_target_pairs={{0,12},{4,8},{8,4},{12,0},{16,28},{20,24},{24,20},{28,16},{1,13},{... | collective-permute-start | bytes 884744 | tf_op jit(solution)/shard_map/ppermute | solution.py:1301
  164.1 26.8 %collective-permute-start.18 = (bf16[384,384]{1,0:T(8,128)(2,1)S(1)}, bf16[384,384]{1,0:T(8,128)(2,1)S(1)}, u32[]{:S(2)}, u32[]{:S(2)}) collective-permute-start(bf16[384,384]{1,0:T(8,128)(2,1)S(1)} %get-tuple-element.180), channel_id=1, source_target_pairs={{0,4},{4,0},{8,12},{12,8},{16,20},{20,16},{24,28},{28,24},{1,5},{5... | collective-permute-start | bytes 884744 | tf_op jit(solution)/shard_map/ppermute | solution.py:1301
  164.2 29.5 %collective-permute-start.19 = (bf16[384,384]{1,0:T(8,128)(2,1)S(1)}, bf16[384,384]{1,0:T(8,128)(2,1)S(1)}, u32[]{:S(2)}, u32[]{:S(2)}) collective-permute-start(bf16[384,384]{1,0:T(8,128)(2,1)S(1)} %get-tuple-element.181), channel_id=1, source_target_pairs={{0,8},{4,12},{8,0},{12,4},{16,24},{20,28},{24,16},{28,20},{1,9},{5... | collective-permute-start | bytes 884744 | tf_op jit(solution)/shard_map/ppermute | solution.py:1301
  165.1 29.4 %collective-permute-start.20 = (bf16[384,384]{1,0:T(8,128)(2,1)S(1)}, bf16[384,384]{1,0:T(8,128)(2,1)}, u32[]{:S(2)}, u32[]{:S(2)}) collective-permute-start(bf16[384,384]{1,0:T(8,128)(2,1)S(1)} %get-tuple-element.182), channel_id=1, source_target_pairs={{0,12},{4,8},{8,4},{12,0},{16,28},{20,24},{24,20},{28,16},{1,13},{... | collective-permute-start | bytes 884744 | tf_op jit(solution)/shard_map/ppermute | solution.py:1301
  257.8 23.3 %collective-permute-start.37 = (bf16[384,384]{1,0:T(8,128)(2,1)}, bf16[384,384]{1,0:T(8,128)(2,1)}, u32[]{:S(2)}, u32[]{:S(2)}) collective-permute-start(bf16[384,384]{1,0:T(8,128)(2,1)} %get-tuple-element.221), channel_id=1, source_target_pairs={{0,4},{4,0},{8,12},{12,8},{16,20},{20,16},{24,28},{28,24},{1,5},{5... | collective-permute-start | bytes 884744 | tf_op jit(solution)/shard_map/ppermute | solution.py:1301
  257.9 23.3 %collective-permute-start.38 = (bf16[384,384]{1,0:T(8,128)(2,1)}, bf16[384,384]{1,0:T(8,128)(2,1)}, u32[]{:S(2)}, u32[]{:S(2)}) collective-permute-start(bf16[384,384]{1,0:T(8,128)(2,1)} %get-tuple-element.222), channel_id=1, source_target_pairs={{0,8},{4,12},{8,0},{12,4},{16,24},{20,28},{24,16},{28,20},{1,9},{5... | collective-permute-start | bytes 884744 | tf_op jit(solution)/shard_map/ppermute | solution.py:1301
  259.1 22.1 %collective-permute-start.39 = (bf16[384,384]{1,0:T(8,128)(2,1)}, bf16[384,384]{1,0:T(8,128)(2,1)}, u32[]{:S(2)}, u32[]{:S(2)}) collective-permute-start(bf16[384,384]{1,0:T(8,128)(2,1)} %get-tuple-element.223), channel_id=1, source_target_pairs={{0,12},{4,8},{8,4},{12,0},{16,28},{20,24},{24,20},{28,16},{1,13},{... | collective-permute-start | bytes 884744 | tf_op jit(solution)/shard_map/ppermute | solution.py:1301
  278.8 30.9 %collective-permute-start.40 = (bf16[2,2,2,384,384]{4,3,2,1,0:T(8,128)(2,1)}, bf16[2,2,2,384,384]{4,3,2,1,0:T(8,128)(2,1)}, u32[]{:S(2)}, u32[]{:S(2)}) collective-permute-start(bf16[2,2,2,384,384]{4,3,2,1,0:T(8,128)(2,1)} %get-tuple-element.233), channel_id=1, source_target_pairs={{0,1},{1,0},{2,3},{3,2},{4,5},{5,4},{6,7},{7,6},{8,9},{9,8},{10,11... | collective-permute-start | bytes 7077896 | tf_op jit(solution)/shard_map/ppermute | solution.py:1301
  305.3 45.8 %collective-permute-start.44 = (bf16[2,2,2,384,384]{4,3,2,1,0:T(8,128)(2,1)}, bf16[2,2,2,384,384]{4,3,2,1,0:T(8,128)(2,1)}, u32[]{:S(2)}, u32[]{:S(2)}) collective-permute-start(bf16[2,2,2,384,384]{4,3,2,1,0:T(8,128)(2,1)} %get-tuple-element.252), channel_id=1, source_target_pairs={{0,1},{1,0},{2,3},{3,2},{4,5},{5,4},{6,7},{7,6},{8,9},{9,8},{10,11... | collective-permute-start | bytes 7077896 | tf_op jit(solution)/shard_map/ppermute | solution.py:1301
  306.0 26.5 %collective-permute-start.43 = (bf16[2,192,768]{2,1,0:T(8,128)(2,1)S(1)}, bf16[2,192,768]{2,1,0:T(8,128)(2,1)S(1)}, u32[]{:S(2)}, u32[]{:S(2)}) collective-permute-start(bf16[2,192,768]{2,1,0:T(8,128)(2,1)S(1)} %pad_maximum_fusion.5), channel_id=1, source_target_pairs={{0,12},{4,8},{8,4},{12,0},{16,28},{20,24},{24,20},{28,16},{1,13},{... | collective-permute-start | bytes 1769480 | tf_op jit(solution)/shard_map/ppermute | solution.py:1301
  306.8 27.7 %collective-permute-start.42 = (bf16[2,192,768]{2,1,0:T(8,128)(2,1)S(1)}, bf16[2,192,768]{2,1,0:T(8,128)(2,1)S(1)}, u32[]{:S(2)}, u32[]{:S(2)}) collective-permute-start(bf16[2,192,768]{2,1,0:T(8,128)(2,1)S(1)} %pad_maximum_fusion.4), channel_id=1, source_target_pairs={{0,8},{4,12},{8,0},{12,4},{16,24},{20,28},{24,16},{28,20},{1,9},{5... | collective-permute-start | bytes 1769480 | tf_op jit(solution)/shard_map/ppermute | solution.py:1301
  313.5 34.5 %collective-permute-start.45 = (bf16[2,1,2,384,384]{4,3,2,1,0:T(8,128)(2,1)}, bf16[2,1,2,384,384]{4,3,2,1,0:T(8,128)(2,1)}, u32[]{:S(2)}, u32[]{:S(2)}) collective-permute-start(bf16[2,1,2,384,384]{4,3,2,1,0:T(8,128)(2,1)} %get-tuple-element.242.refs_10_), channel_id=1, source_target_pairs={{0,2},{1,3},{2,0},{3,1},{4,6},{5,7},{6,4},{7,5},{8,10},{9,11},{10,... | collective-permute-start | bytes 3538952 | tf_op jit(solution)/shard_map/ppermute | solution.py:1301
  332.4 39.5 %collective-permute-start.48 = (bf16[576,384]{1,0:T(8,128)(2,1)S(1)}, bf16[576,384]{1,0:T(8,128)(2,1)S(1)}, u32[]{:S(2)}, u32[]{:S(2)}) collective-permute-start(bf16[576,384]{1,0:T(8,128)(2,1)S(1)} %get-tuple-element.403), channel_id=1, source_target_pairs={{0,3},{1,0},{2,1},{3,2},{4,7},{5,4},{6,5},{7,6},{8,11},{9,8},{10,9... | collective-permute-start | bytes 1327112 | tf_op jit(solution)/shard_map/ppermute | solution.py:38
  337.8 26.4 %collective-permute-start.46 = (bf16[192,768]{1,0:T(8,128)(2,1)S(1)}, bf16[192,768]{1,0:T(8,128)(2,1)S(1)}, u32[]{:S(2)}, u32[]{:S(2)}) collective-permute-start(bf16[192,768]{1,0:T(8,128)(2,1)S(1)} %get-tuple-element.258), channel_id=1, source_target_pairs={{0,16},{4,20},{8,24},{12,28},{16,0},{20,4},{24,8},{28,12},{1,17},{... | collective-permute-start | bytes 884744 | tf_op jit(solution)/shard_map/ppermute | solution.py:1301
  354.8 41.2 %collective-permute-start.49 = (bf16[2,1,2,384,384]{4,3,2,1,0:T(8,128)(2,1)}, bf16[2,1,2,384,384]{4,3,2,1,0:T(8,128)(2,1)S(1)}, u32[]{:S(2)}, u32[]{:S(2)}) collective-permute-start(bf16[2,1,2,384,384]{4,3,2,1,0:T(8,128)(2,1)} %get-tuple-element.256.refs_13_), channel_id=1, source_target_pairs={{0,2},{1,3},{2,0},{3,1},{4,6},{5,7},{6,4},{7,5},{8,10},{9,11},{10,... | collective-permute-start | bytes 3538952 | tf_op jit(solution)/shard_map/ppermute | solution.py:1301
  364.3 26.0 %collective-permute-start.72 = (bf16[192,768]{1,0:T(8,128)(2,1)S(1)}, bf16[192,768]{1,0:T(8,128)(2,1)S(1)}, u32[]{:S(2)}, u32[]{:S(2)}) collective-permute-start(bf16[192,768]{1,0:T(8,128)(2,1)S(1)} %add_halves.9.refs_4_), channel_id=1, source_target_pairs={{0,2},{1,3},{2,0},{3,1},{4,6},{5,7},{6,4},{7,5},{8,10},{9,11},{10,... | collective-permute-start | bytes 884744 | tf_op jit(solution)/shard_map/ppermute | solution.py:1301
  365.8 35.9 %collective-permute-start.73 = (bf16[192,768]{1,0:T(8,128)(2,1)S(1)}, bf16[192,768]{1,0:T(8,128)(2,1)S(1)}, u32[]{:S(2)}, u32[]{:S(2)}) collective-permute-start(bf16[192,768]{1,0:T(8,128)(2,1)S(1)} %add_halves.9.refs_4_), channel_id=1, source_target_pairs={{0,1},{1,0},{2,3},{3,2},{4,5},{5,4},{6,7},{7,6},{8,9},{9,8},{10,11... | collective-permute-start | bytes 884744 | tf_op jit(solution)/shard_map/ppermute | solution.py:1301
  365.8 28.8 %collective-permute-start.50 = (bf16[2,384,384]{2,1,0:T(8,128)(2,1)S(1)}, bf16[2,384,384]{2,1,0:T(8,128)(2,1)S(1)}, u32[]{:S(2)}, u32[]{:S(2)}) collective-permute-start(bf16[2,384,384]{2,1,0:T(8,128)(2,1)S(1)} %get-tuple-element.255.refs_2_), channel_id=1, source_target_pairs={{0,16},{4,20},{8,24},{12,28},{16,0},{20,4},{24,8},{28,12},{1,17},{... | collective-permute-start | bytes 1769480 | tf_op jit(solution)/shard_map/ppermute | solution.py:1301
  399.9 28.0 %collective-permute-start.51 = (bf16[2,384,384]{2,1,0:T(8,128)(2,1)S(1)}, bf16[2,384,384]{2,1,0:T(8,128)(2,1)S(1)}, u32[]{:S(2)}, u32[]{:S(2)}) collective-permute-start(bf16[2,384,384]{2,1,0:T(8,128)(2,1)S(1)} %get-tuple-element.275.refs_15_), channel_id=1, source_target_pairs={{0,16},{4,20},{8,24},{12,28},{16,0},{20,4},{24,8},{28,12},{1,17},{... | collective-permute-start | bytes 1769480 | tf_op jit(solution)/shard_map/ppermute | solution.py:1301
  402.7 42.0 %collective-permute-start.60 = (bf16[2,384,384]{2,1,0:T(8,128)(2,1)S(1)}, bf16[2,384,384]{2,1,0:T(8,128)(2,1)S(1)}, u32[]{:S(2)}, u32[]{:S(2)}) collective-permute-start(bf16[2,384,384]{2,1,0:T(8,128)(2,1)S(1)} %add_halves.10.refs_2_.refs_1_), channel_id=1, source_target_pairs={{0,2},{1,3},{2,0},{3,1},{4,6},{5,7},{6,4},{7,5},{8,10},{9,11},{10,... | collective-permute-start | bytes 1769480 | tf_op jit(solution)/shard_map/ppermute | solution.py:1301
  453.3 38.6 %collective-permute-start.69 = (bf16[2,384,384]{2,1,0:T(8,128)(2,1)}, bf16[2,384,384]{2,1,0:T(8,128)(2,1)}, u32[]{:S(2)}, u32[]{:S(2)}) collective-permute-start(bf16[2,384,384]{2,1,0:T(8,128)(2,1)} %add_halves.11.refs_5_.refs_1_), channel_id=1, source_target_pairs={{0,2},{1,3},{2,0},{3,1},{4,6},{5,7},{6,4},{7,5},{8,10},{9,11},{10,... | collective-permute-start | bytes 1769480 | tf_op jit(solution)/shard_map/ppermute | solution.py:1301
  454.6 40.8 %collective-permute-start.70 = (bf16[2,384,384]{2,1,0:T(8,128)(2,1)}, bf16[2,384,384]{2,1,0:T(8,128)(2,1)}, u32[]{:S(2)}, u32[]{:S(2)}) collective-permute-start(bf16[2,384,384]{2,1,0:T(8,128)(2,1)} %add_halves.11.refs_5_.refs_1_), channel_id=1, source_target_pairs={{0,1},{1,0},{2,3},{3,2},{4,5},{5,4},{6,7},{7,6},{8,9},{9,8},{10,11... | collective-permute-start | bytes 1769480 | tf_op jit(solution)/shard_map/ppermute | solution.py:1301
  (163 other events, 1439.4 us)
Sparse Core Ops, SparseCore 0:
  104.5 77.1 all-gather.1

commit v5 on v4

--- a/solution.py
+++ b/solution.py
@@ -13,7 +13,7 @@
 LANES = 128
 SHEAR = 384
 ZONES = 16
-UNROLL = 4
+UNROLL = 8
 COST_SCALE = 0.4
 TILE_HEADS = LANES // HEAD_DIM
 
@@ -639,6 +639,7 @@
 
 
 CHUNK = 576
+WIDE_CHUNK = 1152
 
 
 def pack_rows(dest_row_ref, rows_ref, out_refs):
@@ -725,22 +726,22 @@
     returned = jnp.concatenate([ref[...] for ref in returned_refs], 0)
     tokens, channels = resid_ref.shape
     tiles = tiles_of(channels)
-    lane = lax.broadcasted_iota(jnp.int32, (CHUNK, LANES), 1)
+    lane = lax.broadcasted_iota(jnp.int32, (WIDE_CHUNK, LANES), 1)
 
     def combine(c, carry):
-        rows = rows_at(c * CHUNK, CHUNK)
+        rows = rows_at(c * WIDE_CHUNK, WIDE_CHUNK)
         picked = unpack_rows(dest_col_ref[rows, :], returned)
         picked_scr[rows, :] = picked
         gate = aux_ref[rows, :][:, LANES - 1 : LANES]
         unit, inverse = normalised(gate * picked)
         unit_scr[rows, :] = unit
-        inverse_scr[rows, :] = jnp.broadcast_to(inverse, (CHUNK, LANES))
+        inverse_scr[rows, :] = jnp.broadcast_to(inverse, (WIDE_CHUNK, LANES))
         resid = resid_ref[rows, :] + unit * small_ref[0:1, :] + small_ref[1:2, :]
         for t, lanes in enumerate(tiles):
             token_scr[t, rows, :] = resid[:, lanes]
         return carry
 
-    lax.fori_loop(0, tokens // CHUNK, combine, 0)
+    lax.fori_loop(0, tokens // WIDE_CHUNK, combine, 0)
     pairs = band_cols // 2
     for i in range(WINDOW_SIDE // 2):
         for k in range(4):
@@ -768,7 +769,7 @@
                 ]
 
     def spread(c, carry):
-        rows = rows_at(c * CHUNK, CHUNK)
+        rows = rows_at(c * WIDE_CHUNK, WIDE_CHUNK)
         back = jnp.concatenate([token_scr[t, rows, :] for t in range(len(tiles))], 1)
         dresid_ref[rows, :] = back
         unit = unit_scr[rows, :]
@@ -784,7 +785,7 @@
         dlogits_ref[rows, :] = (probs * (chosen - gate) * dgate).astype(BF)
         return carry
 
-    lax.fori_loop(0, tokens // CHUNK, spread, 0)
+    lax.fori_loop(0, tokens // WIDE_CHUNK, spread, 0)
     pack_rows(dest_row_ref, back_scr, sent_refs)
 
 
@@ -809,7 +810,7 @@
     sums_ref[...] = jnp.zeros_like(sums_ref)
 
     def step(c, carry):
-        rows = rows_at(c * CHUNK, CHUNK)
+        rows = rows_at(c * WIDE_CHUNK, WIDE_CHUNK)
         back = dresid_ref[rows, :] + unpack_rows(dest_col_ref[rows, :], sent)
         back = back + mm_nt(dlogits_ref[rows, :], router_ref[...])
         done_ref[rows, :] = back
@@ -824,7 +825,7 @@
         rows_ref[rows, :] = mm_nt(low, weight_ref[...]).astype(BF)
         return carry
 
-    lax.fori_loop(0, tokens // CHUNK, step, 0)
+    lax.fori_loop(0, tokens // WIDE_CHUNK, step, 0)
 
 
 def dense_body(*refs):

time: 512 us -> 505 us (0.986)
  Pallas kernels: 276 us -> 268 us
    pallas_call x41, Pallas kernels: 182 us -> 175 us  [call_kernel(): pl.pallas_call(skipping(body, len(args), len(after)), name=name, grid=(1,...]
  transfers between devices with their start and end apart: 77 -> 77, of which waited for: 16 -> 16; matrix products, arithmetic and copies ran while one was open for 7% -> 8% of each run, Pallas kernels for 52% -> 52%
where the time goes in v5:
time: 505 us; the launch traced here: 501 us
  Pallas kernels  268 us (53%)
  waiting for transfers between devices  80.1 us (16%)
  starting transfers between devices  75.2 us (15%)
  local copies, waits for them, and re-layouts  44.8 us (9%)
  other arithmetic  16.2 us (3%)
  between operations  16.2 us (3%)
    pallas_call x41, Pallas kernels, call_kernel(): pl.pallas_call(skipping(body, len(args), len(after)), name=name, grid=(1,...  175 us
    pallas_call x8, Pallas kernels, call_expert(): pl.pallas_call(skipping(body, 1 + len(args), len(after)), name=name, grid...  79 us
    ppermute x68, starting transfers between devices, crossed(): return lax.ppermute(array, axis, [(i, i ^ bit) for i in range(count)])  63.6 us
    ppermute x68, waiting for transfers between devices, crossed(): return lax.ppermute(array, axis, [(i, i ^ bit) for i in range(count)])  52.4 us
    ppermute x7, waiting for transfers between devices, passed_along(): lax.ppermute(array, axis, [(i, (i + by) % count) for i in range(count)])  27.6 us
    unnamed x241, local copies, waits for them, and re-layouts  23.1 us
  transfers between devices with their start and end apart: 77, of which 16 were waited for; matrix products, arithmetic and copies ran while one was open for 8% of the time, Pallas kernels for 52%

profile of v5, /device:TPU:0, one launch (start us, length us, event | category | flops | bytes accessed | tf_op | source)
XLA Modules:
  0.0 500.5 jit_solution(4566833372198530097)
XLA Ops:
  9.6 7.3 %all-to-all-start = ((bf16[8,48,512]{2,1,0:T(8,128)(2,1)}), bf16[8,48,512]{2,1,0:T(8,128)(2,1)}, u32[]{:S(2)}, u32[]{:S(2)}) async-start(bf16[8,48,512]{2,1,0:T(8,128)(2,1)} %broadcast_in_dim.211), calls=%async_computation | async-start | bytes 786432 | tf_op jit(solution)/shard_map/all_to_all | solution.py:1228
  46.5 6.7 %spread_bias.1 = (f32[3,144,576]{2,1,0:T(8,128)S(1)}, f32[3,144,576]{2,1,0:T(8,128)}) custom-call(f32[3,512]{1,0:T(4,128)S(1)} %pad_maximum_fusion.11.refs_0_.refs_1_, f32[512,12]{1,0:T(8,128)S(1)} %copy.65.refs_1_.refs_2_, bf16[384,512]{1,0:T(8,128)(2,1)} %collective-permute-done.1.refs_1_.refs_2_, s32[1,1152]{1,0:T(1,128)S(1)} %copy-done.75), custom_call_target="tpu_custom_call" | custom-call | flops 2200000000 | bytes 100000 | tf_op jit(solution)/shard_map/spread_bias/pallas_call | solution.py:157
  53.1 11.0 %collective-permute-done.4.refs_11_.refs_1_.refs_9_.refs_8_ = bf16[2,384,384]{2,1,0:T(8,128)(2,1)S(1)} collective-permute-done((bf16[2,384,384]{2,1,0:T(8,128)(2,1)S(1)}, bf16[2,384,384]{2,1,0:T(8,128)(2,1)S(1)}, u32[]{:S(2)}, u32[]{:S(2)}) %collective-permute-start.4) | collective-permute-done | bytes 589856 | tf_op jit(solution)/shard_map/ppermute | solution.py:1302
  67.5 11.0 %attend_forward.2 = (bf16[576,384]{1,0:T(8,128)(2,1)S(1)}, bf16[576,384]{1,0:T(8,128)(2,1)S(1)}, bf16[1152,384]{1,0:T(8,128)(2,1)}, bf16[1152,1152]{1,0:T(8,128)(2,1)}, f32[1152,768]{1,0:T(8,128)}) custom-call(bf16[1152,384]{1,0:T(8,128)(2,1)} %bitcast.86, bf16[576,384]{1,0:T(8,128)(2,1)} %get-tuple-element.407.refs_1_, ...), custom_call_target="tpu_custom_call" | custom-call | flops 7040000000 | bytes 100000 | tf_op jit(solution)/shard_map/attend_forward/pallas_call | solution.py:157
  79.2 10.8 %attend_forward.3 = (bf16[576,384]{1,0:T(8,128)(2,1)S(1)}, bf16[576,384]{1,0:T(8,128)(2,1)S(1)}, bf16[1152,384]{1,0:T(8,128)(2,1)}, bf16[1152,1152]{1,0:T(8,128)(2,1)}, f32[1152,768]{1,0:T(8,128)}) custom-call(bf16[1152,384]{1,0:T(8,128)(2,1)} %bitcast.84, bf16[576,384]{1,0:T(8,128)(2,1)} %get-tuple-element.408.refs_1_, ...), custom_call_target="tpu_custom_call" | custom-call | flops 7040000000 | bytes 100000 | tf_op jit(solution)/shard_map/attend_forward/pallas_call | solution.py:157
  93.0 5.3 %route.2 = (f32[1152,384]{1,0:T(8,128)}, bf16[1152,384]{1,0:T(8,128)(2,1)}, f32[1152,128]{1,0:T(8,128)}, bf16[1152,384]{1,0:T(8,128)(2,1)}, bf16[384,384]{1,0:T(...) custom-call(bf16[576,384]{1,0:T(8,128)(2,1)S(1)} %collective-permute-done., ...), custom_call_target="tpu_custom_call" | custom-call | flops 5280000000 | bytes 100000 | tf_op jit(solution)/shard_map/route/pallas_call | solution.py:157
  111.8 13.5 %collective-permute-done.17.refs_0_.refs_5_ = bf16[576,384]{1,0:T(8,128)(2,1)S(1)} collective-permute-done((bf16[576,384]{1,0:T(8,128)(2,1)S(1)}, bf16[576,384]{1,0:T(8,128)(2,1)S(1)}, u32[]{:S(2)}, u32[]{:S(2)}) %collective-permute-start.17) | collective-permute-done | bytes 442400 | tf_op jit(solution)/shard_map/ppermute | solution.py:38
  128.8 5.9 %collective-permute-done.9.refs_10_.refs_3_ = bf16[384,384]{1,0:T(8,128)(2,1)S(1)} collective-permute-done((bf16[384,384]{1,0:T(8,128)(2,1)S(1)}, bf16[384,384]{1,0:T(8,128)(2,1)S(1)}, u32[]{:S(2)}, u32[]{:S(2)}) %collective-permute-start.9) | collective-permute-done | bytes 294944 | tf_op jit(solution)/shard_map/ppermute | solution.py:1302
  136.4 5.3 %route.3 = (f32[1152,384]{1,0:T(8,128)}, bf16[1152,384]{1,0:T(8,128)(2,1)}, f32[1152,128]{1,0:T(8,128)}, bf16[1152,384]{1,0:T(8,128)(2,1)}, bf16[384,384]{1,0:T(...) custom-call(bf16[576,384]{1,0:T(8,128)(2,1)} %copy-done.88, ...), custom_call_target="tpu_custom_call" | custom-call | flops 5280000000 | bytes 100000 | tf_op jit(solution)/shard_map/route/pallas_call | solution.py:157
  146.3 13.6 %expert_forward.2 = (bf16[384,384]{1,0:T(8,128)(2,1)S(1)}, bf16[384,384]{1,0:T(8,128)(2,1)S(1)}, bf16[384,384]{1,0:T(8,128)(2,1)S(1)}, bf16[384,384]{1,0:T(8,128...) custom-call(s32[1]{0:T(128)} %bitcast.me_ref.refs_0_, bf16[384,384]{1,0:T(8,128)(2,1)S(1)} %copy-done.59, ...), custom_call_target="tpu_custom_call" | custom-call | flops 8360000000 | bytes 100000 | tf_op jit(solution)/shard_map/expert_forward/pallas_call | solution.py:974
  164.1 7.2 %collective-permute-done.23.refs_4_.refs_8_ = bf16[384,384]{1,0:T(8,128)(2,1)S(1)} collective-permute-done((bf16[384,384]{1,0:T(8,128)(2,1)S(1)}, bf16[384,384]{1,0:T(8,128)(2,1)S(1)}, u32[]{:S(2)}, u32[]{:S(2)}) %collective-permute-start.23) | collective-permute-done | bytes 294944 | tf_op jit(solution)/shard_map/ppermute | solution.py:1302
  172.1 14.1 %expert_forward.3 = (bf16[384,384]{1,0:T(8,128)(2,1)S(1)}, bf16[384,384]{1,0:T(8,128)(2,1)}, bf16[384,384]{1,0:T(8,128)(2,1)}, bf16[384,384]{1,0:T(8,128)(2,1)S(...) custom-call(s32[1]{0:T(128)} %bitcast.me_ref.refs_0_, ...), custom_call_target="tpu_custom_call" | custom-call | flops 8360000000 | bytes 100000 | tf_op jit(solution)/shard_map/expert_forward/pallas_call | solution.py:974
  192.2 11.3 %merge.2 = (bf16[288,768]{1,0:T(8,128)(2,1)}, bf16[288,1536]{1,0:T(8,128)(2,1)}, bf16[288,768]{1,0:T(8,128)(2,1)}, f32[1152,384]{1,0:T(8,128)}, bf16[1152,128]{1...) custom-call(bf16[384,384]{1,0:T(8,128)(2,1)S(1)} %copy-done.74, ...), custom_call_target="tpu_custom_call" | custom-call | flops 6160000000 | bytes 100000 | tf_op jit(solution)/shard_map/merge/pallas_call | solution.py:157
  207.0 11.4 %merge.3 = (bf16[288,768]{1,0:T(8,128)(2,1)}, bf16[288,1536]{1,0:T(8,128)(2,1)}, bf16[288,768]{1,0:T(8,128)(2,1)}, f32[1152,384]{1,0:T(8,128)}, bf16[1152,128]{1...) custom-call(bf16[384,384]{1,0:T(8,128)(2,1)S(1)} %copy-done.72, ...), custom_call_target="tpu_custom_call" | custom-call | flops 6160000000 | bytes 100000 | tf_op jit(solution)/shard_map/merge/pallas_call | solution.py:157
  223.4 11.6 %expert_backward.2 = (bf16[384,384]{1,0:T(8,128)(2,1)S(1)}, bf16[384,384]{1,0:T(8,128)(2,1)S(1)}, bf16[384,384]{1,0:T(8,128)(2,1)S(1)}, bf16[384,384]{1,0:T(8,12...) custom-call(s32[1]{0:T(128)} %bitcast.me_ref.refs_0_, ...), custom_call_target="tpu_custom_call" | custom-call | flops 5280000000 | bytes 100000 | tf_op jit(solution)/shard_map/expert_backward/pallas_call | solution.py:974
  239.4 11.8 %expert_backward.3 = (bf16[384,384]{1,0:T(8,128)(2,1)S(1)}, bf16[384,384]{1,0:T(8,128)(2,1)}, bf16[384,384]{1,0:T(8,128)(2,1)}, bf16[384,384]{1,0:T(8,128)(2,1)}...) custom-call(s32[1]{0:T(128)} %bitcast.me_ref.refs_0_, ...), custom_call_target="tpu_custom_call" | custom-call | flops 5280000000 | bytes 100000 | tf_op jit(solution)/shard_map/expert_backward/pallas_call | solution.py:974
  255.4 7.0 %settle.2 = (f32[1152,384]{1,0:T(8,128)}, bf16[1152,384]{1,0:T(8,128)(2,1)}, bf16[1152,384]{1,0:T(8,128)(2,1)}, f32[8,384]{1,0:T(8,128)S(1)}) custom-call(bf16[384,384]{1,0:T(8,128)(2,1)S(1)} %get-tuple-element.202.refs_0_, bf16[384,384]{1,0:T(8,128)(2,1)S(1)} %collective-permute-done.30.refs_1_, bf16[384,384]{1,0:T(8,128)(2,1)S(1)} %collective-permute-done.31.refs_2_, ...), custom_call_target="tpu_custom_call" | custom-call | flops 3080000000 | bytes 100000 | tf_op jit(solution)/shard_map/settle/pallas_call | solution.py:157
  262.5 10.1 %expert_weight_grads.2 = (bf16[2,2,2,384,384]{4,3,2,1,0:T(8,128)(2,1)}, bf16[2,2,2,384,384]{4,3,2,1,0:T(8,128)(2,1)}, f32[4,1,384]{2,1,0:T(1,128)}) custom-call(s32[1]{0:T(128)} %bitcast.me_ref.refs_0_, bf16[384,384]{1,0:T(8,128)(2,1)S(1)} %copy-done.60, bf16[384,384]{1,0:T(8,128)(2,1)S(1)} %copy-done.24, bf16[384,384]{1,0:T(8,128)(2,1)S(1)} %copy-done.26, ...), custom_call_target="tpu_custom_call" | custom-call | flops 5720000000 | bytes 100000 | tf_op jit(solution)/shard_map/expert_weight_grads/pallas_call | solution.py:974
  275.0 7.3 %settle.3 = (f32[1152,384]{1,0:T(8,128)}, bf16[1152,384]{1,0:T(8,128)(2,1)}, bf16[1152,384]{1,0:T(8,128)(2,1)}, f32[8,384]{1,0:T(8,128)S(1)}) custom-call(bf16[384,384]{1,0:T(8,128)(2,1)S(1)} %copy-done.52, bf16[384,384]{1,0:T(8,128)(2,1)} %collective-permute-done.37.refs_1_, bf16[384,384]{1,0:T(8,128)(2,1)} %collective-permute-done.38.refs_2_, ...), custom_call_target="tpu_custom_call" | custom-call | flops 3080000000 | bytes 100000 | tf_op jit(solution)/shard_map/settle/pallas_call | solution.py:157
  282.3 5.6 %merge_weight_grad.1.refs_11_ = bf16[1536,768]{1,0:T(8,128)(2,1)} custom-call(bf16[288,1536]{1,0:T(8,128)(2,1)S(1)} %copy-done.47, bf16[288,768]{1,0:T(8,128)(2,1)S(1)} %copy-done.48, bf16[288,1536]{1,0:T(8,128)(2,1)} %get-tuple-element.238.refs_2_, bf16[288,768]{1,0:T(8,128)(2,1)S(1)} %copy-done.49, f32[8,384]{1,0:T(8,128)S(1)} %get-tuple-element.240.refs_4_.refs_10_), custom_call_target="tpu_custom_call" | custom-call | flops 2200000000 | bytes 100000 | tf_op jit(solution)/shard_map/merge_weight_grad/pallas_call | solution.py:862
  288.0 10.6 %expert_weight_grads.3 = (bf16[2,2,2,384,384]{4,3,2,1,0:T(8,128)(2,1)}, bf16[2,2,2,384,384]{4,3,2,1,0:T(8,128)(2,1)}, f32[4,1,384]{2,1,0:T(1,128)S(1)}) custom-call(s32[1]{0:T(128)} %bitcast.me_ref.refs_0_, bf16[384,384]{1,0:T(8,128)(2,1)S(1)} %copy-done.54, bf16[384,384]{1,0:T(8,128)(2,1)S(1)} %copy-done.28, bf16[384,384]{1,0:T(8,128)(2,1)S(1)} %copy-done.30, ...), custom_call_target="tpu_custom_call" | custom-call | flops 5720000000 | bytes 100000 | tf_op jit(solution)/shard_map/expert_weight_grads/pallas_call | solution.py:974
  317.3 8.7 %attend_backward.6 = (bf16[1152,384]{1,0:T(8,128)(2,1)}, f32[384,384]{1,0:T(8,128)S(1)}, f32[144,576]{1,0:T(8,128)S(1)}, f32[8,128]{1,0:T(8,128)S(1)}) custom-call(bf16[1152,384]{1,0:T(8,128)(2,1)} %copy-done, bf16[1152,1152]{1,0:T(8,128)(2,1)} %get-tuple-element.244.refs_1_.refs_2_.refs_3_, bf16[1152,1152]{1,0:T(8,128)(2,1)} %get-tuple-element.244.refs_1_.refs_2_.refs_3_, ...), custom_call_target="tpu_custom_call" | custom-call | flops 4400000000 | bytes 100000 | tf_op jit(solution)/shard_map/attend_backward/pallas_call | solution.py:157
  332.0 8.8 %attend_backward.7 = (bf16[1152,384]{1,0:T(8,128)(2,1)}, f32[384,384]{1,0:T(8,128)S(1)}, f32[144,576]{1,0:T(8,128)S(1)}, f32[8,128]{1,0:T(8,128)S(1)}) custom-call(bf16[1152,384]{1,0:T(8,128)(2,1)} %copy-done, bf16[1152,1152]{1,0:T(8,128)(2,1)} %get-tuple-element.244.refs_1_.refs_2_.refs_3_, bf16[1152,1152]{1,0:T(8,128)(2,1)} %get-tuple-element.244.refs_1_.refs_2_.refs_3_, ...), custom_call_target="tpu_custom_call" | custom-call | flops 4400000000 | bytes 100000 | tf_op jit(solution)/shard_map/attend_backward/pallas_call | solution.py:157
  349.0 8.9 %attend_backward.8 = (bf16[1152,384]{1,0:T(8,128)(2,1)}, f32[384,384]{1,0:T(8,128)S(1)}, f32[144,576]{1,0:T(8,128)S(1)}, f32[8,128]{1,0:T(8,128)S(1)}) custom-call(bf16[1152,384]{1,0:T(8,128)(2,1)} %copy-done, bf16[1152,1152]{1,0:T(8,128)(2,1)} %get-tuple-element.244.refs_1_.refs_2_.refs_3_, bf16[1152,1152]{1,0:T(8,128)(2,1)} %get-tuple-element.244.refs_1_.refs_2_.refs_3_, ...), custom_call_target="tpu_custom_call" | custom-call | flops 4400000000 | bytes 100000 | tf_op jit(solution)/shard_map/attend_backward/pallas_call | solution.py:157
  366.9 9.0 %attend_backward.9 = (bf16[1152,384]{1,0:T(8,128)(2,1)}, bf16[384,384]{1,0:T(8,128)(2,1)S(1)}, f32[144,576]{1,0:T(8,128)S(1)}, f32[8,128]{1,0:T(8,128)S(1)}) custom-call(bf16[1152,384]{1,0:T(8,128)(2,1)} %window_grads.3.refs_0_.refs_15_, bf16[1152,1152]{1,0:T(8,128)(2,1)} %get-tuple-element.264.refs_1_.refs_2_.refs_3_, ...), custom_call_target="tpu_custom_call" | custom-call | flops 4400000000 | bytes 100000 | tf_op jit(solution)/shard_map/attend_backward/pallas_call | solution.py:157
  375.9 7.1 %collective-permute-done.72 = bf16[192,768]{1,0:T(8,128)(2,1)S(1)} collective-permute-done((bf16[192,768]{1,0:T(8,128)(2,1)S(1)}, bf16[192,768]{1,0:T(8,128)(2,1)S(1)}, u32[]{:S(2)}, u32[]{:S(2)}) %collective-permute-start.72) | collective-permute-done | bytes 294944 | tf_op jit(solution)/shard_map/ppermute | solution.py:1302
  397.8 9.3 %attend_backward.10 = (bf16[1152,384]{1,0:T(8,128)(2,1)}, bf16[384,384]{1,0:T(8,128)(2,1)S(1)}, f32[144,576]{1,0:T(8,128)S(1)}, f32[8,128]{1,0:T(8,128)S(1)}) custom-call(bf16[1152,384]{1,0:T(8,128)(2,1)} %window_grads.3.refs_0_.refs_15_, bf16[1152,1152]{1,0:T(8,128)(2,1)} %get-tuple-element.264.refs_1_.refs_2_.refs_3_, ...), custom_call_target="tpu_custom_call" | custom-call | flops 220000000 | bytes 100000 | tf_op jit(solution)/shard_map/attend_backward/pallas_call | solution.py:157
  407.1 8.9 %attend_backward.11 = (bf16[1152,384]{1,0:T(8,128)(2,1)}, bf16[384,384]{1,0:T(8,128)(2,1)S(1)}, f32[144,576]{1,0:T(8,128)S(1)}, f32[8,128]{1,0:T(8,128)S(1)}) custom-call(bf16[1152,384]{1,0:T(8,128)(2,1)} %window_grads.3.refs_0_.refs_15_, bf16[1152,1152]{1,0:T(8,128)(2,1)} %get-tuple-element.264.refs_1_.refs_2_.refs_3_, ...), custom_call_target="tpu_custom_call" | custom-call | flops 220000000 | bytes 100000 | tf_op jit(solution)/shard_map/attend_backward/pallas_call | solution.py:157
  416.0 5.4 %collective-permute-done.51.refs_17_.refs_1_ = bf16[2,384,384]{2,1,0:T(8,128)(2,1)S(1)} collective-permute-done((bf16[2,384,384]{2,1,0:T(8,128)(2,1)S(1)}, bf16[2,384,384]{2,1,0:T(8,128)(2,1)S(1)}, u32[]{:S(2)}, u32[]{:S(2)}) %collective-permute-start.51) | collective-permute-done | bytes 589856 | tf_op jit(solution)/shard_map/ppermute | solution.py:1302
  433.1 5.2 %input_grad.3 = (f32[576,384]{1,0:T(8,128)S(1)}, bf16[576,384]{1,0:T(8,128)(2,1)}) custom-call(bf16[1152,384]{1,0:T(8,128)(2,1)} %get-tuple-element.269.refs_0_, bf16[1152,384]{1,0:T(8,128)(2,1)} %get-tuple-element.276.refs_1_, bf16[1152,384]{1,0:T(8,128)(2,1)} %get-tuple-element.280.refs_2_, bf16[384,1152]{1,0:T(8,128)(2,1)} %get-tuple-element.161.refs_2_.refs_3_, ...), custom_call_target="tpu_custom_call" | custom-call | flops 2200000000 | bytes 100000 | tf_op jit(solution)/shard_map/input_grad/pallas_call | solution.py:157
  457.9 9.1 %collective-permute-done.52 = bf16[576,384]{1,0:T(8,128)(2,1)} collective-permute-done((bf16[576,384]{1,0:T(8,128)(2,1)}, bf16[576,384]{1,0:T(8,128)(2,1)}, u32[]{:S(2)}, u32[]{:S(2)}) %collective-permute-start.52) | collective-permute-done | bytes 442400 | tf_op jit(solution)/shard_map/ppermute | solution.py:38
  474.9 6.8 %bias_network_back.1 = (f32[3,512]{1,0:T(4,128)S(1)}, f32[512,12]{1,0:T(8,128)S(1)}) custom-call(f32[40,384]{1,0:T(8,128)S(1)} %add_halves.17.refs_0_.refs_5_, f32[3,512]{1,0:T(4,128)S(1)} %copy-done.15, f32[512,12]{1,0:T(8,128)S(1)} %copy.65.refs_1_.refs_2_), custom_call_target="tpu_custom_call" | custom-call | flops 88000000 | bytes 100000 | tf_op jit(solution)/shard_map/bias_network_back/pallas_call | solution.py:157
  (537 shorter events, 198.9 us)
Async XLA Ops:
  9.6 22.7 %all-to-all-start = ((bf16[8,48,512]{2,1,0:T(8,128)(2,1)}), bf16[8,48,512]{2,1,0:T(8,128)(2,1)}, u32[]{:S(2)}, u32[]{:S(2)}) async-start(bf16[8,48,512]{2,1,0:T(8,128)(2,1)} %broadcast_in_dim.211), calls=%async_computation | async-start | bytes 786432 | tf_op jit(solution)/shard_map/all_to_all | solution.py:1228
  16.9 174.3 %all-gather.2.cloned.1.call-start = ((), (), s32[]{:S(2)}) async-start(), calls=%async_computation.1 | async-start | bytes 2654208 | tf_op jit(solution)/shard_map/all_gather | solution.py:1540
  19.1 25.2 %collective-permute-start = (bf16[2,576,384]{2,1,0:T(8,128)(2,1)}, bf16[2,576,384]{2,1,0:T(8,128)(2,1)}, u32[]{:S(2)}, u32[]{:S(2)}) collective-permute-start(bf16[2,576,384]{2,1,0:T(8,128)(2,1)} %slice.185), channel_id=1, source_target_pairs={{0,3},{1,0},{2,1},{3,2},{4,7},{5,4},{6,5},{7,6},{8,11},{9,8},{10,9... | collective-permute-start | bytes 2654216 | tf_op jit(solution)/shard_map/ppermute | solution.py:38
  34.5 30.4 %collective-permute-start.2 = (bf16[384,512]{1,0:T(8,128)(2,1)}, bf16[384,512]{1,0:T(8,128)(2,1)}, u32[]{:S(2)}, u32[]{:S(2)}) collective-permute-start(bf16[384,512]{1,0:T(8,128)(2,1)} %bitcast.4.refs_0_.refs_2_.refs_1_), channel_id=1, source_target_pairs={{0,1},{1,0},{2,3},{3,2},{4,5},{5,4},{6,7},{7,6},{8,9},{9,8},{10,11... | collective-permute-start | bytes 1179656 | tf_op jit(solution)/shard_map/ppermute | solution.py:1302
  34.8 29.4 %collective-permute-start.4 = (bf16[2,384,384]{2,1,0:T(8,128)(2,1)S(1)}, bf16[2,384,384]{2,1,0:T(8,128)(2,1)S(1)}, u32[]{:S(2)}, u32[]{:S(2)}) collective-permute-start(bf16[2,384,384]{2,1,0:T(8,128)(2,1)S(1)} %hold.3), channel_id=1, source_target_pairs={{0,16},{4,20},{8,24},{12,28},{16,0},{20,4},{24,8},{28,12},{1,17},{... | collective-permute-start | bytes 1769480 | tf_op jit(solution)/shard_map/ppermute | solution.py:1302
  64.2 28.7 %collective-permute-start.6 = (bf16[2,384,384]{2,1,0:T(8,128)(2,1)S(1)}, bf16[2,384,384]{2,1,0:T(8,128)(2,1)}, u32[]{:S(2)}, u32[]{:S(2)}) collective-permute-start(bf16[2,384,384]{2,1,0:T(8,128)(2,1)S(1)} %hold.4), channel_id=1, source_target_pairs={{0,16},{4,20},{8,24},{12,28},{16,0},{20,4},{24,8},{28,12},{1,17},{... | collective-permute-start | bytes 1769480 | tf_op jit(solution)/shard_map/ppermute | solution.py:1302
  64.3 28.6 %collective-permute-start.7 = (bf16[2,384,384]{2,1,0:T(8,128)(2,1)S(1)}, bf16[2,384,384]{2,1,0:T(8,128)(2,1)}, u32[]{:S(2)}, u32[]{:S(2)}) collective-permute-start(bf16[2,384,384]{2,1,0:T(8,128)(2,1)S(1)} %collective-permute-done.4.refs_11_.refs_1_.refs_9_.refs_8_), channel_id=1, source_target_pairs={{0,2},{1,3},{2,0},{3,1},{4,6},{5,7},{6,4},{7,5},{8,10},{9,11},{10,... | collective-permute-start | bytes 1769480 | tf_op jit(solution)/shard_map/ppermute | solution.py:1302
  104.1 24.2 %collective-permute-start.14 = (bf16[2,384,384]{2,1,0:T(8,128)(2,1)}, bf16[2,384,384]{2,1,0:T(8,128)(2,1)S(1)}, u32[]{:S(2)}, u32[]{:S(2)}) collective-permute-start(bf16[2,384,384]{2,1,0:T(8,128)(2,1)} %collective-permute-done.6.refs_9_.refs_13_.refs_12_), channel_id=1, source_target_pairs={{0,2},{1,3},{2,0},{3,1},{4,6},{5,7},{6,4},{7,5},{8,10},{9,11},{10,... | collective-permute-start | bytes 1769480 | tf_op jit(solution)/shard_map/ppermute | solution.py:1302
  111.2 23.5 %collective-permute-start.9 = (bf16[384,384]{1,0:T(8,128)(2,1)S(1)}, bf16[384,384]{1,0:T(8,128)(2,1)S(1)}, u32[]{:S(2)}, u32[]{:S(2)}) collective-permute-start(bf16[384,384]{1,0:T(8,128)(2,1)S(1)} %copy-done.36), channel_id=1, source_target_pairs={{0,8},{4,12},{8,0},{12,4},{16,24},{20,28},{24,16},{28,20},{1,9},{5... | collective-permute-start | bytes 884744 | tf_op jit(solution)/shard_map/ppermute | solution.py:1302
  141.8 22.3 %collective-permute-start.22 = (bf16[384,384]{1,0:T(8,128)(2,1)S(1)}, bf16[384,384]{1,0:T(8,128)(2,1)S(1)}, u32[]{:S(2)}, u32[]{:S(2)}) collective-permute-start(bf16[384,384]{1,0:T(8,128)(2,1)S(1)} %get-tuple-element.187), channel_id=1, source_target_pairs={{0,8},{4,12},{8,0},{12,4},{16,24},{20,28},{24,16},{28,20},{1,9},{5... | collective-permute-start | bytes 884744 | tf_op jit(solution)/shard_map/ppermute | solution.py:1302
  142.7 28.6 %collective-permute-start.23 = (bf16[384,384]{1,0:T(8,128)(2,1)S(1)}, bf16[384,384]{1,0:T(8,128)(2,1)S(1)}, u32[]{:S(2)}, u32[]{:S(2)}) collective-permute-start(bf16[384,384]{1,0:T(8,128)(2,1)S(1)} %get-tuple-element.188), channel_id=1, source_target_pairs={{0,12},{4,8},{8,4},{12,0},{16,28},{20,24},{24,20},{28,16},{1,13},{... | collective-permute-start | bytes 884744 | tf_op jit(solution)/shard_map/ppermute | solution.py:1302
  160.6 27.6 %collective-permute-start.18 = (bf16[384,384]{1,0:T(8,128)(2,1)S(1)}, bf16[384,384]{1,0:T(8,128)(2,1)S(1)}, u32[]{:S(2)}, u32[]{:S(2)}) collective-permute-start(bf16[384,384]{1,0:T(8,128)(2,1)S(1)} %get-tuple-element.180), channel_id=1, source_target_pairs={{0,4},{4,0},{8,12},{12,8},{16,20},{20,16},{24,28},{28,24},{1,5},{5... | collective-permute-start | bytes 884744 | tf_op jit(solution)/shard_map/ppermute | solution.py:1302
  160.7 29.7 %collective-permute-start.19 = (bf16[384,384]{1,0:T(8,128)(2,1)S(1)}, bf16[384,384]{1,0:T(8,128)(2,1)S(1)}, u32[]{:S(2)}, u32[]{:S(2)}) collective-permute-start(bf16[384,384]{1,0:T(8,128)(2,1)S(1)} %get-tuple-element.181), channel_id=1, source_target_pairs={{0,8},{4,12},{8,0},{12,4},{16,24},{20,28},{24,16},{28,20},{1,9},{5... | collective-permute-start | bytes 884744 | tf_op jit(solution)/shard_map/ppermute | solution.py:1302
  161.6 29.6 %collective-permute-start.20 = (bf16[384,384]{1,0:T(8,128)(2,1)S(1)}, bf16[384,384]{1,0:T(8,128)(2,1)}, u32[]{:S(2)}, u32[]{:S(2)}) collective-permute-start(bf16[384,384]{1,0:T(8,128)(2,1)S(1)} %get-tuple-element.182), channel_id=1, source_target_pairs={{0,12},{4,8},{8,4},{12,0},{16,28},{20,24},{24,20},{28,16},{1,13},{... | collective-permute-start | bytes 884744 | tf_op jit(solution)/shard_map/ppermute | solution.py:1302
  251.9 23.1 %collective-permute-start.37 = (bf16[384,384]{1,0:T(8,128)(2,1)}, bf16[384,384]{1,0:T(8,128)(2,1)}, u32[]{:S(2)}, u32[]{:S(2)}) collective-permute-start(bf16[384,384]{1,0:T(8,128)(2,1)} %get-tuple-element.221), channel_id=1, source_target_pairs={{0,4},{4,0},{8,12},{12,8},{16,20},{20,16},{24,28},{28,24},{1,5},{5... | collective-permute-start | bytes 884744 | tf_op jit(solution)/shard_map/ppermute | solution.py:1302
  252.4 22.5 %collective-permute-start.38 = (bf16[384,384]{1,0:T(8,128)(2,1)}, bf16[384,384]{1,0:T(8,128)(2,1)}, u32[]{:S(2)}, u32[]{:S(2)}) collective-permute-start(bf16[384,384]{1,0:T(8,128)(2,1)} %get-tuple-element.222), channel_id=1, source_target_pairs={{0,8},{4,12},{8,0},{12,4},{16,24},{20,28},{24,16},{28,20},{1,9},{5... | collective-permute-start | bytes 884744 | tf_op jit(solution)/shard_map/ppermute | solution.py:1302
  253.2 21.7 %collective-permute-start.39 = (bf16[384,384]{1,0:T(8,128)(2,1)}, bf16[384,384]{1,0:T(8,128)(2,1)}, u32[]{:S(2)}, u32[]{:S(2)}) collective-permute-start(bf16[384,384]{1,0:T(8,128)(2,1)} %get-tuple-element.223), channel_id=1, source_target_pairs={{0,12},{4,8},{8,4},{12,0},{16,28},{20,24},{24,20},{28,16},{1,13},{... | collective-permute-start | bytes 884744 | tf_op jit(solution)/shard_map/ppermute | solution.py:1302
  272.6 30.9 %collective-permute-start.40 = (bf16[2,2,2,384,384]{4,3,2,1,0:T(8,128)(2,1)}, bf16[2,2,2,384,384]{4,3,2,1,0:T(8,128)(2,1)}, u32[]{:S(2)}, u32[]{:S(2)}) collective-permute-start(bf16[2,2,2,384,384]{4,3,2,1,0:T(8,128)(2,1)} %get-tuple-element.233), channel_id=1, source_target_pairs={{0,1},{1,0},{2,3},{3,2},{4,5},{5,4},{6,7},{7,6},{8,9},{9,8},{10,11... | collective-permute-start | bytes 7077896 | tf_op jit(solution)/shard_map/ppermute | solution.py:1302
  298.6 45.3 %collective-permute-start.44 = (bf16[2,2,2,384,384]{4,3,2,1,0:T(8,128)(2,1)}, bf16[2,2,2,384,384]{4,3,2,1,0:T(8,128)(2,1)}, u32[]{:S(2)}, u32[]{:S(2)}) collective-permute-start(bf16[2,2,2,384,384]{4,3,2,1,0:T(8,128)(2,1)} %get-tuple-element.252), channel_id=1, source_target_pairs={{0,1},{1,0},{2,3},{3,2},{4,5},{5,4},{6,7},{7,6},{8,9},{9,8},{10,11... | collective-permute-start | bytes 7077896 | tf_op jit(solution)/shard_map/ppermute | solution.py:1302
  299.2 26.7 %collective-permute-start.43 = (bf16[2,192,768]{2,1,0:T(8,128)(2,1)S(1)}, bf16[2,192,768]{2,1,0:T(8,128)(2,1)S(1)}, u32[]{:S(2)}, u32[]{:S(2)}) collective-permute-start(bf16[2,192,768]{2,1,0:T(8,128)(2,1)S(1)} %pad_maximum_fusion.5), channel_id=1, source_target_pairs={{0,12},{4,8},{8,4},{12,0},{16,28},{20,24},{24,20},{28,16},{1,13},{... | collective-permute-start | bytes 1769480 | tf_op jit(solution)/shard_map/ppermute | solution.py:1302
  300.2 27.9 %collective-permute-start.42 = (bf16[2,192,768]{2,1,0:T(8,128)(2,1)S(1)}, bf16[2,192,768]{2,1,0:T(8,128)(2,1)S(1)}, u32[]{:S(2)}, u32[]{:S(2)}) collective-permute-start(bf16[2,192,768]{2,1,0:T(8,128)(2,1)S(1)} %pad_maximum_fusion.4), channel_id=1, source_target_pairs={{0,8},{4,12},{8,0},{12,4},{16,24},{20,28},{24,16},{28,20},{1,9},{5... | collective-permute-start | bytes 1769480 | tf_op jit(solution)/shard_map/ppermute | solution.py:1302
  307.3 33.5 %collective-permute-start.45 = (bf16[2,1,2,384,384]{4,3,2,1,0:T(8,128)(2,1)}, bf16[2,1,2,384,384]{4,3,2,1,0:T(8,128)(2,1)}, u32[]{:S(2)}, u32[]{:S(2)}) collective-permute-start(bf16[2,1,2,384,384]{4,3,2,1,0:T(8,128)(2,1)} %get-tuple-element.242.refs_10_), channel_id=1, source_target_pairs={{0,2},{1,3},{2,0},{3,1},{4,6},{5,7},{6,4},{7,5},{8,10},{9,11},{10,... | collective-permute-start | bytes 3538952 | tf_op jit(solution)/shard_map/ppermute | solution.py:1302
  326.0 39.3 %collective-permute-start.48 = (bf16[576,384]{1,0:T(8,128)(2,1)S(1)}, bf16[576,384]{1,0:T(8,128)(2,1)S(1)}, u32[]{:S(2)}, u32[]{:S(2)}) collective-permute-start(bf16[576,384]{1,0:T(8,128)(2,1)S(1)} %get-tuple-element.403), channel_id=1, source_target_pairs={{0,3},{1,0},{2,1},{3,2},{4,7},{5,4},{6,5},{7,6},{8,11},{9,8},{10,9... | collective-permute-start | bytes 1327112 | tf_op jit(solution)/shard_map/ppermute | solution.py:38
  331.4 26.5 %collective-permute-start.46 = (bf16[192,768]{1,0:T(8,128)(2,1)S(1)}, bf16[192,768]{1,0:T(8,128)(2,1)S(1)}, u32[]{:S(2)}, u32[]{:S(2)}) collective-permute-start(bf16[192,768]{1,0:T(8,128)(2,1)S(1)} %get-tuple-element.258), channel_id=1, source_target_pairs={{0,16},{4,20},{8,24},{12,28},{16,0},{20,4},{24,8},{28,12},{1,17},{... | collective-permute-start | bytes 884744 | tf_op jit(solution)/shard_map/ppermute | solution.py:1302
  347.6 41.7 %collective-permute-start.49 = (bf16[2,1,2,384,384]{4,3,2,1,0:T(8,128)(2,1)}, bf16[2,1,2,384,384]{4,3,2,1,0:T(8,128)(2,1)S(1)}, u32[]{:S(2)}, u32[]{:S(2)}) collective-permute-start(bf16[2,1,2,384,384]{4,3,2,1,0:T(8,128)(2,1)} %get-tuple-element.256.refs_13_), channel_id=1, source_target_pairs={{0,2},{1,3},{2,0},{3,1},{4,6},{5,7},{6,4},{7,5},{8,10},{9,11},{10,... | collective-permute-start | bytes 3538952 | tf_op jit(solution)/shard_map/ppermute | solution.py:1302
  358.0 25.1 %collective-permute-start.72 = (bf16[192,768]{1,0:T(8,128)(2,1)S(1)}, bf16[192,768]{1,0:T(8,128)(2,1)S(1)}, u32[]{:S(2)}, u32[]{:S(2)}) collective-permute-start(bf16[192,768]{1,0:T(8,128)(2,1)S(1)} %add_halves.9.refs_4_), channel_id=1, source_target_pairs={{0,2},{1,3},{2,0},{3,1},{4,6},{5,7},{6,4},{7,5},{8,10},{9,11},{10,... | collective-permute-start | bytes 884744 | tf_op jit(solution)/shard_map/ppermute | solution.py:1302
  358.7 36.5 %collective-permute-start.73 = (bf16[192,768]{1,0:T(8,128)(2,1)S(1)}, bf16[192,768]{1,0:T(8,128)(2,1)S(1)}, u32[]{:S(2)}, u32[]{:S(2)}) collective-permute-start(bf16[192,768]{1,0:T(8,128)(2,1)S(1)} %add_halves.9.refs_4_), channel_id=1, source_target_pairs={{0,1},{1,0},{2,3},{3,2},{4,5},{5,4},{6,7},{7,6},{8,9},{9,8},{10,11... | collective-permute-start | bytes 884744 | tf_op jit(solution)/shard_map/ppermute | solution.py:1302
  358.7 29.2 %collective-permute-start.50 = (bf16[2,384,384]{2,1,0:T(8,128)(2,1)S(1)}, bf16[2,384,384]{2,1,0:T(8,128)(2,1)S(1)}, u32[]{:S(2)}, u32[]{:S(2)}) collective-permute-start(bf16[2,384,384]{2,1,0:T(8,128)(2,1)S(1)} %get-tuple-element.255.refs_2_), channel_id=1, source_target_pairs={{0,16},{4,20},{8,24},{12,28},{16,0},{20,4},{24,8},{28,12},{1,17},{... | collective-permute-start | bytes 1769480 | tf_op jit(solution)/shard_map/ppermute | solution.py:1302
  393.2 28.3 %collective-permute-start.51 = (bf16[2,384,384]{2,1,0:T(8,128)(2,1)S(1)}, bf16[2,384,384]{2,1,0:T(8,128)(2,1)S(1)}, u32[]{:S(2)}, u32[]{:S(2)}) collective-permute-start(bf16[2,384,384]{2,1,0:T(8,128)(2,1)S(1)} %get-tuple-element.275.refs_15_), channel_id=1, source_target_pairs={{0,16},{4,20},{8,24},{12,28},{16,0},{20,4},{24,8},{28,12},{1,17},{... | collective-permute-start | bytes 1769480 | tf_op jit(solution)/shard_map/ppermute | solution.py:1302
  396.2 42.1 %collective-permute-start.60 = (bf16[2,384,384]{2,1,0:T(8,128)(2,1)S(1)}, bf16[2,384,384]{2,1,0:T(8,128)(2,1)S(1)}, u32[]{:S(2)}, u32[]{:S(2)}) collective-permute-start(bf16[2,384,384]{2,1,0:T(8,128)(2,1)S(1)} %add_halves.10.refs_2_.refs_1_), channel_id=1, source_target_pairs={{0,2},{1,3},{2,0},{3,1},{4,6},{5,7},{6,4},{7,5},{8,10},{9,11},{10,... | collective-permute-start | bytes 1769480 | tf_op jit(solution)/shard_map/ppermute | solution.py:1302
  447.0 38.4 %collective-permute-start.69 = (bf16[2,384,384]{2,1,0:T(8,128)(2,1)}, bf16[2,384,384]{2,1,0:T(8,128)(2,1)}, u32[]{:S(2)}, u32[]{:S(2)}) collective-permute-start(bf16[2,384,384]{2,1,0:T(8,128)(2,1)} %add_halves.11.refs_5_.refs_1_), channel_id=1, source_target_pairs={{0,2},{1,3},{2,0},{3,1},{4,6},{5,7},{6,4},{7,5},{8,10},{9,11},{10,... | collective-permute-start | bytes 1769480 | tf_op jit(solution)/shard_map/ppermute | solution.py:1302
  448.0 41.0 %collective-permute-start.70 = (bf16[2,384,384]{2,1,0:T(8,128)(2,1)}, bf16[2,384,384]{2,1,0:T(8,128)(2,1)}, u32[]{:S(2)}, u32[]{:S(2)}) collective-permute-start(bf16[2,384,384]{2,1,0:T(8,128)(2,1)} %add_halves.11.refs_5_.refs_1_), channel_id=1, source_target_pairs={{0,1},{1,0},{2,3},{3,2},{4,5},{5,4},{6,7},{7,6},{8,9},{9,8},{10,11... | collective-permute-start | bytes 1769480 | tf_op jit(solution)/shard_map/ppermute | solution.py:1302
  (163 other events, 1406.5 us)
Sparse Core Ops, SparseCore 0:
  102.5 76.1 all-gather.1
